TPU v7x, 256 devices: a whole 4x4x8 slice. The times are simulated.
256 devices in a mesh: section: 2 (over x_lo), dp: 8 (over y, core), tensor: 16 (over z, x_hi).
Axes of the slice: x: 4 (x_hi: 2, x_lo: 2; x = x_hi * 2 + x_lo), y: 4, z: 8, core: 2. Of those that a mesh axis runs over, the one named last changes fastest.
Arguments:
- segment_input: bfloat16 [2, 2048, 12288], P('section', ('dp', 'tensor')), may hold values from -6 to 6
- context: bfloat16 [2, 2048, 6144], P('section', 'dp', 'tensor'), may hold values from -8 to 8
- out_proj: bfloat16 [2, 12288, 6144], P('section', None, 'tensor'), may hold values from -0.078125 to 0.078125
- grad_output: bfloat16 [2, 2048, 12288], P('section', ('dp', 'tensor')), may hold values from -24 to 24
Outputs:
- forward: bfloat16 [2, 2048, 12288], P('section', ('dp', 'tensor'))
- moved: bfloat16 [2, 2048, 12288], P('section', ('dp', 'tensor'))
- context_grad: bfloat16 [2, 2048, 6144], P('section', 'dp', 'tensor')
- proj_grad: bfloat16 [2, 12288, 6144], P('section', 'dp', 'tensor')
All inputs are finite; a program needn't handle non-finite values.
Results may differ from a plain program's by a relative error of at most 0.02.
Values may be sent and summed in bfloat16 or wider, within the bound.
No kernel may reach another device: no remote copies, remote signals or barrier semaphores. Data moves between devices by JAX's collectives and lax.ppermute only.
A program may use at most 128 MiB of HBM per device.

v0:
```python
import math

import jax
import jax.numpy as jnp
from jax import lax
from jax.sharding import PartitionSpec as P


def partner(value, axis, apart):
    return lax.ppermute(value, axis, [(i, i ^ 1 << apart) for i in range(lax.axis_size(axis))])


def shards(segment_input, context, out_proj, grad_output):
    residual = segment_input[0]
    contexts = context[0]
    weights = out_proj[0]
    upstream = grad_output[0]
    own_count = residual.shape[0]
    partial_branch = lax.dot_general(
        contexts, weights, (((1,), (1,)), ((), ())), preferred_element_type=jnp.float32
    )
    summed = lax.psum(partial_branch.astype(jnp.bfloat16), "tensor").astype(jnp.float32)
    own_branch = lax.dynamic_slice_in_dim(
        summed, lax.axis_index("tensor") * own_count, own_count, 0
    )
    forward = (residual.astype(jnp.float32) + own_branch).astype(jnp.bfloat16)
    full_grad = lax.all_gather(upstream, "tensor", axis=0, tiled=True)
    ctx_grad = jnp.dot(full_grad, weights, preferred_element_type=jnp.float32).astype(jnp.bfloat16)
    group_count = lax.axis_size("dp")
    group_tokens = full_grad.shape[0]
    norm_factor = 1.0 / math.sqrt(group_tokens * group_count)
    product = lax.dot_general(
        full_grad, contexts, (((0,), (0,)), ((), ())), preferred_element_type=jnp.float32
    )
    weight_grad = lax.psum_scatter(
        (norm_factor * product).astype(jnp.bfloat16), "dp", scatter_dimension=0, tiled=True
    )
    outgoing = jnp.where(lax.axis_index("section") == 0, forward, upstream)
    received = partner(outgoing, "section", 0)
    return (forward[None], received[None], ctx_grad[None], weight_grad[None])


def solution(mesh):
    in_specs = (
        P("section", ("dp", "tensor"), None),
        P("section", "dp", "tensor"),
        P("section", None, "tensor"),
        P("section", ("dp", "tensor"), None),
    )
    out_specs = (
        P("section", ("dp", "tensor"), None),
        P("section", ("dp", "tensor"), None),
        P("section", "dp", "tensor"),
        P("section", "dp", "tensor"),
    )
    return jax.shard_map(shards, mesh=mesh, in_specs=in_specs, out_specs=out_specs, check_vma=False)
```

profile of v0, /device:TPU:2, one launch (start us, length us, event | category | flops | bytes accessed | tf_op | source)
XLA Modules:
  0.0 487.2 jit_solution(18241544798808945162)
XLA Ops:
  7.2 0.0 copy-start
  7.2 0.0 all-gather.3.cloned.1.call-start
  7.2 0.7 all-gather.3.cloned.1.call-update
  7.9 0.0 all-reduce.2.cloned.1.call-start
  8.0 0.1 copy-done
  8.1 11.5 %convolution_convert_fusion = bf16[256,12288]{1,0:T(8,128)(2,1)} fusion(bf16[1,12288,384]{2,1,0:T(8,128)(2,1)} %param.6, bf16[1,256,384]{2,1,0:T(8,128)(2,1)S(1)} %copy-done), kind=kOutput, calls=%fused_computation.1 | convolution fusion | flops 2419064832 | bytes 15925248 | tf_op jit(solution)/shard_map/dot_general | solution.py:19
  19.6 0.0 all-reduce.2.cloned.1.call-update
  19.6 0.0 reduce-scatter.2.cloned.1.call-start
  19.7 108.8 %all-gather.3.cloned.1.call-done = bf16[1,256,12288]{2,1,0:T(8,128)(2,1)} async-done(((bf16[1,16,12288]{2,1,0:T(8,128)(2,1)}), bf16[1,256,12288]{2,1,0:T(8,128)(2,1)}) %all-gather.3.cloned.1.call-update) | async-done | bytes 6291472 | tf_op jit(solution)/shard_map/all_gather | solution.py:27
  128.5 9.9 %multiply_convert_fusion = bf16[12288,384]{1,0:T(8,128)(2,1)} fusion(bf16[1,256,12288]{2,1,0:T(8,128)(2,1)} %all-gather.3.cloned.1.call-done, bf16[1,256,384]{2,1,0:T(8,128)(2,1)S(1)} %copy-done), kind=kOutput, calls=%fused_computation | convolution fusion | flops 2425356288 | bytes 15925248 | tf_op jit(solution)/shard_map/dot_general | solution.py:32
  138.4 0.0 copy-start.1
  138.4 0.0 copy-start.2
  138.4 0.0 reduce-scatter.2.cloned.1.call-update
  138.4 275.4 %all-reduce.2.cloned.1.call-done = bf16[256,12288]{1,0:T(8,128)(2,1)} async-done(((bf16[256,12288]{1,0:T(8,128)(2,1)}), bf16[256,12288]{1,0:T(8,128)(2,1)}) %all-reduce.2.cloned.1.call-update) | async-done | bytes 6291472 | tf_op jit(solution)/shard_map/psum | solution.py:22
  413.8 0.0 copy-done.1
  413.8 0.0 copy-done.2
  413.8 1.1 bitcast_select_fusion
  414.9 2.1 collective-permute-start
  417.0 1.8 fusion.18
  418.9 6.4 %collective-permute-done = bf16[16,12288]{1,0:T(8,128)(2,1)S(1)} collective-permute-done((bf16[16,12288]{1,0:T(8,128)(2,1)S(1)}, bf16[16,12288]{1,0:T(8,128)(2,1)S(1)}, u32[]{:S(2)}, u32[]{:S(2)}) %collective-permute-start) | collective-permute-done | bytes 393248 | tf_op jit(solution)/shard_map/ppermute | solution.py:10
  425.3 9.6 %fusion.10 = bf16[1,256,384]{2,1,0:T(8,128)(2,1)} fusion(bf16[1,12288,384]{2,1,0:T(8,128)(2,1)} %param.6, bf16[1,256,12288]{2,1,0:T(8,128)(2,1)} %all-gather.3.cloned.1.call-done), kind=kOutput, calls=%fused_computation.8 | convolution fusion | flops 2416017408 | bytes 15925248 | tf_op jit(solution)/shard_map/dot_general | solution.py:28
  434.9 45.0 %reduce-scatter.2.cloned.1.call-done = bf16[1536,384]{1,0:T(8,128)(2,1)} async-done(((bf16[12288,384]{1,0:T(8,128)(2,1)}), bf16[1536,384]{1,0:T(8,128)(2,1)}) %reduce-scatter.2.cloned.1.call-update) | async-done | bytes 1179664 | tf_op jit(solution)/shard_map/reduce_scatter | solution.py:35
  479.9 0.7 copy.10
Async XLA Ops:
  7.2 0.9 copy-start
  7.2 121.3 %all-gather.3.cloned.1.call-start = ((), (), s32[]{:S(2)}) async-start(), calls=%async_computation.3 | async-start | bytes 6684672 | tf_op jit(solution)/shard_map/all_gather | solution.py:27
  7.9 405.9 %all-reduce.2.cloned.1.call-start = ((), (), s32[]{:S(2)}) async-start(), calls=%async_computation.1 | async-start | bytes 12582912 | tf_op jit(solution)/shard_map/psum | solution.py:22
  19.6 460.3 %reduce-scatter.2.cloned.1.call-start = ((), (), s32[]{:S(2)}) async-start(), calls=%async_computation.2 | async-start | bytes 10616832 | tf_op jit(solution)/shard_map/reduce_scatter | solution.py:35
  138.4 275.4 %copy-start.1 = (bf16[1,16,12288]{2,1,0:T(8,128)(2,1)S(1)}, bf16[1,16,12288]{2,1,0:T(8,128)(2,1)}, u32[]{:S(2)}) copy-start(bf16[1,16,12288]{2,1,0:T(8,128)(2,1)} %param.7) | copy-start | bytes 1179652
  138.4 275.4 %copy-start.2 = (bf16[1,16,12288]{2,1,0:T(8,128)(2,1)S(1)}, bf16[1,16,12288]{2,1,0:T(8,128)(2,1)}, u32[]{:S(2)}) copy-start(bf16[1,16,12288]{2,1,0:T(8,128)(2,1)} %param.4) | copy-start | bytes 1179652
  414.9 10.3 %collective-permute-start = (bf16[16,12288]{1,0:T(8,128)(2,1)S(1)}, bf16[16,12288]{1,0:T(8,128)(2,1)S(1)}, u32[]{:S(2)}, u32[]{:S(2)}) collective-permute-start(bf16[16,12288]{1,0:T(8,128)(2,1)S(1)} %bitcast_select_fusion), channel_id=1, source_target_pairs={{0,128},{128,0},{1,129},{129,1},{2,130},{130,2},{3,131},{131,3},{4... | collective-permute-start | bytes 1179656 | tf_op jit(solution)/shard_map/ppermute | solution.py:10
Sparse Core Ops, SparseCore 0:
  10.6 117.8 all-gather.2
  131.1 282.5 all-reduce.1
  416.9 62.9 reduce-scatter.1
where the time goes:
time: 488 us; the launch traced here: 487 us
  waiting for transfers between devices  436 us (89%)
  matrix products  31 us (6%)
  between operations  13.8 us (3%)
    psum x1, waiting for transfers between devices, shards(): lax.psum(partial_branch.astype(jnp.bfloat16), 'tensor').astype(jnp.float32)  275 us
    all_gather x1, waiting for transfers between devices, shards(): full_grad = lax.all_gather(upstream, 'tensor', axis=0, tiled=True)  109 us
    reduce_scatter x1, waiting for transfers between devices, shards(): lax.psum_scatter((norm_factor * product).astype(jnp.bfloat16), 'dp', scat...  45 us
    dot_general x1, matrix products, shards(): lax.dot_general(contexts, weights, (((1,), (1,)), ((), ())), preferred_el...  11.5 us
    dot_general x1, matrix products, shards(): lax.dot_general(full_grad, contexts, (((0,), (0,)), ((), ())), preferred_...  9.88 us
  transfers between devices with their start and end apart: 4, of which 4 were waited for; matrix products, arithmetic and copies ran while one was open for 7% of the time, Pallas kernels for 0%

commit v1 on v0

v1 whole, which is shorter than its diff:
```python
import math

import jax
import jax.numpy as jnp
from jax import lax
from jax.sharding import Mesh
from jax.sharding import PartitionSpec as P

BF16 = jnp.bfloat16
F32 = jnp.float32
GROUP = ("y", "core", "xh")


def shift(value, axis, by):
    n = lax.axis_size(axis)
    return lax.ppermute(value, axis, [(i, (i + by) % n) for i in range(n)])


def swap(value, axis):
    return shift(value, axis, 1)


def add(a, b):
    return (a.astype(F32) + b.astype(F32)).astype(BF16)


def wrap(index, n):
    return index & (n - 1)


def pick(stack, index):
    return lax.dynamic_index_in_dim(stack, index, 0, keepdims=False)


def place(buffer, block, starts):
    return lax.dynamic_update_slice(buffer, block, starts)


def ring_sum(chunk_of, position, axis):
    n = lax.axis_size(axis)
    far = n // 2
    opposite = chunk_of(wrap(position + far, n))
    half = opposite.shape[-1] // 2
    right = shift(opposite[..., :half], axis, 1)
    left = shift(opposite[..., half:], axis, -1)
    for away in range(far - 1, 0, -1):
        ahead = chunk_of(wrap(position + away, n))
        behind = chunk_of(wrap(position - away, n))
        if away == far - 1:
            right = jnp.concatenate([add(ahead[..., :half], right), ahead[..., half:]], -1)
            left = jnp.concatenate([behind[..., :half], add(behind[..., half:], left)], -1)
        else:
            right = add(ahead, right)
            left = add(behind, left)
        right = shift(right, axis, 1)
        left = shift(left, axis, -1)
    own = chunk_of(position)
    return (own.astype(F32) + right.astype(F32) + left.astype(F32)).astype(BF16)


def ring_gather(block, axis):
    n = lax.axis_size(axis)
    far = n // 2
    half = block.shape[0] // 2
    blocks = {0: block}
    right = left = block
    for away in range(1, far):
        right = shift(right, axis, 1)
        left = shift(left, axis, -1)
        blocks[-away] = right
        blocks[away] = left
    blocks[far] = jnp.concatenate([shift(right[:half], axis, 1), shift(left[half:], axis, -1)], 0)
    return blocks


def shards(segment_input, context, out_proj, grad_output):
    residual = segment_input[0]
    contexts = context[0]
    weights = out_proj[0]
    upstream = grad_output[0]
    y, core, z, xh = (lax.axis_index(name) for name in ("y", "core", "z", "xh"))
    n_y, n_core, n_z, n_xh = (lax.axis_size(name) for name in ("y", "core", "z", "xh"))
    n_group = n_y * n_core * n_xh
    own_count, model = upstream.shape
    group_tokens, width = contexts.shape
    features = model // n_group
    tokens = group_tokens * n_y * n_core
    z_tokens = own_count * n_xh

    both = jnp.concatenate([contexts, swap(contexts, "xh")], 1)
    row = (y * n_core + core) * n_xh
    own_rows = lax.dynamic_slice_in_dim(weights, (row + xh) * features, features, 0)
    partner_rows = lax.dynamic_slice_in_dim(weights, (row + 1 - xh) * features, features, 0)
    block = jnp.concatenate([own_rows, swap(partner_rows, "xh")], 1)

    spread = upstream.reshape(own_count, n_group, features).transpose(1, 0, 2)
    spread = lax.all_to_all(spread, GROUP, 0, 0, tiled=True)
    grad_blocks = ring_gather(spread.reshape(n_group * own_count, features), "z")

    ctx_all = jnp.zeros((n_z, n_y, n_core, z_tokens, 2 * width), BF16)
    for away, piece in ring_gather(both, "y").items():
        there = wrap(y + away, n_y)
        for at, part in ((core, piece), (1 - core, swap(piece, "core"))):
            ctx_all = place(ctx_all, part.reshape(n_z, 1, 1, z_tokens, 2 * width), (0, there, at, 0, 0))
    ctx_flat = ctx_all.reshape(tokens, 2 * width)

    partial_branch = lax.dot_general(
        ctx_flat, block, (((1,), (1,)), ((), ())), preferred_element_type=F32
    ).astype(BF16).reshape(n_z, tokens // n_z, features)
    branch = ring_sum(lambda at: pick(partial_branch, at), z, "z")
    branch = lax.all_to_all(branch.reshape(n_group, own_count, features), GROUP, 0, 0, tiled=True)
    branch = branch.transpose(1, 0, 2).reshape(own_count, model)
    forward = add(residual, branch)
    outgoing = jnp.where(lax.axis_index("section") == 0, forward, upstream)
    received = swap(outgoing, "section")

    grad_all = jnp.zeros((n_z, tokens // n_z, features), BF16)
    for away, piece in grad_blocks.items():
        grad_all = place(grad_all, piece[None], (wrap(z + away, n_z), 0, 0))
    grad_flat = grad_all.reshape(tokens, features)

    partial_ctx = jnp.dot(grad_flat, block, preferred_element_type=F32).astype(BF16)
    partial_ctx = partial_ctx.reshape(n_z, n_y, n_core, z_tokens, 2 * width)
    other = lax.dynamic_index_in_dim(partial_ctx, 1 - core, 2, keepdims=False)
    mine = lax.dynamic_index_in_dim(partial_ctx, core, 2, keepdims=False)
    by_y = add(mine, swap(other, "core"))
    summed = ring_sum(lambda at: lax.dynamic_index_in_dim(by_y, at, 1, keepdims=False), y, "y")
    summed = summed.reshape(group_tokens, 2 * width)
    ctx_grad = add(summed[:, :width], swap(summed[:, width:], "xh"))

    norm_factor = 1.0 / math.sqrt(tokens)
    product = lax.dot_general(grad_flat, ctx_flat, (((0,), (0,)), ((), ())), preferred_element_type=F32)
    product = (norm_factor * product).astype(BF16)
    kept = product[:, :width]
    came = swap(product[:, width:], "xh")
    first = xh == 0
    weight_grad = jnp.concatenate([jnp.where(first, kept, came), jnp.where(first, came, kept)], 0)
    return (forward[None], received[None], ctx_grad[None], weight_grad[None])


def solution(mesh):
    fine = Mesh(mesh.devices.reshape(2, 4, 2, 8, 2), ("section", "y", "core", "z", "xh"))
    tokens = P("section", ("y", "core", "z", "xh"), None)
    heads = P("section", ("y", "core"), ("z", "xh"))
    return jax.shard_map(
        shards,
        mesh=fine,
        in_specs=(tokens, heads, P("section", None, ("z", "xh")), tokens),
        out_specs=(tokens, tokens, heads, heads),
        check_vma=False,
    )
```

time: 488 us -> 169 us (0.35)
  waiting for transfers between devices: 436 us -> 67.3 us
  starting transfers between devices: 2.24 us -> 62.5 us
  matrix products: 31 us -> 9.42 us
  between operations: 13.8 us -> 1.23 us
  local copies, waits for them, and re-layouts: 0.9 us -> 12.9 us
  other arithmetic: 2.97 us -> 14.8 us
    psum x1 -> x0, waiting for transfers between devices: 275 us -> none  [shards(): lax.psum(partial_branch.astype(jnp.bfloat16), 'tensor').astype(jnp.float32)]
    all_gather x1 -> x0, waiting for transfers between devices: 109 us -> none  [shards(): full_grad = lax.all_gather(upstream, 'tensor', axis=0, tiled=True)]
    ppermute x1 -> x34, waiting for transfers between devices: 6.38 us -> 62.9 us  [shift(): return lax.ppermute(value, axis, [(i, (i + by) % n) for i in range(n)])]
    ppermute x1 -> x34, starting transfers between devices: 2.12 us -> 52.3 us  [shift(): return lax.ppermute(value, axis, [(i, (i + by) % n) for i in range(n)])]
    reduce_scatter x1 -> x0, waiting for transfers between devices: 45 us -> none  [shards(): lax.psum_scatter((norm_factor * product).astype(jnp.bfloat16), 'dp', scat...]
    dot_general x3, matrix products: 31 us -> 9.42 us  [the longest x1 3.93 us: shards(): lax.dot_general(ctx_flat, block, (((1,), (1,)), ((), ())), preferred_elem...]
    all_to_all x0 -> x2, starting transfers between devices: none -> 10.1 us  [the longest x1 5.42 us: shards(): spread = lax.all_to_all(spread, GROUP, 0, 0, tiled=True)]
    convert_element_type x0 -> x11, other arithmetic: none -> 7.86 us  [the longest x9 5.68 us: add(): return (a.astype(F32) + b.astype(F32)).astype(BF16)]
  transfers between devices with their start and end apart: 4 -> 36, of which waited for: 4 -> 13; matrix products, arithmetic and copies ran while one was open for 7% -> 20% of each run, Pallas kernels for 0% -> 0%
where the time goes in v1:
time: 169 us; the launch traced here: 168 us
  waiting for transfers between devices  67.3 us (40%)
  starting transfers between devices  62.5 us (37%)
  other arithmetic  14.8 us (9%)
  local copies, waits for them, and re-layouts  12.9 us (8%)
  matrix products  9.42 us (6%)
    ppermute x34, waiting for transfers between devices, shift(): return lax.ppermute(value, axis, [(i, (i + by) % n) for i in range(n)])  62.9 us
    ppermute x34, starting transfers between devices, shift(): return lax.ppermute(value, axis, [(i, (i + by) % n) for i in range(n)])  52.3 us
    convert_element_type x9, other arithmetic, add(): return (a.astype(F32) + b.astype(F32)).astype(BF16)  5.68 us
    all_to_all x1, starting transfers between devices, shards(): spread = lax.all_to_all(spread, GROUP, 0, 0, tiled=True)  5.42 us
    all_to_all x1, starting transfers between devices, shards(): lax.all_to_all(branch.reshape(n_group, own_count, features), GROUP, 0, 0,...  4.72 us
    unnamed x21, local copies, waits for them, and re-layouts  4.62 us
    all_to_all x1, waiting for transfers between devices, shards(): lax.all_to_all(branch.reshape(n_group, own_count, features), GROUP, 0, 0,...  4.32 us
    dot_general x1, matrix products, shards(): lax.dot_general(ctx_flat, block, (((1,), (1,)), ((), ())), preferred_elem...  3.93 us
  transfers between devices with their start and end apart: 36, of which 13 were waited for; matrix products, arithmetic and copies ran while one was open for 20% of the time, Pallas kernels for 0%

profile of v1, /device:TPU:2, one launch (start us, length us, event | category | flops | bytes accessed | tf_op | source)
XLA Modules:
  0.0 168.1 jit_solution(17508561699398972338)
XLA Ops:
  0.6 2.2 %collective-permute-start = (bf16[256,384]{1,0:T(8,128)(2,1)}, bf16[256,384]{1,0:T(8,128)(2,1)S(1)}, u32[]{:S(2)}, u32[]{:S(2)}) collective-permute-start(bf16[256,384]{1,0:T(8,128)(2,1)} %bitcast.126), channel_id=1, source_target_pairs={{0,1},{1,0},{2,3},{3,2},{4,5},{5,4},{6,7},{7,6},{8,9},{9,8},{10,11... | collective-permute-start | bytes 589832 | tf_op jit(solution)/shard_map/ppermute | solution.py:16
  2.8 1.1 copy.18
  3.9 0.9 copy.16
  4.8 5.4 %all-to-all-start.1 = ((bf16[16,16,768]{2,1,0:T(8,128)(2,1)}), bf16[16,16,768]{2,1,0:T(8,128)(2,1)S(1)}, u32[]{:S(2)}, u32[]{:S(2)}) async-start(bf16[16,16,768]{2,1,0:T(8,128)(2,1)} %copy.16), calls=%async_computation.1 | async-start | bytes 786432 | tf_op jit(solution)/shard_map/all_to_all | solution.py:97
  10.2 1.0 pad_maximum_fusion.3
  11.2 2.0 %collective-permute-start.2 = (bf16[256,768]{1,0:T(8,128)(2,1)S(1)}, bf16[256,768]{1,0:T(8,128)(2,1)S(1)}, u32[]{:S(2)}, u32[]{:S(2)}) collective-permute-start(bf16[256,768]{1,0:T(8,128)(2,1)S(1)} %pad_maximum_fusion.3), channel_id=1, source_target_pairs={{0,32},{32,64},{64,96},{96,0},{1,33},{33,65},{65,97},{97,1},{2,34}... | collective-permute-start | bytes 1179656 | tf_op jit(solution)/shard_map/ppermute | solution.py:16
  13.2 1.3 collective-permute-start.4
  14.6 2.2 %dynamic-slice_bitcast_fusion.2 = (bf16[768,384]{1,0:T(8,128)(2,1)}, bf16[768,384]{1,0:T(8,128)(2,1)S(1)}) fusion(bf16[1,12288,384]{2,1,0:T(8,128)(2,1)} %param.6, s32[]{:T(128)S(6)} %select_n.105, s32[]{:T(128)S(6)} %select_n.106), kind=kLoop, calls=%fused_computation.30 | loop fusion | bytes 2359304 | tf_op jit(solution)/shard_map/dynamic_slice | solution.py:92
  16.7 3.4 %collective-permute-start.9 = (bf16[768,384]{1,0:T(8,128)(2,1)S(1)}, bf16[768,384]{1,0:T(8,128)(2,1)S(1)}, u32[]{:S(2)}, u32[]{:S(2)}) collective-permute-start(bf16[768,384]{1,0:T(8,128)(2,1)S(1)} %get-tuple-element.5), channel_id=1, source_target_pairs={{0,1},{1,0},{2,3},{3,2},{4,5},{5,4},{6,7},{7,6},{8,9},{9,8},{10,11... | collective-permute-start | bytes 1769480 | tf_op jit(solution)/shard_map/ppermute | solution.py:16
  20.2 1.9 %collective-permute-start.19 = (bf16[256,768]{1,0:T(8,128)(2,1)S(1)}, bf16[256,768]{1,0:T(8,128)(2,1)S(1)}, u32[]{:S(2)}, u32[]{:S(2)}) collective-permute-start(bf16[256,768]{1,0:T(8,128)(2,1)S(1)} %bitcast.118), channel_id=1, source_target_pairs={{0,2},{2,4},{4,6},{6,8},{8,10},{10,12},{12,14},{14,0},{1,3},{3,5},... | collective-permute-start | bytes 1179656 | tf_op jit(solution)/shard_map/ppermute | solution.py:16
  22.1 0.4 broadcast_in_dim.37
  22.8 4.4 %collective-permute-done.2 = bf16[256,768]{1,0:T(8,128)(2,1)S(1)} collective-permute-done((bf16[256,768]{1,0:T(8,128)(2,1)S(1)}, bf16[256,768]{1,0:T(8,128)(2,1)S(1)}, u32[]{:S(2)}, u32[]{:S(2)}) %collective-permute-start.2) | collective-permute-done | bytes 393248 | tf_op jit(solution)/shard_map/ppermute | solution.py:16
  27.2 5.9 %collective-permute-start.20 = (bf16[256,768]{1,0:T(8,128)(2,1)S(1)}, bf16[256,768]{1,0:T(8,128)(2,1)S(1)}, u32[]{:S(2)}, u32[]{:S(2)}) collective-permute-start(bf16[256,768]{1,0:T(8,128)(2,1)S(1)} %bitcast.120), channel_id=1, source_target_pairs={{0,14},{2,0},{4,2},{6,4},{8,6},{10,8},{12,10},{14,12},{1,15},{3,1}... | collective-permute-start | bytes 1179656 | tf_op jit(solution)/shard_map/ppermute | solution.py:16
  33.2 3.3 %collective-permute-start.7 = (bf16[128,768]{1,0:T(8,128)(2,1)S(1)}, bf16[128,768]{1,0:T(8,128)(2,1)S(1)}, u32[]{:S(2)}, u32[]{:S(2)}) collective-permute-start(bf16[128,768]{1,0:T(8,128)(2,1)S(1)} %slice.81), channel_id=1, source_target_pairs={{0,96},{32,0},{64,32},{96,64},{1,97},{33,1},{65,33},{97,65},{2,98}... | collective-permute-start | bytes 589832 | tf_op jit(solution)/shard_map/ppermute | solution.py:16
  36.7 4.6 %collective-permute-done.20 = bf16[256,768]{1,0:T(8,128)(2,1)S(1)} collective-permute-done((bf16[256,768]{1,0:T(8,128)(2,1)S(1)}, bf16[256,768]{1,0:T(8,128)(2,1)S(1)}, u32[]{:S(2)}, u32[]{:S(2)}) %collective-permute-start.20) | collective-permute-done | bytes 393248 | tf_op jit(solution)/shard_map/ppermute | solution.py:16
  41.5 3.8 %collective-permute-start.22 = (bf16[256,768]{1,0:T(8,128)(2,1)S(1)}, bf16[256,768]{1,0:T(8,128)(2,1)S(1)}, u32[]{:S(2)}, u32[]{:S(2)}) collective-permute-start(bf16[256,768]{1,0:T(8,128)(2,1)S(1)} %collective-permute-done.20), channel_id=1, source_target_pairs={{0,14},{2,0},{4,2},{6,4},{8,6},{10,8},{12,10},{14,12},{1,15},{3,1}... | collective-permute-start | bytes 1179656 | tf_op jit(solution)/shard_map/ppermute | solution.py:16
  45.3 0.3 collective-permute-start.8
  45.8 9.1 %collective-permute-done.21 = bf16[256,768]{1,0:T(8,128)(2,1)S(1)} collective-permute-done((bf16[256,768]{1,0:T(8,128)(2,1)S(1)}, bf16[256,768]{1,0:T(8,128)(2,1)S(1)}, u32[]{:S(2)}, u32[]{:S(2)}) %collective-permute-start.21) | collective-permute-done | bytes 393248 | tf_op jit(solution)/shard_map/ppermute | solution.py:16
  54.9 3.2 %collective-permute-start.24 = (bf16[256,768]{1,0:T(8,128)(2,1)S(1)}, bf16[256,768]{1,0:T(8,128)(2,1)S(1)}, u32[]{:S(2)}, u32[]{:S(2)}) collective-permute-start(bf16[256,768]{1,0:T(8,128)(2,1)S(1)} %collective-permute-done.22), channel_id=1, source_target_pairs={{0,14},{2,0},{4,2},{6,4},{8,6},{10,8},{12,10},{14,12},{1,15},{3,1}... | collective-permute-start | bytes 1179656 | tf_op jit(solution)/shard_map/ppermute | solution.py:16
  58.3 0.8 copy-done.7
  59.1 3.9 %convolution_convert_fusion.1 = bf16[2048,768]{1,0:T(8,128)(2,1)S(1)} fusion(bf16[2048,768]{1,0:T(8,128)(2,1)S(1)} %bitcast.109, bf16[768,384]{1,0:T(8,128)(2,1)} %copy-done.7, bf16[768,384]{1,0:T(8,128)(2,1)S(1)} %copy-done.5), kind=kOutput, calls=%fused_computation.1 | convolution fusion | flops 2419851264 | bytes 7471104 | tf_op jit(solution)/shard_map/dot_general | solution.py:107
  63.2 0.6 collective-permute-start.14
  63.8 1.6 collective-permute-start.10
  65.4 5.1 %collective-permute-done.14 = bf16[256,384]{1,0:T(8,128)(2,1)S(1)} collective-permute-done((bf16[256,384]{1,0:T(8,128)(2,1)S(1)}, bf16[256,384]{1,0:T(8,128)(2,1)S(1)}, u32[]{:S(2)}, u32[]{:S(2)}) %collective-permute-start.14) | collective-permute-done | bytes 196640 | tf_op jit(solution)/shard_map/ppermute | solution.py:16
  70.7 3.8 %collective-permute-start.15 = (bf16[256,768]{1,0:T(8,128)(2,1)S(1)}, bf16[256,768]{1,0:T(8,128)(2,1)S(1)}, u32[]{:S(2)}, u32[]{:S(2)}) collective-permute-start(bf16[256,768]{1,0:T(8,128)(2,1)S(1)} %pad_maximum_fusion.5), channel_id=1, source_target_pairs={{0,14},{2,0},{4,2},{6,4},{8,6},{10,8},{12,10},{14,12},{1,15},{3,1}... | collective-permute-start | bytes 1179656 | tf_op jit(solution)/shard_map/ppermute | solution.py:16
  74.8 3.3 %collective-permute-start.26 = (bf16[128,768]{1,0:T(8,128)(2,1)S(1)}, bf16[128,768]{1,0:T(8,128)(2,1)S(1)}, u32[]{:S(2)}, u32[]{:S(2)}) collective-permute-start(bf16[128,768]{1,0:T(8,128)(2,1)S(1)} %slice.89), channel_id=1, source_target_pairs={{0,14},{2,0},{4,2},{6,4},{8,6},{10,8},{12,10},{14,12},{1,15},{3,1}... | collective-permute-start | bytes 589832 | tf_op jit(solution)/shard_map/ppermute | solution.py:16
  78.2 11.4 %collective-permute-done.25 = bf16[128,768]{1,0:T(8,128)(2,1)S(1)} collective-permute-done((bf16[128,768]{1,0:T(8,128)(2,1)S(1)}, bf16[128,768]{1,0:T(8,128)(2,1)S(1)}, u32[]{:S(2)}, u32[]{:S(2)}) %collective-permute-start.25) | collective-permute-done | bytes 196640 | tf_op jit(solution)/shard_map/ppermute | solution.py:16
  89.8 2.8 %convolution_convert_fusion = bf16[2048,768]{1,0:T(8,128)(2,1)S(1)} fusion(bf16[2048,768]{1,0:T(8,128)(2,1)S(1)} %bitcast.107, bf16[768,384]{1,0:T(8,128)(2,1)S(1)} %copy-done.8, bf16[768,384]{1,0:T(8,128)(2,1)S(1)} %copy-done.5), kind=kOutput, calls=%fused_computation | convolution fusion | flops 2419851264 | bytes 7471104 | tf_op jit(solution)/shard_map/dot_general | solution.py:122
  92.6 1.4 dynamic-slice_bitcast_fusion
  94.1 5.5 %collective-permute-done.12 = bf16[256,768]{1,0:T(8,128)(2,1)S(1)} collective-permute-done((bf16[256,768]{1,0:T(8,128)(2,1)S(1)}, bf16[256,768]{1,0:T(8,128)(2,1)S(1)}, u32[]{:S(2)}, u32[]{:S(2)}) %collective-permute-start.12) | collective-permute-done | bytes 393248 | tf_op jit(solution)/shard_map/ppermute | solution.py:16
  99.5 1.1 fusion.9
  100.6 2.7 %multiply_convert_fusion = bf16[768,768]{1,0:T(8,128)(2,1)S(1)} fusion(bf16[2048,768]{1,0:T(8,128)(2,1)S(1)} %bitcast.108, bf16[2048,768]{1,0:T(8,128)(2,1)S(1)} %bitcast.110), kind=kOutput, calls=%fused_computation.4 | convolution fusion | flops 2417098752 | bytes 7471104 | tf_op jit(solution)/shard_map/dot_general | solution.py:132
  103.3 0.9 slice.99
  104.5 3.0 %collective-permute-start.33 = (bf16[768,384]{1,0:T(8,128)(2,1)}, bf16[768,384]{1,0:T(8,128)(2,1)}, u32[]{:S(2)}, u32[]{:S(2)}) collective-permute-start(bf16[768,384]{1,0:T(8,128)(2,1)} %slice.99), channel_id=1, source_target_pairs={{0,1},{1,0},{2,3},{3,2},{4,5},{5,4},{6,7},{7,6},{8,9},{9,8},{10,11... | collective-permute-start | bytes 1769480 | tf_op jit(solution)/shard_map/ppermute | solution.py:16
  107.5 2.0 %collective-permute-start.13 = (bf16[256,768]{1,0:T(8,128)(2,1)}, bf16[256,768]{1,0:T(8,128)(2,1)S(1)}, u32[]{:S(2)}, u32[]{:S(2)}) collective-permute-start(bf16[256,768]{1,0:T(8,128)(2,1)} %get-tuple-element.6), channel_id=1, source_target_pairs={{0,2},{2,4},{4,6},{6,8},{8,10},{10,12},{12,14},{14,0},{1,3},{3,5},... | collective-permute-start | bytes 1179656 | tf_op jit(solution)/shard_map/ppermute | solution.py:16
  109.7 1.8 %collective-permute-start.17 = (bf16[256,768]{1,0:T(8,128)(2,1)S(1)}, bf16[256,768]{1,0:T(8,128)(2,1)S(1)}, u32[]{:S(2)}, u32[]{:S(2)}) collective-permute-start(bf16[256,768]{1,0:T(8,128)(2,1)S(1)} %fusion.7), channel_id=1, source_target_pairs={{0,14},{2,0},{4,2},{6,4},{8,6},{10,8},{12,10},{14,12},{1,15},{3,1}... | collective-permute-start | bytes 1179656 | tf_op jit(solution)/shard_map/ppermute | solution.py:16
  111.5 8.0 %collective-permute-done.33 = bf16[768,384]{1,0:T(8,128)(2,1)} collective-permute-done((bf16[768,384]{1,0:T(8,128)(2,1)}, bf16[768,384]{1,0:T(8,128)(2,1)}, u32[]{:S(2)}, u32[]{:S(2)}) %collective-permute-start.33) | collective-permute-done | bytes 589856 | tf_op jit(solution)/shard_map/ppermute | solution.py:16
  119.5 1.4 broadcast_select_fusion.1
  120.9 1.1 maximum_bitcast_fusion
  122.0 0.9 fusion.11
  122.9 4.7 %all-to-all-start = ((bf16[16,16,768]{2,1,0:T(8,128)(2,1)}), bf16[16,16,768]{2,1,0:T(8,128)(2,1)S(1)}, u32[]{:S(2)}, u32[]{:S(2)}) async-start(bf16[16,16,768]{2,1,0:T(8,128)(2,1)} %bitcast.22), calls=%async_computation | async-start | bytes 786432 | tf_op jit(solution)/shard_map/all_to_all | solution.py:111
  127.6 2.5 %fusion = bf16[8,4,32,768]{3,2,1,0:T(8,128)(2,1)S(1)} fusion(bf16[8,4,32,768]{3,2,1,0:T(8,128)(2,1)} %collective-permute-done.27, bf16[8,4,2,32,768]{4,3,2,1,0:T(8,128)(2,1)} %bitcast.105, s32[]{:T(128)S(6)} %select_n.100), kind=kLoop, calls=%fused_computation.3 | loop fusion | flops 3145728 | bytes 4718596 | tf_op jit(solution)/shard_map/convert_element_type | solution.py:24
  130.2 0.8 fusion.17
  131.0 1.9 %collective-permute-start.28 = (bf16[8,32,384]{2,1,0:T(8,128)(2,1)}, bf16[8,32,384]{2,1,0:T(8,128)(2,1)}, u32[]{:S(2)}, u32[]{:S(2)}) collective-permute-start(bf16[8,32,384]{2,1,0:T(8,128)(2,1)} %get-tuple-element.16), channel_id=1, source_target_pairs={{0,32},{32,64},{64,96},{96,0},{1,33},{33,65},{65,97},{97,1},{2,34}... | collective-permute-start | bytes 589832 | tf_op jit(solution)/shard_map/ppermute | solution.py:16
  132.9 4.3 %all-to-all-done = bf16[16,16,768]{2,1,0:T(8,128)(2,1)S(1)} async-done(((bf16[16,16,768]{2,1,0:T(8,128)(2,1)}), bf16[16,16,768]{2,1,0:T(8,128)(2,1)S(1)}, u32[]{:S(2)}, u32[]{:S(2)}) %all-to-all-start) | async-done | bytes 393248 | tf_op jit(solution)/shard_map/all_to_all | solution.py:111
  137.5 0.7 copy-done.6
  138.2 1.9 %collective-permute-start.30 = (bf16[8,32,384]{2,1,0:T(8,128)(2,1)S(1)}, bf16[8,32,384]{2,1,0:T(8,128)(2,1)S(1)}, u32[]{:S(2)}, u32[]{:S(2)}) collective-permute-start(bf16[8,32,384]{2,1,0:T(8,128)(2,1)S(1)} %copy-done.6), channel_id=1, source_target_pairs={{0,96},{32,0},{64,32},{96,64},{1,97},{33,1},{65,33},{97,65},{2,98}... | collective-permute-start | bytes 589832 | tf_op jit(solution)/shard_map/ppermute | solution.py:16
  140.1 1.1 collective-permute-done.28
  141.2 1.0 add_convert_fusion.2
  142.2 0.8 pad_maximum_fusion.6
  143.0 2.3 %collective-permute-done.30 = bf16[8,32,384]{2,1,0:T(8,128)(2,1)S(1)} collective-permute-done((bf16[8,32,384]{2,1,0:T(8,128)(2,1)S(1)}, bf16[8,32,384]{2,1,0:T(8,128)(2,1)S(1)}, u32[]{:S(2)}, u32[]{:S(2)}) %collective-permute-start.30) | collective-permute-done | bytes 196640 | tf_op jit(solution)/shard_map/ppermute | solution.py:16
  145.4 0.8 pad_maximum_fusion.7
  146.2 2.5 %collective-permute-start.31 = (bf16[8,32,768]{2,1,0:T(8,128)(2,1)}, bf16[8,32,768]{2,1,0:T(8,128)(2,1)}, u32[]{:S(2)}, u32[]{:S(2)}) collective-permute-start(bf16[8,32,768]{2,1,0:T(8,128)(2,1)} %pad_maximum_fusion.7), channel_id=1, source_target_pairs={{0,96},{32,0},{64,32},{96,64},{1,97},{33,1},{65,33},{97,65},{2,98}... | collective-permute-start | bytes 1179656 | tf_op jit(solution)/shard_map/ppermute | solution.py:16
  148.6 0.9 fusion.12
  149.5 0.6 collective-permute-start.18
  150.1 0.5 copy.14
  150.7 4.9 %collective-permute-done.29 = bf16[8,32,768]{2,1,0:T(8,128)(2,1)} collective-permute-done((bf16[8,32,768]{2,1,0:T(8,128)(2,1)}, bf16[8,32,768]{2,1,0:T(8,128)(2,1)}, u32[]{:S(2)}, u32[]{:S(2)}) %collective-permute-start.29) | collective-permute-done | bytes 393248 | tf_op jit(solution)/shard_map/ppermute | solution.py:16
  155.6 1.4 collective-permute-done.31
  157.1 1.3 fusion.5
  158.4 1.5 collective-permute-start.32
  159.9 0.8 fusion.1
  160.7 4.9 %collective-permute-done.32 = bf16[256,384]{1,0:T(8,128)(2,1)S(1)} collective-permute-done((bf16[256,384]{1,0:T(8,128)(2,1)S(1)}, bf16[256,384]{1,0:T(8,128)(2,1)S(1)}, u32[]{:S(2)}, u32[]{:S(2)}) %collective-permute-start.32) | collective-permute-done | bytes 196640 | tf_op jit(solution)/shard_map/ppermute | solution.py:16
  165.6 0.7 fusion.14
  166.3 1.8 %copy.37 = bf16[1,16,12288]{2,1,0:T(8,128)(2,1)} copy(bf16[1,16,12288]{2,1,0:T(8,128)(2,1)} %bitcast.26) | data formatting | bytes 786432
  (92 shorter events, 2.8 us)
Async XLA Ops:
  0.6 9.6 %collective-permute-start = (bf16[256,384]{1,0:T(8,128)(2,1)}, bf16[256,384]{1,0:T(8,128)(2,1)S(1)}, u32[]{:S(2)}, u32[]{:S(2)}) collective-permute-start(bf16[256,384]{1,0:T(8,128)(2,1)} %bitcast.126), channel_id=1, source_target_pairs={{0,1},{1,0},{2,3},{3,2},{4,5},{5,4},{6,7},{7,6},{8,9},{9,8},{10,11... | collective-permute-start | bytes 589832 | tf_op jit(solution)/shard_map/ppermute | solution.py:16
  4.8 15.4 %all-to-all-start.1 = ((bf16[16,16,768]{2,1,0:T(8,128)(2,1)}), bf16[16,16,768]{2,1,0:T(8,128)(2,1)S(1)}, u32[]{:S(2)}, u32[]{:S(2)}) async-start(bf16[16,16,768]{2,1,0:T(8,128)(2,1)} %copy.16), calls=%async_computation.1 | async-start | bytes 786432 | tf_op jit(solution)/shard_map/all_to_all | solution.py:97
  10.2 12.3 %copy-start.4 = (bf16[1,256,384]{2,1,0:T(8,128)(2,1)S(1)}, bf16[1,256,384]{2,1,0:T(8,128)(2,1)}, u32[]{:S(2)}) copy-start(bf16[1,256,384]{2,1,0:T(8,128)(2,1)} %param.5) | copy-start | bytes 589828
  11.2 16.0 %collective-permute-start.2 = (bf16[256,768]{1,0:T(8,128)(2,1)S(1)}, bf16[256,768]{1,0:T(8,128)(2,1)S(1)}, u32[]{:S(2)}, u32[]{:S(2)}) collective-permute-start(bf16[256,768]{1,0:T(8,128)(2,1)S(1)} %pad_maximum_fusion.3), channel_id=1, source_target_pairs={{0,32},{32,64},{64,96},{96,0},{1,33},{33,65},{65,97},{97,1},{2,34}... | collective-permute-start | bytes 1179656 | tf_op jit(solution)/shard_map/ppermute | solution.py:16
  13.2 19.8 %collective-permute-start.4 = (bf16[256,768]{1,0:T(8,128)(2,1)S(1)}, bf16[256,768]{1,0:T(8,128)(2,1)S(1)}, u32[]{:S(2)}, u32[]{:S(2)}) collective-permute-start(bf16[256,768]{1,0:T(8,128)(2,1)S(1)} %pad_maximum_fusion.3), channel_id=1, source_target_pairs={{0,96},{32,0},{64,32},{96,64},{1,97},{33,1},{65,33},{97,65},{2,98}... | collective-permute-start | bytes 1179656 | tf_op jit(solution)/shard_map/ppermute | solution.py:16
  14.5 18.6 %collective-permute-start.1 = (bf16[256,768]{1,0:T(8,128)(2,1)S(1)}, bf16[256,768]{1,0:T(8,128)(2,1)S(1)}, u32[]{:S(2)}, u32[]{:S(2)}) collective-permute-start(bf16[256,768]{1,0:T(8,128)(2,1)S(1)} %pad_maximum_fusion.3), channel_id=1, source_target_pairs={{0,16},{16,0},{1,17},{17,1},{2,18},{18,2},{3,19},{19,3},{4,20},{20... | collective-permute-start | bytes 1179656 | tf_op jit(solution)/shard_map/ppermute | solution.py:16
  16.7 41.5 %collective-permute-start.9 = (bf16[768,384]{1,0:T(8,128)(2,1)S(1)}, bf16[768,384]{1,0:T(8,128)(2,1)S(1)}, u32[]{:S(2)}, u32[]{:S(2)}) collective-permute-start(bf16[768,384]{1,0:T(8,128)(2,1)S(1)} %get-tuple-element.5), channel_id=1, source_target_pairs={{0,1},{1,0},{2,3},{3,2},{4,5},{5,4},{6,7},{7,6},{8,9},{9,8},{10,11... | collective-permute-start | bytes 1769480 | tf_op jit(solution)/shard_map/ppermute | solution.py:16
  20.2 16.4 %collective-permute-start.19 = (bf16[256,768]{1,0:T(8,128)(2,1)S(1)}, bf16[256,768]{1,0:T(8,128)(2,1)S(1)}, u32[]{:S(2)}, u32[]{:S(2)}) collective-permute-start(bf16[256,768]{1,0:T(8,128)(2,1)S(1)} %bitcast.118), channel_id=1, source_target_pairs={{0,2},{2,4},{4,6},{6,8},{8,10},{10,12},{12,14},{14,0},{1,3},{3,5},... | collective-permute-start | bytes 1179656 | tf_op jit(solution)/shard_map/ppermute | solution.py:16
  27.2 14.1 %collective-permute-start.20 = (bf16[256,768]{1,0:T(8,128)(2,1)S(1)}, bf16[256,768]{1,0:T(8,128)(2,1)S(1)}, u32[]{:S(2)}, u32[]{:S(2)}) collective-permute-start(bf16[256,768]{1,0:T(8,128)(2,1)S(1)} %bitcast.120), channel_id=1, source_target_pairs={{0,14},{2,0},{4,2},{6,4},{8,6},{10,8},{12,10},{14,12},{1,15},{3,1}... | collective-permute-start | bytes 1179656 | tf_op jit(solution)/shard_map/ppermute | solution.py:16
  33.1 8.3 %collective-permute-start.6 = (bf16[128,768]{1,0:T(8,128)(2,1)S(1)}, bf16[128,768]{1,0:T(8,128)(2,1)S(1)}, u32[]{:S(2)}, u32[]{:S(2)}) collective-permute-start(bf16[128,768]{1,0:T(8,128)(2,1)S(1)} %slice.80), channel_id=1, source_target_pairs={{0,32},{32,64},{64,96},{96,0},{1,33},{33,65},{65,97},{97,1},{2,34}... | collective-permute-start | bytes 589832 | tf_op jit(solution)/shard_map/ppermute | solution.py:16
  33.2 8.3 %collective-permute-start.7 = (bf16[128,768]{1,0:T(8,128)(2,1)S(1)}, bf16[128,768]{1,0:T(8,128)(2,1)S(1)}, u32[]{:S(2)}, u32[]{:S(2)}) collective-permute-start(bf16[128,768]{1,0:T(8,128)(2,1)S(1)} %slice.81), channel_id=1, source_target_pairs={{0,96},{32,0},{64,32},{96,64},{1,97},{33,1},{65,33},{97,65},{2,98}... | collective-permute-start | bytes 589832 | tf_op jit(solution)/shard_map/ppermute | solution.py:16
  36.6 8.7 %collective-permute-start.3 = (bf16[256,768]{1,0:T(8,128)(2,1)S(1)}, bf16[256,768]{1,0:T(8,128)(2,1)S(1)}, u32[]{:S(2)}, u32[]{:S(2)}) collective-permute-start(bf16[256,768]{1,0:T(8,128)(2,1)S(1)} %collective-permute-done.2), channel_id=1, source_target_pairs={{0,16},{16,0},{1,17},{17,1},{2,18},{18,2},{3,19},{19,3},{4,20},{20... | collective-permute-start | bytes 1179656 | tf_op jit(solution)/shard_map/ppermute | solution.py:16
  36.7 22.3 %copy-start.5 = (bf16[768,384]{1,0:T(8,128)(2,1)S(1)}, bf16[768,384]{1,0:T(8,128)(2,1)}, u32[]{:S(2)}) copy-start(bf16[768,384]{1,0:T(8,128)(2,1)} %get-tuple-element.4) | copy-start | bytes 1769476
  41.3 4.4 %collective-permute-start.5 = (bf16[256,768]{1,0:T(8,128)(2,1)S(1)}, bf16[256,768]{1,0:T(8,128)(2,1)S(1)}, u32[]{:S(2)}, u32[]{:S(2)}) collective-permute-start(bf16[256,768]{1,0:T(8,128)(2,1)S(1)} %collective-permute-done.4), channel_id=1, source_target_pairs={{0,16},{16,0},{1,17},{17,1},{2,18},{18,2},{3,19},{19,3},{4,20},{20... | collective-permute-start | bytes 1179656 | tf_op jit(solution)/shard_map/ppermute | solution.py:16
  41.4 13.6 %collective-permute-start.21 = (bf16[256,768]{1,0:T(8,128)(2,1)S(1)}, bf16[256,768]{1,0:T(8,128)(2,1)S(1)}, u32[]{:S(2)}, u32[]{:S(2)}) collective-permute-start(bf16[256,768]{1,0:T(8,128)(2,1)S(1)} %collective-permute-done.19), channel_id=1, source_target_pairs={{0,2},{2,4},{4,6},{6,8},{8,10},{10,12},{12,14},{14,0},{1,3},{3,5},... | collective-permute-start | bytes 1179656 | tf_op jit(solution)/shard_map/ppermute | solution.py:16
  41.5 13.4 %collective-permute-start.22 = (bf16[256,768]{1,0:T(8,128)(2,1)S(1)}, bf16[256,768]{1,0:T(8,128)(2,1)S(1)}, u32[]{:S(2)}, u32[]{:S(2)}) collective-permute-start(bf16[256,768]{1,0:T(8,128)(2,1)S(1)} %collective-permute-done.20), channel_id=1, source_target_pairs={{0,14},{2,0},{4,2},{6,4},{8,6},{10,8},{12,10},{14,12},{1,15},{3,1}... | collective-permute-start | bytes 1179656 | tf_op jit(solution)/shard_map/ppermute | solution.py:16
  45.3 12.9 %collective-permute-start.8 = (bf16[256,768]{1,0:T(8,128)(2,1)S(1)}, bf16[256,768]{1,0:T(8,128)(2,1)S(1)}, u32[]{:S(2)}, u32[]{:S(2)}) collective-permute-start(bf16[256,768]{1,0:T(8,128)(2,1)S(1)} %constant_dynamic-update-slice_fusion.7), channel_id=1, source_target_pairs={{0,16},{16,0},{1,17},{17,1},{2,18},{18,2},{3,19},{19,3},{4,20},{20... | collective-permute-start | bytes 1179656 | tf_op jit(solution)/shard_map/ppermute | solution.py:16
  54.9 19.7 %collective-permute-start.23 = (bf16[256,768]{1,0:T(8,128)(2,1)S(1)}, bf16[256,768]{1,0:T(8,128)(2,1)S(1)}, u32[]{:S(2)}, u32[]{:S(2)}) collective-permute-start(bf16[256,768]{1,0:T(8,128)(2,1)S(1)} %collective-permute-done.21), channel_id=1, source_target_pairs={{0,2},{2,4},{4,6},{6,8},{8,10},{10,12},{12,14},{14,0},{1,3},{3,5},... | collective-permute-start | bytes 1179656 | tf_op jit(solution)/shard_map/ppermute | solution.py:16
  54.9 19.8 %collective-permute-start.24 = (bf16[256,768]{1,0:T(8,128)(2,1)S(1)}, bf16[256,768]{1,0:T(8,128)(2,1)S(1)}, u32[]{:S(2)}, u32[]{:S(2)}) collective-permute-start(bf16[256,768]{1,0:T(8,128)(2,1)S(1)} %collective-permute-done.22), channel_id=1, source_target_pairs={{0,14},{2,0},{4,2},{6,4},{8,6},{10,8},{12,10},{14,12},{1,15},{3,1}... | collective-permute-start | bytes 1179656 | tf_op jit(solution)/shard_map/ppermute | solution.py:16
  58.2 0.8 copy-start.7
  63.2 7.4 %collective-permute-start.14 = (bf16[256,384]{1,0:T(8,128)(2,1)S(1)}, bf16[256,384]{1,0:T(8,128)(2,1)S(1)}, u32[]{:S(2)}, u32[]{:S(2)}) collective-permute-start(bf16[256,384]{1,0:T(8,128)(2,1)S(1)} %get-tuple-element.21), channel_id=1, source_target_pairs={{0,14},{2,0},{4,2},{6,4},{8,6},{10,8},{12,10},{14,12},{1,15},{3,1}... | collective-permute-start | bytes 589832 | tf_op jit(solution)/shard_map/ppermute | solution.py:16
  63.8 10.6 %collective-permute-start.10 = (bf16[256,384]{1,0:T(8,128)(2,1)S(1)}, bf16[256,384]{1,0:T(8,128)(2,1)S(1)}, u32[]{:S(2)}, u32[]{:S(2)}) collective-permute-start(bf16[256,384]{1,0:T(8,128)(2,1)S(1)} %get-tuple-element.20), channel_id=1, source_target_pairs={{0,2},{2,4},{4,6},{6,8},{8,10},{10,12},{12,14},{14,0},{1,3},{3,5},... | collective-permute-start | bytes 589832 | tf_op jit(solution)/shard_map/ppermute | solution.py:16
  70.6 19.2 %copy-start.8 = (bf16[768,384]{1,0:T(8,128)(2,1)S(1)}, bf16[768,384]{1,0:T(8,128)(2,1)}, u32[]{:S(2)}) copy-start(bf16[768,384]{1,0:T(8,128)(2,1)} %copy-done.7) | copy-start | bytes 1769476
  70.7 23.4 %collective-permute-start.15 = (bf16[256,768]{1,0:T(8,128)(2,1)S(1)}, bf16[256,768]{1,0:T(8,128)(2,1)S(1)}, u32[]{:S(2)}, u32[]{:S(2)}) collective-permute-start(bf16[256,768]{1,0:T(8,128)(2,1)S(1)} %pad_maximum_fusion.5), channel_id=1, source_target_pairs={{0,14},{2,0},{4,2},{6,4},{8,6},{10,8},{12,10},{14,12},{1,15},{3,1}... | collective-permute-start | bytes 1179656 | tf_op jit(solution)/shard_map/ppermute | solution.py:16
  74.5 15.0 %collective-permute-start.11 = (bf16[256,768]{1,0:T(8,128)(2,1)S(1)}, bf16[256,768]{1,0:T(8,128)(2,1)S(1)}, u32[]{:S(2)}, u32[]{:S(2)}) collective-permute-start(bf16[256,768]{1,0:T(8,128)(2,1)S(1)} %pad_maximum_fusion.4), channel_id=1, source_target_pairs={{0,2},{2,4},{4,6},{6,8},{8,10},{10,12},{12,14},{14,0},{1,3},{3,5},... | collective-permute-start | bytes 1179656 | tf_op jit(solution)/shard_map/ppermute | solution.py:16
  74.7 14.9 %collective-permute-start.25 = (bf16[128,768]{1,0:T(8,128)(2,1)S(1)}, bf16[128,768]{1,0:T(8,128)(2,1)S(1)}, u32[]{:S(2)}, u32[]{:S(2)}) collective-permute-start(bf16[128,768]{1,0:T(8,128)(2,1)S(1)} %slice.88), channel_id=1, source_target_pairs={{0,2},{2,4},{4,6},{6,8},{8,10},{10,12},{12,14},{14,0},{1,3},{3,5},... | collective-permute-start | bytes 589832 | tf_op jit(solution)/shard_map/ppermute | solution.py:16
  74.8 14.7 %collective-permute-start.26 = (bf16[128,768]{1,0:T(8,128)(2,1)S(1)}, bf16[128,768]{1,0:T(8,128)(2,1)S(1)}, u32[]{:S(2)}, u32[]{:S(2)}) collective-permute-start(bf16[128,768]{1,0:T(8,128)(2,1)S(1)} %slice.89), channel_id=1, source_target_pairs={{0,14},{2,0},{4,2},{6,4},{8,6},{10,8},{12,10},{14,12},{1,15},{3,1}... | collective-permute-start | bytes 589832 | tf_op jit(solution)/shard_map/ppermute | solution.py:16
  89.7 9.9 %collective-permute-start.12 = (bf16[256,768]{1,0:T(8,128)(2,1)S(1)}, bf16[256,768]{1,0:T(8,128)(2,1)S(1)}, u32[]{:S(2)}, u32[]{:S(2)}) collective-permute-start(bf16[256,768]{1,0:T(8,128)(2,1)S(1)} %fusion.8), channel_id=1, source_target_pairs={{0,2},{2,4},{4,6},{6,8},{8,10},{10,12},{12,14},{14,0},{1,3},{3,5},... | collective-permute-start | bytes 1179656 | tf_op jit(solution)/shard_map/ppermute | solution.py:16
  92.6 10.7 %copy-start = (bf16[2048,768]{1,0:T(8,128)(2,1)}, bf16[2048,768]{1,0:T(8,128)(2,1)S(1)}, u32[]{:S(2)}) copy-start(bf16[2048,768]{1,0:T(8,128)(2,1)S(1)} %convolution_convert_fusion) | copy-start | bytes 9437188
  94.1 33.6 %collective-permute-start.27 = (bf16[8,4,32,768]{3,2,1,0:T(8,128)(2,1)}, bf16[8,4,32,768]{3,2,1,0:T(8,128)(2,1)}, u32[]{:S(2)}, u32[]{:S(2)}) collective-permute-start(bf16[8,4,32,768]{3,2,1,0:T(8,128)(2,1)} %dynamic-slice_bitcast_fusion), channel_id=1, source_target_pairs={{0,16},{16,0},{1,17},{17,1},{2,18},{18,2},{3,19},{19,3},{4,20},{20... | collective-permute-start | bytes 4718600 | tf_op jit(solution)/shard_map/ppermute | solution.py:16
  100.6 9.0 %collective-permute-start.16 = (bf16[256,768]{1,0:T(8,128)(2,1)}, bf16[256,768]{1,0:T(8,128)(2,1)S(1)}, u32[]{:S(2)}, u32[]{:S(2)}) collective-permute-start(bf16[256,768]{1,0:T(8,128)(2,1)} %get-tuple-element.7), channel_id=1, source_target_pairs={{0,14},{2,0},{4,2},{6,4},{8,6},{10,8},{12,10},{14,12},{1,15},{3,1}... | collective-permute-start | bytes 1179656 | tf_op jit(solution)/shard_map/ppermute | solution.py:16
  103.3 1.2 copy-start.3
  104.5 15.0 %collective-permute-start.33 = (bf16[768,384]{1,0:T(8,128)(2,1)}, bf16[768,384]{1,0:T(8,128)(2,1)}, u32[]{:S(2)}, u32[]{:S(2)}) collective-permute-start(bf16[768,384]{1,0:T(8,128)(2,1)} %slice.99), channel_id=1, source_target_pairs={{0,1},{1,0},{2,3},{3,2},{4,5},{5,4},{6,7},{7,6},{8,9},{9,8},{10,11... | collective-permute-start | bytes 1769480 | tf_op jit(solution)/shard_map/ppermute | solution.py:16
  107.5 14.4 %collective-permute-start.13 = (bf16[256,768]{1,0:T(8,128)(2,1)}, bf16[256,768]{1,0:T(8,128)(2,1)S(1)}, u32[]{:S(2)}, u32[]{:S(2)}) collective-permute-start(bf16[256,768]{1,0:T(8,128)(2,1)} %get-tuple-element.6), channel_id=1, source_target_pairs={{0,2},{2,4},{4,6},{6,8},{8,10},{10,12},{12,14},{14,0},{1,3},{3,5},... | collective-permute-start | bytes 1179656 | tf_op jit(solution)/shard_map/ppermute | solution.py:16
  109.7 12.3 %collective-permute-start.17 = (bf16[256,768]{1,0:T(8,128)(2,1)S(1)}, bf16[256,768]{1,0:T(8,128)(2,1)S(1)}, u32[]{:S(2)}, u32[]{:S(2)}) collective-permute-start(bf16[256,768]{1,0:T(8,128)(2,1)S(1)} %fusion.7), channel_id=1, source_target_pairs={{0,14},{2,0},{4,2},{6,4},{8,6},{10,8},{12,10},{14,12},{1,15},{3,1}... | collective-permute-start | bytes 1179656 | tf_op jit(solution)/shard_map/ppermute | solution.py:16
  122.9 14.3 %all-to-all-start = ((bf16[16,16,768]{2,1,0:T(8,128)(2,1)}), bf16[16,16,768]{2,1,0:T(8,128)(2,1)S(1)}, u32[]{:S(2)}, u32[]{:S(2)}) async-start(bf16[16,16,768]{2,1,0:T(8,128)(2,1)} %bitcast.22), calls=%async_computation | async-start | bytes 786432 | tf_op jit(solution)/shard_map/all_to_all | solution.py:111
  131.0 17.6 %copy-start.1 = (bf16[1,16,12288]{2,1,0:T(8,128)(2,1)S(1)}, bf16[1,16,12288]{2,1,0:T(8,128)(2,1)}, u32[]{:S(2)}) copy-start(bf16[1,16,12288]{2,1,0:T(8,128)(2,1)} %param.7) | copy-start | bytes 1179652
  131.0 17.6 %copy-start.2 = (bf16[1,16,12288]{2,1,0:T(8,128)(2,1)S(1)}, bf16[1,16,12288]{2,1,0:T(8,128)(2,1)}, u32[]{:S(2)}) copy-start(bf16[1,16,12288]{2,1,0:T(8,128)(2,1)} %param.4) | copy-start | bytes 1179652
  131.0 10.2 %collective-permute-start.28 = (bf16[8,32,384]{2,1,0:T(8,128)(2,1)}, bf16[8,32,384]{2,1,0:T(8,128)(2,1)}, u32[]{:S(2)}, u32[]{:S(2)}) collective-permute-start(bf16[8,32,384]{2,1,0:T(8,128)(2,1)} %get-tuple-element.16), channel_id=1, source_target_pairs={{0,32},{32,64},{64,96},{96,0},{1,33},{33,65},{65,97},{97,1},{2,34}... | collective-permute-start | bytes 589832 | tf_op jit(solution)/shard_map/ppermute | solution.py:16
  137.3 0.9 copy-start.6
  138.2 7.2 %collective-permute-start.30 = (bf16[8,32,384]{2,1,0:T(8,128)(2,1)S(1)}, bf16[8,32,384]{2,1,0:T(8,128)(2,1)S(1)}, u32[]{:S(2)}, u32[]{:S(2)}) collective-permute-start(bf16[8,32,384]{2,1,0:T(8,128)(2,1)S(1)} %copy-done.6), channel_id=1, source_target_pairs={{0,96},{32,0},{64,32},{96,64},{1,97},{33,1},{65,33},{97,65},{2,98}... | collective-permute-start | bytes 589832 | tf_op jit(solution)/shard_map/ppermute | solution.py:16
  143.0 12.6 %collective-permute-start.29 = (bf16[8,32,768]{2,1,0:T(8,128)(2,1)}, bf16[8,32,768]{2,1,0:T(8,128)(2,1)}, u32[]{:S(2)}, u32[]{:S(2)}) collective-permute-start(bf16[8,32,768]{2,1,0:T(8,128)(2,1)} %pad_maximum_fusion.6), channel_id=1, source_target_pairs={{0,32},{32,64},{64,96},{96,0},{1,33},{33,65},{65,97},{97,1},{2,34}... | collective-permute-start | bytes 1179656 | tf_op jit(solution)/shard_map/ppermute | solution.py:16
  146.2 10.9 %collective-permute-start.31 = (bf16[8,32,768]{2,1,0:T(8,128)(2,1)}, bf16[8,32,768]{2,1,0:T(8,128)(2,1)}, u32[]{:S(2)}, u32[]{:S(2)}) collective-permute-start(bf16[8,32,768]{2,1,0:T(8,128)(2,1)} %pad_maximum_fusion.7), channel_id=1, source_target_pairs={{0,96},{32,0},{64,32},{96,64},{1,97},{33,1},{65,33},{97,65},{2,98}... | collective-permute-start | bytes 1179656 | tf_op jit(solution)/shard_map/ppermute | solution.py:16
  149.5 11.2 %collective-permute-start.18 = (bf16[16,12288]{1,0:T(8,128)(2,1)}, bf16[16,12288]{1,0:T(8,128)(2,1)}, u32[]{:S(2)}, u32[]{:S(2)}) collective-permute-start(bf16[16,12288]{1,0:T(8,128)(2,1)} %fusion.12), channel_id=1, source_target_pairs={{0,128},{128,0},{1,129},{129,1},{2,130},{130,2},{3,131},{131,3},{4... | collective-permute-start | bytes 1179656 | tf_op jit(solution)/shard_map/ppermute | solution.py:16
  158.4 7.3 %collective-permute-start.32 = (bf16[256,384]{1,0:T(8,128)(2,1)S(1)}, bf16[256,384]{1,0:T(8,128)(2,1)S(1)}, u32[]{:S(2)}, u32[]{:S(2)}) collective-permute-start(bf16[256,384]{1,0:T(8,128)(2,1)S(1)} %slice.97), channel_id=1, source_target_pairs={{0,1},{1,0},{2,3},{3,2},{4,5},{5,4},{6,7},{7,6},{8,9},{9,8},{10,11... | collective-permute-start | bytes 589832 | tf_op jit(solution)/shard_map/ppermute | solution.py:16

commit v2 on v1

--- a/solution.py
+++ b/solution.py
@@ -95,7 +95,8 @@
 
     spread = upstream.reshape(own_count, n_group, features).transpose(1, 0, 2)
     spread = lax.all_to_all(spread, GROUP, 0, 0, tiled=True)
-    grad_blocks = ring_gather(spread.reshape(n_group * own_count, features), "z")
+    spread = spread.reshape(n_group * own_count, features)
+    grad_flat = lax.all_gather(spread, "z", axis=0, tiled=True)
 
     ctx_all = jnp.zeros((n_z, n_y, n_core, z_tokens, 2 * width), BF16)
     for away, piece in ring_gather(both, "y").items():
@@ -113,11 +114,6 @@
     forward = add(residual, branch)
     outgoing = jnp.where(lax.axis_index("section") == 0, forward, upstream)
     received = swap(outgoing, "section")
-
-    grad_all = jnp.zeros((n_z, tokens // n_z, features), BF16)
-    for away, piece in grad_blocks.items():
-        grad_all = place(grad_all, piece[None], (wrap(z + away, n_z), 0, 0))
-    grad_flat = grad_all.reshape(tokens, features)
 
     partial_ctx = jnp.dot(grad_flat, block, preferred_element_type=F32).astype(BF16)
     partial_ctx = partial_ctx.reshape(n_z, n_y, n_core, z_tokens, 2 * width)

time: 169 us -> 211 us (1.25)
  waiting for transfers between devices: 67.3 us -> 85.2 us
  between operations: 1.23 us -> 14.5 us
  starting transfers between devices: 62.5 us -> 50.4 us
  local copies, waits for them, and re-layouts: 12.9 us -> 25 us
  other arithmetic: 14.8 us -> 19.5 us
  matrix products: 9.42 us -> 13.5 us
    ppermute x34 -> x26, starting transfers between devices: 52.3 us -> 37.7 us  [shift(): return lax.ppermute(value, axis, [(i, (i + by) % n) for i in range(n)])]
    ppermute x34 -> x26, waiting for transfers between devices: 62.9 us -> 73.7 us  [shift(): return lax.ppermute(value, axis, [(i, (i + by) % n) for i in range(n)])]
    all_to_all x1, waiting for transfers between devices: 4.32 us -> 9.61 us  [shards(): lax.all_to_all(branch.reshape(n_group, own_count, features), GROUP, 0, 0,...]
    convert_element_type x9, other arithmetic: 5.68 us -> 9.91 us  [add(): return (a.astype(F32) + b.astype(F32)).astype(BF16)]
    convert_element_type x3, local copies, waits for them, and re-layouts: 0.66 us -> 4.5 us  [add(): return (a.astype(F32) + b.astype(F32)).astype(BF16)]
    dot_general x1, matrix products: 2.82 us -> 6.45 us  [shards(): jnp.dot(grad_flat, block, preferred_element_type=F32).astype(BF16)]
    convert_element_type x0 -> x1, local copies, waits for them, and re-layouts: none -> 3.18 us  [shards(): jnp.dot(grad_flat, block, preferred_element_type=F32).astype(BF16)]
    all_to_all x1, starting transfers between devices: 4.72 us -> 7.67 us  [shards(): lax.all_to_all(branch.reshape(n_group, own_count, features), GROUP, 0, 0,...]
  transfers between devices with their start and end apart: 36 -> 29, of which waited for: 13 -> 16; matrix products, arithmetic and copies ran while one was open for 20% -> 19% of each run, Pallas kernels for 0% -> 0%
where the time goes in v2:
time: 211 us; the launch traced here: 208 us
  waiting for transfers between devices  85.2 us (40%)
  starting transfers between devices  50.4 us (24%)
  local copies, waits for them, and re-layouts  25 us (12%)
  other arithmetic  19.5 us (9%)
  between operations  14.5 us (7%)
  matrix products  13.5 us (6%)
    ppermute x26, waiting for transfers between devices, shift(): return lax.ppermute(value, axis, [(i, (i + by) % n) for i in range(n)])  73.7 us
    ppermute x26, starting transfers between devices, shift(): return lax.ppermute(value, axis, [(i, (i + by) % n) for i in range(n)])  37.7 us
    convert_element_type x9, other arithmetic, add(): return (a.astype(F32) + b.astype(F32)).astype(BF16)  9.91 us
    all_to_all x1, waiting for transfers between devices, shards(): lax.all_to_all(branch.reshape(n_group, own_count, features), GROUP, 0, 0,...  9.61 us
    all_to_all x1, starting transfers between devices, shards(): lax.all_to_all(branch.reshape(n_group, own_count, features), GROUP, 0, 0,...  7.67 us
    dot_general x1, matrix products, shards(): jnp.dot(grad_flat, block, preferred_element_type=F32).astype(BF16)  6.45 us
    unnamed x33, local copies, waits for them, and re-layouts  6.05 us
    all_to_all x1, starting transfers between devices, shards(): spread = lax.all_to_all(spread, GROUP, 0, 0, tiled=True)  5.04 us
  transfers between devices with their start and end apart: 29, of which 16 were waited for; matrix products, arithmetic and copies ran while one was open for 19% of the time, Pallas kernels for 0%

profile of v2, /device:TPU:2, one launch (start us, length us, event | category | flops | bytes accessed | tf_op | source)
XLA Modules:
  0.0 208.0 jit_solution(7480658995881543551)
XLA Ops:
  7.2 2.2 %collective-permute-start = (bf16[256,384]{1,0:T(8,128)(2,1)}, bf16[256,384]{1,0:T(8,128)(2,1)S(1)}, u32[]{:S(2)}, u32[]{:S(2)}) collective-permute-start(bf16[256,384]{1,0:T(8,128)(2,1)} %bitcast.104), channel_id=1, source_target_pairs={{0,1},{1,0},{2,3},{3,2},{4,5},{5,4},{6,7},{7,6},{8,9},{9,8},{10,11... | collective-permute-start | bytes 589832 | tf_op jit(solution)/shard_map/ppermute | solution.py:16
  9.4 6.2 %collective-permute-done = bf16[256,384]{1,0:T(8,128)(2,1)S(1)} collective-permute-done((bf16[256,384]{1,0:T(8,128)(2,1)}, bf16[256,384]{1,0:T(8,128)(2,1)S(1)}, u32[]{:S(2)}, u32[]{:S(2)}) %collective-permute-start) | collective-permute-done | bytes 196640 | tf_op jit(solution)/shard_map/ppermute | solution.py:16
  15.6 1.8 pad_maximum_fusion.3
  17.4 1.6 collective-permute-start.2
  19.0 1.7 collective-permute-start.4
  20.6 1.1 copy.22
  21.7 0.9 copy.19
  22.6 5.0 %all-to-all-start.1 = ((bf16[16,16,768]{2,1,0:T(8,128)(2,1)}), bf16[16,16,768]{2,1,0:T(8,128)(2,1)S(1)}, u32[]{:S(2)}, u32[]{:S(2)}) async-start(bf16[16,16,768]{2,1,0:T(8,128)(2,1)} %copy.19), calls=%async_computation.1 | async-start | bytes 786432 | tf_op jit(solution)/shard_map/all_to_all | solution.py:97
  27.7 2.4 %dynamic-slice_bitcast_fusion.2 = (bf16[768,384]{1,0:T(8,128)(2,1)}, bf16[768,384]{1,0:T(8,128)(2,1)}) fusion(bf16[1,12288,384]{2,1,0:T(8,128)(2,1)} %param.6, s32[]{:T(128)S(6)} %select_n.95, s32[]{:T(128)S(6)} %select_n.96), kind=kLoop, calls=%fused_computation.32 | loop fusion | bytes 2359304 | tf_op jit(solution)/shard_map/dynamic_slice | solution.py:92
  30.0 3.4 %collective-permute-start.9 = (bf16[768,384]{1,0:T(8,128)(2,1)}, bf16[768,384]{1,0:T(8,128)(2,1)}, u32[]{:S(2)}, u32[]{:S(2)}) collective-permute-start(bf16[768,384]{1,0:T(8,128)(2,1)} %get-tuple-element.5), channel_id=1, source_target_pairs={{0,1},{1,0},{2,3},{3,2},{4,5},{5,4},{6,7},{7,6},{8,9},{9,8},{10,11... | collective-permute-start | bytes 1769480 | tf_op jit(solution)/shard_map/ppermute | solution.py:16
  34.4 1.0 maximum_dynamic-update-slice_fusion
  35.4 1.9 all-to-all-done.1
  37.2 0.8 copy-done.7
  38.0 0.9 slice.72
  39.0 1.2 collective-permute-start.6
  40.2 0.9 slice.73
  41.1 2.1 %collective-permute-start.7 = (bf16[128,768]{1,0:T(8,128)(2,1)S(1)}, bf16[128,768]{1,0:T(8,128)(2,1)S(1)}, u32[]{:S(2)}, u32[]{:S(2)}) collective-permute-start(bf16[128,768]{1,0:T(8,128)(2,1)S(1)} %slice.73), channel_id=1, source_target_pairs={{0,96},{32,0},{64,32},{96,64},{1,97},{33,1},{65,33},{97,65},{2,98}... | collective-permute-start | bytes 589832 | tf_op jit(solution)/shard_map/ppermute | solution.py:16
  43.3 1.1 constant_dynamic-update-slice_fusion.8
  45.0 1.0 constant_dynamic-update-slice_fusion.7
  46.0 1.4 collective-permute-done.6
  48.1 1.0 constant_dynamic-update-slice_fusion.5
  49.8 4.4 %convolution_convert_fusion.1 = bf16[2048,768]{1,0:T(8,128)(2,1)S(1)} fusion(bf16[2048,768]{1,0:T(8,128)(2,1)S(1)} %bitcast.91, bf16[768,384]{1,0:T(8,128)(2,1)} %collective-permute-done.9, bf16[768,384]{1,0:T(8,128)(2,1)S(1)} %copy-done.12), kind=kOutput, calls=%fused_computation.1 | convolution fusion | flops 2419851264 | bytes 7471104 | tf_op jit(solution)/shard_map/dot_general | solution.py:108
  54.3 1.7 copy-done.5
  56.8 1.9 collective-permute-start.10
  58.7 3.9 %collective-permute-start.14 = (bf16[256,384]{1,0:T(8,128)(2,1)}, bf16[256,384]{1,0:T(8,128)(2,1)}, u32[]{:S(2)}, u32[]{:S(2)}) collective-permute-start(bf16[256,384]{1,0:T(8,128)(2,1)} %get-tuple-element.21), channel_id=1, source_target_pairs={{0,14},{2,0},{4,2},{6,4},{8,6},{10,8},{12,10},{14,12},{1,15},{3,1}... | collective-permute-start | bytes 589832 | tf_op jit(solution)/shard_map/ppermute | solution.py:16
  62.6 9.6 %collective-permute-done.10 = bf16[256,384]{1,0:T(8,128)(2,1)S(1)} collective-permute-done((bf16[256,384]{1,0:T(8,128)(2,1)S(1)}, bf16[256,384]{1,0:T(8,128)(2,1)S(1)}, u32[]{:S(2)}, u32[]{:S(2)}) %collective-permute-start.10) | collective-permute-done | bytes 196640 | tf_op jit(solution)/shard_map/ppermute | solution.py:16
  72.3 0.8 pad_maximum_fusion.4
  73.1 1.0 add_convert_fusion.3
  74.2 3.5 %collective-permute-start.15 = (bf16[256,768]{1,0:T(8,128)(2,1)S(1)}, bf16[256,768]{1,0:T(8,128)(2,1)}, u32[]{:S(2)}, u32[]{:S(2)}) collective-permute-start(bf16[256,768]{1,0:T(8,128)(2,1)S(1)} %pad_maximum_fusion.5), channel_id=1, source_target_pairs={{0,14},{2,0},{4,2},{6,4},{8,6},{10,8},{12,10},{14,12},{1,15},{3,1}... | collective-permute-start | bytes 1179656 | tf_op jit(solution)/shard_map/ppermute | solution.py:16
  77.7 16.8 %collective-permute-done.11 = bf16[256,768]{1,0:T(8,128)(2,1)} collective-permute-done((bf16[256,768]{1,0:T(8,128)(2,1)}, bf16[256,768]{1,0:T(8,128)(2,1)}, u32[]{:S(2)}, u32[]{:S(2)}) %collective-permute-start.11) | collective-permute-done | bytes 393248 | tf_op jit(solution)/shard_map/ppermute | solution.py:16
  94.5 1.8 fusion.10
  96.3 11.1 %collective-permute-done.12 = bf16[256,768]{1,0:T(8,128)(2,1)} collective-permute-done((bf16[256,768]{1,0:T(8,128)(2,1)}, bf16[256,768]{1,0:T(8,128)(2,1)}, u32[]{:S(2)}, u32[]{:S(2)}) %collective-permute-start.12) | collective-permute-done | bytes 393248 | tf_op jit(solution)/shard_map/ppermute | solution.py:16
  107.4 2.2 %fusion.11 = (bf16[256,768]{1,0:T(8,128)(2,1)}, bf16[256,768]{1,0:T(8,128)(2,1)}) fusion(bf16[256,768]{1,0:T(8,128)(2,1)} %collective-permute-done.12, bf16[8,256,768]{2,1,0:T(8,128)(2,1)S(1)} %bitcast.95, s32[]{:T(128)S(6)} %select_n.98, bf16[256,768]{1,0:T(8,128)(2,1)} %collective-permute-done.15, s32[]{:T(128)S(6)} %select_n.103), kind=kLoop, calls=%fused_computation.27 | loop fusion | flops 1572864 | bytes 2359304 | tf_op jit(solution)/shard_map/convert_element_type | solution.py:24
  109.6 2.0 collective-permute-start.13
  111.6 6.9 %collective-permute-done.16 = bf16[256,768]{1,0:T(8,128)(2,1)} collective-permute-done((bf16[256,768]{1,0:T(8,128)(2,1)}, bf16[256,768]{1,0:T(8,128)(2,1)}, u32[]{:S(2)}, u32[]{:S(2)}) %collective-permute-start.16) | collective-permute-done | bytes 393248 | tf_op jit(solution)/shard_map/ppermute | solution.py:16
  118.6 1.8 fusion.9
  120.4 1.5 collective-permute-start.17
  121.9 6.6 %collective-permute-done.17 = bf16[256,768]{1,0:T(8,128)(2,1)} collective-permute-done((bf16[256,768]{1,0:T(8,128)(2,1)}, bf16[256,768]{1,0:T(8,128)(2,1)}, u32[]{:S(2)}, u32[]{:S(2)}) %collective-permute-start.17) | collective-permute-done | bytes 393248 | tf_op jit(solution)/shard_map/ppermute | solution.py:16
  128.5 1.9 fusion.13
  130.4 7.7 %all-to-all-start = ((bf16[16,16,768]{2,1,0:T(8,128)(2,1)}), bf16[16,16,768]{2,1,0:T(8,128)(2,1)S(1)}, u32[]{:S(2)}, u32[]{:S(2)}) async-start(bf16[16,16,768]{2,1,0:T(8,128)(2,1)} %bitcast.22), calls=%async_computation | async-start | bytes 786432 | tf_op jit(solution)/shard_map/all_to_all | solution.py:112
  138.1 9.6 %all-to-all-done = bf16[16,16,768]{2,1,0:T(8,128)(2,1)S(1)} async-done(((bf16[16,16,768]{2,1,0:T(8,128)(2,1)}), bf16[16,16,768]{2,1,0:T(8,128)(2,1)S(1)}, u32[]{:S(2)}, u32[]{:S(2)}) %all-to-all-start) | async-done | bytes 393248 | tf_op jit(solution)/shard_map/all_to_all | solution.py:112
  147.7 1.0 convert_bitcast_fusion
  148.7 1.0 copy.21
  149.7 6.4 %fusion.1 = bf16[2048,768]{0,1:T(8,128)(2,1)} fusion(bf16[2048,768]{1,0:T(8,128)(2,1)} %all-gather.2.cloned.1.call-done, bf16[768,384]{1,0:T(8,128)(2,1)} %collective-permute-done.9, bf16[768,384]{1,0:T(8,128)(2,1)S(1)} %copy-done.13), kind=kOutput, calls=%fused_computation.4 | convolution fusion | flops 2419851264 | bytes 7471104 | tf_op jit(solution)/shard_map/dot_general | solution.py:118
  156.2 3.2 %copy.20 = bf16[2048,768]{1,0:T(8,128)(2,1)S(1)} copy(bf16[2048,768]{0,1:T(8,128)(2,1)} %fusion.1) | data formatting | bytes 6291456 | tf_op jit(solution)/shard_map/convert_element_type | solution.py:118
  159.4 1.4 dynamic-slice_bitcast_fusion
  161.3 0.9 fusion.14
  162.8 1.3 copy.17
  164.1 2.2 %reshape.102 = f32[1,16,12288]{2,1,0:T(8,128)} reshape(f32[16,16,768]{2,1,0:T(8,128)} %copy.17) | data formatting | bytes 1572864 | tf_op jit(solution)/shard_map/convert_element_type | solution.py:24
  166.3 2.1 %fusion = bf16[8,4,32,768]{3,2,1,0:T(8,128)(2,1)S(1)} fusion(bf16[8,4,32,768]{3,2,1,0:T(8,128)(2,1)} %collective-permute-done.19, bf16[8,4,2,32,768]{4,3,2,1,0:T(8,128)(2,1)S(1)} %bitcast.89, s32[]{:T(128)S(6)} %select_n.90), kind=kLoop, calls=%fused_computation.3 | loop fusion | flops 3145728 | bytes 4718596 | tf_op jit(solution)/shard_map/convert_element_type | solution.py:24
  168.6 1.3 collective-permute-start.20
  169.9 2.7 %fusion.2 = bf16[768,768]{1,0:T(8,128)(2,1)S(1)} fusion(bf16[2048,768]{1,0:T(8,128)(2,1)S(1)} %bitcast.92, bf16[2048,768]{1,0:T(8,128)(2,1)S(1)} %copy-done.14), kind=kOutput, calls=%fused_computation.7 | convolution fusion | flops 2417098752 | bytes 7471104 | tf_op jit(solution)/shard_map/dot_general | solution.py:128
  172.7 1.1 collective-permute-start.25
  173.8 2.6 %collective-permute-start.22 = (bf16[8,32,384]{2,1,0:T(8,128)(2,1)S(1)}, bf16[8,32,384]{2,1,0:T(8,128)(2,1)S(1)}, u32[]{:S(2)}, u32[]{:S(2)}) collective-permute-start(bf16[8,32,384]{2,1,0:T(8,128)(2,1)S(1)} %get-tuple-element.17), channel_id=1, source_target_pairs={{0,96},{32,0},{64,32},{96,64},{1,97},{33,1},{65,33},{97,65},{2,98}... | collective-permute-start | bytes 589832 | tf_op jit(solution)/shard_map/ppermute | solution.py:16
  177.2 3.3 %collective-permute-done.22 = bf16[8,32,384]{2,1,0:T(8,128)(2,1)S(1)} collective-permute-done((bf16[8,32,384]{2,1,0:T(8,128)(2,1)S(1)}, bf16[8,32,384]{2,1,0:T(8,128)(2,1)S(1)}, u32[]{:S(2)}, u32[]{:S(2)}) %collective-permute-start.22) | collective-permute-done | bytes 196640 | tf_op jit(solution)/shard_map/ppermute | solution.py:16
  180.6 3.5 %collective-permute-start.23 = (bf16[8,32,768]{2,1,0:T(8,128)(2,1)S(1)}, bf16[8,32,768]{2,1,0:T(8,128)(2,1)S(1)}, u32[]{:S(2)}, u32[]{:S(2)}) collective-permute-start(bf16[8,32,768]{2,1,0:T(8,128)(2,1)S(1)} %pad_maximum_fusion.7), channel_id=1, source_target_pairs={{0,96},{32,0},{64,32},{96,64},{1,97},{33,1},{65,33},{97,65},{2,98}... | collective-permute-start | bytes 1179656 | tf_op jit(solution)/shard_map/ppermute | solution.py:16
  184.1 0.8 fusion.3
  184.9 4.3 %collective-permute-done.25 = bf16[768,384]{1,0:T(8,128)(2,1)S(1)} collective-permute-done((bf16[768,384]{1,0:T(8,128)(2,1)S(1)}, bf16[768,384]{1,0:T(8,128)(2,1)S(1)}, u32[]{:S(2)}, u32[]{:S(2)}) %collective-permute-start.25) | collective-permute-done | bytes 589856 | tf_op jit(solution)/shard_map/ppermute | solution.py:16
  189.4 1.9 collective-permute-done.23
  191.4 2.3 %collective-permute-start.24 = (bf16[256,384]{1,0:T(8,128)(2,1)S(1)}, bf16[256,384]{1,0:T(8,128)(2,1)S(1)}, u32[]{:S(2)}, u32[]{:S(2)}) collective-permute-start(bf16[256,384]{1,0:T(8,128)(2,1)S(1)} %slice.87), channel_id=1, source_target_pairs={{0,1},{1,0},{2,3},{3,2},{4,5},{5,4},{6,7},{7,6},{8,9},{9,8},{10,11... | collective-permute-start | bytes 589832 | tf_op jit(solution)/shard_map/ppermute | solution.py:16
  193.7 1.1 maximum_bitcast_fusion
  194.8 3.9 %collective-permute-done.24 = bf16[256,384]{1,0:T(8,128)(2,1)S(1)} collective-permute-done((bf16[256,384]{1,0:T(8,128)(2,1)S(1)}, bf16[256,384]{1,0:T(8,128)(2,1)S(1)}, u32[]{:S(2)}, u32[]{:S(2)}) %collective-permute-start.24) | collective-permute-done | bytes 196640 | tf_op jit(solution)/shard_map/ppermute | solution.py:16
  198.7 0.7 fusion.15
  199.4 1.8 copy.33
  (81 shorter events, 6.4 us)
Async XLA Ops:
  7.2 8.4 %collective-permute-start = (bf16[256,384]{1,0:T(8,128)(2,1)}, bf16[256,384]{1,0:T(8,128)(2,1)S(1)}, u32[]{:S(2)}, u32[]{:S(2)}) collective-permute-start(bf16[256,384]{1,0:T(8,128)(2,1)} %bitcast.104), channel_id=1, source_target_pairs={{0,1},{1,0},{2,3},{3,2},{4,5},{5,4},{6,7},{7,6},{8,9},{9,8},{10,11... | collective-permute-start | bytes 589832 | tf_op jit(solution)/shard_map/ppermute | solution.py:16
  15.6 17.9 %copy-start.10 = (bf16[256,384]{1,0:T(8,128)(2,1)}, bf16[256,384]{1,0:T(8,128)(2,1)S(1)}, u32[]{:S(2)}) copy-start(bf16[256,384]{1,0:T(8,128)(2,1)S(1)} %collective-permute-done) | copy-start | bytes 589828
  17.4 20.6 %collective-permute-start.2 = (bf16[256,768]{1,0:T(8,128)(2,1)}, bf16[256,768]{1,0:T(8,128)(2,1)}, u32[]{:S(2)}, u32[]{:S(2)}) collective-permute-start(bf16[256,768]{1,0:T(8,128)(2,1)} %pad_maximum_fusion.3), channel_id=1, source_target_pairs={{0,32},{32,64},{64,96},{96,0},{1,33},{33,65},{65,97},{97,1},{2,34}... | collective-permute-start | bytes 1179656 | tf_op jit(solution)/shard_map/ppermute | solution.py:16
  19.0 21.2 %collective-permute-start.4 = (bf16[256,768]{1,0:T(8,128)(2,1)}, bf16[256,768]{1,0:T(8,128)(2,1)}, u32[]{:S(2)}, u32[]{:S(2)}) collective-permute-start(bf16[256,768]{1,0:T(8,128)(2,1)} %pad_maximum_fusion.3), channel_id=1, source_target_pairs={{0,96},{32,0},{64,32},{96,64},{1,97},{33,1},{65,33},{97,65},{2,98}... | collective-permute-start | bytes 1179656 | tf_op jit(solution)/shard_map/ppermute | solution.py:16
  20.6 22.7 %collective-permute-start.1 = (bf16[256,768]{1,0:T(8,128)(2,1)}, bf16[256,768]{1,0:T(8,128)(2,1)}, u32[]{:S(2)}, u32[]{:S(2)}) collective-permute-start(bf16[256,768]{1,0:T(8,128)(2,1)} %pad_maximum_fusion.3), channel_id=1, source_target_pairs={{0,16},{16,0},{1,17},{17,1},{2,18},{18,2},{3,19},{19,3},{4,20},{20... | collective-permute-start | bytes 1179656 | tf_op jit(solution)/shard_map/ppermute | solution.py:16
  22.6 14.7 %all-to-all-start.1 = ((bf16[16,16,768]{2,1,0:T(8,128)(2,1)}), bf16[16,16,768]{2,1,0:T(8,128)(2,1)S(1)}, u32[]{:S(2)}, u32[]{:S(2)}) async-start(bf16[16,16,768]{2,1,0:T(8,128)(2,1)} %copy.19), calls=%async_computation.1 | async-start | bytes 786432 | tf_op jit(solution)/shard_map/all_to_all | solution.py:97
  27.6 122.1 %all-gather.2.cloned.1.call-start = ((), (), s32[]{:S(2)}) async-start(), calls=%async_computation.2 | async-start | bytes 3538944 | tf_op jit(solution)/shard_map/all_gather | solution.py:99
  30.0 19.8 %collective-permute-start.9 = (bf16[768,384]{1,0:T(8,128)(2,1)}, bf16[768,384]{1,0:T(8,128)(2,1)}, u32[]{:S(2)}, u32[]{:S(2)}) collective-permute-start(bf16[768,384]{1,0:T(8,128)(2,1)} %get-tuple-element.5), channel_id=1, source_target_pairs={{0,1},{1,0},{2,3},{3,2},{4,5},{5,4},{6,7},{7,6},{8,9},{9,8},{10,11... | collective-permute-start | bytes 1769480 | tf_op jit(solution)/shard_map/ppermute | solution.py:16
  33.5 0.9 copy-start.11
  37.2 0.8 copy-start.7
  39.0 8.4 %collective-permute-start.6 = (bf16[128,768]{1,0:T(8,128)(2,1)S(1)}, bf16[128,768]{1,0:T(8,128)(2,1)S(1)}, u32[]{:S(2)}, u32[]{:S(2)}) collective-permute-start(bf16[128,768]{1,0:T(8,128)(2,1)S(1)} %slice.72), channel_id=1, source_target_pairs={{0,32},{32,64},{64,96},{96,0},{1,33},{33,65},{65,97},{97,1},{2,34}... | collective-permute-start | bytes 589832 | tf_op jit(solution)/shard_map/ppermute | solution.py:16
  41.1 6.8 %collective-permute-start.7 = (bf16[128,768]{1,0:T(8,128)(2,1)S(1)}, bf16[128,768]{1,0:T(8,128)(2,1)S(1)}, u32[]{:S(2)}, u32[]{:S(2)}) collective-permute-start(bf16[128,768]{1,0:T(8,128)(2,1)S(1)} %slice.73), channel_id=1, source_target_pairs={{0,96},{32,0},{64,32},{96,64},{1,97},{33,1},{65,33},{97,65},{2,98}... | collective-permute-start | bytes 589832 | tf_op jit(solution)/shard_map/ppermute | solution.py:16
  43.3 4.8 %collective-permute-start.3 = (bf16[256,768]{1,0:T(8,128)(2,1)}, bf16[256,768]{1,0:T(8,128)(2,1)S(1)}, u32[]{:S(2)}, u32[]{:S(2)}) collective-permute-start(bf16[256,768]{1,0:T(8,128)(2,1)} %collective-permute-done.2), channel_id=1, source_target_pairs={{0,16},{16,0},{1,17},{17,1},{2,18},{18,2},{3,19},{19,3},{4,20},{20... | collective-permute-start | bytes 1179656 | tf_op jit(solution)/shard_map/ppermute | solution.py:16
  43.3 6.5 %copy-start.12 = (bf16[768,384]{1,0:T(8,128)(2,1)S(1)}, bf16[768,384]{1,0:T(8,128)(2,1)}, u32[]{:S(2)}) copy-start(bf16[768,384]{1,0:T(8,128)(2,1)} %get-tuple-element.4) | copy-start | bytes 1769476
  44.4 4.8 %collective-permute-start.5 = (bf16[256,768]{1,0:T(8,128)(2,1)}, bf16[256,768]{1,0:T(8,128)(2,1)S(1)}, u32[]{:S(2)}, u32[]{:S(2)}) collective-permute-start(bf16[256,768]{1,0:T(8,128)(2,1)} %collective-permute-done.4), channel_id=1, source_target_pairs={{0,16},{16,0},{1,17},{17,1},{2,18},{18,2},{3,19},{19,3},{4,20},{20... | collective-permute-start | bytes 1179656 | tf_op jit(solution)/shard_map/ppermute | solution.py:16
  48.0 1.8 collective-permute-start.8
  49.8 4.5 %copy-start.2 = (bf16[8,4,2,32,768]{4,3,2,1,0:T(8,128)(2,1)}, bf16[8,4,2,32,768]{4,3,2,1,0:T(8,128)(2,1)S(1)}, u32[]{:S(2)}) copy-start(bf16[8,4,2,32,768]{4,3,2,1,0:T(8,128)(2,1)S(1)} %constant_dynamic-update-slice_fusion.2) | copy-start | bytes 9437188
  54.3 1.7 copy-start.5
  56.1 38.4 %copy-start.6 = (bf16[2048,768]{1,0:T(8,128)(2,1)S(1)}, bf16[2048,768]{1,0:T(8,128)(2,1)}, u32[]{:S(2)}) copy-start(bf16[2048,768]{1,0:T(8,128)(2,1)} %copy-done.5) | copy-start | bytes 9437188
  56.8 15.5 %collective-permute-start.10 = (bf16[256,384]{1,0:T(8,128)(2,1)S(1)}, bf16[256,384]{1,0:T(8,128)(2,1)S(1)}, u32[]{:S(2)}, u32[]{:S(2)}) collective-permute-start(bf16[256,384]{1,0:T(8,128)(2,1)S(1)} %get-tuple-element.20), channel_id=1, source_target_pairs={{0,2},{2,4},{4,6},{6,8},{8,10},{10,12},{12,14},{14,0},{1,3},{3,5},... | collective-permute-start | bytes 589832 | tf_op jit(solution)/shard_map/ppermute | solution.py:16
  58.7 14.5 %collective-permute-start.14 = (bf16[256,384]{1,0:T(8,128)(2,1)}, bf16[256,384]{1,0:T(8,128)(2,1)}, u32[]{:S(2)}, u32[]{:S(2)}) collective-permute-start(bf16[256,384]{1,0:T(8,128)(2,1)} %get-tuple-element.21), channel_id=1, source_target_pairs={{0,14},{2,0},{4,2},{6,4},{8,6},{10,8},{12,10},{14,12},{1,15},{3,1}... | collective-permute-start | bytes 589832 | tf_op jit(solution)/shard_map/ppermute | solution.py:16
  73.1 21.4 %collective-permute-start.11 = (bf16[256,768]{1,0:T(8,128)(2,1)}, bf16[256,768]{1,0:T(8,128)(2,1)}, u32[]{:S(2)}, u32[]{:S(2)}) collective-permute-start(bf16[256,768]{1,0:T(8,128)(2,1)} %pad_maximum_fusion.4), channel_id=1, source_target_pairs={{0,2},{2,4},{4,6},{6,8},{8,10},{10,12},{12,14},{14,0},{1,3},{3,5},... | collective-permute-start | bytes 1179656 | tf_op jit(solution)/shard_map/ppermute | solution.py:16
  74.2 22.2 %collective-permute-start.15 = (bf16[256,768]{1,0:T(8,128)(2,1)S(1)}, bf16[256,768]{1,0:T(8,128)(2,1)}, u32[]{:S(2)}, u32[]{:S(2)}) collective-permute-start(bf16[256,768]{1,0:T(8,128)(2,1)S(1)} %pad_maximum_fusion.5), channel_id=1, source_target_pairs={{0,14},{2,0},{4,2},{6,4},{8,6},{10,8},{12,10},{14,12},{1,15},{3,1}... | collective-permute-start | bytes 1179656 | tf_op jit(solution)/shard_map/ppermute | solution.py:16
  96.3 11.1 %collective-permute-start.12 = (bf16[256,768]{1,0:T(8,128)(2,1)}, bf16[256,768]{1,0:T(8,128)(2,1)}, u32[]{:S(2)}, u32[]{:S(2)}) collective-permute-start(bf16[256,768]{1,0:T(8,128)(2,1)} %fusion.10), channel_id=1, source_target_pairs={{0,2},{2,4},{4,6},{6,8},{8,10},{10,12},{12,14},{14,0},{1,3},{3,5},... | collective-permute-start | bytes 1179656 | tf_op jit(solution)/shard_map/ppermute | solution.py:16
  109.6 9.0 %collective-permute-start.16 = (bf16[256,768]{1,0:T(8,128)(2,1)}, bf16[256,768]{1,0:T(8,128)(2,1)}, u32[]{:S(2)}, u32[]{:S(2)}) collective-permute-start(bf16[256,768]{1,0:T(8,128)(2,1)} %get-tuple-element.7), channel_id=1, source_target_pairs={{0,14},{2,0},{4,2},{6,4},{8,6},{10,8},{12,10},{14,12},{1,15},{3,1}... | collective-permute-start | bytes 1179656 | tf_op jit(solution)/shard_map/ppermute | solution.py:16
  109.6 12.3 %collective-permute-start.13 = (bf16[256,768]{1,0:T(8,128)(2,1)}, bf16[256,768]{1,0:T(8,128)(2,1)S(1)}, u32[]{:S(2)}, u32[]{:S(2)}) collective-permute-start(bf16[256,768]{1,0:T(8,128)(2,1)} %get-tuple-element.6), channel_id=1, source_target_pairs={{0,2},{2,4},{4,6},{6,8},{8,10},{10,12},{12,14},{14,0},{1,3},{3,5},... | collective-permute-start | bytes 1179656 | tf_op jit(solution)/shard_map/ppermute | solution.py:16
  120.4 8.1 %collective-permute-start.17 = (bf16[256,768]{1,0:T(8,128)(2,1)}, bf16[256,768]{1,0:T(8,128)(2,1)}, u32[]{:S(2)}, u32[]{:S(2)}) collective-permute-start(bf16[256,768]{1,0:T(8,128)(2,1)} %fusion.9), channel_id=1, source_target_pairs={{0,14},{2,0},{4,2},{6,4},{8,6},{10,8},{12,10},{14,12},{1,15},{3,1}... | collective-permute-start | bytes 1179656 | tf_op jit(solution)/shard_map/ppermute | solution.py:16
  130.4 19.3 %copy-start.13 = (bf16[768,384]{1,0:T(8,128)(2,1)S(1)}, bf16[768,384]{1,0:T(8,128)(2,1)}, u32[]{:S(2)}) copy-start(bf16[768,384]{1,0:T(8,128)(2,1)} %get-tuple-element.4) | copy-start | bytes 1769476
  130.4 17.3 %all-to-all-start = ((bf16[16,16,768]{2,1,0:T(8,128)(2,1)}), bf16[16,16,768]{2,1,0:T(8,128)(2,1)S(1)}, u32[]{:S(2)}, u32[]{:S(2)}) async-start(bf16[16,16,768]{2,1,0:T(8,128)(2,1)} %bitcast.22), calls=%async_computation | async-start | bytes 786432 | tf_op jit(solution)/shard_map/all_to_all | solution.py:112
  159.3 1.8 copy-start.1
  159.3 1.8 copy-start.8
  159.4 1.9 copy-start.9
  159.4 3.4 %copy-start.4 = (f32[16,16,768]{2,0,1:T(8,128)S(1)}, f32[16,16,768]{2,0,1:T(8,128)}, u32[]{:S(2)}) copy-start(f32[16,16,768]{2,0,1:T(8,128)} %get-tuple-element.19) | copy-start | bytes 2359300
  160.8 5.6 %collective-permute-start.19 = (bf16[8,4,32,768]{3,2,1,0:T(8,128)(2,1)}, bf16[8,4,32,768]{3,2,1,0:T(8,128)(2,1)}, u32[]{:S(2)}, u32[]{:S(2)}) collective-permute-start(bf16[8,4,32,768]{3,2,1,0:T(8,128)(2,1)} %dynamic-slice_bitcast_fusion), channel_id=1, source_target_pairs={{0,16},{16,0},{1,17},{17,1},{2,18},{18,2},{3,19},{19,3},{4,20},{20... | collective-permute-start | bytes 4718600 | tf_op jit(solution)/shard_map/ppermute | solution.py:16
  162.1 22.8 %collective-permute-start.18 = (bf16[16,12288]{1,0:T(8,128)(2,1)}, bf16[16,12288]{1,0:T(8,128)(2,1)}, u32[]{:S(2)}, u32[]{:S(2)}) collective-permute-start(bf16[16,12288]{1,0:T(8,128)(2,1)} %fusion.14), channel_id=1, source_target_pairs={{0,128},{128,0},{1,129},{129,1},{2,130},{130,2},{3,131},{131,3},{4... | collective-permute-start | bytes 1179656 | tf_op jit(solution)/shard_map/ppermute | solution.py:16
  166.3 3.6 %copy-start.3 = (bf16[8,4,2,32,768]{4,3,2,1,0:T(8,128)(2,1)S(1)}, bf16[8,4,2,32,768]{4,3,2,1,0:T(8,128)(2,1)}, u32[]{:S(2)}) copy-start(bf16[8,4,2,32,768]{4,3,2,1,0:T(8,128)(2,1)} %copy-done.2) | copy-start | bytes 9437188
  166.3 3.6 %copy-start.14 = (bf16[2048,768]{1,0:T(8,128)(2,1)S(1)}, bf16[2048,768]{1,0:T(8,128)(2,1)}, u32[]{:S(2)}) copy-start(bf16[2048,768]{1,0:T(8,128)(2,1)} %all-gather.2.cloned.1.call-done) | copy-start | bytes 9437188
  168.6 8.4 %collective-permute-start.20 = (bf16[8,32,384]{2,1,0:T(8,128)(2,1)S(1)}, bf16[8,32,384]{2,1,0:T(8,128)(2,1)S(1)}, u32[]{:S(2)}, u32[]{:S(2)}) collective-permute-start(bf16[8,32,384]{2,1,0:T(8,128)(2,1)S(1)} %get-tuple-element.16), channel_id=1, source_target_pairs={{0,32},{32,64},{64,96},{96,0},{1,33},{33,65},{65,97},{97,1},{2,34}... | collective-permute-start | bytes 589832 | tf_op jit(solution)/shard_map/ppermute | solution.py:16
  172.6 11.5 %copy-start = (f32[1,16,12288]{2,1,0:T(8,128)S(1)}, f32[1,16,12288]{2,1,0:T(8,128)}, u32[]{:S(2)}) copy-start(f32[1,16,12288]{2,1,0:T(8,128)} %reshape.102) | copy-start | bytes 2359300
  172.7 16.6 %collective-permute-start.25 = (bf16[768,384]{1,0:T(8,128)(2,1)S(1)}, bf16[768,384]{1,0:T(8,128)(2,1)S(1)}, u32[]{:S(2)}, u32[]{:S(2)}) collective-permute-start(bf16[768,384]{1,0:T(8,128)(2,1)S(1)} %slice.89), channel_id=1, source_target_pairs={{0,1},{1,0},{2,3},{3,2},{4,5},{5,4},{6,7},{7,6},{8,9},{9,8},{10,11... | collective-permute-start | bytes 1769480 | tf_op jit(solution)/shard_map/ppermute | solution.py:16
  173.8 6.7 %collective-permute-start.22 = (bf16[8,32,384]{2,1,0:T(8,128)(2,1)S(1)}, bf16[8,32,384]{2,1,0:T(8,128)(2,1)S(1)}, u32[]{:S(2)}, u32[]{:S(2)}) collective-permute-start(bf16[8,32,384]{2,1,0:T(8,128)(2,1)S(1)} %get-tuple-element.17), channel_id=1, source_target_pairs={{0,96},{32,0},{64,32},{96,64},{1,97},{33,1},{65,33},{97,65},{2,98}... | collective-permute-start | bytes 589832 | tf_op jit(solution)/shard_map/ppermute | solution.py:16
  177.1 12.3 %collective-permute-start.21 = (bf16[8,32,768]{2,1,0:T(8,128)(2,1)S(1)}, bf16[8,32,768]{2,1,0:T(8,128)(2,1)S(1)}, u32[]{:S(2)}, u32[]{:S(2)}) collective-permute-start(bf16[8,32,768]{2,1,0:T(8,128)(2,1)S(1)} %pad_maximum_fusion.6), channel_id=1, source_target_pairs={{0,32},{32,64},{64,96},{96,0},{1,33},{33,65},{65,97},{97,1},{2,34}... | collective-permute-start | bytes 1179656 | tf_op jit(solution)/shard_map/ppermute | solution.py:16
  180.6 10.7 %collective-permute-start.23 = (bf16[8,32,768]{2,1,0:T(8,128)(2,1)S(1)}, bf16[8,32,768]{2,1,0:T(8,128)(2,1)S(1)}, u32[]{:S(2)}, u32[]{:S(2)}) collective-permute-start(bf16[8,32,768]{2,1,0:T(8,128)(2,1)S(1)} %pad_maximum_fusion.7), channel_id=1, source_target_pairs={{0,96},{32,0},{64,32},{96,64},{1,97},{33,1},{65,33},{97,65},{2,98}... | collective-permute-start | bytes 1179656 | tf_op jit(solution)/shard_map/ppermute | solution.py:16
  191.4 7.3 %collective-permute-start.24 = (bf16[256,384]{1,0:T(8,128)(2,1)S(1)}, bf16[256,384]{1,0:T(8,128)(2,1)S(1)}, u32[]{:S(2)}, u32[]{:S(2)}) collective-permute-start(bf16[256,384]{1,0:T(8,128)(2,1)S(1)} %slice.87), channel_id=1, source_target_pairs={{0,1},{1,0},{2,3},{3,2},{4,5},{5,4},{6,7},{7,6},{8,9},{9,8},{10,11... | collective-permute-start | bytes 589832 | tf_op jit(solution)/shard_map/ppermute | solution.py:16
Sparse Core Ops, SparseCore 0:
  38.1 58.5 all-gather.1

commit v3 on v1

v3 whole, which is shorter than its diff:
```python
import math

import jax
import jax.numpy as jnp
from jax import lax
from jax.sharding import Mesh
from jax.sharding import PartitionSpec as P

BF16 = jnp.bfloat16
F32 = jnp.float32
GROUP = ("y", "core", "xh")


def shift(value, axis, by):
    n = lax.axis_size(axis)
    return lax.ppermute(value, axis, [(i, (i + by) % n) for i in range(n)])


def swap(value, axis):
    return shift(value, axis, 1)


def add(a, b):
    return (a.astype(F32) + b.astype(F32)).astype(BF16)


def wrap(index, n):
    return index & (n - 1)


def pick(stack, index):
    return lax.dynamic_index_in_dim(stack, index, 0, keepdims=False)


def place(buffer, block, starts):
    return lax.dynamic_update_slice(buffer, block, starts)


def tie(*values):
    return lax.optimization_barrier(values)


def both_ways(right, left, axis):
    return shift(right, axis, 1), shift(left, axis, -1)


def shards(segment_input, context, out_proj, grad_output):
    residual = segment_input[0]
    contexts = context[0]
    weights = out_proj[0]
    upstream = grad_output[0]
    section, y, core, z, xh = (lax.axis_index(name) for name in ("section", "y", "core", "z", "xh"))
    n_y, n_core, n_z, n_xh = (lax.axis_size(name) for name in ("y", "core", "z", "xh"))
    n_group = n_y * n_core * n_xh
    own_count, model = upstream.shape
    group_tokens, width = contexts.shape
    features = model // n_group
    tokens = group_tokens * n_y * n_core
    z_tokens = own_count * n_xh
    half = group_tokens // 2
    left_half = features // 2

    spread = upstream.reshape(own_count, n_group, features).transpose(1, 0, 2)
    spread = lax.all_to_all(spread, GROUP, 0, 0, tiled=True).reshape(n_group * own_count, features)
    row = (y * n_core + core) * n_xh
    own_rows = lax.dynamic_slice_in_dim(weights, (row + xh) * features, features, 0)
    partner_rows = lax.dynamic_slice_in_dim(weights, (row + 1 - xh) * features, features, 0)
    both = jnp.concatenate([contexts, swap(contexts, "xh")], 1)

    both, partner_rows = tie(both, partner_rows)
    ctx_left, ctx_right = both_ways(both, both, "y")
    came_rows = swap(partner_rows, "xh")
    block = jnp.concatenate([own_rows, came_rows], 1)

    ctx_left, ctx_right, spread = tie(ctx_left, ctx_right, spread)
    grads = {0: spread}
    grads[-1], grads[1] = both_ways(spread, spread, "z")
    across_low, across_high = both_ways(ctx_left[:half], ctx_right[half:], "y")
    near = swap(jnp.stack([both, ctx_left, ctx_right]), "core")

    grads[-1], grads[1], across_low, across_high, near = tie(grads[-1], grads[1], across_low, across_high, near)
    grads[-2], grads[2] = both_ways(grads[-1], grads[1], "z")
    across = jnp.concatenate([across_low, across_high], 0)
    far = swap(across, "core")
    ctx_all = jnp.zeros((n_z, n_y, n_core, z_tokens, 2 * width), BF16)
    for away, mine, other in ((0, both, near[0]), (-1, ctx_left, near[1]), (1, ctx_right, near[2]), (2, across, far)):
        there = wrap(y + away, n_y)
        for at, part in ((core, mine), (1 - core, other)):
            ctx_all = place(ctx_all, part.reshape(n_z, 1, 1, z_tokens, 2 * width), (0, there, at, 0, 0))
    ctx_flat = ctx_all.reshape(tokens, 2 * width)
    partial_branch = lax.dot_general(
        ctx_flat, block, (((1,), (1,)), ((), ())), preferred_element_type=F32
    ).astype(BF16).reshape(n_z, tokens // n_z, features)

    def chunk(away):
        return pick(partial_branch, wrap(z + away, n_z))

    opposite = chunk(4)
    low, high = opposite[:, :left_half], opposite[:, left_half:]
    grads[-2], grads[2], low, high = tie(grads[-2], grads[2], low, high)
    grads[-3], grads[3] = both_ways(grads[-2], grads[2], "z")
    low, high = both_ways(low, high, "z")
    early = swap(jnp.where(section == 0, residual, upstream), "section")

    grads[-3], grads[3], low, high = tie(grads[-3], grads[3], low, high)
    far_low, far_high = both_ways(grads[-3][:half], grads[3][half:], "z")
    ahead, behind = chunk(3), chunk(-3)
    right = jnp.concatenate([add(ahead[:, :left_half], low), ahead[:, left_half:]], 1)
    left = jnp.concatenate([behind[:, :left_half], add(behind[:, left_half:], high)], 1)
    right, left = both_ways(right, left, "z")

    right, left, far_low, far_high = tie(right, left, far_low, far_high)
    grads[4] = jnp.concatenate([far_low, far_high], 0)
    right, left = both_ways(add(chunk(2), right), add(chunk(-2), left), "z")
    grad_all = jnp.zeros((n_z, tokens // n_z, features), BF16)
    for away, piece in grads.items():
        grad_all = place(grad_all, piece[None], (wrap(z + away, n_z), 0, 0))
    grad_flat = grad_all.reshape(tokens, features)
    partial_ctx = jnp.dot(grad_flat, block, preferred_element_type=F32).astype(BF16)
    partial_ctx = partial_ctx.reshape(n_z, n_y, n_core, z_tokens, 2 * width)
    other_ctx = swap(lax.dynamic_index_in_dim(partial_ctx, 1 - core, 2, keepdims=False), "core")
    norm_factor = 1.0 / math.sqrt(tokens)
    product = lax.dot_general(grad_flat, ctx_flat, (((0,), (0,)), ((), ())), preferred_element_type=F32)
    product = (norm_factor * product).astype(BF16)

    right, left, other_ctx = tie(right, left, other_ctx)
    right, left = both_ways(add(chunk(1), right), add(chunk(-1), left), "z")
    by_y = add(lax.dynamic_index_in_dim(partial_ctx, core, 2, keepdims=False), other_ctx)

    def of_y(away):
        return lax.dynamic_index_in_dim(by_y, wrap(y + away, n_y), 1, keepdims=False).reshape(group_tokens, 2 * width)

    across = of_y(2)
    sum_low, sum_high = both_ways(across[:, :width], across[:, width:], "y")
    came = swap(product[:, width:], "xh")

    right, left, sum_low, sum_high = tie(right, left, sum_low, sum_high)
    own = chunk(0).astype(F32) + right.astype(F32) + left.astype(F32)
    own = own.astype(BF16).reshape(1, n_group, own_count, features)
    sent = jnp.concatenate([own, own], 0).reshape(2 * n_group, own_count, features)
    branch = lax.all_to_all(sent, ("section",) + GROUP, 0, 0, tiled=True)
    ahead, behind = of_y(1), of_y(-1)
    ctx_right = jnp.concatenate([add(ahead[:, :width], sum_low), ahead[:, width:]], 1)
    ctx_left = jnp.concatenate([behind[:, :width], add(behind[:, width:], sum_high)], 1)
    ctx_right, ctx_left = both_ways(ctx_right, ctx_left, "y")
    summed = of_y(0).astype(F32) + ctx_right.astype(F32) + ctx_left.astype(F32)
    ctx_grad = add(summed[:, :width], swap(summed[:, width:].astype(BF16), "xh"))

    branch = branch.reshape(2, n_group, own_count, features).transpose(0, 2, 1, 3).reshape(2, own_count, model)
    forward = add(residual, pick(branch, section))
    received = jnp.where(section == 0, early, add(early, branch[0]))
    kept = product[:, :width]
    first = xh == 0
    weight_grad = jnp.concatenate([jnp.where(first, kept, came), jnp.where(first, came, kept)], 0)
    return (forward[None], received[None], ctx_grad[None], weight_grad[None])


def solution(mesh):
    fine = Mesh(mesh.devices.reshape(2, 4, 2, 8, 2), ("section", "y", "core", "z", "xh"))
    tokens = P("section", ("y", "core", "z", "xh"), None)
    heads = P("section", ("y", "core"), ("z", "xh"))
    return jax.shard_map(
        shards,
        mesh=fine,
        in_specs=(tokens, heads, P("section", None, ("z", "xh")), tokens),
        out_specs=(tokens, tokens, heads, heads),
        check_vma=False,
    )
```

time: 169 us -> 170 us (level)
  blocking collectives: 0 us -> 14.3 us
  local copies, waits for them, and re-layouts: 12.9 us -> 6.8 us
  waiting for transfers between devices: 67.3 us -> 62.5 us
  starting transfers between devices: 62.5 us -> 58.6 us
    all_to_all x0 -> x1, blocking collectives: none -> 14.3 us  [shards(): lax.all_to_all(spread, GROUP, 0, 0, tiled=True)]
    all_to_all x2 -> x1, starting transfers between devices: 10.1 us -> 5.48 us  [shards(): branch = lax.all_to_all(sent, ('section',) + GROUP, 0, 0, tiled=True)]
    unnamed x21 -> x23, local copies, waits for them, and re-layouts: 4.62 us -> 0.18 us
    all_to_all x2 -> x1, waiting for transfers between devices: 4.32 us -> 0.01 us  [shards(): branch = lax.all_to_all(sent, ('section',) + GROUP, 0, 0, tiled=True)]
    broadcast_in_dim x2 -> x3, other arithmetic: 1.86 us -> 3.83 us  [shards(): return (forward[None], received[None], ctx_grad[None], weight_grad[None])]
    ppermute x34 -> x32, starting transfers between devices: 52.3 us -> 53.1 us  [shift(): return lax.ppermute(value, axis, [(i, (i + by) % n) for i in range(n)])]
    ppermute x34 -> x32, waiting for transfers between devices: 62.9 us -> 62.5 us  [shift(): return lax.ppermute(value, axis, [(i, (i + by) % n) for i in range(n)])]
    convert_element_type x9 -> x8, other arithmetic: 5.68 us -> 5.61 us  [add(): return (a.astype(F32) + b.astype(F32)).astype(BF16)]
  transfers between devices with their start and end apart: 36 -> 33, of which waited for: 13 -> 9; matrix products, arithmetic and copies ran while one was open for 20% -> 14% of each run, Pallas kernels for 0% -> 0%
where the time goes in v3:
time: 170 us; the launch traced here: 168 us
  waiting for transfers between devices  62.5 us (37%)
  starting transfers between devices  58.6 us (34%)
  other arithmetic  16 us (9%)
  blocking collectives  14.3 us (8%)
  matrix products  8.46 us (5%)
  local copies, waits for them, and re-layouts  6.8 us (4%)
    ppermute x32, waiting for transfers between devices, shift(): return lax.ppermute(value, axis, [(i, (i + by) % n) for i in range(n)])  62.5 us
    ppermute x32, starting transfers between devices, shift(): return lax.ppermute(value, axis, [(i, (i + by) % n) for i in range(n)])  53.1 us
    all_to_all x1, blocking collectives, shards(): lax.all_to_all(spread, GROUP, 0, 0, tiled=True)  14.3 us
    convert_element_type x8, other arithmetic, add(): return (a.astype(F32) + b.astype(F32)).astype(BF16)  5.61 us
    all_to_all x1, starting transfers between devices, shards(): branch = lax.all_to_all(sent, ('section',) + GROUP, 0, 0, tiled=True)  5.48 us
    broadcast_in_dim x3, other arithmetic, shards(): return (forward[None], received[None], ctx_grad[None], weight_grad[None])  3.83 us
  transfers between devices with their start and end apart: 33, of which 9 were waited for; matrix products, arithmetic and copies ran while one was open for 14% of the time, Pallas kernels for 0%

profile of v3, /device:TPU:2, one launch (start us, length us, event | category | flops | bytes accessed | tf_op | source)
XLA Modules:
  0.0 168.1 jit_solution(6839484127988413950)
XLA Ops:
  0.6 2.2 %collective-permute-start = (bf16[256,384]{1,0:T(8,128)(2,1)}, bf16[256,384]{1,0:T(8,128)(2,1)S(1)}, u32[]{:S(2)}, u32[]{:S(2)}) collective-permute-start(bf16[256,384]{1,0:T(8,128)(2,1)} %bitcast.136), channel_id=1, source_target_pairs={{0,1},{1,0},{2,3},{3,2},{4,5},{5,4},{6,7},{7,6},{8,9},{9,8},{10,11... | collective-permute-start | bytes 589832 | tf_op jit(solution)/shard_map/ppermute | solution.py:16
  2.9 2.4 %dynamic-slice_bitcast_fusion.1 = (bf16[768,384]{1,0:T(8,128)(2,1)}, bf16[768,384]{1,0:T(8,128)(2,1)}) fusion(bf16[1,12288,384]{2,1,0:T(8,128)(2,1)} %param.6, s32[]{:T(128)S(6)} %select_n.115, s32[]{:T(128)S(6)} %select_n.108), kind=kLoop, calls=%fused_computation.26 | loop fusion | bytes 2359304 | tf_op jit(solution)/shard_map/dynamic_slice | solution.py:66
  5.3 3.8 %collective-permute-done = bf16[256,384]{1,0:T(8,128)(2,1)S(1)} collective-permute-done((bf16[256,384]{1,0:T(8,128)(2,1)}, bf16[256,384]{1,0:T(8,128)(2,1)S(1)}, u32[]{:S(2)}, u32[]{:S(2)}) %collective-permute-start) | collective-permute-done | bytes 196640 | tf_op jit(solution)/shard_map/ppermute | solution.py:16
  9.1 1.0 pad_maximum_fusion.5
  10.0 1.7 collective-permute-start.1
  11.7 1.7 collective-permute-start.2
  13.4 0.1 copy.11
  13.6 14.3 %all_to_all.10 = bf16[16,16,768]{2,1,0:T(8,128)(2,1)S(1)} all-to-all(bf16[16,16,768]{2,1,0:T(8,128)(2,1)S(1)} %copy.11), channel_id=1, replica_groups=mesh['section'=2,'y'=4,'core'=2,'z'=8,'xh'=2] {'y','core','xh'}, dimensions={0} | all-to-all | bytes 786432 | tf_op jit(solution)/shard_map/all_to_all | solution.py:64
  27.9 1.1 pad_maximum_fusion
  29.1 0.3 collective-permute-start.7
  29.4 1.9 %collective-permute-start.3 = (bf16[256,768]{1,0:T(8,128)(2,1)S(1)}, bf16[256,768]{1,0:T(8,128)(2,1)S(1)}, u32[]{:S(2)}, u32[]{:S(2)}) collective-permute-start(bf16[256,768]{1,0:T(8,128)(2,1)S(1)} %bitcast.122), channel_id=1, source_target_pairs={{0,2},{2,4},{4,6},{6,8},{8,10},{10,12},{12,14},{14,0},{1,3},{3,5},... | collective-permute-start | bytes 1179656 | tf_op jit(solution)/shard_map/ppermute | solution.py:16
  31.3 3.9 %collective-permute-start.4 = (bf16[256,768]{1,0:T(8,128)(2,1)S(1)}, bf16[256,768]{1,0:T(8,128)(2,1)}, u32[]{:S(2)}, u32[]{:S(2)}) collective-permute-start(bf16[256,768]{1,0:T(8,128)(2,1)S(1)} %bitcast.123), channel_id=1, source_target_pairs={{0,14},{2,0},{4,2},{6,4},{8,6},{10,8},{12,10},{14,12},{1,15},{3,1}... | collective-permute-start | bytes 1179656 | tf_op jit(solution)/shard_map/ppermute | solution.py:16
  35.3 0.4 broadcast_in_dim.40
  35.7 0.9 collective-permute-start.5
  36.6 2.4 %collective-permute-start.6 = (bf16[128,768]{1,0:T(8,128)(2,1)S(1)}, bf16[128,768]{1,0:T(8,128)(2,1)S(1)}, u32[]{:S(2)}, u32[]{:S(2)}) collective-permute-start(bf16[128,768]{1,0:T(8,128)(2,1)S(1)} %slice.75), channel_id=1, source_target_pairs={{0,96},{32,0},{64,32},{96,64},{1,97},{33,1},{65,33},{97,65},{2,98}... | collective-permute-start | bytes 589832 | tf_op jit(solution)/shard_map/ppermute | solution.py:16
  39.1 0.2 broadcast_in_dim.41
  39.3 4.4 %collective-permute-done.5 = bf16[128,768]{1,0:T(8,128)(2,1)S(1)} collective-permute-done((bf16[128,768]{1,0:T(8,128)(2,1)S(1)}, bf16[128,768]{1,0:T(8,128)(2,1)S(1)}, u32[]{:S(2)}, u32[]{:S(2)}) %collective-permute-start.5) | collective-permute-done | bytes 196640 | tf_op jit(solution)/shard_map/ppermute | solution.py:16
  43.7 1.9 %collective-permute-start.9 = (bf16[768,384]{1,0:T(8,128)(2,1)S(1)}, bf16[768,384]{1,0:T(8,128)(2,1)S(1)}, u32[]{:S(2)}, u32[]{:S(2)}) collective-permute-start(bf16[768,384]{1,0:T(8,128)(2,1)S(1)} %copy-done.9), channel_id=1, source_target_pairs={{0,1},{1,0},{2,3},{3,2},{4,5},{5,4},{6,7},{7,6},{8,9},{9,8},{10,11... | collective-permute-start | bytes 1769480 | tf_op jit(solution)/shard_map/ppermute | solution.py:16
  45.7 0.1 collective-permute-start.8
  45.8 0.1 collective-permute-start.10
  45.9 3.2 %collective-permute-start.11 = (bf16[256,768]{1,0:T(8,128)(2,1)}, bf16[256,768]{1,0:T(8,128)(2,1)S(1)}, u32[]{:S(2)}, u32[]{:S(2)}) collective-permute-start(bf16[256,768]{1,0:T(8,128)(2,1)} %collective-permute-done.4), channel_id=1, source_target_pairs={{0,14},{2,0},{4,2},{6,4},{8,6},{10,8},{12,10},{14,12},{1,15},{3,1}... | collective-permute-start | bytes 1179656 | tf_op jit(solution)/shard_map/ppermute | solution.py:16
  49.2 1.1 fusion.15
  50.6 8.8 %collective-permute-done.9 = bf16[768,384]{1,0:T(8,128)(2,1)S(1)} collective-permute-done((bf16[768,384]{1,0:T(8,128)(2,1)S(1)}, bf16[768,384]{1,0:T(8,128)(2,1)S(1)}, u32[]{:S(2)}, u32[]{:S(2)}) %collective-permute-start.9) | collective-permute-done | bytes 589856 | tf_op jit(solution)/shard_map/ppermute | solution.py:16
  59.5 2.9 %convolution_convert_fusion.1 = bf16[2048,768]{1,0:T(8,128)(2,1)S(1)} fusion(bf16[2048,768]{1,0:T(8,128)(2,1)S(1)} %bitcast.107, bf16[768,384]{1,0:T(8,128)(2,1)S(1)} %collective-permute-done.9, bf16[768,384]{1,0:T(8,128)(2,1)S(1)} %copy-done.8), kind=kOutput, calls=%fused_computation.1 | convolution fusion | flops 2419851264 | bytes 7471104 | tf_op jit(solution)/shard_map/dot_general | solution.py:91
  62.4 0.1 dynamic-slice_bitcast_fusion.3
  62.5 0.1 collective-permute-start.12
  62.6 3.2 %collective-permute-start.13 = (bf16[256,768]{1,0:T(8,128)(2,1)S(1)}, bf16[256,768]{1,0:T(8,128)(2,1)S(1)}, u32[]{:S(2)}, u32[]{:S(2)}) collective-permute-start(bf16[256,768]{1,0:T(8,128)(2,1)S(1)} %collective-permute-done.11), channel_id=1, source_target_pairs={{0,14},{2,0},{4,2},{6,4},{8,6},{10,8},{12,10},{14,12},{1,15},{3,1}... | collective-permute-start | bytes 1179656 | tf_op jit(solution)/shard_map/ppermute | solution.py:16
  65.8 3.2 %collective-permute-start.15 = (bf16[256,384]{1,0:T(8,128)(2,1)S(1)}, bf16[256,384]{1,0:T(8,128)(2,1)S(1)}, u32[]{:S(2)}, u32[]{:S(2)}) collective-permute-start(bf16[256,384]{1,0:T(8,128)(2,1)S(1)} %get-tuple-element.46), channel_id=1, source_target_pairs={{0,14},{2,0},{4,2},{6,4},{8,6},{10,8},{12,10},{14,12},{1,15},{3,1}... | collective-permute-start | bytes 589832 | tf_op jit(solution)/shard_map/ppermute | solution.py:16
  69.2 7.9 %collective-permute-done.14 = bf16[256,384]{1,0:T(8,128)(2,1)S(1)} collective-permute-done((bf16[256,384]{1,0:T(8,128)(2,1)S(1)}, bf16[256,384]{1,0:T(8,128)(2,1)S(1)}, u32[]{:S(2)}, u32[]{:S(2)}) %collective-permute-start.14) | collective-permute-done | bytes 196640 | tf_op jit(solution)/shard_map/ppermute | solution.py:16
  77.3 3.0 %collective-permute-start.17 = (bf16[256,768]{1,0:T(8,128)(2,1)S(1)}, bf16[256,768]{1,0:T(8,128)(2,1)S(1)}, u32[]{:S(2)}, u32[]{:S(2)}) collective-permute-start(bf16[256,768]{1,0:T(8,128)(2,1)S(1)} %pad_maximum_fusion.7), channel_id=1, source_target_pairs={{0,14},{2,0},{4,2},{6,4},{8,6},{10,8},{12,10},{14,12},{1,15},{3,1}... | collective-permute-start | bytes 1179656 | tf_op jit(solution)/shard_map/ppermute | solution.py:16
  80.4 0.1 collective-permute-start.16
  80.5 0.1 collective-permute-start.18
  80.6 3.3 %collective-permute-start.19 = (bf16[128,768]{1,0:T(8,128)(2,1)S(1)}, bf16[128,768]{1,0:T(8,128)(2,1)S(1)}, u32[]{:S(2)}, u32[]{:S(2)}) collective-permute-start(bf16[128,768]{1,0:T(8,128)(2,1)S(1)} %slice.86), channel_id=1, source_target_pairs={{0,14},{2,0},{4,2},{6,4},{8,6},{10,8},{12,10},{14,12},{1,15},{3,1}... | collective-permute-start | bytes 589832 | tf_op jit(solution)/shard_map/ppermute | solution.py:16
  84.0 9.5 %collective-permute-done.18 = bf16[128,768]{1,0:T(8,128)(2,1)S(1)} collective-permute-done((bf16[128,768]{1,0:T(8,128)(2,1)S(1)}, bf16[128,768]{1,0:T(8,128)(2,1)S(1)}, u32[]{:S(2)}, u32[]{:S(2)}) %collective-permute-start.18) | collective-permute-done | bytes 196640 | tf_op jit(solution)/shard_map/ppermute | solution.py:16
  93.6 2.8 %convolution_convert_fusion = bf16[2048,768]{1,0:T(8,128)(2,1)S(1)} fusion(bf16[2048,768]{1,0:T(8,128)(2,1)S(1)} %bitcast.109, bf16[768,384]{1,0:T(8,128)(2,1)S(1)} %collective-permute-done.9, bf16[768,384]{1,0:T(8,128)(2,1)S(1)} %copy-done.8), kind=kOutput, calls=%fused_computation | convolution fusion | flops 2419851264 | bytes 7471104 | tf_op jit(solution)/shard_map/dot_general | solution.py:119
  96.4 1.3 dynamic-slice_bitcast_fusion
  97.7 1.1 fusion.3
  98.8 3.2 %collective-permute-start.21 = (bf16[256,768]{1,0:T(8,128)(2,1)}, bf16[256,768]{1,0:T(8,128)(2,1)}, u32[]{:S(2)}, u32[]{:S(2)}) collective-permute-start(bf16[256,768]{1,0:T(8,128)(2,1)} %get-tuple-element.66), channel_id=1, source_target_pairs={{0,14},{2,0},{4,2},{6,4},{8,6},{10,8},{12,10},{14,12},{1,15},{3,1}... | collective-permute-start | bytes 1179656 | tf_op jit(solution)/shard_map/ppermute | solution.py:16
  102.0 0.8 select_bitcast_fusion
  102.8 1.4 collective-permute-start.27
  104.3 7.6 %collective-permute-done.20 = bf16[256,768]{1,0:T(8,128)(2,1)} collective-permute-done((bf16[256,768]{1,0:T(8,128)(2,1)}, bf16[256,768]{1,0:T(8,128)(2,1)}, u32[]{:S(2)}, u32[]{:S(2)}) %collective-permute-start.20) | collective-permute-done | bytes 393248 | tf_op jit(solution)/shard_map/ppermute | solution.py:16
  111.9 2.0 %fusion = bf16[8,4,32,768]{3,2,1,0:T(8,128)(2,1)S(1)} fusion(bf16[8,4,32,768]{3,2,1,0:T(8,128)(2,1)} %collective-permute-done.22, bf16[8,4,2,32,768]{4,3,2,1,0:T(8,128)(2,1)S(1)} %bitcast.105, s32[]{:T(128)S(6)} %select_n.110), kind=kLoop, calls=%fused_computation.3 | loop fusion | flops 3145728 | bytes 4718596 | tf_op jit(solution)/shard_map/convert_element_type | solution.py:24
  113.8 0.1 constant_dynamic-slice_fusion.2
  114.0 0.9 collective-permute-start.25
  114.9 2.4 %collective-permute-start.26 = (bf16[256,384]{1,0:T(8,128)(2,1)S(1)}, bf16[256,384]{1,0:T(8,128)(2,1)S(1)}, u32[]{:S(2)}, u32[]{:S(2)}) collective-permute-start(bf16[256,384]{1,0:T(8,128)(2,1)S(1)} %get-tuple-element.80), channel_id=1, source_target_pairs={{0,96},{32,0},{64,32},{96,64},{1,97},{33,1},{65,33},{97,65},{2,98}... | collective-permute-start | bytes 589832 | tf_op jit(solution)/shard_map/ppermute | solution.py:16
  117.3 1.5 fusion.2
  118.9 0.3 collective-permute-start.23
  119.2 3.2 %collective-permute-start.24 = (bf16[256,768]{1,0:T(8,128)(2,1)S(1)}, bf16[256,768]{1,0:T(8,128)(2,1)S(1)}, u32[]{:S(2)}, u32[]{:S(2)}) collective-permute-start(bf16[256,768]{1,0:T(8,128)(2,1)S(1)} %get-tuple-element.64), channel_id=1, source_target_pairs={{0,14},{2,0},{4,2},{6,4},{8,6},{10,8},{12,10},{14,12},{1,15},{3,1}... | collective-permute-start | bytes 1179656 | tf_op jit(solution)/shard_map/ppermute | solution.py:16
  122.4 2.8 %multiply_convert_fusion = bf16[768,768]{1,0:T(8,128)(2,1)S(1)} fusion(bf16[2048,768]{1,0:T(8,128)(2,1)S(1)} %bitcast.110, bf16[2048,768]{1,0:T(8,128)(2,1)S(1)} %bitcast.108), kind=kOutput, calls=%fused_computation.4 | convolution fusion | flops 2417098752 | bytes 7471104 | tf_op jit(solution)/shard_map/dot_general | solution.py:123
  125.3 2.7 %collective-permute-start.31 = (bf16[768,384]{1,0:T(8,128)(2,1)S(1)}, bf16[768,384]{1,0:T(8,128)(2,1)S(1)}, u32[]{:S(2)}, u32[]{:S(2)}) collective-permute-start(bf16[768,384]{1,0:T(8,128)(2,1)S(1)} %slice.114), channel_id=1, source_target_pairs={{0,1},{1,0},{2,3},{3,2},{4,5},{5,4},{6,7},{7,6},{8,9},{9,8},{10,11... | collective-permute-start | bytes 1769480 | tf_op jit(solution)/shard_map/ppermute | solution.py:16
  128.0 2.5 %collective-permute-done.23 = bf16[256,768]{1,0:T(8,128)(2,1)S(1)} collective-permute-done((bf16[256,768]{1,0:T(8,128)(2,1)S(1)}, bf16[256,768]{1,0:T(8,128)(2,1)S(1)}, u32[]{:S(2)}, u32[]{:S(2)}) %collective-permute-start.23) | collective-permute-done | bytes 393248 | tf_op jit(solution)/shard_map/ppermute | solution.py:16
  130.9 3.3 %collective-permute-start.29 = (bf16[256,768]{1,0:T(8,128)(2,1)S(1)}, bf16[256,768]{1,0:T(8,128)(2,1)}, u32[]{:S(2)}, u32[]{:S(2)}) collective-permute-start(bf16[256,768]{1,0:T(8,128)(2,1)S(1)} %pad_maximum_fusion.9), channel_id=1, source_target_pairs={{0,96},{32,0},{64,32},{96,64},{1,97},{33,1},{65,33},{97,65},{2,98}... | collective-permute-start | bytes 1179656 | tf_op jit(solution)/shard_map/ppermute | solution.py:16
  134.2 6.6 %collective-permute-done.31 = bf16[768,384]{1,0:T(8,128)(2,1)S(1)} collective-permute-done((bf16[768,384]{1,0:T(8,128)(2,1)S(1)}, bf16[768,384]{1,0:T(8,128)(2,1)S(1)}, u32[]{:S(2)}, u32[]{:S(2)}) %collective-permute-start.31) | collective-permute-done | bytes 589856 | tf_op jit(solution)/shard_map/ppermute | solution.py:16
  140.8 0.1 broadcast_select_fusion.1
  140.9 1.2 fusion.7
  142.1 1.0 pad_maximum_fusion.2
  143.0 5.5 %all-to-all-start.1 = ((bf16[32,16,768]{2,1,0:T(8,128)(2,1)}), bf16[32,16,768]{2,1,0:T(8,128)(2,1)S(1)}, u32[]{:S(2)}, u32[]{:S(2)}) async-start(bf16[32,16,768]{2,1,0:T(8,128)(2,1)} %bitcast.40), calls=%async_computation.1 | async-start | bytes 1572864 | tf_op jit(solution)/shard_map/all_to_all | solution.py:141
  148.6 1.2 fusion.1
  149.8 2.2 %collective-permute-start.30 = (bf16[256,384]{1,0:T(8,128)(2,1)S(1)}, bf16[256,384]{1,0:T(8,128)(2,1)S(1)}, u32[]{:S(2)}, u32[]{:S(2)}) collective-permute-start(bf16[256,384]{1,0:T(8,128)(2,1)S(1)} %slice.128), channel_id=1, source_target_pairs={{0,1},{1,0},{2,3},{3,2},{4,5},{5,4},{6,7},{7,6},{8,9},{9,8},{10,11... | collective-permute-start | bytes 589832 | tf_op jit(solution)/shard_map/ppermute | solution.py:16
  151.9 1.1 maximum_bitcast_fusion
  153.1 11.3 %collective-permute-done.30 = bf16[256,384]{1,0:T(8,128)(2,1)S(1)} collective-permute-done((bf16[256,384]{1,0:T(8,128)(2,1)S(1)}, bf16[256,384]{1,0:T(8,128)(2,1)S(1)}, u32[]{:S(2)}, u32[]{:S(2)}) %collective-permute-start.30) | collective-permute-done | bytes 196640 | tf_op jit(solution)/shard_map/ppermute | solution.py:16
  164.3 0.7 fusion.12
  165.1 0.8 add_convert_fusion.1
  166.1 2.0 %fusion.9 = bf16[1,16,12288]{2,1,0:T(8,128)(2,1)} fusion(bf16[16,12288]{1,0:T(8,128)(2,1)} %collective-permute-done.27, f32[16,12288]{1,0:T(8,128)S(1)} %bitcast.106, pred[]{:T(512)S(6)} %eq.7), kind=kLoop, calls=%fused_computation.30 | loop fusion | flops 786432 | bytes 1572865 | tf_op jit(solution)/shard_map/broadcast_in_dim | solution.py:155
  (89 shorter events, 1.6 us)
Async XLA Ops:
  0.6 12.7 %copy-start.5 = (bf16[1,16,12288]{2,1,0:T(8,128)(2,1)S(1)}, bf16[1,16,12288]{2,1,0:T(8,128)(2,1)}, u32[]{:S(2)}) copy-start(bf16[1,16,12288]{2,1,0:T(8,128)(2,1)} %param.7) | copy-start | bytes 1179652
  0.6 8.4 %collective-permute-start = (bf16[256,384]{1,0:T(8,128)(2,1)}, bf16[256,384]{1,0:T(8,128)(2,1)S(1)}, u32[]{:S(2)}, u32[]{:S(2)}) collective-permute-start(bf16[256,384]{1,0:T(8,128)(2,1)} %bitcast.136), channel_id=1, source_target_pairs={{0,1},{1,0},{2,3},{3,2},{4,5},{5,4},{6,7},{7,6},{8,9},{9,8},{10,11... | collective-permute-start | bytes 589832 | tf_op jit(solution)/shard_map/ppermute | solution.py:16
  10.0 17.9 %collective-permute-start.1 = (bf16[256,768]{1,0:T(8,128)(2,1)S(1)}, bf16[256,768]{1,0:T(8,128)(2,1)S(1)}, u32[]{:S(2)}, u32[]{:S(2)}) collective-permute-start(bf16[256,768]{1,0:T(8,128)(2,1)S(1)} %pad_maximum_fusion.5), channel_id=1, source_target_pairs={{0,32},{32,64},{64,96},{96,0},{1,33},{33,65},{65,97},{97,1},{2,34}... | collective-permute-start | bytes 1179656 | tf_op jit(solution)/shard_map/ppermute | solution.py:16
  11.7 16.2 %collective-permute-start.2 = (bf16[256,768]{1,0:T(8,128)(2,1)S(1)}, bf16[256,768]{1,0:T(8,128)(2,1)S(1)}, u32[]{:S(2)}, u32[]{:S(2)}) collective-permute-start(bf16[256,768]{1,0:T(8,128)(2,1)S(1)} %pad_maximum_fusion.5), channel_id=1, source_target_pairs={{0,96},{32,0},{64,32},{96,64},{1,97},{33,1},{65,33},{97,65},{2,98}... | collective-permute-start | bytes 1179656 | tf_op jit(solution)/shard_map/ppermute | solution.py:16
  29.1 16.6 %collective-permute-start.7 = (bf16[3,256,768]{2,1,0:T(8,128)(2,1)}, bf16[3,256,768]{2,1,0:T(8,128)(2,1)S(1)}, u32[]{:S(2)}, u32[]{:S(2)}) collective-permute-start(bf16[3,256,768]{2,1,0:T(8,128)(2,1)} %pad_maximum_fusion), channel_id=1, source_target_pairs={{0,16},{16,0},{1,17},{17,1},{2,18},{18,2},{3,19},{19,3},{4,20},{20... | collective-permute-start | bytes 3538952 | tf_op jit(solution)/shard_map/ppermute | solution.py:16
  29.4 16.3 %collective-permute-start.3 = (bf16[256,768]{1,0:T(8,128)(2,1)S(1)}, bf16[256,768]{1,0:T(8,128)(2,1)S(1)}, u32[]{:S(2)}, u32[]{:S(2)}) collective-permute-start(bf16[256,768]{1,0:T(8,128)(2,1)S(1)} %bitcast.122), channel_id=1, source_target_pairs={{0,2},{2,4},{4,6},{6,8},{8,10},{10,12},{12,14},{14,0},{1,3},{3,5},... | collective-permute-start | bytes 1179656 | tf_op jit(solution)/shard_map/ppermute | solution.py:16
  31.3 14.3 %collective-permute-start.4 = (bf16[256,768]{1,0:T(8,128)(2,1)S(1)}, bf16[256,768]{1,0:T(8,128)(2,1)}, u32[]{:S(2)}, u32[]{:S(2)}) collective-permute-start(bf16[256,768]{1,0:T(8,128)(2,1)S(1)} %bitcast.123), channel_id=1, source_target_pairs={{0,14},{2,0},{4,2},{6,4},{8,6},{10,8},{12,10},{14,12},{1,15},{3,1}... | collective-permute-start | bytes 1179656 | tf_op jit(solution)/shard_map/ppermute | solution.py:16
  35.6 8.1 %copy-start.9 = (bf16[768,384]{1,0:T(8,128)(2,1)S(1)}, bf16[768,384]{1,0:T(8,128)(2,1)}, u32[]{:S(2)}) copy-start(bf16[768,384]{1,0:T(8,128)(2,1)} %get-tuple-element.40) | copy-start | bytes 1769476
  35.7 8.0 %collective-permute-start.5 = (bf16[128,768]{1,0:T(8,128)(2,1)S(1)}, bf16[128,768]{1,0:T(8,128)(2,1)S(1)}, u32[]{:S(2)}, u32[]{:S(2)}) collective-permute-start(bf16[128,768]{1,0:T(8,128)(2,1)S(1)} %slice.74), channel_id=1, source_target_pairs={{0,32},{32,64},{64,96},{96,0},{1,33},{33,65},{65,97},{97,1},{2,34}... | collective-permute-start | bytes 589832 | tf_op jit(solution)/shard_map/ppermute | solution.py:16
  36.6 9.0 %collective-permute-start.6 = (bf16[128,768]{1,0:T(8,128)(2,1)S(1)}, bf16[128,768]{1,0:T(8,128)(2,1)S(1)}, u32[]{:S(2)}, u32[]{:S(2)}) collective-permute-start(bf16[128,768]{1,0:T(8,128)(2,1)S(1)} %slice.75), channel_id=1, source_target_pairs={{0,96},{32,0},{64,32},{96,64},{1,97},{33,1},{65,33},{97,65},{2,98}... | collective-permute-start | bytes 589832 | tf_op jit(solution)/shard_map/ppermute | solution.py:16
  43.7 15.8 %collective-permute-start.9 = (bf16[768,384]{1,0:T(8,128)(2,1)S(1)}, bf16[768,384]{1,0:T(8,128)(2,1)S(1)}, u32[]{:S(2)}, u32[]{:S(2)}) collective-permute-start(bf16[768,384]{1,0:T(8,128)(2,1)S(1)} %copy-done.9), channel_id=1, source_target_pairs={{0,1},{1,0},{2,3},{3,2},{4,5},{5,4},{6,7},{7,6},{8,9},{9,8},{10,11... | collective-permute-start | bytes 1769480 | tf_op jit(solution)/shard_map/ppermute | solution.py:16
  45.7 4.9 %collective-permute-start.8 = (bf16[256,768]{1,0:T(8,128)(2,1)S(1)}, bf16[256,768]{1,0:T(8,128)(2,1)S(1)}, u32[]{:S(2)}, u32[]{:S(2)}) collective-permute-start(bf16[256,768]{1,0:T(8,128)(2,1)S(1)} %constant_dynamic-update-slice_fusion.8), channel_id=1, source_target_pairs={{0,16},{16,0},{1,17},{17,1},{2,18},{18,2},{3,19},{19,3},{4,20},{20... | collective-permute-start | bytes 1179656 | tf_op jit(solution)/shard_map/ppermute | solution.py:16
  45.8 16.7 %collective-permute-start.10 = (bf16[256,768]{1,0:T(8,128)(2,1)S(1)}, bf16[256,768]{1,0:T(8,128)(2,1)S(1)}, u32[]{:S(2)}, u32[]{:S(2)}) collective-permute-start(bf16[256,768]{1,0:T(8,128)(2,1)S(1)} %collective-permute-done.3), channel_id=1, source_target_pairs={{0,2},{2,4},{4,6},{6,8},{8,10},{10,12},{12,14},{14,0},{1,3},{3,5},... | collective-permute-start | bytes 1179656 | tf_op jit(solution)/shard_map/ppermute | solution.py:16
  45.9 16.6 %collective-permute-start.11 = (bf16[256,768]{1,0:T(8,128)(2,1)}, bf16[256,768]{1,0:T(8,128)(2,1)S(1)}, u32[]{:S(2)}, u32[]{:S(2)}) collective-permute-start(bf16[256,768]{1,0:T(8,128)(2,1)} %collective-permute-done.4), channel_id=1, source_target_pairs={{0,14},{2,0},{4,2},{6,4},{8,6},{10,8},{12,10},{14,12},{1,15},{3,1}... | collective-permute-start | bytes 1179656 | tf_op jit(solution)/shard_map/ppermute | solution.py:16
  50.3 9.2 %copy-start.8 = (bf16[768,384]{1,0:T(8,128)(2,1)S(1)}, bf16[768,384]{1,0:T(8,128)(2,1)}, u32[]{:S(2)}) copy-start(bf16[768,384]{1,0:T(8,128)(2,1)} %get-tuple-element.62) | copy-start | bytes 1769476
  50.6 11.7 %copy-start = (bf16[8,4,2,32,768]{4,3,2,1,0:T(8,128)(2,1)}, bf16[8,4,2,32,768]{4,3,2,1,0:T(8,128)(2,1)S(1)}, u32[]{:S(2)}) copy-start(bf16[8,4,2,32,768]{4,3,2,1,0:T(8,128)(2,1)S(1)} %constant_dynamic-update-slice_fusion) | copy-start | bytes 9437188
  62.4 35.4 %copy-start.4 = (bf16[2048,768]{1,0:T(8,128)(2,1)}, bf16[2048,768]{1,0:T(8,128)(2,1)S(1)}, u32[]{:S(2)}) copy-start(bf16[2048,768]{1,0:T(8,128)(2,1)S(1)} %convolution_convert_fusion.1) | copy-start | bytes 9437188
  62.5 14.6 %collective-permute-start.12 = (bf16[256,768]{1,0:T(8,128)(2,1)S(1)}, bf16[256,768]{1,0:T(8,128)(2,1)S(1)}, u32[]{:S(2)}, u32[]{:S(2)}) collective-permute-start(bf16[256,768]{1,0:T(8,128)(2,1)S(1)} %collective-permute-done.10), channel_id=1, source_target_pairs={{0,2},{2,4},{4,6},{6,8},{8,10},{10,12},{12,14},{14,0},{1,3},{3,5},... | collective-permute-start | bytes 1179656 | tf_op jit(solution)/shard_map/ppermute | solution.py:16
  62.6 14.5 %collective-permute-start.13 = (bf16[256,768]{1,0:T(8,128)(2,1)S(1)}, bf16[256,768]{1,0:T(8,128)(2,1)S(1)}, u32[]{:S(2)}, u32[]{:S(2)}) collective-permute-start(bf16[256,768]{1,0:T(8,128)(2,1)S(1)} %collective-permute-done.11), channel_id=1, source_target_pairs={{0,14},{2,0},{4,2},{6,4},{8,6},{10,8},{12,10},{14,12},{1,15},{3,1}... | collective-permute-start | bytes 1179656 | tf_op jit(solution)/shard_map/ppermute | solution.py:16
  65.8 11.3 %collective-permute-start.14 = (bf16[256,384]{1,0:T(8,128)(2,1)S(1)}, bf16[256,384]{1,0:T(8,128)(2,1)S(1)}, u32[]{:S(2)}, u32[]{:S(2)}) collective-permute-start(bf16[256,384]{1,0:T(8,128)(2,1)S(1)} %get-tuple-element.45), channel_id=1, source_target_pairs={{0,2},{2,4},{4,6},{6,8},{8,10},{10,12},{12,14},{14,0},{1,3},{3,5},... | collective-permute-start | bytes 589832 | tf_op jit(solution)/shard_map/ppermute | solution.py:16
  65.8 11.3 %collective-permute-start.15 = (bf16[256,384]{1,0:T(8,128)(2,1)S(1)}, bf16[256,384]{1,0:T(8,128)(2,1)S(1)}, u32[]{:S(2)}, u32[]{:S(2)}) collective-permute-start(bf16[256,384]{1,0:T(8,128)(2,1)S(1)} %get-tuple-element.46), channel_id=1, source_target_pairs={{0,14},{2,0},{4,2},{6,4},{8,6},{10,8},{12,10},{14,12},{1,15},{3,1}... | collective-permute-start | bytes 589832 | tf_op jit(solution)/shard_map/ppermute | solution.py:16
  77.3 16.3 %collective-permute-start.17 = (bf16[256,768]{1,0:T(8,128)(2,1)S(1)}, bf16[256,768]{1,0:T(8,128)(2,1)S(1)}, u32[]{:S(2)}, u32[]{:S(2)}) collective-permute-start(bf16[256,768]{1,0:T(8,128)(2,1)S(1)} %pad_maximum_fusion.7), channel_id=1, source_target_pairs={{0,14},{2,0},{4,2},{6,4},{8,6},{10,8},{12,10},{14,12},{1,15},{3,1}... | collective-permute-start | bytes 1179656 | tf_op jit(solution)/shard_map/ppermute | solution.py:16
  80.4 13.1 %collective-permute-start.16 = (bf16[256,768]{1,0:T(8,128)(2,1)S(1)}, bf16[256,768]{1,0:T(8,128)(2,1)S(1)}, u32[]{:S(2)}, u32[]{:S(2)}) collective-permute-start(bf16[256,768]{1,0:T(8,128)(2,1)S(1)} %pad_maximum_fusion.6), channel_id=1, source_target_pairs={{0,2},{2,4},{4,6},{6,8},{8,10},{10,12},{12,14},{14,0},{1,3},{3,5},... | collective-permute-start | bytes 1179656 | tf_op jit(solution)/shard_map/ppermute | solution.py:16
  80.5 13.0 %collective-permute-start.18 = (bf16[128,768]{1,0:T(8,128)(2,1)S(1)}, bf16[128,768]{1,0:T(8,128)(2,1)S(1)}, u32[]{:S(2)}, u32[]{:S(2)}) collective-permute-start(bf16[128,768]{1,0:T(8,128)(2,1)S(1)} %slice.85), channel_id=1, source_target_pairs={{0,2},{2,4},{4,6},{6,8},{8,10},{10,12},{12,14},{14,0},{1,3},{3,5},... | collective-permute-start | bytes 589832 | tf_op jit(solution)/shard_map/ppermute | solution.py:16
  80.6 12.9 %collective-permute-start.19 = (bf16[128,768]{1,0:T(8,128)(2,1)S(1)}, bf16[128,768]{1,0:T(8,128)(2,1)S(1)}, u32[]{:S(2)}, u32[]{:S(2)}) collective-permute-start(bf16[128,768]{1,0:T(8,128)(2,1)S(1)} %slice.86), channel_id=1, source_target_pairs={{0,14},{2,0},{4,2},{6,4},{8,6},{10,8},{12,10},{14,12},{1,15},{3,1}... | collective-permute-start | bytes 589832 | tf_op jit(solution)/shard_map/ppermute | solution.py:16
  93.6 2.8 %copy-start.2 = (bf16[8,256,768]{2,1,0:T(8,128)(2,1)}, bf16[8,256,768]{2,1,0:T(8,128)(2,1)S(1)}, u32[]{:S(2)}) copy-start(bf16[8,256,768]{2,1,0:T(8,128)(2,1)S(1)} %fusion.11) | copy-start | bytes 9437188
  96.4 5.6 %copy-start.6 = (bf16[1,16,12288]{2,1,0:T(8,128)(2,1)S(1)}, bf16[1,16,12288]{2,1,0:T(8,128)(2,1)}, u32[]{:S(2)}) copy-start(bf16[1,16,12288]{2,1,0:T(8,128)(2,1)} %param.4) | copy-start | bytes 1179652
  97.7 14.1 %collective-permute-start.22 = (bf16[8,4,32,768]{3,2,1,0:T(8,128)(2,1)}, bf16[8,4,32,768]{3,2,1,0:T(8,128)(2,1)}, u32[]{:S(2)}, u32[]{:S(2)}) collective-permute-start(bf16[8,4,32,768]{3,2,1,0:T(8,128)(2,1)} %dynamic-slice_bitcast_fusion), channel_id=1, source_target_pairs={{0,16},{16,0},{1,17},{17,1},{2,18},{18,2},{3,19},{19,3},{4,20},{20... | collective-permute-start | bytes 4718600 | tf_op jit(solution)/shard_map/ppermute | solution.py:16
  98.8 13.1 %collective-permute-start.20 = (bf16[256,768]{1,0:T(8,128)(2,1)}, bf16[256,768]{1,0:T(8,128)(2,1)}, u32[]{:S(2)}, u32[]{:S(2)}) collective-permute-start(bf16[256,768]{1,0:T(8,128)(2,1)} %get-tuple-element.67), channel_id=1, source_target_pairs={{0,2},{2,4},{4,6},{6,8},{8,10},{10,12},{12,14},{14,0},{1,3},{3,5},... | collective-permute-start | bytes 1179656 | tf_op jit(solution)/shard_map/ppermute | solution.py:16
  98.8 13.1 %collective-permute-start.21 = (bf16[256,768]{1,0:T(8,128)(2,1)}, bf16[256,768]{1,0:T(8,128)(2,1)}, u32[]{:S(2)}, u32[]{:S(2)}) collective-permute-start(bf16[256,768]{1,0:T(8,128)(2,1)} %get-tuple-element.66), channel_id=1, source_target_pairs={{0,14},{2,0},{4,2},{6,4},{8,6},{10,8},{12,10},{14,12},{1,15},{3,1}... | collective-permute-start | bytes 1179656 | tf_op jit(solution)/shard_map/ppermute | solution.py:16
  102.8 63.2 %collective-permute-start.27 = (bf16[16,12288]{1,0:T(8,128)(2,1)}, bf16[16,12288]{1,0:T(8,128)(2,1)}, u32[]{:S(2)}, u32[]{:S(2)}) collective-permute-start(bf16[16,12288]{1,0:T(8,128)(2,1)} %select_bitcast_fusion), channel_id=1, source_target_pairs={{0,128},{128,0},{1,129},{129,1},{2,130},{130,2},{3,131},{131,3},{4... | collective-permute-start | bytes 1179656 | tf_op jit(solution)/shard_map/ppermute | solution.py:16
  113.8 8.6 %copy-start.1 = (bf16[8,4,2,32,768]{4,3,2,1,0:T(8,128)(2,1)S(1)}, bf16[8,4,2,32,768]{4,3,2,1,0:T(8,128)(2,1)}, u32[]{:S(2)}) copy-start(bf16[8,4,2,32,768]{4,3,2,1,0:T(8,128)(2,1)} %copy-done) | copy-start | bytes 9437188
  113.8 8.6 %copy-start.3 = (bf16[8,256,768]{2,1,0:T(8,128)(2,1)S(1)}, bf16[8,256,768]{2,1,0:T(8,128)(2,1)}, u32[]{:S(2)}) copy-start(bf16[8,256,768]{2,1,0:T(8,128)(2,1)} %copy-done.2) | copy-start | bytes 9437188
  114.0 11.3 %collective-permute-start.25 = (bf16[256,384]{1,0:T(8,128)(2,1)S(1)}, bf16[256,384]{1,0:T(8,128)(2,1)S(1)}, u32[]{:S(2)}, u32[]{:S(2)}) collective-permute-start(bf16[256,384]{1,0:T(8,128)(2,1)S(1)} %get-tuple-element.81), channel_id=1, source_target_pairs={{0,32},{32,64},{64,96},{96,0},{1,33},{33,65},{65,97},{97,1},{2,34}... | collective-permute-start | bytes 589832 | tf_op jit(solution)/shard_map/ppermute | solution.py:16
  114.9 13.1 %collective-permute-start.26 = (bf16[256,384]{1,0:T(8,128)(2,1)S(1)}, bf16[256,384]{1,0:T(8,128)(2,1)S(1)}, u32[]{:S(2)}, u32[]{:S(2)}) collective-permute-start(bf16[256,384]{1,0:T(8,128)(2,1)S(1)} %get-tuple-element.80), channel_id=1, source_target_pairs={{0,96},{32,0},{64,32},{96,64},{1,97},{33,1},{65,33},{97,65},{2,98}... | collective-permute-start | bytes 589832 | tf_op jit(solution)/shard_map/ppermute | solution.py:16
  118.9 11.7 %collective-permute-start.23 = (bf16[256,768]{1,0:T(8,128)(2,1)S(1)}, bf16[256,768]{1,0:T(8,128)(2,1)S(1)}, u32[]{:S(2)}, u32[]{:S(2)}) collective-permute-start(bf16[256,768]{1,0:T(8,128)(2,1)S(1)} %get-tuple-element.65), channel_id=1, source_target_pairs={{0,2},{2,4},{4,6},{6,8},{8,10},{10,12},{12,14},{14,0},{1,3},{3,5},... | collective-permute-start | bytes 1179656 | tf_op jit(solution)/shard_map/ppermute | solution.py:16
  119.2 11.4 %collective-permute-start.24 = (bf16[256,768]{1,0:T(8,128)(2,1)S(1)}, bf16[256,768]{1,0:T(8,128)(2,1)S(1)}, u32[]{:S(2)}, u32[]{:S(2)}) collective-permute-start(bf16[256,768]{1,0:T(8,128)(2,1)S(1)} %get-tuple-element.64), channel_id=1, source_target_pairs={{0,14},{2,0},{4,2},{6,4},{8,6},{10,8},{12,10},{14,12},{1,15},{3,1}... | collective-permute-start | bytes 1179656 | tf_op jit(solution)/shard_map/ppermute | solution.py:16
  125.3 15.4 %collective-permute-start.31 = (bf16[768,384]{1,0:T(8,128)(2,1)S(1)}, bf16[768,384]{1,0:T(8,128)(2,1)S(1)}, u32[]{:S(2)}, u32[]{:S(2)}) collective-permute-start(bf16[768,384]{1,0:T(8,128)(2,1)S(1)} %slice.114), channel_id=1, source_target_pairs={{0,1},{1,0},{2,3},{3,2},{4,5},{5,4},{6,7},{7,6},{8,9},{9,8},{10,11... | collective-permute-start | bytes 1769480 | tf_op jit(solution)/shard_map/ppermute | solution.py:16
  130.7 17.9 %collective-permute-start.28 = (bf16[256,768]{1,0:T(8,128)(2,1)S(1)}, bf16[256,768]{1,0:T(8,128)(2,1)S(1)}, u32[]{:S(2)}, u32[]{:S(2)}) collective-permute-start(bf16[256,768]{1,0:T(8,128)(2,1)S(1)} %pad_maximum_fusion.8), channel_id=1, source_target_pairs={{0,32},{32,64},{64,96},{96,0},{1,33},{33,65},{65,97},{97,1},{2,34}... | collective-permute-start | bytes 1179656 | tf_op jit(solution)/shard_map/ppermute | solution.py:16
  130.9 17.7 %collective-permute-start.29 = (bf16[256,768]{1,0:T(8,128)(2,1)S(1)}, bf16[256,768]{1,0:T(8,128)(2,1)}, u32[]{:S(2)}, u32[]{:S(2)}) collective-permute-start(bf16[256,768]{1,0:T(8,128)(2,1)S(1)} %pad_maximum_fusion.9), channel_id=1, source_target_pairs={{0,96},{32,0},{64,32},{96,64},{1,97},{33,1},{65,33},{97,65},{2,98}... | collective-permute-start | bytes 1179656 | tf_op jit(solution)/shard_map/ppermute | solution.py:16
  143.0 22.0 %all-to-all-start.1 = ((bf16[32,16,768]{2,1,0:T(8,128)(2,1)}), bf16[32,16,768]{2,1,0:T(8,128)(2,1)S(1)}, u32[]{:S(2)}, u32[]{:S(2)}) async-start(bf16[32,16,768]{2,1,0:T(8,128)(2,1)} %bitcast.40), calls=%async_computation.1 | async-start | bytes 1572864 | tf_op jit(solution)/shard_map/all_to_all | solution.py:141
  148.5 16.6 %copy-start.7 = (bf16[1,16,12288]{2,1,0:T(8,128)(2,1)S(1)}, bf16[1,16,12288]{2,1,0:T(8,128)(2,1)}, u32[]{:S(2)}) copy-start(bf16[1,16,12288]{2,1,0:T(8,128)(2,1)} %param.4) | copy-start | bytes 1179652
  149.8 14.6 %collective-permute-start.30 = (bf16[256,384]{1,0:T(8,128)(2,1)S(1)}, bf16[256,384]{1,0:T(8,128)(2,1)S(1)}, u32[]{:S(2)}, u32[]{:S(2)}) collective-permute-start(bf16[256,384]{1,0:T(8,128)(2,1)S(1)} %slice.128), channel_id=1, source_target_pairs={{0,1},{1,0},{2,3},{3,2},{4,5},{5,4},{6,7},{7,6},{8,9},{9,8},{10,11... | collective-permute-start | bytes 589832 | tf_op jit(solution)/shard_map/ppermute | solution.py:16

commit v4 on v2

v4 whole, which is shorter than its diff:
```python
import math

import jax
import jax.numpy as jnp
from jax import lax
from jax.sharding import Mesh
from jax.sharding import PartitionSpec as P

BF16 = jnp.bfloat16
F32 = jnp.float32


def shift(value, axis, by):
    n = lax.axis_size(axis)
    return lax.ppermute(value, axis, [(i, (i + by) % n) for i in range(n)])


def swap(value, axis):
    return shift(value, axis, 1)


def add(a, b):
    return (a.astype(F32) + b.astype(F32)).astype(BF16)


def wrap(index, n):
    return index & (n - 1)


def pick(stack, index, axis=0):
    return lax.dynamic_index_in_dim(stack, index, axis, keepdims=False)


def place(buffer, block, starts):
    return lax.dynamic_update_slice(buffer, block, starts)


def both_ways(right, left, axis):
    return shift(right, axis, 1), shift(left, axis, -1)


def ring_gather(block, axis):
    far = lax.axis_size(axis) // 2
    half = block.shape[0] // 2
    blocks = {0: block}
    right = left = block
    for away in range(1, far):
        right, left = both_ways(right, left, axis)
        blocks[-away], blocks[away] = right, left
    blocks[far] = jnp.concatenate(both_ways(right[:half], left[half:], axis), 0)
    return blocks


def ring_sum(chunk, axis):
    far = lax.axis_size(axis) // 2
    opposite = chunk(far)
    half = opposite.shape[1] // 2
    low, high = both_ways(opposite[:, :half], opposite[:, half:], axis)
    ahead, behind = chunk(far - 1), chunk(1 - far)
    right = jnp.concatenate([add(ahead[:, :half], low), ahead[:, half:]], 1)
    left = jnp.concatenate([behind[:, :half], add(behind[:, half:], high)], 1)
    for away in range(far - 2, 0, -1):
        right, left = both_ways(right, left, axis)
        right, left = add(chunk(away), right), add(chunk(-away), left)
    right, left = both_ways(right, left, axis)
    return chunk(0).astype(F32) + right.astype(F32) + left.astype(F32)


def shards(segment_input, context, out_proj, grad_output):
    residual = segment_input[0]
    contexts = context[0]
    weights = out_proj[0]
    upstream = grad_output[0]
    section, y, core, z, xh = (lax.axis_index(name) for name in ("section", "y", "core", "z", "xh"))
    n_y, n_core, n_z, n_xh = (lax.axis_size(name) for name in ("y", "core", "z", "xh"))
    own_count, model = upstream.shape
    group_tokens, width = contexts.shape
    piece = model // (n_y * n_core * n_xh)
    group = n_y * n_xh
    features = n_core * piece
    tokens = group_tokens * n_y
    z_tokens = own_count * n_xh
    block_tokens = own_count * group

    both = jnp.concatenate([contexts, swap(contexts, "xh")], 1)
    ctx_all = jnp.zeros((n_z, n_y, z_tokens, 2 * width), BF16)
    for away, part in ring_gather(both, "y").items():
        ctx_all = place(ctx_all, part.reshape(n_z, 1, z_tokens, 2 * width), (0, wrap(y + away, n_y), 0, 0))
    ctx_flat = ctx_all.reshape(tokens, 2 * width)

    def rows(core_at, xh_at):
        return lax.dynamic_slice_in_dim(weights, ((y * n_core + core_at) * n_xh + xh_at) * piece, piece, 0)

    came_rows = swap(rows(core, 1 - xh), "xh")
    other_rows = swap(came_rows, "core")
    block = jnp.concatenate(
        [jnp.concatenate([rows(core, xh), came_rows], 1), jnp.concatenate([rows(1 - core, xh), other_rows], 1)], 0
    )

    spread = upstream.reshape(own_count, n_y, n_core, n_xh, piece)
    spread = jnp.stack([pick(spread, core, 2), pick(spread, 1 - core, 2)], 3)
    spread = spread.transpose(1, 2, 0, 3, 4).reshape(group, own_count, features)
    spread = lax.all_to_all(spread, ("y", "xh"), 0, 0, tiled=True).reshape(block_tokens, features)
    grad_all = jnp.zeros((n_z, block_tokens, features), BF16)
    for away, part in ring_gather(spread, "z").items():
        grad_all = place(grad_all, part[None], (wrap(z + away, n_z), 0, 0))
    grad_flat = grad_all.reshape(tokens, features)

    partial_branch = lax.dot_general(
        ctx_flat, block, (((1,), (1,)), ((), ())), preferred_element_type=F32
    ).astype(BF16).reshape(n_z, block_tokens, features)
    branch = ring_sum(lambda away: pick(partial_branch, wrap(z + away, n_z)), "z").astype(BF16)
    branch = branch.reshape(1, group, own_count, features)
    branch = jnp.concatenate([branch, branch], 0).reshape(2 * group, own_count, features)
    branch = lax.all_to_all(branch, ("section", "y", "xh"), 0, 0, tiled=True)
    branch = branch.reshape(2, n_y, n_xh, own_count, n_core, piece)
    branch = jnp.where(core == 0, branch, jnp.flip(branch, 4))
    branch = branch.transpose(0, 3, 1, 4, 2, 5).reshape(2, own_count, model)
    forward = add(residual, pick(branch, section))
    early = swap(jnp.where(section == 0, residual, upstream), "section")
    received = jnp.where(section == 0, early, add(early, branch[0]))

    partial_ctx = jnp.dot(grad_flat, block, preferred_element_type=F32).astype(BF16)
    partial_ctx = partial_ctx.reshape(n_z, n_y, z_tokens, 2 * width)
    summed = ring_sum(lambda away: pick(partial_ctx, wrap(y + away, n_y), 1).reshape(group_tokens, 2 * width), "y")
    ctx_grad = add(summed[:, :width], swap(summed[:, width:].astype(BF16), "xh"))

    norm_factor = 1.0 / math.sqrt(tokens * n_core)
    product = lax.dot_general(grad_flat, ctx_flat, (((0,), (0,)), ((), ())), preferred_element_type=F32)
    product = (norm_factor * product).astype(BF16)
    own_rows = add(product[:piece], swap(product[piece:], "core"))
    kept = own_rows[:, :width]
    came = swap(own_rows[:, width:], "xh")
    first = xh == 0
    weight_grad = jnp.concatenate([jnp.where(first, kept, came), jnp.where(first, came, kept)], 0)
    return (forward[None], received[None], ctx_grad[None], weight_grad[None])


def solution(mesh):
    fine = Mesh(mesh.devices.reshape(2, 4, 2, 8, 2), ("section", "y", "core", "z", "xh"))
    tokens = P("section", ("y", "core", "z", "xh"), None)
    heads = P("section", ("y", "core"), ("z", "xh"))
    return jax.shard_map(
        shards,
        mesh=fine,
        in_specs=(tokens, heads, P("section", None, ("z", "xh")), tokens),
        out_specs=(tokens, tokens, heads, heads),
        check_vma=False,
    )
```

time: 211 us -> 142 us (0.67)
  waiting for transfers between devices: 85.2 us -> 52.6 us
  local copies, waits for them, and re-layouts: 25 us -> 11.2 us
  between operations: 14.5 us -> 1.22 us
  other arithmetic: 19.5 us -> 11.1 us
  starting transfers between devices: 50.4 us -> 54.1 us
  matrix products: 13.5 us -> 10.3 us
    ppermute x26 -> x31, waiting for transfers between devices: 73.7 us -> 45.9 us  [shift(): return lax.ppermute(value, axis, [(i, (i + by) % n) for i in range(n)])]
    convert_element_type x9 -> x10, other arithmetic: 9.91 us -> 1.85 us  [add(): return (a.astype(F32) + b.astype(F32)).astype(BF16)]
    ppermute x26 -> x31, starting transfers between devices: 37.7 us -> 44 us  [shift(): return lax.ppermute(value, axis, [(i, (i + by) % n) for i in range(n)])]
    unnamed x33 -> x12, local copies, waits for them, and re-layouts: 6.05 us -> 0.04 us
    all_to_all x2, waiting for transfers between devices: 11.5 us -> 6.71 us  [the longest x1 6.7 us: shards(): branch = lax.all_to_all(branch, ('section', 'y', 'xh'), 0, 0, tiled=True)]
    convert_element_type x3 -> x2, local copies, waits for them, and re-layouts: 4.5 us -> 1.24 us  [add(): return (a.astype(F32) + b.astype(F32)).astype(BF16)]
    convert_element_type x1 -> x0, local copies, waits for them, and re-layouts: 3.18 us -> none  [shards(): jnp.dot(grad_flat, block, preferred_element_type=F32).astype(BF16)]
    dynamic_update_slice x7 -> x10, local copies, waits for them, and re-layouts: 3.28 us -> 0.31 us  [place(): return lax.dynamic_update_slice(buffer, block, starts)]
  transfers between devices with their start and end apart: 29 -> 33, of which waited for: 16 -> 15; matrix products, arithmetic and copies ran while one was open for 19% -> 22% of each run, Pallas kernels for 0% -> 0%
where the time goes in v4:
time: 142 us; the launch traced here: 141 us
  starting transfers between devices  54.1 us (38%)
  waiting for transfers between devices  52.6 us (37%)
  local copies, waits for them, and re-layouts  11.2 us (8%)
  other arithmetic  11.1 us (8%)
  matrix products  10.3 us (7%)
    ppermute x31, waiting for transfers between devices, shift(): return lax.ppermute(value, axis, [(i, (i + by) % n) for i in range(n)])  45.9 us
    ppermute x31, starting transfers between devices, shift(): return lax.ppermute(value, axis, [(i, (i + by) % n) for i in range(n)])  44 us
    all_to_all x1, waiting for transfers between devices, shards(): branch = lax.all_to_all(branch, ('section', 'y', 'xh'), 0, 0, tiled=True)  6.7 us
    all_to_all x1, starting transfers between devices, shards(): lax.all_to_all(spread, ('y', 'xh'), 0, 0, tiled=True)  5.31 us
    all_to_all x1, starting transfers between devices, shards(): branch = lax.all_to_all(branch, ('section', 'y', 'xh'), 0, 0, tiled=True)  4.8 us
    broadcast_in_dim x3, other arithmetic, shards(): return (forward[None], received[None], ctx_grad[None], weight_grad[None])  4.76 us
    dot_general x1, matrix products, shards(): lax.dot_general(ctx_flat, block, (((1,), (1,)), ((), ())), preferred_elem...  3.71 us
    dot_general x1, matrix products, shards(): jnp.dot(grad_flat, block, preferred_element_type=F32).astype(BF16)  3.66 us
  transfers between devices with their start and end apart: 33, of which 15 were waited for; matrix products, arithmetic and copies ran while one was open for 22% of the time, Pallas kernels for 0%

profile of v4, /device:TPU:2, one launch (start us, length us, event | category | flops | bytes accessed | tf_op | source)
XLA Modules:
  0.0 140.6 jit_solution(14470698932249647229)
XLA Ops:
  0.6 2.2 %collective-permute-start = (bf16[256,384]{1,0:T(8,128)(2,1)}, bf16[256,384]{1,0:T(8,128)(2,1)S(1)}, u32[]{:S(2)}, u32[]{:S(2)}) collective-permute-start(bf16[256,384]{1,0:T(8,128)(2,1)} %bitcast.107), channel_id=1, source_target_pairs={{0,1},{1,0},{2,3},{3,2},{4,5},{5,4},{6,7},{7,6},{8,9},{9,8},{10,11... | collective-permute-start | bytes 589832 | tf_op jit(solution)/shard_map/ppermute | solution.py:15
  2.8 1.3 reshape_squeeze.3
  4.1 0.3 constant_dynamic-slice_fusion.5
  4.6 0.3 copy.24
  4.9 1.0 reshape.97
  5.9 5.3 %all-to-all-start.1 = ((bf16[8,16,1536]{2,1,0:T(8,128)(2,1)}), bf16[8,16,1536]{2,1,0:T(8,128)(2,1)S(1)}, u32[]{:S(2)}, u32[]{:S(2)}) async-start(bf16[8,16,1536]{2,1,0:T(8,128)(2,1)} %reshape.97), calls=%async_computation.1 | async-start | bytes 786432 | tf_op jit(solution)/shard_map/all_to_all | solution.py:103
  11.2 2.7 %dynamic-slice_bitcast_fusion.2 = (bf16[768,384]{1,0:T(8,128)(2,1)}, bf16[768,384]{1,0:T(8,128)(2,1)}, bf16[768,384]{1,0:T(8,128)(2,1)}) fusion(bf16[1,12288,384]{2,1,0:T(8,128)(2,1)} %param.6, s32[]{:T(128)S(6)} %select_n.112, s32[]{:T(128)S(6)} %select_n.114, s32[]{:T(128)S(6)} %select_n.113), kind=kLoop, calls=%fused_computation.27 | loop fusion | bytes 3538956 | tf_op jit(solution)/shard_map/dynamic_slice | solution.py:92
  13.9 3.5 %collective-permute-start.5 = (bf16[768,384]{1,0:T(8,128)(2,1)}, bf16[768,384]{1,0:T(8,128)(2,1)}, u32[]{:S(2)}, u32[]{:S(2)}) collective-permute-start(bf16[768,384]{1,0:T(8,128)(2,1)} %get-tuple-element.6), channel_id=1, source_target_pairs={{0,1},{1,0},{2,3},{3,2},{4,5},{5,4},{6,7},{7,6},{8,9},{9,8},{10,11... | collective-permute-start | bytes 1769480 | tf_op jit(solution)/shard_map/ppermute | solution.py:15
  17.4 0.8 pad_maximum_fusion.1
  18.2 1.5 %collective-permute-start.1 = (bf16[256,768]{1,0:T(8,128)(2,1)}, bf16[256,768]{1,0:T(8,128)(2,1)S(1)}, u32[]{:S(2)}, u32[]{:S(2)}) collective-permute-start(bf16[256,768]{1,0:T(8,128)(2,1)} %pad_maximum_fusion.1), channel_id=1, source_target_pairs={{0,32},{32,64},{64,96},{96,0},{1,33},{33,65},{65,97},{97,1},{2,34}... | collective-permute-start | bytes 1179656 | tf_op jit(solution)/shard_map/ppermute | solution.py:15
  19.7 1.8 %collective-permute-start.2 = (bf16[256,768]{1,0:T(8,128)(2,1)}, bf16[256,768]{1,0:T(8,128)(2,1)S(1)}, u32[]{:S(2)}, u32[]{:S(2)}) collective-permute-start(bf16[256,768]{1,0:T(8,128)(2,1)} %pad_maximum_fusion.1), channel_id=1, source_target_pairs={{0,96},{32,0},{64,32},{96,64},{1,97},{33,1},{65,33},{97,65},{2,98}... | collective-permute-start | bytes 1179656 | tf_op jit(solution)/shard_map/ppermute | solution.py:15
  21.5 0.8 select_bitcast_fusion
  22.5 2.0 %collective-permute-start.16 = (bf16[128,1536]{1,0:T(8,128)(2,1)S(1)}, bf16[128,1536]{1,0:T(8,128)(2,1)S(1)}, u32[]{:S(2)}, u32[]{:S(2)}) collective-permute-start(bf16[128,1536]{1,0:T(8,128)(2,1)S(1)} %bitcast.94), channel_id=1, source_target_pairs={{0,2},{2,4},{4,6},{6,8},{8,10},{10,12},{12,14},{14,0},{1,3},{3,5},... | collective-permute-start | bytes 1179656 | tf_op jit(solution)/shard_map/ppermute | solution.py:15
  24.5 4.0 %collective-permute-start.17 = (bf16[128,1536]{1,0:T(8,128)(2,1)S(1)}, bf16[128,1536]{1,0:T(8,128)(2,1)S(1)}, u32[]{:S(2)}, u32[]{:S(2)}) collective-permute-start(bf16[128,1536]{1,0:T(8,128)(2,1)S(1)} %bitcast.95), channel_id=1, source_target_pairs={{0,14},{2,0},{4,2},{6,4},{8,6},{10,8},{12,10},{14,12},{1,15},{3,1}... | collective-permute-start | bytes 1179656 | tf_op jit(solution)/shard_map/ppermute | solution.py:15
  28.5 0.3 broadcast_in_dim.39
  28.8 1.0 collective-permute-done.1
  29.9 0.2 collective-permute-start.3
  30.1 3.2 %collective-permute-start.4 = (bf16[128,768]{1,0:T(8,128)(2,1)S(1)}, bf16[128,768]{1,0:T(8,128)(2,1)S(1)}, u32[]{:S(2)}, u32[]{:S(2)}) collective-permute-start(bf16[128,768]{1,0:T(8,128)(2,1)S(1)} %slice.95), channel_id=1, source_target_pairs={{0,96},{32,0},{64,32},{96,64},{1,97},{33,1},{65,33},{97,65},{2,98}... | collective-permute-start | bytes 589832 | tf_op jit(solution)/shard_map/ppermute | solution.py:15
  33.4 2.4 %collective-permute-done.16 = bf16[128,1536]{1,0:T(8,128)(2,1)S(1)} collective-permute-done((bf16[128,1536]{1,0:T(8,128)(2,1)S(1)}, bf16[128,1536]{1,0:T(8,128)(2,1)S(1)}, u32[]{:S(2)}, u32[]{:S(2)}) %collective-permute-start.16) | collective-permute-done | bytes 393248 | tf_op jit(solution)/shard_map/ppermute | solution.py:15
  35.9 3.6 %collective-permute-start.19 = (bf16[128,1536]{1,0:T(8,128)(2,1)S(1)}, bf16[128,1536]{1,0:T(8,128)(2,1)S(1)}, u32[]{:S(2)}, u32[]{:S(2)}) collective-permute-start(bf16[128,1536]{1,0:T(8,128)(2,1)S(1)} %collective-permute-done.17), channel_id=1, source_target_pairs={{0,14},{2,0},{4,2},{6,4},{8,6},{10,8},{12,10},{14,12},{1,15},{3,1}... | collective-permute-start | bytes 1179656 | tf_op jit(solution)/shard_map/ppermute | solution.py:15
  39.5 0.7 collective-permute-start.15
  40.3 6.1 %collective-permute-done.18 = bf16[128,1536]{1,0:T(8,128)(2,1)S(1)} collective-permute-done((bf16[128,1536]{1,0:T(8,128)(2,1)S(1)}, bf16[128,1536]{1,0:T(8,128)(2,1)S(1)}, u32[]{:S(2)}, u32[]{:S(2)}) %collective-permute-start.18) | collective-permute-done | bytes 393248 | tf_op jit(solution)/shard_map/ppermute | solution.py:15
  46.4 3.2 %collective-permute-start.21 = (bf16[128,1536]{1,0:T(8,128)(2,1)S(1)}, bf16[128,1536]{1,0:T(8,128)(2,1)S(1)}, u32[]{:S(2)}, u32[]{:S(2)}) collective-permute-start(bf16[128,1536]{1,0:T(8,128)(2,1)S(1)} %collective-permute-done.19), channel_id=1, source_target_pairs={{0,14},{2,0},{4,2},{6,4},{8,6},{10,8},{12,10},{14,12},{1,15},{3,1}... | collective-permute-start | bytes 1179656 | tf_op jit(solution)/shard_map/ppermute | solution.py:15
  49.7 3.7 %convolution_convert_fusion = bf16[1024,1536]{1,0:T(8,128)(2,1)S(1)} fusion(bf16[1024,768]{1,0:T(8,128)(2,1)S(1)} %bitcast.92, bf16[768,384]{1,0:T(8,128)(2,1)S(1)} %collective-permute-done.6, bf16[768,384]{1,0:T(8,128)(2,1)S(1)} %copy-done.4, bf16[768,384]{1,0:T(8,128)(2,1)} %collective-permute-done.5, bf16[768,384]{1,0:T(8,128)(2,1)S(1)} %copy-done.3), kind=kOutput, calls=%fused_computation.1 | convolution fusion | flops 2426929152 | bytes 7077888 | tf_op jit(solution)/shard_map/dot_general | solution.py:109
  53.5 1.1 collective-permute-start.11
  54.7 1.1 collective-permute-start.7
  55.8 3.5 %collective-permute-done.11 = bf16[128,768]{1,0:T(8,128)(2,1)S(1)} collective-permute-done((bf16[128,768]{1,0:T(8,128)(2,1)S(1)}, bf16[128,768]{1,0:T(8,128)(2,1)S(1)}, u32[]{:S(2)}, u32[]{:S(2)}) %collective-permute-start.11) | collective-permute-done | bytes 196640 | tf_op jit(solution)/shard_map/ppermute | solution.py:15
  59.4 3.7 %collective-permute-start.12 = (bf16[128,1536]{1,0:T(8,128)(2,1)S(1)}, bf16[128,1536]{1,0:T(8,128)(2,1)S(1)}, u32[]{:S(2)}, u32[]{:S(2)}) collective-permute-start(bf16[128,1536]{1,0:T(8,128)(2,1)S(1)} %pad_maximum_fusion.4), channel_id=1, source_target_pairs={{0,14},{2,0},{4,2},{6,4},{8,6},{10,8},{12,10},{14,12},{1,15},{3,1}... | collective-permute-start | bytes 1179656 | tf_op jit(solution)/shard_map/ppermute | solution.py:15
  63.5 3.3 %collective-permute-start.23 = (bf16[64,1536]{1,0:T(8,128)(2,1)S(1)}, bf16[64,1536]{1,0:T(8,128)(2,1)S(1)}, u32[]{:S(2)}, u32[]{:S(2)}) collective-permute-start(bf16[64,1536]{1,0:T(8,128)(2,1)S(1)} %slice.104), channel_id=1, source_target_pairs={{0,14},{2,0},{4,2},{6,4},{8,6},{10,8},{12,10},{14,12},{1,15},{3,1}... | collective-permute-start | bytes 589832 | tf_op jit(solution)/shard_map/ppermute | solution.py:15
  66.8 8.5 %collective-permute-done.22 = bf16[64,1536]{1,0:T(8,128)(2,1)S(1)} collective-permute-done((bf16[64,1536]{1,0:T(8,128)(2,1)S(1)}, bf16[64,1536]{1,0:T(8,128)(2,1)S(1)}, u32[]{:S(2)}, u32[]{:S(2)}) %collective-permute-start.22) | collective-permute-done | bytes 196640 | tf_op jit(solution)/shard_map/ppermute | solution.py:15
  75.4 3.7 %convolution_convert_fusion.1 = bf16[1024,768]{1,0:T(8,128)(2,1)S(1)} fusion(bf16[1024,1536]{1,0:T(8,128)(2,1)S(1)} %bitcast.85, bf16[768,384]{1,0:T(8,128)(2,1)S(1)} %collective-permute-done.6, bf16[768,384]{1,0:T(8,128)(2,1)S(1)} %copy-done.4, bf16[768,384]{1,0:T(8,128)(2,1)} %collective-permute-done.5, bf16[768,384]{1,0:T(8,128)(2,1)S(1)} %copy-done.3), kind=kOutput, calls=%fused_computation.4 | convolution fusion | flops 2426142720 | bytes 7077888 | tf_op jit(solution)/shard_map/dot_general | solution.py:123
  79.5 2.9 %multiply_convert_fusion = bf16[1536,768]{1,0:T(8,128)(2,1)S(1)} fusion(bf16[1024,1536]{1,0:T(8,128)(2,1)S(1)} %bitcast.86, bf16[1024,768]{1,0:T(8,128)(2,1)S(1)} %bitcast.93), kind=kOutput, calls=%fused_computation | convolution fusion | flops 2418278400 | bytes 7077888 | tf_op jit(solution)/shard_map/dot_general | solution.py:129
  82.5 0.3 collective-permute-start.29
  82.9 3.2 %collective-permute-done.24 = bf16[256,384]{1,0:T(8,128)(2,1)S(1)} collective-permute-done((bf16[256,384]{1,0:T(8,128)(2,1)S(1)}, bf16[256,384]{1,0:T(8,128)(2,1)S(1)}, u32[]{:S(2)}, u32[]{:S(2)}) %collective-permute-start.24) | collective-permute-done | bytes 196640 | tf_op jit(solution)/shard_map/ppermute | solution.py:15
  86.3 2.2 %collective-permute-done.9 = bf16[128,1536]{1,0:T(8,128)(2,1)S(1)} collective-permute-done((bf16[128,1536]{1,0:T(8,128)(2,1)S(1)}, bf16[128,1536]{1,0:T(8,128)(2,1)S(1)}, u32[]{:S(2)}, u32[]{:S(2)}) %collective-permute-start.9) | collective-permute-done | bytes 393248 | tf_op jit(solution)/shard_map/ppermute | solution.py:15
  88.5 0.2 fusion.5
  88.7 1.1 collective-permute-start.13
  89.9 1.9 %collective-permute-done.26 = bf16[256,384]{1,0:T(8,128)(2,1)S(1)} collective-permute-done((bf16[256,384]{1,0:T(8,128)(2,1)S(1)}, bf16[256,384]{1,0:T(8,128)(2,1)S(1)}, u32[]{:S(2)}, u32[]{:S(2)}) %collective-permute-start.26) | collective-permute-done | bytes 196640 | tf_op jit(solution)/shard_map/ppermute | solution.py:15
  91.9 3.0 %collective-permute-start.27 = (bf16[256,768]{1,0:T(8,128)(2,1)S(1)}, bf16[256,768]{1,0:T(8,128)(2,1)S(1)}, u32[]{:S(2)}, u32[]{:S(2)}) collective-permute-start(bf16[256,768]{1,0:T(8,128)(2,1)S(1)} %pad_maximum_fusion.6), channel_id=1, source_target_pairs={{0,96},{32,0},{64,32},{96,64},{1,97},{33,1},{65,33},{97,65},{2,98}... | collective-permute-start | bytes 1179656 | tf_op jit(solution)/shard_map/ppermute | solution.py:15
  94.9 3.6 %collective-permute-done.13 = bf16[128,1536]{1,0:T(8,128)(2,1)S(1)} collective-permute-done((bf16[128,1536]{1,0:T(8,128)(2,1)S(1)}, bf16[128,1536]{1,0:T(8,128)(2,1)S(1)}, u32[]{:S(2)}, u32[]{:S(2)}) %collective-permute-start.13) | collective-permute-done | bytes 393248 | tf_op jit(solution)/shard_map/ppermute | solution.py:15
  98.5 0.2 collective-permute-start.10
  98.8 3.2 %collective-permute-done.25 = bf16[256,768]{1,0:T(8,128)(2,1)S(1)} collective-permute-done((bf16[256,768]{1,0:T(8,128)(2,1)S(1)}, bf16[256,768]{1,0:T(8,128)(2,1)S(1)}, u32[]{:S(2)}, u32[]{:S(2)}) %collective-permute-start.25) | collective-permute-done | bytes 393248 | tf_op jit(solution)/shard_map/ppermute | solution.py:15
  102.1 0.4 collective-permute-start.14
  102.4 0.7 collective-permute-done.27
  103.3 0.7 slice.131
  104.0 2.3 %collective-permute-start.28 = (bf16[256,384]{1,0:T(8,128)(2,1)}, bf16[256,384]{1,0:T(8,128)(2,1)}, u32[]{:S(2)}, u32[]{:S(2)}) collective-permute-start(bf16[256,384]{1,0:T(8,128)(2,1)} %slice.131), channel_id=1, source_target_pairs={{0,1},{1,0},{2,3},{3,2},{4,5},{5,4},{6,7},{7,6},{8,9},{9,8},{10,11... | collective-permute-start | bytes 589832 | tf_op jit(solution)/shard_map/ppermute | solution.py:15
  106.4 0.3 add_convert_fusion
  106.7 0.9 slice.116
  107.6 1.2 collective-permute-start.30
  108.8 2.1 %collective-permute-done.10 = bf16[128,1536]{1,0:T(8,128)(2,1)S(1)} collective-permute-done((bf16[128,1536]{1,0:T(8,128)(2,1)S(1)}, bf16[128,1536]{1,0:T(8,128)(2,1)S(1)}, u32[]{:S(2)}, u32[]{:S(2)}) %collective-permute-start.10) | collective-permute-done | bytes 393248 | tf_op jit(solution)/shard_map/ppermute | solution.py:15
  110.9 1.3 collective-permute-done.14
  112.3 1.0 pad_maximum_fusion
  113.3 4.8 %all-to-all-start = ((bf16[16,16,1536]{2,1,0:T(8,128)(2,1)}), bf16[16,16,1536]{2,1,0:T(8,128)(2,1)S(1)}, u32[]{:S(2)}, u32[]{:S(2)}) async-start(bf16[16,16,1536]{2,1,0:T(8,128)(2,1)} %bitcast.20), calls=%async_computation | async-start | bytes 1572864 | tf_op jit(solution)/shard_map/all_to_all | solution.py:115
  118.1 1.6 %fusion.12 = bf16[1,256,384]{2,1,0:T(8,128)(2,1)} fusion(bf16[256,384]{1,0:T(8,128)(2,1)} %collective-permute-done.28, f32[256,768]{1,0:T(8,128)S(1)} %fusion.1), kind=kLoop, calls=%fused_computation.60 | loop fusion | flops 294912 | bytes 786432 | tf_op jit(solution)/shard_map/broadcast_in_dim | solution.py:136
  119.7 6.0 %collective-permute-done.30 = bf16[768,384]{1,0:T(8,128)(2,1)} collective-permute-done((bf16[768,384]{1,0:T(8,128)(2,1)}, bf16[768,384]{1,0:T(8,128)(2,1)}, u32[]{:S(2)}, u32[]{:S(2)}) %collective-permute-start.30) | collective-permute-done | bytes 589856 | tf_op jit(solution)/shard_map/ppermute | solution.py:15
  125.7 1.2 broadcast_select_fusion.1
  126.9 1.1 maximum_bitcast_fusion
  128.0 6.7 %all-to-all-done = bf16[16,16,1536]{2,1,0:T(8,128)(2,1)S(1)} async-done(((bf16[16,16,1536]{2,1,0:T(8,128)(2,1)}), bf16[16,16,1536]{2,1,0:T(8,128)(2,1)S(1)}, u32[]{:S(2)}, u32[]{:S(2)}) %all-to-all-start) | async-done | bytes 786464 | tf_op jit(solution)/shard_map/all_to_all | solution.py:115
  135.2 0.6 copy.20
  135.8 0.6 reshape.96
  136.4 0.8 add_convert_fusion.2
  137.4 0.6 copy.21
  138.0 0.6 reshape.109
  138.6 2.0 %fusion.9 = bf16[1,16,12288]{2,1,0:T(8,128)(2,1)} fusion(bf16[16,12288]{1,0:T(8,128)(2,1)} %collective-permute-done.15, f32[16,12288]{1,0:T(8,128)S(1)} %reshape.109, pred[]{:T(512)S(6)} %eq.11), kind=kLoop, calls=%fused_computation.30 | loop fusion | flops 786432 | bytes 1572865 | tf_op jit(solution)/shard_map/broadcast_in_dim | solution.py:136
  (84 shorter events, 3.1 us)
Async XLA Ops:
  0.6 16.8 %collective-permute-start = (bf16[256,384]{1,0:T(8,128)(2,1)}, bf16[256,384]{1,0:T(8,128)(2,1)S(1)}, u32[]{:S(2)}, u32[]{:S(2)}) collective-permute-start(bf16[256,384]{1,0:T(8,128)(2,1)} %bitcast.107), channel_id=1, source_target_pairs={{0,1},{1,0},{2,3},{3,2},{4,5},{5,4},{6,7},{7,6},{8,9},{9,8},{10,11... | collective-permute-start | bytes 589832 | tf_op jit(solution)/shard_map/ppermute | solution.py:15
  4.5 12.9 %copy-start.2 = (bf16[1,256,384]{2,1,0:T(8,128)(2,1)S(1)}, bf16[1,256,384]{2,1,0:T(8,128)(2,1)}, u32[]{:S(2)}) copy-start(bf16[1,256,384]{2,1,0:T(8,128)(2,1)} %param.5) | copy-start | bytes 589828
  4.9 16.6 %copy-start = (bf16[1,16,12288]{2,1,0:T(8,128)(2,1)S(1)}, bf16[1,16,12288]{2,1,0:T(8,128)(2,1)}, u32[]{:S(2)}) copy-start(bf16[1,16,12288]{2,1,0:T(8,128)(2,1)} %param.7) | copy-start | bytes 1179652
  4.9 16.6 %copy-start.1 = (bf16[1,16,12288]{2,1,0:T(8,128)(2,1)S(1)}, bf16[1,16,12288]{2,1,0:T(8,128)(2,1)}, u32[]{:S(2)}) copy-start(bf16[1,16,12288]{2,1,0:T(8,128)(2,1)} %param.4) | copy-start | bytes 1179652
  5.9 16.6 %all-to-all-start.1 = ((bf16[8,16,1536]{2,1,0:T(8,128)(2,1)}), bf16[8,16,1536]{2,1,0:T(8,128)(2,1)S(1)}, u32[]{:S(2)}, u32[]{:S(2)}) async-start(bf16[8,16,1536]{2,1,0:T(8,128)(2,1)} %reshape.97), calls=%async_computation.1 | async-start | bytes 786432 | tf_op jit(solution)/shard_map/all_to_all | solution.py:103
  13.9 25.6 %collective-permute-start.5 = (bf16[768,384]{1,0:T(8,128)(2,1)}, bf16[768,384]{1,0:T(8,128)(2,1)}, u32[]{:S(2)}, u32[]{:S(2)}) collective-permute-start(bf16[768,384]{1,0:T(8,128)(2,1)} %get-tuple-element.6), channel_id=1, source_target_pairs={{0,1},{1,0},{2,3},{3,2},{4,5},{5,4},{6,7},{7,6},{8,9},{9,8},{10,11... | collective-permute-start | bytes 1769480 | tf_op jit(solution)/shard_map/ppermute | solution.py:15
  18.2 11.7 %collective-permute-start.1 = (bf16[256,768]{1,0:T(8,128)(2,1)}, bf16[256,768]{1,0:T(8,128)(2,1)S(1)}, u32[]{:S(2)}, u32[]{:S(2)}) collective-permute-start(bf16[256,768]{1,0:T(8,128)(2,1)} %pad_maximum_fusion.1), channel_id=1, source_target_pairs={{0,32},{32,64},{64,96},{96,0},{1,33},{33,65},{65,97},{97,1},{2,34}... | collective-permute-start | bytes 1179656 | tf_op jit(solution)/shard_map/ppermute | solution.py:15
  19.7 10.4 %collective-permute-start.2 = (bf16[256,768]{1,0:T(8,128)(2,1)}, bf16[256,768]{1,0:T(8,128)(2,1)S(1)}, u32[]{:S(2)}, u32[]{:S(2)}) collective-permute-start(bf16[256,768]{1,0:T(8,128)(2,1)} %pad_maximum_fusion.1), channel_id=1, source_target_pairs={{0,96},{32,0},{64,32},{96,64},{1,97},{33,1},{65,33},{97,65},{2,98}... | collective-permute-start | bytes 1179656 | tf_op jit(solution)/shard_map/ppermute | solution.py:15
  22.5 13.4 %collective-permute-start.16 = (bf16[128,1536]{1,0:T(8,128)(2,1)S(1)}, bf16[128,1536]{1,0:T(8,128)(2,1)S(1)}, u32[]{:S(2)}, u32[]{:S(2)}) collective-permute-start(bf16[128,1536]{1,0:T(8,128)(2,1)S(1)} %bitcast.94), channel_id=1, source_target_pairs={{0,2},{2,4},{4,6},{6,8},{8,10},{10,12},{12,14},{14,0},{1,3},{3,5},... | collective-permute-start | bytes 1179656 | tf_op jit(solution)/shard_map/ppermute | solution.py:15
  24.5 11.4 %collective-permute-start.17 = (bf16[128,1536]{1,0:T(8,128)(2,1)S(1)}, bf16[128,1536]{1,0:T(8,128)(2,1)S(1)}, u32[]{:S(2)}, u32[]{:S(2)}) collective-permute-start(bf16[128,1536]{1,0:T(8,128)(2,1)S(1)} %bitcast.95), channel_id=1, source_target_pairs={{0,14},{2,0},{4,2},{6,4},{8,6},{10,8},{12,10},{14,12},{1,15},{3,1}... | collective-permute-start | bytes 1179656 | tf_op jit(solution)/shard_map/ppermute | solution.py:15
  28.8 10.8 %copy-start.5 = (bf16[16,12288]{1,0:T(8,128)(2,1)S(1)}, bf16[16,12288]{1,0:T(8,128)(2,1)}, u32[]{:S(2)}) copy-start(bf16[16,12288]{1,0:T(8,128)(2,1)} %select_bitcast_fusion) | copy-start | bytes 1179652
  28.8 20.8 %copy-start.3 = (bf16[768,384]{1,0:T(8,128)(2,1)S(1)}, bf16[768,384]{1,0:T(8,128)(2,1)}, u32[]{:S(2)}) copy-start(bf16[768,384]{1,0:T(8,128)(2,1)} %get-tuple-element.4) | copy-start | bytes 1769476
  28.8 20.8 %copy-start.4 = (bf16[768,384]{1,0:T(8,128)(2,1)S(1)}, bf16[768,384]{1,0:T(8,128)(2,1)}, u32[]{:S(2)}) copy-start(bf16[768,384]{1,0:T(8,128)(2,1)} %get-tuple-element.5) | copy-start | bytes 1769476
  29.9 10.3 %collective-permute-start.3 = (bf16[128,768]{1,0:T(8,128)(2,1)S(1)}, bf16[128,768]{1,0:T(8,128)(2,1)S(1)}, u32[]{:S(2)}, u32[]{:S(2)}) collective-permute-start(bf16[128,768]{1,0:T(8,128)(2,1)S(1)} %slice.94), channel_id=1, source_target_pairs={{0,32},{32,64},{64,96},{96,0},{1,33},{33,65},{65,97},{97,1},{2,34}... | collective-permute-start | bytes 589832 | tf_op jit(solution)/shard_map/ppermute | solution.py:15
  30.1 10.1 %collective-permute-start.4 = (bf16[128,768]{1,0:T(8,128)(2,1)S(1)}, bf16[128,768]{1,0:T(8,128)(2,1)S(1)}, u32[]{:S(2)}, u32[]{:S(2)}) collective-permute-start(bf16[128,768]{1,0:T(8,128)(2,1)S(1)} %slice.95), channel_id=1, source_target_pairs={{0,96},{32,0},{64,32},{96,64},{1,97},{33,1},{65,33},{97,65},{2,98}... | collective-permute-start | bytes 589832 | tf_op jit(solution)/shard_map/ppermute | solution.py:15
  35.9 10.5 %collective-permute-start.18 = (bf16[128,1536]{1,0:T(8,128)(2,1)S(1)}, bf16[128,1536]{1,0:T(8,128)(2,1)S(1)}, u32[]{:S(2)}, u32[]{:S(2)}) collective-permute-start(bf16[128,1536]{1,0:T(8,128)(2,1)S(1)} %collective-permute-done.16), channel_id=1, source_target_pairs={{0,2},{2,4},{4,6},{6,8},{8,10},{10,12},{12,14},{14,0},{1,3},{3,5},... | collective-permute-start | bytes 1179656 | tf_op jit(solution)/shard_map/ppermute | solution.py:15
  35.9 10.5 %collective-permute-start.19 = (bf16[128,1536]{1,0:T(8,128)(2,1)S(1)}, bf16[128,1536]{1,0:T(8,128)(2,1)S(1)}, u32[]{:S(2)}, u32[]{:S(2)}) collective-permute-start(bf16[128,1536]{1,0:T(8,128)(2,1)S(1)} %collective-permute-done.17), channel_id=1, source_target_pairs={{0,14},{2,0},{4,2},{6,4},{8,6},{10,8},{12,10},{14,12},{1,15},{3,1}... | collective-permute-start | bytes 1179656 | tf_op jit(solution)/shard_map/ppermute | solution.py:15
  39.5 99.1 %collective-permute-start.15 = (bf16[16,12288]{1,0:T(8,128)(2,1)S(1)}, bf16[16,12288]{1,0:T(8,128)(2,1)}, u32[]{:S(2)}, u32[]{:S(2)}) collective-permute-start(bf16[16,12288]{1,0:T(8,128)(2,1)S(1)} %copy-done.5), channel_id=1, source_target_pairs={{0,128},{128,0},{1,129},{129,1},{2,130},{130,2},{3,131},{131,3},{4... | collective-permute-start | bytes 1179656 | tf_op jit(solution)/shard_map/ppermute | solution.py:15
  40.2 9.4 %collective-permute-start.6 = (bf16[768,384]{1,0:T(8,128)(2,1)}, bf16[768,384]{1,0:T(8,128)(2,1)S(1)}, u32[]{:S(2)}, u32[]{:S(2)}) collective-permute-start(bf16[768,384]{1,0:T(8,128)(2,1)} %collective-permute-done.5), channel_id=1, source_target_pairs={{0,16},{16,0},{1,17},{17,1},{2,18},{18,2},{3,19},{19,3},{4,20},{20... | collective-permute-start | bytes 1769480 | tf_op jit(solution)/shard_map/ppermute | solution.py:15
  46.4 16.9 %collective-permute-start.20 = (bf16[128,1536]{1,0:T(8,128)(2,1)S(1)}, bf16[128,1536]{1,0:T(8,128)(2,1)S(1)}, u32[]{:S(2)}, u32[]{:S(2)}) collective-permute-start(bf16[128,1536]{1,0:T(8,128)(2,1)S(1)} %collective-permute-done.18), channel_id=1, source_target_pairs={{0,2},{2,4},{4,6},{6,8},{8,10},{10,12},{12,14},{14,0},{1,3},{3,5},... | collective-permute-start | bytes 1179656 | tf_op jit(solution)/shard_map/ppermute | solution.py:15
  46.4 17.0 %collective-permute-start.21 = (bf16[128,1536]{1,0:T(8,128)(2,1)S(1)}, bf16[128,1536]{1,0:T(8,128)(2,1)S(1)}, u32[]{:S(2)}, u32[]{:S(2)}) collective-permute-start(bf16[128,1536]{1,0:T(8,128)(2,1)S(1)} %collective-permute-done.19), channel_id=1, source_target_pairs={{0,14},{2,0},{4,2},{6,4},{8,6},{10,8},{12,10},{14,12},{1,15},{3,1}... | collective-permute-start | bytes 1179656 | tf_op jit(solution)/shard_map/ppermute | solution.py:15
  53.5 5.7 %collective-permute-start.11 = (bf16[128,768]{1,0:T(8,128)(2,1)S(1)}, bf16[128,768]{1,0:T(8,128)(2,1)S(1)}, u32[]{:S(2)}, u32[]{:S(2)}) collective-permute-start(bf16[128,768]{1,0:T(8,128)(2,1)S(1)} %get-tuple-element.23), channel_id=1, source_target_pairs={{0,14},{2,0},{4,2},{6,4},{8,6},{10,8},{12,10},{14,12},{1,15},{3,1}... | collective-permute-start | bytes 589832 | tf_op jit(solution)/shard_map/ppermute | solution.py:15
  54.7 8.4 %collective-permute-start.7 = (bf16[128,768]{1,0:T(8,128)(2,1)S(1)}, bf16[128,768]{1,0:T(8,128)(2,1)S(1)}, u32[]{:S(2)}, u32[]{:S(2)}) collective-permute-start(bf16[128,768]{1,0:T(8,128)(2,1)S(1)} %get-tuple-element.22), channel_id=1, source_target_pairs={{0,2},{2,4},{4,6},{6,8},{8,10},{10,12},{12,14},{14,0},{1,3},{3,5},... | collective-permute-start | bytes 589832 | tf_op jit(solution)/shard_map/ppermute | solution.py:15
  59.4 26.9 %collective-permute-start.12 = (bf16[128,1536]{1,0:T(8,128)(2,1)S(1)}, bf16[128,1536]{1,0:T(8,128)(2,1)S(1)}, u32[]{:S(2)}, u32[]{:S(2)}) collective-permute-start(bf16[128,1536]{1,0:T(8,128)(2,1)S(1)} %pad_maximum_fusion.4), channel_id=1, source_target_pairs={{0,14},{2,0},{4,2},{6,4},{8,6},{10,8},{12,10},{14,12},{1,15},{3,1}... | collective-permute-start | bytes 1179656 | tf_op jit(solution)/shard_map/ppermute | solution.py:15
  63.2 16.1 %collective-permute-start.8 = (bf16[128,1536]{1,0:T(8,128)(2,1)S(1)}, bf16[128,1536]{1,0:T(8,128)(2,1)S(1)}, u32[]{:S(2)}, u32[]{:S(2)}) collective-permute-start(bf16[128,1536]{1,0:T(8,128)(2,1)S(1)} %pad_maximum_fusion.3), channel_id=1, source_target_pairs={{0,2},{2,4},{4,6},{6,8},{8,10},{10,12},{12,14},{14,0},{1,3},{3,5},... | collective-permute-start | bytes 1179656 | tf_op jit(solution)/shard_map/ppermute | solution.py:15
  63.3 12.0 %collective-permute-start.22 = (bf16[64,1536]{1,0:T(8,128)(2,1)S(1)}, bf16[64,1536]{1,0:T(8,128)(2,1)S(1)}, u32[]{:S(2)}, u32[]{:S(2)}) collective-permute-start(bf16[64,1536]{1,0:T(8,128)(2,1)S(1)} %slice.103), channel_id=1, source_target_pairs={{0,2},{2,4},{4,6},{6,8},{8,10},{10,12},{12,14},{14,0},{1,3},{3,5},... | collective-permute-start | bytes 589832 | tf_op jit(solution)/shard_map/ppermute | solution.py:15
  63.5 11.9 %collective-permute-start.23 = (bf16[64,1536]{1,0:T(8,128)(2,1)S(1)}, bf16[64,1536]{1,0:T(8,128)(2,1)S(1)}, u32[]{:S(2)}, u32[]{:S(2)}) collective-permute-start(bf16[64,1536]{1,0:T(8,128)(2,1)S(1)} %slice.104), channel_id=1, source_target_pairs={{0,14},{2,0},{4,2},{6,4},{8,6},{10,8},{12,10},{14,12},{1,15},{3,1}... | collective-permute-start | bytes 589832 | tf_op jit(solution)/shard_map/ppermute | solution.py:15
  79.2 7.0 %collective-permute-start.24 = (bf16[256,384]{1,0:T(8,128)(2,1)S(1)}, bf16[256,384]{1,0:T(8,128)(2,1)S(1)}, u32[]{:S(2)}, u32[]{:S(2)}) collective-permute-start(bf16[256,384]{1,0:T(8,128)(2,1)S(1)} %get-tuple-element.18), channel_id=1, source_target_pairs={{0,32},{32,64},{64,96},{96,0},{1,33},{33,65},{65,97},{97,1},{2,34}... | collective-permute-start | bytes 589832 | tf_op jit(solution)/shard_map/ppermute | solution.py:15
  79.4 9.1 %collective-permute-start.9 = (bf16[128,1536]{1,0:T(8,128)(2,1)S(1)}, bf16[128,1536]{1,0:T(8,128)(2,1)S(1)}, u32[]{:S(2)}, u32[]{:S(2)}) collective-permute-start(bf16[128,1536]{1,0:T(8,128)(2,1)S(1)} %fusion.4), channel_id=1, source_target_pairs={{0,2},{2,4},{4,6},{6,8},{8,10},{10,12},{12,14},{14,0},{1,3},{3,5},... | collective-permute-start | bytes 1179656 | tf_op jit(solution)/shard_map/ppermute | solution.py:15
  82.5 23.8 %collective-permute-start.29 = (bf16[768,768]{1,0:T(8,128)(2,1)S(1)}, bf16[768,768]{1,0:T(8,128)(2,1)S(1)}, u32[]{:S(2)}, u32[]{:S(2)}) collective-permute-start(bf16[768,768]{1,0:T(8,128)(2,1)S(1)} %slice.114), channel_id=1, source_target_pairs={{0,16},{16,0},{1,17},{17,1},{2,18},{18,2},{3,19},{19,3},{4,20},{20... | collective-permute-start | bytes 3538952 | tf_op jit(solution)/shard_map/ppermute | solution.py:15
  86.2 5.7 %collective-permute-start.26 = (bf16[256,384]{1,0:T(8,128)(2,1)S(1)}, bf16[256,384]{1,0:T(8,128)(2,1)S(1)}, u32[]{:S(2)}, u32[]{:S(2)}) collective-permute-start(bf16[256,384]{1,0:T(8,128)(2,1)S(1)} %get-tuple-element.19), channel_id=1, source_target_pairs={{0,96},{32,0},{64,32},{96,64},{1,97},{33,1},{65,33},{97,65},{2,98}... | collective-permute-start | bytes 589832 | tf_op jit(solution)/shard_map/ppermute | solution.py:15
  88.7 9.8 %collective-permute-start.13 = (bf16[128,1536]{1,0:T(8,128)(2,1)S(1)}, bf16[128,1536]{1,0:T(8,128)(2,1)S(1)}, u32[]{:S(2)}, u32[]{:S(2)}) collective-permute-start(bf16[128,1536]{1,0:T(8,128)(2,1)S(1)} %get-tuple-element.8), channel_id=1, source_target_pairs={{0,14},{2,0},{4,2},{6,4},{8,6},{10,8},{12,10},{14,12},{1,15},{3,1}... | collective-permute-start | bytes 1179656 | tf_op jit(solution)/shard_map/ppermute | solution.py:15
  89.8 12.2 %collective-permute-start.25 = (bf16[256,768]{1,0:T(8,128)(2,1)S(1)}, bf16[256,768]{1,0:T(8,128)(2,1)S(1)}, u32[]{:S(2)}, u32[]{:S(2)}) collective-permute-start(bf16[256,768]{1,0:T(8,128)(2,1)S(1)} %pad_maximum_fusion.5), channel_id=1, source_target_pairs={{0,32},{32,64},{64,96},{96,0},{1,33},{33,65},{65,97},{97,1},{2,34}... | collective-permute-start | bytes 1179656 | tf_op jit(solution)/shard_map/ppermute | solution.py:15
  91.9 11.2 %collective-permute-start.27 = (bf16[256,768]{1,0:T(8,128)(2,1)S(1)}, bf16[256,768]{1,0:T(8,128)(2,1)S(1)}, u32[]{:S(2)}, u32[]{:S(2)}) collective-permute-start(bf16[256,768]{1,0:T(8,128)(2,1)S(1)} %pad_maximum_fusion.6), channel_id=1, source_target_pairs={{0,96},{32,0},{64,32},{96,64},{1,97},{33,1},{65,33},{97,65},{2,98}... | collective-permute-start | bytes 1179656 | tf_op jit(solution)/shard_map/ppermute | solution.py:15
  98.5 12.4 %collective-permute-start.10 = (bf16[128,1536]{1,0:T(8,128)(2,1)S(1)}, bf16[128,1536]{1,0:T(8,128)(2,1)S(1)}, u32[]{:S(2)}, u32[]{:S(2)}) collective-permute-start(bf16[128,1536]{1,0:T(8,128)(2,1)S(1)} %get-tuple-element.7), channel_id=1, source_target_pairs={{0,2},{2,4},{4,6},{6,8},{8,10},{10,12},{12,14},{14,0},{1,3},{3,5},... | collective-permute-start | bytes 1179656 | tf_op jit(solution)/shard_map/ppermute | solution.py:15
  102.1 10.1 %collective-permute-start.14 = (bf16[128,1536]{1,0:T(8,128)(2,1)S(1)}, bf16[128,1536]{1,0:T(8,128)(2,1)S(1)}, u32[]{:S(2)}, u32[]{:S(2)}) collective-permute-start(bf16[128,1536]{1,0:T(8,128)(2,1)S(1)} %fusion.3), channel_id=1, source_target_pairs={{0,14},{2,0},{4,2},{6,4},{8,6},{10,8},{12,10},{14,12},{1,15},{3,1}... | collective-permute-start | bytes 1179656 | tf_op jit(solution)/shard_map/ppermute | solution.py:15
  104.0 14.0 %collective-permute-start.28 = (bf16[256,384]{1,0:T(8,128)(2,1)}, bf16[256,384]{1,0:T(8,128)(2,1)}, u32[]{:S(2)}, u32[]{:S(2)}) collective-permute-start(bf16[256,384]{1,0:T(8,128)(2,1)} %slice.131), channel_id=1, source_target_pairs={{0,1},{1,0},{2,3},{3,2},{4,5},{5,4},{6,7},{7,6},{8,9},{9,8},{10,11... | collective-permute-start | bytes 589832 | tf_op jit(solution)/shard_map/ppermute | solution.py:15
  107.6 18.1 %collective-permute-start.30 = (bf16[768,384]{1,0:T(8,128)(2,1)}, bf16[768,384]{1,0:T(8,128)(2,1)}, u32[]{:S(2)}, u32[]{:S(2)}) collective-permute-start(bf16[768,384]{1,0:T(8,128)(2,1)} %slice.116), channel_id=1, source_target_pairs={{0,1},{1,0},{2,3},{3,2},{4,5},{5,4},{6,7},{7,6},{8,9},{9,8},{10,11... | collective-permute-start | bytes 1769480 | tf_op jit(solution)/shard_map/ppermute | solution.py:15
  113.3 21.5 %all-to-all-start = ((bf16[16,16,1536]{2,1,0:T(8,128)(2,1)}), bf16[16,16,1536]{2,1,0:T(8,128)(2,1)S(1)}, u32[]{:S(2)}, u32[]{:S(2)}) async-start(bf16[16,16,1536]{2,1,0:T(8,128)(2,1)} %bitcast.20), calls=%async_computation | async-start | bytes 1572864 | tf_op jit(solution)/shard_map/all_to_all | solution.py:115

commit v5 on v4

--- a/solution.py
+++ b/solution.py
@@ -35,6 +35,10 @@
     return lax.dynamic_update_slice(buffer, block, starts)
 
 
+def tie(*values):
+    return lax.optimization_barrier(values)
+
+
 def both_ways(right, left, axis):
     return shift(right, axis, 1), shift(left, axis, -1)
 
@@ -47,23 +51,22 @@
     for away in range(1, far):
         right, left = both_ways(right, left, axis)
         blocks[-away], blocks[away] = right, left
-    blocks[far] = jnp.concatenate(both_ways(right[:half], left[half:], axis), 0)
-    return blocks
+    return blocks, both_ways(right[:half], left[half:], axis)
 
 
-def ring_sum(chunk, axis):
+def ring_steps(chunk, axis):
     far = lax.axis_size(axis) // 2
     opposite = chunk(far)
     half = opposite.shape[1] // 2
-    low, high = both_ways(opposite[:, :half], opposite[:, half:], axis)
+    low, high = yield both_ways(opposite[:, :half], opposite[:, half:], axis)
     ahead, behind = chunk(far - 1), chunk(1 - far)
     right = jnp.concatenate([add(ahead[:, :half], low), ahead[:, half:]], 1)
     left = jnp.concatenate([behind[:, :half], add(behind[:, half:], high)], 1)
     for away in range(far - 2, 0, -1):
-        right, left = both_ways(right, left, axis)
+        right, left = yield both_ways(right, left, axis)
         right, left = add(chunk(away), right), add(chunk(-away), left)
-    right, left = both_ways(right, left, axis)
-    return chunk(0).astype(F32) + right.astype(F32) + left.astype(F32)
+    right, left = yield both_ways(right, left, axis)
+    yield chunk(0).astype(F32) + right.astype(F32) + left.astype(F32)
 
 
 def shards(segment_input, context, out_proj, grad_output):
@@ -83,33 +86,55 @@
     block_tokens = own_count * group
 
     both = jnp.concatenate([contexts, swap(contexts, "xh")], 1)
-    ctx_all = jnp.zeros((n_z, n_y, z_tokens, 2 * width), BF16)
-    for away, part in ring_gather(both, "y").items():
-        ctx_all = place(ctx_all, part.reshape(n_z, 1, z_tokens, 2 * width), (0, wrap(y + away, n_y), 0, 0))
-    ctx_flat = ctx_all.reshape(tokens, 2 * width)
-
     def rows(core_at, xh_at):
         return lax.dynamic_slice_in_dim(weights, ((y * n_core + core_at) * n_xh + xh_at) * piece, piece, 0)
 
-    came_rows = swap(rows(core, 1 - xh), "xh")
+    both, partner_rows = tie(both, rows(core, 1 - xh))
+    came_rows = swap(partner_rows, "xh")
     other_rows = swap(came_rows, "core")
+    outgoing, came_rows = tie(jnp.where(section == 0, residual, upstream), came_rows)
+    early = swap(outgoing, "section")
     block = jnp.concatenate(
         [jnp.concatenate([rows(core, xh), came_rows], 1), jnp.concatenate([rows(1 - core, xh), other_rows], 1)], 0
     )
+
+    ctx_all = jnp.zeros((n_z, n_y, z_tokens, 2 * width), BF16)
+    ctx_blocks, across = ring_gather(both, "y")
+    ctx_blocks[n_y // 2] = jnp.concatenate(across, 0)
+    for away, part in ctx_blocks.items():
+        ctx_all = place(ctx_all, part.reshape(n_z, 1, z_tokens, 2 * width), (0, wrap(y + away, n_y), 0, 0))
+    ctx_flat = ctx_all.reshape(tokens, 2 * width)
 
     spread = upstream.reshape(own_count, n_y, n_core, n_xh, piece)
     spread = jnp.stack([pick(spread, core, 2), pick(spread, 1 - core, 2)], 3)
     spread = spread.transpose(1, 2, 0, 3, 4).reshape(group, own_count, features)
     spread = lax.all_to_all(spread, ("y", "xh"), 0, 0, tiled=True).reshape(block_tokens, features)
     grad_all = jnp.zeros((n_z, block_tokens, features), BF16)
-    for away, part in ring_gather(spread, "z").items():
+    grad_blocks, far_blocks = ring_gather(spread, "z")
+    for away, part in grad_blocks.items():
         grad_all = place(grad_all, part[None], (wrap(z + away, n_z), 0, 0))
-    grad_flat = grad_all.reshape(tokens, features)
 
     partial_branch = lax.dot_general(
         ctx_flat, block, (((1,), (1,)), ((), ())), preferred_element_type=F32
     ).astype(BF16).reshape(n_z, block_tokens, features)
-    branch = ring_sum(lambda away: pick(partial_branch, wrap(z + away, n_z)), "z").astype(BF16)
+    ring = ring_steps(lambda away: pick(partial_branch, wrap(z + away, n_z)), "z")
+    *step, early = tie(*next(ring), early)
+    step = ring.send(step)
+    *step, far_low, far_high = tie(*step, *far_blocks)
+    step = ring.send(step)
+    grad_all = place(grad_all, jnp.concatenate([far_low, far_high], 0)[None], (wrap(z + n_z // 2, n_z), 0, 0))
+    grad_flat = grad_all.reshape(tokens, features)
+    partial_ctx = jnp.dot(grad_flat, block, preferred_element_type=F32).astype(BF16)
+    norm_factor = 1.0 / math.sqrt(tokens * n_core)
+    product = lax.dot_general(grad_flat, ctx_flat, (((0,), (0,)), ((), ())), preferred_element_type=F32)
+    product = (norm_factor * product).astype(BF16)
+    *step, partial_ctx, product = tie(*step, partial_ctx, product)
+    step = ring.send(step)
+    partial_ctx = partial_ctx.reshape(n_z, n_y, z_tokens, 2 * width)
+    ctx_ring = ring_steps(lambda away: pick(partial_ctx, wrap(y + away, n_y), 1).reshape(group_tokens, 2 * width), "y")
+    ctx_step = next(ctx_ring)
+    *step, ctx_low, ctx_high, product = tie(*step, *ctx_step, product)
+    branch = ring.send(step).astype(BF16)
     branch = branch.reshape(1, group, own_count, features)
     branch = jnp.concatenate([branch, branch], 0).reshape(2 * group, own_count, features)
     branch = lax.all_to_all(branch, ("section", "y", "xh"), 0, 0, tiled=True)
@@ -117,17 +142,11 @@
     branch = jnp.where(core == 0, branch, jnp.flip(branch, 4))
     branch = branch.transpose(0, 3, 1, 4, 2, 5).reshape(2, own_count, model)
     forward = add(residual, pick(branch, section))
-    early = swap(jnp.where(section == 0, residual, upstream), "section")
     received = jnp.where(section == 0, early, add(early, branch[0]))
 
-    partial_ctx = jnp.dot(grad_flat, block, preferred_element_type=F32).astype(BF16)
-    partial_ctx = partial_ctx.reshape(n_z, n_y, z_tokens, 2 * width)
-    summed = ring_sum(lambda away: pick(partial_ctx, wrap(y + away, n_y), 1).reshape(group_tokens, 2 * width), "y")
+    summed = ctx_ring.send(ctx_ring.send((ctx_low, ctx_high)))
     ctx_grad = add(summed[:, :width], swap(summed[:, width:].astype(BF16), "xh"))
 
-    norm_factor = 1.0 / math.sqrt(tokens * n_core)
-    product = lax.dot_general(grad_flat, ctx_flat, (((0,), (0,)), ((), ())), preferred_element_type=F32)
-    product = (norm_factor * product).astype(BF16)
     own_rows = add(product[:piece], swap(product[piece:], "core"))
     kept = own_rows[:, :width]
     came = swap(own_rows[:, width:], "xh")

time: 142 us -> 143 us (level)
  starting transfers between devices: 54.1 us -> 61.4 us
  waiting for transfers between devices: 52.6 us -> 47.1 us
  other arithmetic: 11.1 us -> 8.71 us
    ppermute x31, starting transfers between devices: 44 us -> 51.2 us  [shift(): return lax.ppermute(value, axis, [(i, (i + by) % n) for i in range(n)])]
    all_to_all x1, waiting for transfers between devices: 6.7 us -> 0.01 us  [shards(): branch = lax.all_to_all(branch, ('section', 'y', 'xh'), 0, 0, tiled=True)]
    slice x1, local copies, waits for them, and re-layouts: 0.08 us -> 2.36 us  [shards(): own_rows = add(product[:piece], swap(product[piece:], 'core'))]
    broadcast_in_dim x3, other arithmetic: 4.76 us -> 2.69 us  [shards(): return (forward[None], received[None], ctx_grad[None], weight_grad[None])]
    convert_element_type x10 -> x9, other arithmetic: 1.85 us -> 3.45 us  [add(): return (a.astype(F32) + b.astype(F32)).astype(BF16)]
  transfers between devices with their start and end apart: 33 -> 33, of which waited for: 15 -> 11; matrix products, arithmetic and copies ran while one was open for 22% -> 20% of each run, Pallas kernels for 0% -> 0%
where the time goes in v5:
time: 143 us; the launch traced here: 142 us
  starting transfers between devices  61.4 us (43%)
  waiting for transfers between devices  47.1 us (33%)
  local copies, waits for them, and re-layouts  12.1 us (8%)
  matrix products  11.4 us (8%)
  other arithmetic  8.71 us (6%)
    ppermute x31, starting transfers between devices, shift(): return lax.ppermute(value, axis, [(i, (i + by) % n) for i in range(n)])  51.2 us
    ppermute x31, waiting for transfers between devices, shift(): return lax.ppermute(value, axis, [(i, (i + by) % n) for i in range(n)])  47.1 us
    all_to_all x1, starting transfers between devices, shards(): lax.all_to_all(spread, ('y', 'xh'), 0, 0, tiled=True)  5.31 us
    all_to_all x1, starting transfers between devices, shards(): branch = lax.all_to_all(branch, ('section', 'y', 'xh'), 0, 0, tiled=True)  4.81 us
    dot_general x1, matrix products, shards(): lax.dot_general(grad_flat, ctx_flat, (((0,), (0,)), ((), ())), preferred_...  3.98 us
    dot_general x1, matrix products, shards(): lax.dot_general(ctx_flat, block, (((1,), (1,)), ((), ())), preferred_elem...  3.71 us
    dot_general x1, matrix products, shards(): jnp.dot(grad_flat, block, preferred_element_type=F32).astype(BF16)  3.66 us
    convert_element_type x9, other arithmetic, add(): return (a.astype(F32) + b.astype(F32)).astype(BF16)  3.45 us
  transfers between devices with their start and end apart: 33, of which 11 were waited for; matrix products, arithmetic and copies ran while one was open for 20% of the time, Pallas kernels for 0%

profile of v5, /device:TPU:2, one launch (start us, length us, event | category | flops | bytes accessed | tf_op | source)
XLA Modules:
  0.0 141.8 jit_solution(11184569429192358385)
XLA Ops:
  0.6 2.2 %collective-permute-start = (bf16[256,384]{1,0:T(8,128)(2,1)}, bf16[256,384]{1,0:T(8,128)(2,1)S(1)}, u32[]{:S(2)}, u32[]{:S(2)}) collective-permute-start(bf16[256,384]{1,0:T(8,128)(2,1)} %bitcast.106), channel_id=1, source_target_pairs={{0,1},{1,0},{2,3},{3,2},{4,5},{5,4},{6,7},{7,6},{8,9},{9,8},{10,11... | collective-permute-start | bytes 589832 | tf_op jit(solution)/shard_map/ppermute | solution.py:15
  2.8 1.3 reshape_squeeze.3
  4.1 0.3 constant_dynamic-slice_fusion.5
  4.6 0.3 copy.20
  4.9 1.0 reshape.93
  5.9 5.3 %all-to-all-start = ((bf16[8,16,1536]{2,1,0:T(8,128)(2,1)}), bf16[8,16,1536]{2,1,0:T(8,128)(2,1)S(1)}, u32[]{:S(2)}, u32[]{:S(2)}) async-start(bf16[8,16,1536]{2,1,0:T(8,128)(2,1)} %reshape.93), calls=%async_computation | async-start | bytes 786432 | tf_op jit(solution)/shard_map/all_to_all | solution.py:111
  11.2 2.7 %dynamic-slice_bitcast_fusion.1 = (bf16[768,384]{1,0:T(8,128)(2,1)}, bf16[768,384]{1,0:T(8,128)(2,1)}, bf16[768,384]{1,0:T(8,128)(2,1)}) fusion(bf16[1,12288,384]{2,1,0:T(8,128)(2,1)} %param.6, s32[]{:T(128)S(6)} %select_n.113, s32[]{:T(128)S(6)} %select_n.108, s32[]{:T(128)S(6)} %select_n.117), kind=kLoop, calls=%fused_computation.26 | loop fusion | bytes 3538956 | tf_op jit(solution)/shard_map/dynamic_slice | solution.py:90
  14.0 2.1 %collective-permute-start.1 = (bf16[256,768]{1,0:T(8,128)(2,1)S(1)}, bf16[256,768]{1,0:T(8,128)(2,1)S(1)}, u32[]{:S(2)}, u32[]{:S(2)}) collective-permute-start(bf16[256,768]{1,0:T(8,128)(2,1)S(1)} %pad_maximum_fusion.1), channel_id=1, source_target_pairs={{0,32},{32,64},{64,96},{96,0},{1,33},{33,65},{65,97},{97,1},{2,34}... | collective-permute-start | bytes 1179656 | tf_op jit(solution)/shard_map/ppermute | solution.py:15
  16.1 1.3 collective-permute-start.2
  17.4 0.8 select_bitcast_fusion
  18.2 3.4 %collective-permute-start.5 = (bf16[768,384]{1,0:T(8,128)(2,1)}, bf16[768,384]{1,0:T(8,128)(2,1)}, u32[]{:S(2)}, u32[]{:S(2)}) collective-permute-start(bf16[768,384]{1,0:T(8,128)(2,1)} %get-tuple-element.25), channel_id=1, source_target_pairs={{0,1},{1,0},{2,3},{3,2},{4,5},{5,4},{6,7},{7,6},{8,9},{9,8},{10,11... | collective-permute-start | bytes 1769480 | tf_op jit(solution)/shard_map/ppermute | solution.py:15
  21.6 0.2 broadcast_in_dim.37
  21.8 2.0 %collective-permute-start.12 = (bf16[128,1536]{1,0:T(8,128)(2,1)S(1)}, bf16[128,1536]{1,0:T(8,128)(2,1)S(1)}, u32[]{:S(2)}, u32[]{:S(2)}) collective-permute-start(bf16[128,1536]{1,0:T(8,128)(2,1)S(1)} %bitcast.92), channel_id=1, source_target_pairs={{0,2},{2,4},{4,6},{6,8},{8,10},{10,12},{12,14},{14,0},{1,3},{3,5},... | collective-permute-start | bytes 1179656 | tf_op jit(solution)/shard_map/ppermute | solution.py:15
  23.8 4.0 %collective-permute-start.16 = (bf16[128,1536]{1,0:T(8,128)(2,1)S(1)}, bf16[128,1536]{1,0:T(8,128)(2,1)S(1)}, u32[]{:S(2)}, u32[]{:S(2)}) collective-permute-start(bf16[128,1536]{1,0:T(8,128)(2,1)S(1)} %bitcast.93), channel_id=1, source_target_pairs={{0,14},{2,0},{4,2},{6,4},{8,6},{10,8},{12,10},{14,12},{1,15},{3,1}... | collective-permute-start | bytes 1179656 | tf_op jit(solution)/shard_map/ppermute | solution.py:15
  27.9 0.3 broadcast_in_dim.38
  28.2 0.3 collective-permute-start.3
  28.6 3.1 %collective-permute-start.4 = (bf16[128,768]{1,0:T(8,128)(2,1)S(1)}, bf16[128,768]{1,0:T(8,128)(2,1)S(1)}, u32[]{:S(2)}, u32[]{:S(2)}) collective-permute-start(bf16[128,768]{1,0:T(8,128)(2,1)S(1)} %slice.95), channel_id=1, source_target_pairs={{0,96},{32,0},{64,32},{96,64},{1,97},{33,1},{65,33},{97,65},{2,98}... | collective-permute-start | bytes 589832 | tf_op jit(solution)/shard_map/ppermute | solution.py:15
  31.7 3.5 %collective-permute-done.12 = bf16[128,1536]{1,0:T(8,128)(2,1)S(1)} collective-permute-done((bf16[128,1536]{1,0:T(8,128)(2,1)S(1)}, bf16[128,1536]{1,0:T(8,128)(2,1)S(1)}, u32[]{:S(2)}, u32[]{:S(2)}) %collective-permute-start.12) | collective-permute-done | bytes 393248 | tf_op jit(solution)/shard_map/ppermute | solution.py:15
  35.2 3.2 %collective-permute-start.17 = (bf16[128,1536]{1,0:T(8,128)(2,1)S(1)}, bf16[128,1536]{1,0:T(8,128)(2,1)S(1)}, u32[]{:S(2)}, u32[]{:S(2)}) collective-permute-start(bf16[128,1536]{1,0:T(8,128)(2,1)S(1)} %collective-permute-done.16), channel_id=1, source_target_pairs={{0,14},{2,0},{4,2},{6,4},{8,6},{10,8},{12,10},{14,12},{1,15},{3,1}... | collective-permute-start | bytes 1179656 | tf_op jit(solution)/shard_map/ppermute | solution.py:15
  38.5 0.7 collective-permute-start.9
  39.3 6.5 %collective-permute-done.13 = bf16[128,1536]{1,0:T(8,128)(2,1)S(1)} collective-permute-done((bf16[128,1536]{1,0:T(8,128)(2,1)S(1)}, bf16[128,1536]{1,0:T(8,128)(2,1)S(1)}, u32[]{:S(2)}, u32[]{:S(2)}) %collective-permute-start.13) | collective-permute-done | bytes 393248 | tf_op jit(solution)/shard_map/ppermute | solution.py:15
  45.8 3.2 %collective-permute-start.18 = (bf16[128,1536]{1,0:T(8,128)(2,1)S(1)}, bf16[128,1536]{1,0:T(8,128)(2,1)S(1)}, u32[]{:S(2)}, u32[]{:S(2)}) collective-permute-start(bf16[128,1536]{1,0:T(8,128)(2,1)S(1)} %collective-permute-done.17), channel_id=1, source_target_pairs={{0,14},{2,0},{4,2},{6,4},{8,6},{10,8},{12,10},{14,12},{1,15},{3,1}... | collective-permute-start | bytes 1179656 | tf_op jit(solution)/shard_map/ppermute | solution.py:15
  49.2 3.7 %convolution_convert_fusion = bf16[1024,1536]{1,0:T(8,128)(2,1)S(1)} fusion(bf16[1024,768]{1,0:T(8,128)(2,1)S(1)} %bitcast.90, bf16[768,384]{1,0:T(8,128)(2,1)S(1)} %collective-permute-done.6, bf16[768,384]{1,0:T(8,128)(2,1)S(1)} %copy-done.3, bf16[768,384]{1,0:T(8,128)(2,1)} %collective-permute-done.5, bf16[768,384]{1,0:T(8,128)(2,1)S(1)} %copy-done.2), kind=kOutput, calls=%fused_computation.1 | convolution fusion | flops 2426929152 | bytes 7077888 | tf_op jit(solution)/shard_map/dot_general | solution.py:117
  53.1 3.2 %collective-permute-start.8 = (bf16[128,768]{1,0:T(8,128)(2,1)S(1)}, bf16[128,768]{1,0:T(8,128)(2,1)S(1)}, u32[]{:S(2)}, u32[]{:S(2)}) collective-permute-start(bf16[128,768]{1,0:T(8,128)(2,1)S(1)} %get-tuple-element.64), channel_id=1, source_target_pairs={{0,14},{2,0},{4,2},{6,4},{8,6},{10,8},{12,10},{14,12},{1,15},{3,1}... | collective-permute-start | bytes 589832 | tf_op jit(solution)/shard_map/ppermute | solution.py:15
  56.4 0.8 collective-permute-done.14
  57.3 3.3 %collective-permute-start.19 = (bf16[64,1536]{1,0:T(8,128)(2,1)S(1)}, bf16[64,1536]{1,0:T(8,128)(2,1)S(1)}, u32[]{:S(2)}, u32[]{:S(2)}) collective-permute-start(bf16[64,1536]{1,0:T(8,128)(2,1)S(1)} %slice.103), channel_id=1, source_target_pairs={{0,14},{2,0},{4,2},{6,4},{8,6},{10,8},{12,10},{14,12},{1,15},{3,1}... | collective-permute-start | bytes 589832 | tf_op jit(solution)/shard_map/ppermute | solution.py:15
  60.6 1.2 collective-permute-done.7
  61.9 3.4 %collective-permute-start.11 = (bf16[128,1536]{1,0:T(8,128)(2,1)S(1)}, bf16[128,1536]{1,0:T(8,128)(2,1)S(1)}, u32[]{:S(2)}, u32[]{:S(2)}) collective-permute-start(bf16[128,1536]{1,0:T(8,128)(2,1)S(1)} %pad_maximum_fusion.4), channel_id=1, source_target_pairs={{0,14},{2,0},{4,2},{6,4},{8,6},{10,8},{12,10},{14,12},{1,15},{3,1}... | collective-permute-start | bytes 1179656 | tf_op jit(solution)/shard_map/ppermute | solution.py:15
  65.5 0.3 collective-permute-done.19
  65.8 5.8 %collective-permute-done.11 = bf16[128,1536]{1,0:T(8,128)(2,1)S(1)} collective-permute-done((bf16[128,1536]{1,0:T(8,128)(2,1)S(1)}, bf16[128,1536]{1,0:T(8,128)(2,1)S(1)}, u32[]{:S(2)}, u32[]{:S(2)}) %collective-permute-start.11) | collective-permute-done | bytes 393248 | tf_op jit(solution)/shard_map/ppermute | solution.py:15
  71.6 3.9 %collective-permute-done.10 = bf16[128,1536]{1,0:T(8,128)(2,1)S(1)} collective-permute-done((bf16[128,1536]{1,0:T(8,128)(2,1)S(1)}, bf16[128,1536]{1,0:T(8,128)(2,1)S(1)}, u32[]{:S(2)}, u32[]{:S(2)}) %collective-permute-start.10) | collective-permute-done | bytes 393248 | tf_op jit(solution)/shard_map/ppermute | solution.py:15
  75.5 0.2 fusion.3
  75.8 3.2 %collective-permute-start.21 = (bf16[128,1536]{1,0:T(8,128)(2,1)S(1)}, bf16[128,1536]{1,0:T(8,128)(2,1)S(1)}, u32[]{:S(2)}, u32[]{:S(2)}) collective-permute-start(bf16[128,1536]{1,0:T(8,128)(2,1)S(1)} %get-tuple-element.49), channel_id=1, source_target_pairs={{0,14},{2,0},{4,2},{6,4},{8,6},{10,8},{12,10},{14,12},{1,15},{3,1}... | collective-permute-start | bytes 1179656 | tf_op jit(solution)/shard_map/ppermute | solution.py:15
  79.1 3.7 %convolution_convert_fusion.1 = bf16[1024,768]{1,0:T(8,128)(2,1)S(1)} fusion(bf16[1024,1536]{1,0:T(8,128)(2,1)S(1)} %bitcast.84, bf16[768,384]{1,0:T(8,128)(2,1)S(1)} %collective-permute-done.6, bf16[768,384]{1,0:T(8,128)(2,1)S(1)} %copy-done.3, bf16[768,384]{1,0:T(8,128)(2,1)} %collective-permute-done.5, bf16[768,384]{1,0:T(8,128)(2,1)S(1)} %copy-done.2), kind=kOutput, calls=%fused_computation.4 | convolution fusion | flops 2426142720 | bytes 7077888 | tf_op jit(solution)/shard_map/dot_general | solution.py:127
  82.8 4.0 %multiply_convert_fusion = bf16[1536,768]{1,0:T(8,128)(2,1)} fusion(bf16[1024,1536]{1,0:T(8,128)(2,1)S(1)} %bitcast.85, bf16[1024,768]{1,0:T(8,128)(2,1)S(1)} %bitcast.91), kind=kOutput, calls=%fused_computation | convolution fusion | flops 2418278400 | bytes 7077888 | tf_op jit(solution)/shard_map/dot_general | solution.py:129
  86.7 0.1 constant_dynamic-slice_fusion.2
  86.9 0.2 fusion.2
  87.1 0.3 collective-permute-start.22
  87.4 3.2 %collective-permute-start.23 = (bf16[128,1536]{1,0:T(8,128)(2,1)S(1)}, bf16[128,1536]{1,0:T(8,128)(2,1)S(1)}, u32[]{:S(2)}, u32[]{:S(2)}) collective-permute-start(bf16[128,1536]{1,0:T(8,128)(2,1)S(1)} %get-tuple-element.47), channel_id=1, source_target_pairs={{0,14},{2,0},{4,2},{6,4},{8,6},{10,8},{12,10},{14,12},{1,15},{3,1}... | collective-permute-start | bytes 1179656 | tf_op jit(solution)/shard_map/ppermute | solution.py:15
  90.7 3.2 %collective-permute-start.25 = (bf16[256,384]{1,0:T(8,128)(2,1)S(1)}, bf16[256,384]{1,0:T(8,128)(2,1)S(1)}, u32[]{:S(2)}, u32[]{:S(2)}) collective-permute-start(bf16[256,384]{1,0:T(8,128)(2,1)S(1)} %get-tuple-element.60), channel_id=1, source_target_pairs={{0,96},{32,0},{64,32},{96,64},{1,97},{33,1},{65,33},{97,65},{2,98}... | collective-permute-start | bytes 589832 | tf_op jit(solution)/shard_map/ppermute | solution.py:15
  94.0 5.7 %collective-permute-done.24 = bf16[256,384]{1,0:T(8,128)(2,1)S(1)} collective-permute-done((bf16[256,384]{1,0:T(8,128)(2,1)S(1)}, bf16[256,384]{1,0:T(8,128)(2,1)S(1)}, u32[]{:S(2)}, u32[]{:S(2)}) %collective-permute-start.24) | collective-permute-done | bytes 196640 | tf_op jit(solution)/shard_map/ppermute | solution.py:15
  100.0 3.3 %collective-permute-start.27 = (bf16[256,768]{1,0:T(8,128)(2,1)S(1)}, bf16[256,768]{1,0:T(8,128)(2,1)S(1)}, u32[]{:S(2)}, u32[]{:S(2)}) collective-permute-start(bf16[256,768]{1,0:T(8,128)(2,1)S(1)} %pad_maximum_fusion.6), channel_id=1, source_target_pairs={{0,96},{32,0},{64,32},{96,64},{1,97},{33,1},{65,33},{97,65},{2,98}... | collective-permute-start | bytes 1179656 | tf_op jit(solution)/shard_map/ppermute | solution.py:15
  103.3 0.2 fusion.7
  103.5 0.9 pad_maximum_fusion
  104.4 4.8 %all-to-all-start.1 = ((bf16[16,16,1536]{2,1,0:T(8,128)(2,1)}), bf16[16,16,1536]{2,1,0:T(8,128)(2,1)S(1)}, u32[]{:S(2)}, u32[]{:S(2)}) async-start(bf16[16,16,1536]{2,1,0:T(8,128)(2,1)} %bitcast.35), calls=%async_computation.1 | async-start | bytes 1572864 | tf_op jit(solution)/shard_map/all_to_all | solution.py:140
  109.2 3.9 %collective-permute-done.26 = bf16[256,768]{1,0:T(8,128)(2,1)S(1)} collective-permute-done((bf16[256,768]{1,0:T(8,128)(2,1)S(1)}, bf16[256,768]{1,0:T(8,128)(2,1)S(1)}, u32[]{:S(2)}, u32[]{:S(2)}) %collective-permute-start.26) | collective-permute-done | bytes 393248 | tf_op jit(solution)/shard_map/ppermute | solution.py:15
  113.1 0.2 fusion.1
  113.3 1.0 collective-permute-start.28
  114.3 2.4 %slice.91 = bf16[768,768]{1,0:T(8,128)(2,1)} slice(bf16[1536,768]{1,0:T(8,128)(2,1)} %multiply_convert_fusion), slice={[768:1536], [0:768]} | slice | bytes 2359296 | tf_op jit(solution)/shard_map/slice | solution.py:150
  116.7 3.9 %collective-permute-done.28 = bf16[256,384]{1,0:T(8,128)(2,1)S(1)} collective-permute-done((bf16[256,384]{1,0:T(8,128)(2,1)S(1)}, bf16[256,384]{1,0:T(8,128)(2,1)S(1)}, u32[]{:S(2)}, u32[]{:S(2)}) %collective-permute-start.28) | collective-permute-done | bytes 196640 | tf_op jit(solution)/shard_map/ppermute | solution.py:15
  120.6 0.7 fusion.12
  121.3 0.2 reshape.100
  121.6 0.2 fusion
  121.8 0.6 copy.24
  122.4 0.6 reshape.109
  123.1 0.8 fusion.9
  123.9 0.6 copy.23
  124.5 0.6 reshape.101
  125.2 1.9 %add_convert_fusion = bf16[768,768]{1,0:T(8,128)(2,1)S(1)} fusion(bf16[768,768]{1,0:T(8,128)(2,1)} %collective-permute-done.29, bf16[1536,768]{1,0:T(8,128)(2,1)} %multiply_convert_fusion), kind=kLoop, calls=%fused_computation.3 | loop fusion | flops 2359296 | bytes 3538944 | tf_op jit(solution)/shard_map/convert_element_type | solution.py:23
  127.1 1.0 collective-permute-start.30
  128.1 0.8 add_convert_fusion.2
  129.0 11.6 %collective-permute-done.30 = bf16[768,384]{1,0:T(8,128)(2,1)S(1)} collective-permute-done((bf16[768,384]{1,0:T(8,128)(2,1)S(1)}, bf16[768,384]{1,0:T(8,128)(2,1)S(1)}, u32[]{:S(2)}, u32[]{:S(2)}) %collective-permute-start.30) | collective-permute-done | bytes 589856 | tf_op jit(solution)/shard_map/ppermute | solution.py:15
  140.6 0.1 broadcast_select_fusion.1
  140.7 1.1 maximum_bitcast_fusion
  (83 shorter events, 2.1 us)
Async XLA Ops:
  0.6 13.3 %collective-permute-start = (bf16[256,384]{1,0:T(8,128)(2,1)}, bf16[256,384]{1,0:T(8,128)(2,1)S(1)}, u32[]{:S(2)}, u32[]{:S(2)}) collective-permute-start(bf16[256,384]{1,0:T(8,128)(2,1)} %bitcast.106), channel_id=1, source_target_pairs={{0,1},{1,0},{2,3},{3,2},{4,5},{5,4},{6,7},{7,6},{8,9},{9,8},{10,11... | collective-permute-start | bytes 589832 | tf_op jit(solution)/shard_map/ppermute | solution.py:15
  4.5 9.4 %copy-start.5 = (bf16[1,256,384]{2,1,0:T(8,128)(2,1)S(1)}, bf16[1,256,384]{2,1,0:T(8,128)(2,1)}, u32[]{:S(2)}) copy-start(bf16[1,256,384]{2,1,0:T(8,128)(2,1)} %param.5) | copy-start | bytes 589828
  4.9 12.5 %copy-start = (bf16[1,16,12288]{2,1,0:T(8,128)(2,1)S(1)}, bf16[1,16,12288]{2,1,0:T(8,128)(2,1)}, u32[]{:S(2)}) copy-start(bf16[1,16,12288]{2,1,0:T(8,128)(2,1)} %param.7) | copy-start | bytes 1179652
  4.9 12.5 %copy-start.1 = (bf16[1,16,12288]{2,1,0:T(8,128)(2,1)S(1)}, bf16[1,16,12288]{2,1,0:T(8,128)(2,1)}, u32[]{:S(2)}) copy-start(bf16[1,16,12288]{2,1,0:T(8,128)(2,1)} %param.4) | copy-start | bytes 1179652
  5.9 15.9 %all-to-all-start = ((bf16[8,16,1536]{2,1,0:T(8,128)(2,1)}), bf16[8,16,1536]{2,1,0:T(8,128)(2,1)S(1)}, u32[]{:S(2)}, u32[]{:S(2)}) async-start(bf16[8,16,1536]{2,1,0:T(8,128)(2,1)} %reshape.93), calls=%async_computation | async-start | bytes 786432 | tf_op jit(solution)/shard_map/all_to_all | solution.py:111
  14.0 14.2 %collective-permute-start.1 = (bf16[256,768]{1,0:T(8,128)(2,1)S(1)}, bf16[256,768]{1,0:T(8,128)(2,1)S(1)}, u32[]{:S(2)}, u32[]{:S(2)}) collective-permute-start(bf16[256,768]{1,0:T(8,128)(2,1)S(1)} %pad_maximum_fusion.1), channel_id=1, source_target_pairs={{0,32},{32,64},{64,96},{96,0},{1,33},{33,65},{65,97},{97,1},{2,34}... | collective-permute-start | bytes 1179656 | tf_op jit(solution)/shard_map/ppermute | solution.py:15
  16.1 12.5 %collective-permute-start.2 = (bf16[256,768]{1,0:T(8,128)(2,1)S(1)}, bf16[256,768]{1,0:T(8,128)(2,1)S(1)}, u32[]{:S(2)}, u32[]{:S(2)}) collective-permute-start(bf16[256,768]{1,0:T(8,128)(2,1)S(1)} %pad_maximum_fusion.1), channel_id=1, source_target_pairs={{0,96},{32,0},{64,32},{96,64},{1,97},{33,1},{65,33},{97,65},{2,98}... | collective-permute-start | bytes 1179656 | tf_op jit(solution)/shard_map/ppermute | solution.py:15
  18.2 20.4 %collective-permute-start.5 = (bf16[768,384]{1,0:T(8,128)(2,1)}, bf16[768,384]{1,0:T(8,128)(2,1)}, u32[]{:S(2)}, u32[]{:S(2)}) collective-permute-start(bf16[768,384]{1,0:T(8,128)(2,1)} %get-tuple-element.25), channel_id=1, source_target_pairs={{0,1},{1,0},{2,3},{3,2},{4,5},{5,4},{6,7},{7,6},{8,9},{9,8},{10,11... | collective-permute-start | bytes 1769480 | tf_op jit(solution)/shard_map/ppermute | solution.py:15
  21.8 13.4 %collective-permute-start.12 = (bf16[128,1536]{1,0:T(8,128)(2,1)S(1)}, bf16[128,1536]{1,0:T(8,128)(2,1)S(1)}, u32[]{:S(2)}, u32[]{:S(2)}) collective-permute-start(bf16[128,1536]{1,0:T(8,128)(2,1)S(1)} %bitcast.92), channel_id=1, source_target_pairs={{0,2},{2,4},{4,6},{6,8},{8,10},{10,12},{12,14},{14,0},{1,3},{3,5},... | collective-permute-start | bytes 1179656 | tf_op jit(solution)/shard_map/ppermute | solution.py:15
  23.8 11.4 %collective-permute-start.16 = (bf16[128,1536]{1,0:T(8,128)(2,1)S(1)}, bf16[128,1536]{1,0:T(8,128)(2,1)S(1)}, u32[]{:S(2)}, u32[]{:S(2)}) collective-permute-start(bf16[128,1536]{1,0:T(8,128)(2,1)S(1)} %bitcast.93), channel_id=1, source_target_pairs={{0,14},{2,0},{4,2},{6,4},{8,6},{10,8},{12,10},{14,12},{1,15},{3,1}... | collective-permute-start | bytes 1179656 | tf_op jit(solution)/shard_map/ppermute | solution.py:15
  28.1 10.4 %copy-start.4 = (bf16[16,12288]{1,0:T(8,128)(2,1)S(1)}, bf16[16,12288]{1,0:T(8,128)(2,1)}, u32[]{:S(2)}) copy-start(bf16[16,12288]{1,0:T(8,128)(2,1)} %select_bitcast_fusion) | copy-start | bytes 1179652
  28.2 11.0 %collective-permute-start.3 = (bf16[128,768]{1,0:T(8,128)(2,1)S(1)}, bf16[128,768]{1,0:T(8,128)(2,1)S(1)}, u32[]{:S(2)}, u32[]{:S(2)}) collective-permute-start(bf16[128,768]{1,0:T(8,128)(2,1)S(1)} %slice.94), channel_id=1, source_target_pairs={{0,32},{32,64},{64,96},{96,0},{1,33},{33,65},{65,97},{97,1},{2,34}... | collective-permute-start | bytes 589832 | tf_op jit(solution)/shard_map/ppermute | solution.py:15
  28.6 10.7 %collective-permute-start.4 = (bf16[128,768]{1,0:T(8,128)(2,1)S(1)}, bf16[128,768]{1,0:T(8,128)(2,1)S(1)}, u32[]{:S(2)}, u32[]{:S(2)}) collective-permute-start(bf16[128,768]{1,0:T(8,128)(2,1)S(1)} %slice.95), channel_id=1, source_target_pairs={{0,96},{32,0},{64,32},{96,64},{1,97},{33,1},{65,33},{97,65},{2,98}... | collective-permute-start | bytes 589832 | tf_op jit(solution)/shard_map/ppermute | solution.py:15
  31.6 17.5 %copy-start.2 = (bf16[768,384]{1,0:T(8,128)(2,1)S(1)}, bf16[768,384]{1,0:T(8,128)(2,1)}, u32[]{:S(2)}) copy-start(bf16[768,384]{1,0:T(8,128)(2,1)} %get-tuple-element.44) | copy-start | bytes 1769476
  31.6 17.5 %copy-start.3 = (bf16[768,384]{1,0:T(8,128)(2,1)S(1)}, bf16[768,384]{1,0:T(8,128)(2,1)}, u32[]{:S(2)}) copy-start(bf16[768,384]{1,0:T(8,128)(2,1)} %get-tuple-element.46) | copy-start | bytes 1769476
  35.2 10.6 %collective-permute-start.13 = (bf16[128,1536]{1,0:T(8,128)(2,1)S(1)}, bf16[128,1536]{1,0:T(8,128)(2,1)S(1)}, u32[]{:S(2)}, u32[]{:S(2)}) collective-permute-start(bf16[128,1536]{1,0:T(8,128)(2,1)S(1)} %collective-permute-done.12), channel_id=1, source_target_pairs={{0,2},{2,4},{4,6},{6,8},{8,10},{10,12},{12,14},{14,0},{1,3},{3,5},... | collective-permute-start | bytes 1179656 | tf_op jit(solution)/shard_map/ppermute | solution.py:15
  35.2 10.6 %collective-permute-start.17 = (bf16[128,1536]{1,0:T(8,128)(2,1)S(1)}, bf16[128,1536]{1,0:T(8,128)(2,1)S(1)}, u32[]{:S(2)}, u32[]{:S(2)}) collective-permute-start(bf16[128,1536]{1,0:T(8,128)(2,1)S(1)} %collective-permute-done.16), channel_id=1, source_target_pairs={{0,14},{2,0},{4,2},{6,4},{8,6},{10,8},{12,10},{14,12},{1,15},{3,1}... | collective-permute-start | bytes 1179656 | tf_op jit(solution)/shard_map/ppermute | solution.py:15
  38.5 22.1 %collective-permute-start.9 = (bf16[16,12288]{1,0:T(8,128)(2,1)S(1)}, bf16[16,12288]{1,0:T(8,128)(2,1)S(1)}, u32[]{:S(2)}, u32[]{:S(2)}) collective-permute-start(bf16[16,12288]{1,0:T(8,128)(2,1)S(1)} %copy-done.4), channel_id=1, source_target_pairs={{0,128},{128,0},{1,129},{129,1},{2,130},{130,2},{3,131},{131,3},{4... | collective-permute-start | bytes 1179656 | tf_op jit(solution)/shard_map/ppermute | solution.py:15
  39.2 9.9 %collective-permute-start.6 = (bf16[768,384]{1,0:T(8,128)(2,1)}, bf16[768,384]{1,0:T(8,128)(2,1)S(1)}, u32[]{:S(2)}, u32[]{:S(2)}) collective-permute-start(bf16[768,384]{1,0:T(8,128)(2,1)} %collective-permute-done.5), channel_id=1, source_target_pairs={{0,16},{16,0},{1,17},{17,1},{2,18},{18,2},{3,19},{19,3},{4,20},{20... | collective-permute-start | bytes 1769480 | tf_op jit(solution)/shard_map/ppermute | solution.py:15
  45.8 11.3 %collective-permute-start.14 = (bf16[128,1536]{1,0:T(8,128)(2,1)S(1)}, bf16[128,1536]{1,0:T(8,128)(2,1)S(1)}, u32[]{:S(2)}, u32[]{:S(2)}) collective-permute-start(bf16[128,1536]{1,0:T(8,128)(2,1)S(1)} %collective-permute-done.13), channel_id=1, source_target_pairs={{0,2},{2,4},{4,6},{6,8},{8,10},{10,12},{12,14},{14,0},{1,3},{3,5},... | collective-permute-start | bytes 1179656 | tf_op jit(solution)/shard_map/ppermute | solution.py:15
  45.8 11.4 %collective-permute-start.18 = (bf16[128,1536]{1,0:T(8,128)(2,1)S(1)}, bf16[128,1536]{1,0:T(8,128)(2,1)S(1)}, u32[]{:S(2)}, u32[]{:S(2)}) collective-permute-start(bf16[128,1536]{1,0:T(8,128)(2,1)S(1)} %collective-permute-done.17), channel_id=1, source_target_pairs={{0,14},{2,0},{4,2},{6,4},{8,6},{10,8},{12,10},{14,12},{1,15},{3,1}... | collective-permute-start | bytes 1179656 | tf_op jit(solution)/shard_map/ppermute | solution.py:15
  53.0 8.8 %collective-permute-start.7 = (bf16[128,768]{1,0:T(8,128)(2,1)S(1)}, bf16[128,768]{1,0:T(8,128)(2,1)S(1)}, u32[]{:S(2)}, u32[]{:S(2)}) collective-permute-start(bf16[128,768]{1,0:T(8,128)(2,1)S(1)} %get-tuple-element.65), channel_id=1, source_target_pairs={{0,2},{2,4},{4,6},{6,8},{8,10},{10,12},{12,14},{14,0},{1,3},{3,5},... | collective-permute-start | bytes 589832 | tf_op jit(solution)/shard_map/ppermute | solution.py:15
  53.1 8.7 %collective-permute-start.8 = (bf16[128,768]{1,0:T(8,128)(2,1)S(1)}, bf16[128,768]{1,0:T(8,128)(2,1)S(1)}, u32[]{:S(2)}, u32[]{:S(2)}) collective-permute-start(bf16[128,768]{1,0:T(8,128)(2,1)S(1)} %get-tuple-element.64), channel_id=1, source_target_pairs={{0,14},{2,0},{4,2},{6,4},{8,6},{10,8},{12,10},{14,12},{1,15},{3,1}... | collective-permute-start | bytes 589832 | tf_op jit(solution)/shard_map/ppermute | solution.py:15
  57.1 8.4 %collective-permute-start.15 = (bf16[64,1536]{1,0:T(8,128)(2,1)S(1)}, bf16[64,1536]{1,0:T(8,128)(2,1)S(1)}, u32[]{:S(2)}, u32[]{:S(2)}) collective-permute-start(bf16[64,1536]{1,0:T(8,128)(2,1)S(1)} %slice.102), channel_id=1, source_target_pairs={{0,2},{2,4},{4,6},{6,8},{8,10},{10,12},{12,14},{14,0},{1,3},{3,5},... | collective-permute-start | bytes 589832 | tf_op jit(solution)/shard_map/ppermute | solution.py:15
  57.3 8.6 %collective-permute-start.19 = (bf16[64,1536]{1,0:T(8,128)(2,1)S(1)}, bf16[64,1536]{1,0:T(8,128)(2,1)S(1)}, u32[]{:S(2)}, u32[]{:S(2)}) collective-permute-start(bf16[64,1536]{1,0:T(8,128)(2,1)S(1)} %slice.103), channel_id=1, source_target_pairs={{0,14},{2,0},{4,2},{6,4},{8,6},{10,8},{12,10},{14,12},{1,15},{3,1}... | collective-permute-start | bytes 589832 | tf_op jit(solution)/shard_map/ppermute | solution.py:15
  61.9 9.7 %collective-permute-start.11 = (bf16[128,1536]{1,0:T(8,128)(2,1)S(1)}, bf16[128,1536]{1,0:T(8,128)(2,1)S(1)}, u32[]{:S(2)}, u32[]{:S(2)}) collective-permute-start(bf16[128,1536]{1,0:T(8,128)(2,1)S(1)} %pad_maximum_fusion.4), channel_id=1, source_target_pairs={{0,14},{2,0},{4,2},{6,4},{8,6},{10,8},{12,10},{14,12},{1,15},{3,1}... | collective-permute-start | bytes 1179656 | tf_op jit(solution)/shard_map/ppermute | solution.py:15
  65.4 10.1 %collective-permute-start.10 = (bf16[128,1536]{1,0:T(8,128)(2,1)S(1)}, bf16[128,1536]{1,0:T(8,128)(2,1)S(1)}, u32[]{:S(2)}, u32[]{:S(2)}) collective-permute-start(bf16[128,1536]{1,0:T(8,128)(2,1)S(1)} %pad_maximum_fusion.3), channel_id=1, source_target_pairs={{0,2},{2,4},{4,6},{6,8},{8,10},{10,12},{12,14},{14,0},{1,3},{3,5},... | collective-permute-start | bytes 1179656 | tf_op jit(solution)/shard_map/ppermute | solution.py:15
  75.7 11.0 %collective-permute-start.20 = (bf16[128,1536]{1,0:T(8,128)(2,1)S(1)}, bf16[128,1536]{1,0:T(8,128)(2,1)S(1)}, u32[]{:S(2)}, u32[]{:S(2)}) collective-permute-start(bf16[128,1536]{1,0:T(8,128)(2,1)S(1)} %get-tuple-element.50), channel_id=1, source_target_pairs={{0,2},{2,4},{4,6},{6,8},{8,10},{10,12},{12,14},{14,0},{1,3},{3,5},... | collective-permute-start | bytes 1179656 | tf_op jit(solution)/shard_map/ppermute | solution.py:15
  75.8 10.9 %collective-permute-start.21 = (bf16[128,1536]{1,0:T(8,128)(2,1)S(1)}, bf16[128,1536]{1,0:T(8,128)(2,1)S(1)}, u32[]{:S(2)}, u32[]{:S(2)}) collective-permute-start(bf16[128,1536]{1,0:T(8,128)(2,1)S(1)} %get-tuple-element.49), channel_id=1, source_target_pairs={{0,14},{2,0},{4,2},{6,4},{8,6},{10,8},{12,10},{14,12},{1,15},{3,1}... | collective-permute-start | bytes 1179656 | tf_op jit(solution)/shard_map/ppermute | solution.py:15
  87.1 12.7 %collective-permute-start.22 = (bf16[128,1536]{1,0:T(8,128)(2,1)S(1)}, bf16[128,1536]{1,0:T(8,128)(2,1)S(1)}, u32[]{:S(2)}, u32[]{:S(2)}) collective-permute-start(bf16[128,1536]{1,0:T(8,128)(2,1)S(1)} %get-tuple-element.48), channel_id=1, source_target_pairs={{0,2},{2,4},{4,6},{6,8},{8,10},{10,12},{12,14},{14,0},{1,3},{3,5},... | collective-permute-start | bytes 1179656 | tf_op jit(solution)/shard_map/ppermute | solution.py:15
  87.4 12.3 %collective-permute-start.23 = (bf16[128,1536]{1,0:T(8,128)(2,1)S(1)}, bf16[128,1536]{1,0:T(8,128)(2,1)S(1)}, u32[]{:S(2)}, u32[]{:S(2)}) collective-permute-start(bf16[128,1536]{1,0:T(8,128)(2,1)S(1)} %get-tuple-element.47), channel_id=1, source_target_pairs={{0,14},{2,0},{4,2},{6,4},{8,6},{10,8},{12,10},{14,12},{1,15},{3,1}... | collective-permute-start | bytes 1179656 | tf_op jit(solution)/shard_map/ppermute | solution.py:15
  90.7 9.1 %collective-permute-start.24 = (bf16[256,384]{1,0:T(8,128)(2,1)S(1)}, bf16[256,384]{1,0:T(8,128)(2,1)S(1)}, u32[]{:S(2)}, u32[]{:S(2)}) collective-permute-start(bf16[256,384]{1,0:T(8,128)(2,1)S(1)} %get-tuple-element.61), channel_id=1, source_target_pairs={{0,32},{32,64},{64,96},{96,0},{1,33},{33,65},{65,97},{97,1},{2,34}... | collective-permute-start | bytes 589832 | tf_op jit(solution)/shard_map/ppermute | solution.py:15
  90.7 9.0 %collective-permute-start.25 = (bf16[256,384]{1,0:T(8,128)(2,1)S(1)}, bf16[256,384]{1,0:T(8,128)(2,1)S(1)}, u32[]{:S(2)}, u32[]{:S(2)}) collective-permute-start(bf16[256,384]{1,0:T(8,128)(2,1)S(1)} %get-tuple-element.60), channel_id=1, source_target_pairs={{0,96},{32,0},{64,32},{96,64},{1,97},{33,1},{65,33},{97,65},{2,98}... | collective-permute-start | bytes 589832 | tf_op jit(solution)/shard_map/ppermute | solution.py:15
  99.8 13.3 %collective-permute-start.26 = (bf16[256,768]{1,0:T(8,128)(2,1)S(1)}, bf16[256,768]{1,0:T(8,128)(2,1)S(1)}, u32[]{:S(2)}, u32[]{:S(2)}) collective-permute-start(bf16[256,768]{1,0:T(8,128)(2,1)S(1)} %pad_maximum_fusion.5), channel_id=1, source_target_pairs={{0,32},{32,64},{64,96},{96,0},{1,33},{33,65},{65,97},{97,1},{2,34}... | collective-permute-start | bytes 1179656 | tf_op jit(solution)/shard_map/ppermute | solution.py:15
  100.0 13.1 %collective-permute-start.27 = (bf16[256,768]{1,0:T(8,128)(2,1)S(1)}, bf16[256,768]{1,0:T(8,128)(2,1)S(1)}, u32[]{:S(2)}, u32[]{:S(2)}) collective-permute-start(bf16[256,768]{1,0:T(8,128)(2,1)S(1)} %pad_maximum_fusion.6), channel_id=1, source_target_pairs={{0,96},{32,0},{64,32},{96,64},{1,97},{33,1},{65,33},{97,65},{2,98}... | collective-permute-start | bytes 1179656 | tf_op jit(solution)/shard_map/ppermute | solution.py:15
  104.4 16.9 %all-to-all-start.1 = ((bf16[16,16,1536]{2,1,0:T(8,128)(2,1)}), bf16[16,16,1536]{2,1,0:T(8,128)(2,1)S(1)}, u32[]{:S(2)}, u32[]{:S(2)}) async-start(bf16[16,16,1536]{2,1,0:T(8,128)(2,1)} %bitcast.35), calls=%async_computation.1 | async-start | bytes 1572864 | tf_op jit(solution)/shard_map/all_to_all | solution.py:140
  113.3 7.3 %collective-permute-start.28 = (bf16[256,384]{1,0:T(8,128)(2,1)S(1)}, bf16[256,384]{1,0:T(8,128)(2,1)S(1)}, u32[]{:S(2)}, u32[]{:S(2)}) collective-permute-start(bf16[256,384]{1,0:T(8,128)(2,1)S(1)} %slice.129), channel_id=1, source_target_pairs={{0,1},{1,0},{2,3},{3,2},{4,5},{5,4},{6,7},{7,6},{8,9},{9,8},{10,11... | collective-permute-start | bytes 589832 | tf_op jit(solution)/shard_map/ppermute | solution.py:15
  116.6 8.5 %collective-permute-start.29 = (bf16[768,768]{1,0:T(8,128)(2,1)}, bf16[768,768]{1,0:T(8,128)(2,1)}, u32[]{:S(2)}, u32[]{:S(2)}) collective-permute-start(bf16[768,768]{1,0:T(8,128)(2,1)} %slice.91), channel_id=1, source_target_pairs={{0,16},{16,0},{1,17},{17,1},{2,18},{18,2},{3,19},{19,3},{4,20},{20... | collective-permute-start | bytes 3538952 | tf_op jit(solution)/shard_map/ppermute | solution.py:15
  127.1 13.4 %collective-permute-start.30 = (bf16[768,384]{1,0:T(8,128)(2,1)S(1)}, bf16[768,384]{1,0:T(8,128)(2,1)S(1)}, u32[]{:S(2)}, u32[]{:S(2)}) collective-permute-start(bf16[768,384]{1,0:T(8,128)(2,1)S(1)} %slice.114), channel_id=1, source_target_pairs={{0,1},{1,0},{2,3},{3,2},{4,5},{5,4},{6,7},{7,6},{8,9},{9,8},{10,11... | collective-permute-start | bytes 1769480 | tf_op jit(solution)/shard_map/ppermute | solution.py:15

commit v6 on v5

--- a/solution.py
+++ b/solution.py
@@ -1,8 +1,11 @@
+import functools
 import math
 
 import jax
 import jax.numpy as jnp
 from jax import lax
+from jax.experimental import pallas as pl
+from jax.experimental.pallas import tpu as pltpu
 from jax.sharding import Mesh
 from jax.sharding import PartitionSpec as P
 
@@ -67,6 +70,62 @@
         right, left = add(chunk(away), right), add(chunk(-away), left)
     right, left = yield both_ways(right, left, axis)
     yield chunk(0).astype(F32) + right.astype(F32) + left.astype(F32)
+
+
+def by_group(n_y, n_core, n_xh, piece):
+    for y in range(n_y):
+        for xh in range(n_xh):
+            for core in range(n_core):
+                yield y * n_xh + xh, core, ((y * n_core + core) * n_xh + xh) * piece
+
+
+def spread_kernel(sizes, at_ref, rows_ref, out_ref):
+    piece = sizes[-1]
+    core = at_ref[1]
+    pieces = {(group, at): rows_ref[:, first : first + piece] for group, at, first in by_group(*sizes)}
+    for group, at in pieces:
+        chosen = jnp.where(core == 0, pieces[group, at], pieces[group, 1 - at])
+        out_ref[group, :, at * piece : (at + 1) * piece] = chosen
+
+
+def finish_kernel(sizes, at_ref, branch_ref, residual_ref, early_ref, forward_ref, received_ref):
+    piece = sizes[-1]
+    section, core = at_ref[0], at_ref[1]
+    for group, at, first in by_group(*sizes):
+        here = slice(first, first + piece)
+
+        def term(of_section):
+            mine, other = branch_ref[of_section, group, :, :piece], branch_ref[of_section, group, :, piece:]
+            return jnp.where(core == at, mine, other).astype(F32)
+
+        one, two = term(0), term(1)
+        forward_ref[:, here] = (residual_ref[:, here].astype(F32) + jnp.where(section == 0, one, two)).astype(BF16)
+        early = early_ref[:, here]
+        received_ref[:, here] = jnp.where(section == 0, early, (early.astype(F32) + one).astype(BF16))
+
+
+def send_kernel(at_ref, context_ref, weights_ref, out_ref, done):
+    count, height = context_ref.shape[0], out_ref.shape[0] - context_ref.shape[0]
+    row = pl.multiple_of(at_ref[2] * height, height)
+    copies = [
+        pltpu.make_async_copy(context_ref, out_ref.at[:count], done.at[0]),
+        pltpu.make_async_copy(weights_ref.at[pl.ds(row, height)], out_ref.at[count:], done.at[1]),
+    ]
+    for copy in copies:
+        copy.start()
+    for copy in copies:
+        copy.wait()
+
+
+def local(kernel, at, arrays, shapes):
+    whole = pl.BlockSpec(memory_space=pltpu.VMEM)
+    return pl.pallas_call(
+        kernel,
+        out_shape=[jax.ShapeDtypeStruct(shape, BF16) for shape in shapes],
+        in_specs=[pl.BlockSpec(memory_space=pltpu.SMEM)] + [whole] * len(arrays),
+        out_specs=[whole] * len(shapes),
+        compiler_params=pltpu.CompilerParams(vmem_limit_bytes=24 * 2**20),
+    )(at, *arrays)
 
 
 def shards(segment_input, context, out_proj, grad_output):
@@ -84,33 +143,43 @@
     tokens = group_tokens * n_y
     z_tokens = own_count * n_xh
     block_tokens = own_count * group
-
-    both = jnp.concatenate([contexts, swap(contexts, "xh")], 1)
+    sizes = (n_y, n_core, n_xh, piece)
+    block_at = (y * n_core + core) * n_xh
+    at = jnp.stack([section, core, block_at + 1 - xh]).astype(jnp.int32)
+
     def rows(core_at, xh_at):
         return lax.dynamic_slice_in_dim(weights, ((y * n_core + core_at) * n_xh + xh_at) * piece, piece, 0)
 
-    both, partner_rows = tie(both, rows(core, 1 - xh))
-    came_rows = swap(partner_rows, "xh")
+    anywhere = pl.BlockSpec(memory_space=pl.ANY)
+    sent = pl.pallas_call(
+        send_kernel,
+        out_shape=jax.ShapeDtypeStruct((group_tokens + piece, width), BF16),
+        in_specs=[pl.BlockSpec(memory_space=pltpu.SMEM), anywhere, anywhere],
+        out_specs=anywhere,
+        scratch_shapes=[pltpu.SemaphoreType.DMA((2,))],
+    )(at, contexts, weights)
+    came = swap(sent, "xh")
+
+    (spread,) = local(functools.partial(spread_kernel, sizes), at, [upstream], [(group, own_count, features)])
+    spread = lax.all_to_all(spread, ("y", "xh"), 0, 0, tiled=True).reshape(block_tokens, features)
+    spread, came = tie(spread, came)
+    both = jnp.concatenate([contexts, came[:group_tokens]], 1)
+    came_rows = came[group_tokens:]
+
     other_rows = swap(came_rows, "core")
-    outgoing, came_rows = tie(jnp.where(section == 0, residual, upstream), came_rows)
-    early = swap(outgoing, "section")
     block = jnp.concatenate(
         [jnp.concatenate([rows(core, xh), came_rows], 1), jnp.concatenate([rows(1 - core, xh), other_rows], 1)], 0
     )
 
-    ctx_all = jnp.zeros((n_z, n_y, z_tokens, 2 * width), BF16)
     ctx_blocks, across = ring_gather(both, "y")
     ctx_blocks[n_y // 2] = jnp.concatenate(across, 0)
+    ctx_all = jnp.zeros((n_z, n_y, z_tokens, 2 * width), BF16)
     for away, part in ctx_blocks.items():
         ctx_all = place(ctx_all, part.reshape(n_z, 1, z_tokens, 2 * width), (0, wrap(y + away, n_y), 0, 0))
     ctx_flat = ctx_all.reshape(tokens, 2 * width)
 
-    spread = upstream.reshape(own_count, n_y, n_core, n_xh, piece)
-    spread = jnp.stack([pick(spread, core, 2), pick(spread, 1 - core, 2)], 3)
-    spread = spread.transpose(1, 2, 0, 3, 4).reshape(group, own_count, features)
-    spread = lax.all_to_all(spread, ("y", "xh"), 0, 0, tiled=True).reshape(block_tokens, features)
+    grad_blocks, far_blocks = ring_gather(spread, "z")
     grad_all = jnp.zeros((n_z, block_tokens, features), BF16)
-    grad_blocks, far_blocks = ring_gather(spread, "z")
     for away, part in grad_blocks.items():
         grad_all = place(grad_all, part[None], (wrap(z + away, n_z), 0, 0))
 
@@ -118,36 +187,40 @@
         ctx_flat, block, (((1,), (1,)), ((), ())), preferred_element_type=F32
     ).astype(BF16).reshape(n_z, block_tokens, features)
     ring = ring_steps(lambda away: pick(partial_branch, wrap(z + away, n_z)), "z")
-    *step, early = tie(*next(ring), early)
+    *step, outgoing = tie(*next(ring), jnp.where(section == 0, residual, upstream))
+    early = swap(outgoing, "section")
     step = ring.send(step)
     *step, far_low, far_high = tie(*step, *far_blocks)
     step = ring.send(step)
     grad_all = place(grad_all, jnp.concatenate([far_low, far_high], 0)[None], (wrap(z + n_z // 2, n_z), 0, 0))
     grad_flat = grad_all.reshape(tokens, features)
-    partial_ctx = jnp.dot(grad_flat, block, preferred_element_type=F32).astype(BF16)
     norm_factor = 1.0 / math.sqrt(tokens * n_core)
     product = lax.dot_general(grad_flat, ctx_flat, (((0,), (0,)), ((), ())), preferred_element_type=F32)
     product = (norm_factor * product).astype(BF16)
-    *step, partial_ctx, product = tie(*step, partial_ctx, product)
+    partial_ctx = jnp.dot(grad_flat, block, preferred_element_type=F32).astype(BF16)
+    *step, partial_ctx, product, early = tie(*step, partial_ctx, product, early)
+    other_product = swap(product[piece:], "core")
     step = ring.send(step)
     partial_ctx = partial_ctx.reshape(n_z, n_y, z_tokens, 2 * width)
     ctx_ring = ring_steps(lambda away: pick(partial_ctx, wrap(y + away, n_y), 1).reshape(group_tokens, 2 * width), "y")
     ctx_step = next(ctx_ring)
-    *step, ctx_low, ctx_high, product = tie(*step, *ctx_step, product)
+    ctx_low, ctx_high, other_product = tie(*ctx_step, other_product)
     branch = ring.send(step).astype(BF16)
     branch = branch.reshape(1, group, own_count, features)
     branch = jnp.concatenate([branch, branch], 0).reshape(2 * group, own_count, features)
     branch = lax.all_to_all(branch, ("section", "y", "xh"), 0, 0, tiled=True)
-    branch = branch.reshape(2, n_y, n_xh, own_count, n_core, piece)
-    branch = jnp.where(core == 0, branch, jnp.flip(branch, 4))
-    branch = branch.transpose(0, 3, 1, 4, 2, 5).reshape(2, own_count, model)
-    forward = add(residual, pick(branch, section))
-    received = jnp.where(section == 0, early, add(early, branch[0]))
 
     summed = ctx_ring.send(ctx_ring.send((ctx_low, ctx_high)))
+    branch, summed = tie(branch, summed)
     ctx_grad = add(summed[:, :width], swap(summed[:, width:].astype(BF16), "xh"))
-
-    own_rows = add(product[:piece], swap(product[piece:], "core"))
+    forward, received = local(
+        functools.partial(finish_kernel, sizes),
+        at,
+        [branch.reshape(2, group, own_count, features), residual, early],
+        [residual.shape, residual.shape],
+    )
+
+    own_rows = add(product[:piece], other_product)
     kept = own_rows[:, :width]
     came = swap(own_rows[:, width:], "xh")
     first = xh == 0

time: 143 us -> 189 us (1.32)
  Pallas kernels: 0 us -> 28.7 us
  waiting for transfers between devices: 47.1 us -> 60.7 us
  other arithmetic: 8.71 us -> 13.5 us
  local copies, waits for them, and re-layouts: 12.1 us -> 8.33 us
  matrix products: 11.4 us -> 14.6 us
    pallas_call x0 -> x3, Pallas kernels: none -> 28.7 us  [the longest x1 25.7 us: shards(): pl.pallas_call(send_kernel, out_shape=jax.ShapeDtypeStruct((group_tokens...]
    all_to_all x1, waiting for transfers between devices: 0.01 us -> 17.4 us  [shards(): lax.all_to_all(spread, ('y', 'xh'), 0, 0, tiled=True)]
    dot_general x1, matrix products: 3.71 us -> 9.09 us  [shards(): lax.dot_general(ctx_flat, block, (((1,), (1,)), ((), ())), preferred_elem...]
    ppermute x31 -> x30, waiting for transfers between devices: 47.1 us -> 43.3 us  [shift(): return lax.ppermute(value, axis, [(i, (i + by) % n) for i in range(n)])]
    convert_element_type x9 -> x7, other arithmetic: 3.45 us -> 4.4 us  [add(): return (a.astype(F32) + b.astype(F32)).astype(BF16)]
    ppermute x31 -> x30, starting transfers between devices: 51.2 us -> 50.4 us  [shift(): return lax.ppermute(value, axis, [(i, (i + by) % n) for i in range(n)])]
  transfers between devices with their start and end apart: 33 -> 32, of which waited for: 11 -> 12; matrix products, arithmetic and copies ran while one was open for 20% -> 18% of each run, Pallas kernels for 0% -> 2%
where the time goes in v6:
time: 189 us; the launch traced here: 188 us
  starting transfers between devices  61.2 us (32%)
  waiting for transfers between devices  60.7 us (32%)
  Pallas kernels  28.7 us (15%)
  matrix products  14.6 us (8%)
  other arithmetic  13.5 us (7%)
  local copies, waits for them, and re-layouts  8.33 us (4%)
    ppermute x30, starting transfers between devices, shift(): return lax.ppermute(value, axis, [(i, (i + by) % n) for i in range(n)])  50.4 us
    ppermute x30, waiting for transfers between devices, shift(): return lax.ppermute(value, axis, [(i, (i + by) % n) for i in range(n)])  43.3 us
    pallas_call x1, Pallas kernels, shards(): pl.pallas_call(send_kernel, out_shape=jax.ShapeDtypeStruct((group_tokens...  25.7 us
    all_to_all x1, waiting for transfers between devices, shards(): lax.all_to_all(spread, ('y', 'xh'), 0, 0, tiled=True)  17.4 us
    dot_general x1, matrix products, shards(): lax.dot_general(ctx_flat, block, (((1,), (1,)), ((), ())), preferred_elem...  9.09 us
    all_to_all x1, starting transfers between devices, shards(): branch = lax.all_to_all(branch, ('section', 'y', 'xh'), 0, 0, tiled=True)  5.52 us
    all_to_all x1, starting transfers between devices, shards(): lax.all_to_all(spread, ('y', 'xh'), 0, 0, tiled=True)  5.31 us
    convert_element_type x7, other arithmetic, add(): return (a.astype(F32) + b.astype(F32)).astype(BF16)  4.4 us
  transfers between devices with their start and end apart: 32, of which 12 were waited for; matrix products, arithmetic and copies ran while one was open for 18% of the time, Pallas kernels for 2%

profile of v6, /device:TPU:2, one launch (start us, length us, event | category | flops | bytes accessed | tf_op | source)
XLA Modules:
  0.0 188.3 jit_solution(1632594394005601694)
XLA Ops:
  0.6 0.7 pad_add_fusion.at_ref
  1.3 25.7 %shard_map.76 = bf16[1024,384]{1,0:T(8,128)(2,1)} custom-call(s32[3]{0:T(128)} %pad_add_fusion.at_ref, bf16[256,384]{1,0:T(8,128)(2,1)} %bitcast.100, bf16[12288,384]{1,0:T(8,128)(2,1)} %bitcast.92), custom_call_target="tpu_custom_call" | custom-call | tf_op jit(solution)/shard_map/pallas_call | solution.py:154
  27.1 2.2 %collective-permute-start = (bf16[1024,384]{1,0:T(8,128)(2,1)}, bf16[1024,384]{1,0:T(8,128)(2,1)S(1)}, u32[]{:S(2)}, u32[]{:S(2)}) collective-permute-start(bf16[1024,384]{1,0:T(8,128)(2,1)} %shard_map.76), channel_id=1, source_target_pairs={{0,1},{1,0},{2,3},{3,2},{4,5},{5,4},{6,7},{7,6},{8,9},{9,8},{10,11... | collective-permute-start | bytes 2359304 | tf_op jit(solution)/shard_map/ppermute | solution.py:18
  29.3 1.3 shard_map.75
  30.6 5.3 %all-to-all-start = ((bf16[8,16,1536]{2,1,0:T(8,128)(2,1)}), bf16[8,16,1536]{2,1,0:T(8,128)(2,1)S(1)}, u32[]{:S(2)}, u32[]{:S(2)}) async-start(bf16[8,16,1536]{2,1,0:T(8,128)(2,1)} %shard_map.75), calls=%async_computation | async-start | bytes 786432 | tf_op jit(solution)/shard_map/all_to_all | solution.py:164
  36.0 1.4 dynamic-slice_bitcast_fusion.1
  37.4 17.4 %all-to-all-done = bf16[8,16,1536]{2,1,0:T(8,128)(2,1)S(1)} async-done(((bf16[8,16,1536]{2,1,0:T(8,128)(2,1)}), bf16[8,16,1536]{2,1,0:T(8,128)(2,1)S(1)}, u32[]{:S(2)}, u32[]{:S(2)}) %all-to-all-start) | async-done | bytes 393248 | tf_op jit(solution)/shard_map/all_to_all | solution.py:164
  54.8 1.9 %collective-permute-start.10 = (bf16[128,1536]{1,0:T(8,128)(2,1)S(1)}, bf16[128,1536]{1,0:T(8,128)(2,1)S(1)}, u32[]{:S(2)}, u32[]{:S(2)}) collective-permute-start(bf16[128,1536]{1,0:T(8,128)(2,1)S(1)} %bitcast.105), channel_id=1, source_target_pairs={{0,2},{2,4},{4,6},{6,8},{8,10},{10,12},{12,14},{14,0},{1,3},{3,5},... | collective-permute-start | bytes 1179656 | tf_op jit(solution)/shard_map/ppermute | solution.py:18
  56.7 3.9 %collective-permute-start.14 = (bf16[128,1536]{1,0:T(8,128)(2,1)S(1)}, bf16[128,1536]{1,0:T(8,128)(2,1)S(1)}, u32[]{:S(2)}, u32[]{:S(2)}) collective-permute-start(bf16[128,1536]{1,0:T(8,128)(2,1)S(1)} %bitcast.106), channel_id=1, source_target_pairs={{0,14},{2,0},{4,2},{6,4},{8,6},{10,8},{12,10},{14,12},{1,15},{3,1}... | collective-permute-start | bytes 1179656 | tf_op jit(solution)/shard_map/ppermute | solution.py:18
  60.8 3.2 %collective-permute-start.2 = (bf16[256,768]{1,0:T(8,128)(2,1)S(1)}, bf16[256,768]{1,0:T(8,128)(2,1)S(1)}, u32[]{:S(2)}, u32[]{:S(2)}) collective-permute-start(bf16[256,768]{1,0:T(8,128)(2,1)S(1)} %pad_maximum_fusion.1), channel_id=1, source_target_pairs={{0,96},{32,0},{64,32},{96,64},{1,97},{33,1},{65,33},{97,65},{2,98}... | collective-permute-start | bytes 1179656 | tf_op jit(solution)/shard_map/ppermute | solution.py:18
  64.2 0.2 broadcast_in_dim.42
  64.5 0.3 broadcast_in_dim.43
  64.8 7.0 %collective-permute-done.1 = bf16[256,768]{1,0:T(8,128)(2,1)S(1)} collective-permute-done((bf16[256,768]{1,0:T(8,128)(2,1)S(1)}, bf16[256,768]{1,0:T(8,128)(2,1)S(1)}, u32[]{:S(2)}, u32[]{:S(2)}) %collective-permute-start.1) | collective-permute-done | bytes 393248 | tf_op jit(solution)/shard_map/ppermute | solution.py:18
  71.9 3.3 %collective-permute-start.4 = (bf16[128,768]{1,0:T(8,128)(2,1)S(1)}, bf16[128,768]{1,0:T(8,128)(2,1)S(1)}, u32[]{:S(2)}, u32[]{:S(2)}) collective-permute-start(bf16[128,768]{1,0:T(8,128)(2,1)S(1)} %slice.98), channel_id=1, source_target_pairs={{0,96},{32,0},{64,32},{96,64},{1,97},{33,1},{65,33},{97,65},{2,98}... | collective-permute-start | bytes 589832 | tf_op jit(solution)/shard_map/ppermute | solution.py:18
  75.2 3.2 %collective-permute-start.15 = (bf16[128,1536]{1,0:T(8,128)(2,1)S(1)}, bf16[128,1536]{1,0:T(8,128)(2,1)S(1)}, u32[]{:S(2)}, u32[]{:S(2)}) collective-permute-start(bf16[128,1536]{1,0:T(8,128)(2,1)S(1)} %collective-permute-done.14), channel_id=1, source_target_pairs={{0,14},{2,0},{4,2},{6,4},{8,6},{10,8},{12,10},{14,12},{1,15},{3,1}... | collective-permute-start | bytes 1179656 | tf_op jit(solution)/shard_map/ppermute | solution.py:18
  78.5 0.2 collective-permute-done.3
  78.8 9.1 %convolution_convert_fusion = bf16[1024,1536]{1,0:T(8,128)(2,1)S(1)} fusion(bf16[1024,768]{1,0:T(8,128)(2,1)S(1)} %bitcast.103, bf16[768,384]{1,0:T(8,128)(2,1)S(1)} %collective-permute-done.5, bf16[768,384]{1,0:T(8,128)(2,1)S(1)} %get-tuple-element.47, bf16[768,384]{1,0:T(8,128)(2,1)S(1)} %slice.76, bf16[768,384]{1,0:T(8,128)(2,1)S(1)} %get-tuple-element.46), kind=kOutput, calls=%fused_computation.1 | convolution fusion | flops 2426929152 | bytes 7077888 | tf_op jit(solution)/shard_map/dot_general | solution.py:186
  88.1 3.2 %collective-permute-start.7 = (bf16[128,768]{1,0:T(8,128)(2,1)S(1)}, bf16[128,768]{1,0:T(8,128)(2,1)S(1)}, u32[]{:S(2)}, u32[]{:S(2)}) collective-permute-start(bf16[128,768]{1,0:T(8,128)(2,1)S(1)} %get-tuple-element.63), channel_id=1, source_target_pairs={{0,14},{2,0},{4,2},{6,4},{8,6},{10,8},{12,10},{14,12},{1,15},{3,1}... | collective-permute-start | bytes 589832 | tf_op jit(solution)/shard_map/ppermute | solution.py:18
  91.4 3.6 %collective-permute-done.6 = bf16[128,768]{1,0:T(8,128)(2,1)S(1)} collective-permute-done((bf16[128,768]{1,0:T(8,128)(2,1)S(1)}, bf16[128,768]{1,0:T(8,128)(2,1)S(1)}, u32[]{:S(2)}, u32[]{:S(2)}) %collective-permute-start.6) | collective-permute-done | bytes 196640 | tf_op jit(solution)/shard_map/ppermute | solution.py:18
  95.0 0.3 collective-permute-done.7
  95.4 3.8 %collective-permute-start.9 = (bf16[128,1536]{1,0:T(8,128)(2,1)S(1)}, bf16[128,1536]{1,0:T(8,128)(2,1)S(1)}, u32[]{:S(2)}, u32[]{:S(2)}) collective-permute-start(bf16[128,1536]{1,0:T(8,128)(2,1)S(1)} %pad_maximum_fusion.4), channel_id=1, source_target_pairs={{0,14},{2,0},{4,2},{6,4},{8,6},{10,8},{12,10},{14,12},{1,15},{3,1}... | collective-permute-start | bytes 1179656 | tf_op jit(solution)/shard_map/ppermute | solution.py:18
  99.4 0.6 collective-permute-start.20
  100.0 3.2 %collective-permute-start.16 = (bf16[128,1536]{1,0:T(8,128)(2,1)S(1)}, bf16[128,1536]{1,0:T(8,128)(2,1)S(1)}, u32[]{:S(2)}, u32[]{:S(2)}) collective-permute-start(bf16[128,1536]{1,0:T(8,128)(2,1)S(1)} %collective-permute-done.15), channel_id=1, source_target_pairs={{0,14},{2,0},{4,2},{6,4},{8,6},{10,8},{12,10},{14,12},{1,15},{3,1}... | collective-permute-start | bytes 1179656 | tf_op jit(solution)/shard_map/ppermute | solution.py:18
  103.3 12.9 %collective-permute-done.12 = bf16[128,1536]{1,0:T(8,128)(2,1)S(1)} collective-permute-done((bf16[128,1536]{1,0:T(8,128)(2,1)S(1)}, bf16[128,1536]{1,0:T(8,128)(2,1)S(1)}, u32[]{:S(2)}, u32[]{:S(2)}) %collective-permute-start.12) | collective-permute-done | bytes 393248 | tf_op jit(solution)/shard_map/ppermute | solution.py:18
  116.4 3.3 %collective-permute-start.17 = (bf16[64,1536]{1,0:T(8,128)(2,1)S(1)}, bf16[64,1536]{1,0:T(8,128)(2,1)S(1)}, u32[]{:S(2)}, u32[]{:S(2)}) collective-permute-start(bf16[64,1536]{1,0:T(8,128)(2,1)S(1)} %slice.106), channel_id=1, source_target_pairs={{0,14},{2,0},{4,2},{6,4},{8,6},{10,8},{12,10},{14,12},{1,15},{3,1}... | collective-permute-start | bytes 589832 | tf_op jit(solution)/shard_map/ppermute | solution.py:18
  119.8 5.6 %collective-permute-done.13 = bf16[64,1536]{1,0:T(8,128)(2,1)S(1)} collective-permute-done((bf16[64,1536]{1,0:T(8,128)(2,1)S(1)}, bf16[64,1536]{1,0:T(8,128)(2,1)S(1)}, u32[]{:S(2)}, u32[]{:S(2)}) %collective-permute-start.13) | collective-permute-done | bytes 196640 | tf_op jit(solution)/shard_map/ppermute | solution.py:18
  125.4 0.2 fusion.2
  125.6 0.3 collective-permute-start.18
  125.9 3.4 %collective-permute-start.19 = (bf16[128,1536]{1,0:T(8,128)(2,1)S(1)}, bf16[128,1536]{1,0:T(8,128)(2,1)S(1)}, u32[]{:S(2)}, u32[]{:S(2)}) collective-permute-start(bf16[128,1536]{1,0:T(8,128)(2,1)S(1)} %get-tuple-element.50), channel_id=1, source_target_pairs={{0,14},{2,0},{4,2},{6,4},{8,6},{10,8},{12,10},{14,12},{1,15},{3,1}... | collective-permute-start | bytes 1179656 | tf_op jit(solution)/shard_map/ppermute | solution.py:18
  129.3 2.6 %convolution_convert_fusion.1 = bf16[1024,768]{1,0:T(8,128)(2,1)S(1)} fusion(bf16[1024,1536]{1,0:T(8,128)(2,1)S(1)} %bitcast.93, bf16[768,384]{1,0:T(8,128)(2,1)S(1)} %collective-permute-done.5, bf16[768,384]{1,0:T(8,128)(2,1)S(1)} %get-tuple-element.47, bf16[768,384]{1,0:T(8,128)(2,1)S(1)} %slice.76, bf16[768,384]{1,0:T(8,128)(2,1)S(1)} %get-tuple-element.46), kind=kOutput, calls=%fused_computation.4 | convolution fusion | flops 2426142720 | bytes 7077888 | tf_op jit(solution)/shard_map/dot_general | solution.py:200
  132.0 2.9 %multiply_convert_fusion = bf16[1536,768]{1,0:T(8,128)(2,1)S(1)} fusion(bf16[1024,1536]{1,0:T(8,128)(2,1)S(1)} %bitcast.94, bf16[1024,768]{1,0:T(8,128)(2,1)S(1)} %bitcast.104), kind=kOutput, calls=%fused_computation | convolution fusion | flops 2418278400 | bytes 7077888 | tf_op jit(solution)/shard_map/dot_general | solution.py:198
  135.0 1.2 slice.88
  136.2 0.2 fusion.4
  136.4 2.3 %collective-permute-start.21 = (bf16[128,1536]{1,0:T(8,128)(2,1)S(1)}, bf16[128,1536]{1,0:T(8,128)(2,1)S(1)}, u32[]{:S(2)}, u32[]{:S(2)}) collective-permute-start(bf16[128,1536]{1,0:T(8,128)(2,1)S(1)} %get-tuple-element.48), channel_id=1, source_target_pairs={{0,2},{2,4},{4,6},{6,8},{8,10},{10,12},{12,14},{14,0},{1,3},{3,5},... | collective-permute-start | bytes 1179656 | tf_op jit(solution)/shard_map/ppermute | solution.py:18
  138.7 1.1 collective-permute-start.22
  139.8 0.9 constant_dynamic-slice_fusion.3
  140.6 0.8 fusion.11
  141.4 3.2 %collective-permute-start.24 = (bf16[256,384]{1,0:T(8,128)(2,1)}, bf16[256,384]{1,0:T(8,128)(2,1)}, u32[]{:S(2)}, u32[]{:S(2)}) collective-permute-start(bf16[256,384]{1,0:T(8,128)(2,1)} %get-tuple-element.61), channel_id=1, source_target_pairs={{0,96},{32,0},{64,32},{96,64},{1,97},{33,1},{65,33},{97,65},{2,98}... | collective-permute-start | bytes 589832 | tf_op jit(solution)/shard_map/ppermute | solution.py:18
  144.6 0.7 slice.110
  145.3 0.7 slice.111
  146.0 3.4 %collective-permute-done.21 = bf16[128,1536]{1,0:T(8,128)(2,1)S(1)} collective-permute-done((bf16[128,1536]{1,0:T(8,128)(2,1)S(1)}, bf16[128,1536]{1,0:T(8,128)(2,1)S(1)}, u32[]{:S(2)}, u32[]{:S(2)}) %collective-permute-start.21) | collective-permute-done | bytes 393248 | tf_op jit(solution)/shard_map/ppermute | solution.py:18
  149.5 0.7 collective-permute-done.22
  150.2 0.2 fusion.6
  150.4 0.9 pad_maximum_fusion
  151.3 5.5 %all-to-all-start.1 = ((bf16[16,16,1536]{2,1,0:T(8,128)(2,1)}), bf16[16,16,1536]{2,1,0:T(8,128)(2,1)S(1)}, u32[]{:S(2)}, u32[]{:S(2)}) async-start(bf16[16,16,1536]{2,1,0:T(8,128)(2,1)} %bitcast.39), calls=%async_computation.1 | async-start | bytes 1572864 | tf_op jit(solution)/shard_map/all_to_all | solution.py:211
  156.9 1.4 add_convert_fusion.3
  158.2 1.7 pad_maximum_fusion.5
  160.0 1.5 collective-permute-start.26
  161.4 1.0 add_convert_fusion.2
  162.4 1.0 pad_maximum_fusion.6
  163.4 1.9 collective-permute-start.27
  165.2 1.6 add_convert_fusion
  166.8 0.9 slice.115
  167.7 2.1 %collective-permute-start.29 = (bf16[768,384]{1,0:T(8,128)(2,1)}, bf16[768,384]{1,0:T(8,128)(2,1)}, u32[]{:S(2)}, u32[]{:S(2)}) collective-permute-start(bf16[768,384]{1,0:T(8,128)(2,1)} %slice.115), channel_id=1, source_target_pairs={{0,1},{1,0},{2,3},{3,2},{4,5},{5,4},{6,7},{7,6},{8,9},{9,8},{10,11... | collective-permute-start | bytes 1769480 | tf_op jit(solution)/shard_map/ppermute | solution.py:18
  169.7 7.0 %collective-permute-done.26 = bf16[256,768]{1,0:T(8,128)(2,1)} collective-permute-done((bf16[256,768]{1,0:T(8,128)(2,1)}, bf16[256,768]{1,0:T(8,128)(2,1)}, u32[]{:S(2)}, u32[]{:S(2)}) %collective-permute-start.26) | collective-permute-done | bytes 393248 | tf_op jit(solution)/shard_map/ppermute | solution.py:18
  176.8 0.7 copy-done.7
  177.5 1.4 fusion
  178.9 2.2 %collective-permute-start.28 = (bf16[256,384]{1,0:T(8,128)(2,1)S(1)}, bf16[256,384]{1,0:T(8,128)(2,1)S(1)}, u32[]{:S(2)}, u32[]{:S(2)}) collective-permute-start(bf16[256,384]{1,0:T(8,128)(2,1)S(1)} %slice.127), channel_id=1, source_target_pairs={{0,1},{1,0},{2,3},{3,2},{4,5},{5,4},{6,7},{7,6},{8,9},{9,8},{10,11... | collective-permute-start | bytes 589832 | tf_op jit(solution)/shard_map/ppermute | solution.py:18
  181.1 1.7 shard_map.77
  182.8 1.1 collective-permute-done.29
  183.9 1.2 broadcast_select_fusion.1
  185.1 1.1 maximum_bitcast_fusion
  186.2 1.3 collective-permute-done.28
  187.5 0.7 fusion.8
  (75 shorter events, 1.6 us)
Async XLA Ops:
  1.3 28.0 %copy-start = (bf16[1,16,12288]{2,1,0:T(8,128)(2,1)S(1)}, bf16[1,16,12288]{2,1,0:T(8,128)(2,1)}, u32[]{:S(2)}) copy-start(bf16[1,16,12288]{2,1,0:T(8,128)(2,1)} %param.7) | copy-start | bytes 1179652
  1.3 28.0 %copy-start.2 = (s32[3]{0:T(128)S(1)}, s32[3]{0:T(128)}, u32[]{:S(2)}) copy-start(s32[3]{0:T(128)} %pad_add_fusion.at_ref) | copy-start | bytes 40
  1.3 34.6 %copy-start.1 = (bf16[1,16,12288]{2,1,0:T(8,128)(2,1)S(1)}, bf16[1,16,12288]{2,1,0:T(8,128)(2,1)}, u32[]{:S(2)}) copy-start(bf16[1,16,12288]{2,1,0:T(8,128)(2,1)} %param.4) | copy-start | bytes 1179652
  27.0 33.6 %copy-start.5 = (bf16[1,256,384]{2,1,0:T(8,128)(2,1)S(1)}, bf16[1,256,384]{2,1,0:T(8,128)(2,1)}, u32[]{:S(2)}) copy-start(bf16[1,256,384]{2,1,0:T(8,128)(2,1)} %param.5) | copy-start | bytes 589828
  27.1 27.8 %collective-permute-start = (bf16[1024,384]{1,0:T(8,128)(2,1)}, bf16[1024,384]{1,0:T(8,128)(2,1)S(1)}, u32[]{:S(2)}, u32[]{:S(2)}) collective-permute-start(bf16[1024,384]{1,0:T(8,128)(2,1)} %shard_map.76), channel_id=1, source_target_pairs={{0,1},{1,0},{2,3},{3,2},{4,5},{5,4},{6,7},{7,6},{8,9},{9,8},{10,11... | collective-permute-start | bytes 2359304 | tf_op jit(solution)/shard_map/ppermute | solution.py:18
  30.6 24.2 %all-to-all-start = ((bf16[8,16,1536]{2,1,0:T(8,128)(2,1)}), bf16[8,16,1536]{2,1,0:T(8,128)(2,1)S(1)}, u32[]{:S(2)}, u32[]{:S(2)}) async-start(bf16[8,16,1536]{2,1,0:T(8,128)(2,1)} %shard_map.75), calls=%async_computation | async-start | bytes 786432 | tf_op jit(solution)/shard_map/all_to_all | solution.py:164
  54.8 20.4 %collective-permute-start.10 = (bf16[128,1536]{1,0:T(8,128)(2,1)S(1)}, bf16[128,1536]{1,0:T(8,128)(2,1)S(1)}, u32[]{:S(2)}, u32[]{:S(2)}) collective-permute-start(bf16[128,1536]{1,0:T(8,128)(2,1)S(1)} %bitcast.105), channel_id=1, source_target_pairs={{0,2},{2,4},{4,6},{6,8},{8,10},{10,12},{12,14},{14,0},{1,3},{3,5},... | collective-permute-start | bytes 1179656 | tf_op jit(solution)/shard_map/ppermute | solution.py:18
  56.7 18.4 %collective-permute-start.14 = (bf16[128,1536]{1,0:T(8,128)(2,1)S(1)}, bf16[128,1536]{1,0:T(8,128)(2,1)S(1)}, u32[]{:S(2)}, u32[]{:S(2)}) collective-permute-start(bf16[128,1536]{1,0:T(8,128)(2,1)S(1)} %bitcast.106), channel_id=1, source_target_pairs={{0,14},{2,0},{4,2},{6,4},{8,6},{10,8},{12,10},{14,12},{1,15},{3,1}... | collective-permute-start | bytes 1179656 | tf_op jit(solution)/shard_map/ppermute | solution.py:18
  60.7 11.0 %collective-permute-start.1 = (bf16[256,768]{1,0:T(8,128)(2,1)S(1)}, bf16[256,768]{1,0:T(8,128)(2,1)S(1)}, u32[]{:S(2)}, u32[]{:S(2)}) collective-permute-start(bf16[256,768]{1,0:T(8,128)(2,1)S(1)} %pad_maximum_fusion.1), channel_id=1, source_target_pairs={{0,32},{32,64},{64,96},{96,0},{1,33},{33,65},{65,97},{97,1},{2,34}... | collective-permute-start | bytes 1179656 | tf_op jit(solution)/shard_map/ppermute | solution.py:18
  60.8 11.0 %collective-permute-start.2 = (bf16[256,768]{1,0:T(8,128)(2,1)S(1)}, bf16[256,768]{1,0:T(8,128)(2,1)S(1)}, u32[]{:S(2)}, u32[]{:S(2)}) collective-permute-start(bf16[256,768]{1,0:T(8,128)(2,1)S(1)} %pad_maximum_fusion.1), channel_id=1, source_target_pairs={{0,96},{32,0},{64,32},{96,64},{1,97},{33,1},{65,33},{97,65},{2,98}... | collective-permute-start | bytes 1179656 | tf_op jit(solution)/shard_map/ppermute | solution.py:18
  64.1 14.7 %collective-permute-start.5 = (bf16[768,384]{1,0:T(8,128)(2,1)S(1)}, bf16[768,384]{1,0:T(8,128)(2,1)S(1)}, u32[]{:S(2)}, u32[]{:S(2)}) collective-permute-start(bf16[768,384]{1,0:T(8,128)(2,1)S(1)} %slice.76), channel_id=1, source_target_pairs={{0,16},{16,0},{1,17},{17,1},{2,18},{18,2},{3,19},{19,3},{4,20},{20... | collective-permute-start | bytes 1769480 | tf_op jit(solution)/shard_map/ppermute | solution.py:18
  71.8 7.0 %collective-permute-start.3 = (bf16[128,768]{1,0:T(8,128)(2,1)S(1)}, bf16[128,768]{1,0:T(8,128)(2,1)S(1)}, u32[]{:S(2)}, u32[]{:S(2)}) collective-permute-start(bf16[128,768]{1,0:T(8,128)(2,1)S(1)} %slice.97), channel_id=1, source_target_pairs={{0,32},{32,64},{64,96},{96,0},{1,33},{33,65},{65,97},{97,1},{2,34}... | collective-permute-start | bytes 589832 | tf_op jit(solution)/shard_map/ppermute | solution.py:18
  71.9 6.8 %collective-permute-start.4 = (bf16[128,768]{1,0:T(8,128)(2,1)S(1)}, bf16[128,768]{1,0:T(8,128)(2,1)S(1)}, u32[]{:S(2)}, u32[]{:S(2)}) collective-permute-start(bf16[128,768]{1,0:T(8,128)(2,1)S(1)} %slice.98), channel_id=1, source_target_pairs={{0,96},{32,0},{64,32},{96,64},{1,97},{33,1},{65,33},{97,65},{2,98}... | collective-permute-start | bytes 589832 | tf_op jit(solution)/shard_map/ppermute | solution.py:18
  75.2 24.8 %collective-permute-start.11 = (bf16[128,1536]{1,0:T(8,128)(2,1)S(1)}, bf16[128,1536]{1,0:T(8,128)(2,1)S(1)}, u32[]{:S(2)}, u32[]{:S(2)}) collective-permute-start(bf16[128,1536]{1,0:T(8,128)(2,1)S(1)} %collective-permute-done.10), channel_id=1, source_target_pairs={{0,2},{2,4},{4,6},{6,8},{8,10},{10,12},{12,14},{14,0},{1,3},{3,5},... | collective-permute-start | bytes 1179656 | tf_op jit(solution)/shard_map/ppermute | solution.py:18
  75.2 24.8 %collective-permute-start.15 = (bf16[128,1536]{1,0:T(8,128)(2,1)S(1)}, bf16[128,1536]{1,0:T(8,128)(2,1)S(1)}, u32[]{:S(2)}, u32[]{:S(2)}) collective-permute-start(bf16[128,1536]{1,0:T(8,128)(2,1)S(1)} %collective-permute-done.14), channel_id=1, source_target_pairs={{0,14},{2,0},{4,2},{6,4},{8,6},{10,8},{12,10},{14,12},{1,15},{3,1}... | collective-permute-start | bytes 1179656 | tf_op jit(solution)/shard_map/ppermute | solution.py:18
  88.0 7.0 %collective-permute-start.6 = (bf16[128,768]{1,0:T(8,128)(2,1)S(1)}, bf16[128,768]{1,0:T(8,128)(2,1)S(1)}, u32[]{:S(2)}, u32[]{:S(2)}) collective-permute-start(bf16[128,768]{1,0:T(8,128)(2,1)S(1)} %get-tuple-element.64), channel_id=1, source_target_pairs={{0,2},{2,4},{4,6},{6,8},{8,10},{10,12},{12,14},{14,0},{1,3},{3,5},... | collective-permute-start | bytes 589832 | tf_op jit(solution)/shard_map/ppermute | solution.py:18
  88.1 7.2 %collective-permute-start.7 = (bf16[128,768]{1,0:T(8,128)(2,1)S(1)}, bf16[128,768]{1,0:T(8,128)(2,1)S(1)}, u32[]{:S(2)}, u32[]{:S(2)}) collective-permute-start(bf16[128,768]{1,0:T(8,128)(2,1)S(1)} %get-tuple-element.63), channel_id=1, source_target_pairs={{0,14},{2,0},{4,2},{6,4},{8,6},{10,8},{12,10},{14,12},{1,15},{3,1}... | collective-permute-start | bytes 589832 | tf_op jit(solution)/shard_map/ppermute | solution.py:18
  95.4 24.3 %collective-permute-start.9 = (bf16[128,1536]{1,0:T(8,128)(2,1)S(1)}, bf16[128,1536]{1,0:T(8,128)(2,1)S(1)}, u32[]{:S(2)}, u32[]{:S(2)}) collective-permute-start(bf16[128,1536]{1,0:T(8,128)(2,1)S(1)} %pad_maximum_fusion.4), channel_id=1, source_target_pairs={{0,14},{2,0},{4,2},{6,4},{8,6},{10,8},{12,10},{14,12},{1,15},{3,1}... | collective-permute-start | bytes 1179656 | tf_op jit(solution)/shard_map/ppermute | solution.py:18
  99.3 20.5 %collective-permute-start.8 = (bf16[128,1536]{1,0:T(8,128)(2,1)S(1)}, bf16[128,1536]{1,0:T(8,128)(2,1)S(1)}, u32[]{:S(2)}, u32[]{:S(2)}) collective-permute-start(bf16[128,1536]{1,0:T(8,128)(2,1)S(1)} %pad_maximum_fusion.3), channel_id=1, source_target_pairs={{0,2},{2,4},{4,6},{6,8},{8,10},{10,12},{12,14},{14,0},{1,3},{3,5},... | collective-permute-start | bytes 1179656 | tf_op jit(solution)/shard_map/ppermute | solution.py:18
  99.4 35.5 %collective-permute-start.20 = (bf16[16,12288]{1,0:T(8,128)(2,1)S(1)}, bf16[16,12288]{1,0:T(8,128)(2,1)S(1)}, u32[]{:S(2)}, u32[]{:S(2)}) collective-permute-start(bf16[16,12288]{1,0:T(8,128)(2,1)S(1)} %broadcast_select_fusion.2), channel_id=1, source_target_pairs={{0,128},{128,0},{1,129},{129,1},{2,130},{130,2},{3,131},{131,3},{4... | collective-permute-start | bytes 1179656 | tf_op jit(solution)/shard_map/ppermute | solution.py:18
  100.0 16.2 %collective-permute-start.12 = (bf16[128,1536]{1,0:T(8,128)(2,1)S(1)}, bf16[128,1536]{1,0:T(8,128)(2,1)S(1)}, u32[]{:S(2)}, u32[]{:S(2)}) collective-permute-start(bf16[128,1536]{1,0:T(8,128)(2,1)S(1)} %collective-permute-done.11), channel_id=1, source_target_pairs={{0,2},{2,4},{4,6},{6,8},{8,10},{10,12},{12,14},{14,0},{1,3},{3,5},... | collective-permute-start | bytes 1179656 | tf_op jit(solution)/shard_map/ppermute | solution.py:18
  100.0 16.3 %collective-permute-start.16 = (bf16[128,1536]{1,0:T(8,128)(2,1)S(1)}, bf16[128,1536]{1,0:T(8,128)(2,1)S(1)}, u32[]{:S(2)}, u32[]{:S(2)}) collective-permute-start(bf16[128,1536]{1,0:T(8,128)(2,1)S(1)} %collective-permute-done.15), channel_id=1, source_target_pairs={{0,14},{2,0},{4,2},{6,4},{8,6},{10,8},{12,10},{14,12},{1,15},{3,1}... | collective-permute-start | bytes 1179656 | tf_op jit(solution)/shard_map/ppermute | solution.py:18
  116.3 9.1 %collective-permute-start.13 = (bf16[64,1536]{1,0:T(8,128)(2,1)S(1)}, bf16[64,1536]{1,0:T(8,128)(2,1)S(1)}, u32[]{:S(2)}, u32[]{:S(2)}) collective-permute-start(bf16[64,1536]{1,0:T(8,128)(2,1)S(1)} %slice.105), channel_id=1, source_target_pairs={{0,2},{2,4},{4,6},{6,8},{8,10},{10,12},{12,14},{14,0},{1,3},{3,5},... | collective-permute-start | bytes 589832 | tf_op jit(solution)/shard_map/ppermute | solution.py:18
  116.4 9.0 %collective-permute-start.17 = (bf16[64,1536]{1,0:T(8,128)(2,1)S(1)}, bf16[64,1536]{1,0:T(8,128)(2,1)S(1)}, u32[]{:S(2)}, u32[]{:S(2)}) collective-permute-start(bf16[64,1536]{1,0:T(8,128)(2,1)S(1)} %slice.106), channel_id=1, source_target_pairs={{0,14},{2,0},{4,2},{6,4},{8,6},{10,8},{12,10},{14,12},{1,15},{3,1}... | collective-permute-start | bytes 589832 | tf_op jit(solution)/shard_map/ppermute | solution.py:18
  125.6 9.4 %collective-permute-start.18 = (bf16[128,1536]{1,0:T(8,128)(2,1)S(1)}, bf16[128,1536]{1,0:T(8,128)(2,1)S(1)}, u32[]{:S(2)}, u32[]{:S(2)}) collective-permute-start(bf16[128,1536]{1,0:T(8,128)(2,1)S(1)} %get-tuple-element.51), channel_id=1, source_target_pairs={{0,2},{2,4},{4,6},{6,8},{8,10},{10,12},{12,14},{14,0},{1,3},{3,5},... | collective-permute-start | bytes 1179656 | tf_op jit(solution)/shard_map/ppermute | solution.py:18
  125.9 9.1 %collective-permute-start.19 = (bf16[128,1536]{1,0:T(8,128)(2,1)S(1)}, bf16[128,1536]{1,0:T(8,128)(2,1)S(1)}, u32[]{:S(2)}, u32[]{:S(2)}) collective-permute-start(bf16[128,1536]{1,0:T(8,128)(2,1)S(1)} %get-tuple-element.50), channel_id=1, source_target_pairs={{0,14},{2,0},{4,2},{6,4},{8,6},{10,8},{12,10},{14,12},{1,15},{3,1}... | collective-permute-start | bytes 1179656 | tf_op jit(solution)/shard_map/ppermute | solution.py:18
  134.9 5.7 %copy-start.3 = (bf16[1536,768]{1,0:T(8,128)(2,1)}, bf16[1536,768]{1,0:T(8,128)(2,1)S(1)}, u32[]{:S(2)}) copy-start(bf16[1536,768]{1,0:T(8,128)(2,1)S(1)} %multiply_convert_fusion) | copy-start | bytes 7077892
  136.2 20.6 %collective-permute-start.25 = (bf16[768,768]{1,0:T(8,128)(2,1)}, bf16[768,768]{1,0:T(8,128)(2,1)S(1)}, u32[]{:S(2)}, u32[]{:S(2)}) collective-permute-start(bf16[768,768]{1,0:T(8,128)(2,1)} %slice.88), channel_id=1, source_target_pairs={{0,16},{16,0},{1,17},{17,1},{2,18},{18,2},{3,19},{19,3},{4,20},{20... | collective-permute-start | bytes 3538952 | tf_op jit(solution)/shard_map/ppermute | solution.py:18
  136.4 13.1 %collective-permute-start.21 = (bf16[128,1536]{1,0:T(8,128)(2,1)S(1)}, bf16[128,1536]{1,0:T(8,128)(2,1)S(1)}, u32[]{:S(2)}, u32[]{:S(2)}) collective-permute-start(bf16[128,1536]{1,0:T(8,128)(2,1)S(1)} %get-tuple-element.48), channel_id=1, source_target_pairs={{0,2},{2,4},{4,6},{6,8},{8,10},{10,12},{12,14},{14,0},{1,3},{3,5},... | collective-permute-start | bytes 1179656 | tf_op jit(solution)/shard_map/ppermute | solution.py:18
  138.7 11.5 %collective-permute-start.22 = (bf16[128,1536]{1,0:T(8,128)(2,1)S(1)}, bf16[128,1536]{1,0:T(8,128)(2,1)S(1)}, u32[]{:S(2)}, u32[]{:S(2)}) collective-permute-start(bf16[128,1536]{1,0:T(8,128)(2,1)S(1)} %get-tuple-element.49), channel_id=1, source_target_pairs={{0,14},{2,0},{4,2},{6,4},{8,6},{10,8},{12,10},{14,12},{1,15},{3,1}... | collective-permute-start | bytes 1179656 | tf_op jit(solution)/shard_map/ppermute | solution.py:18
  141.4 15.4 %collective-permute-start.23 = (bf16[256,384]{1,0:T(8,128)(2,1)}, bf16[256,384]{1,0:T(8,128)(2,1)}, u32[]{:S(2)}, u32[]{:S(2)}) collective-permute-start(bf16[256,384]{1,0:T(8,128)(2,1)} %get-tuple-element.62), channel_id=1, source_target_pairs={{0,32},{32,64},{64,96},{96,0},{1,33},{33,65},{65,97},{97,1},{2,34}... | collective-permute-start | bytes 589832 | tf_op jit(solution)/shard_map/ppermute | solution.py:18
  141.4 15.4 %collective-permute-start.24 = (bf16[256,384]{1,0:T(8,128)(2,1)}, bf16[256,384]{1,0:T(8,128)(2,1)}, u32[]{:S(2)}, u32[]{:S(2)}) collective-permute-start(bf16[256,384]{1,0:T(8,128)(2,1)} %get-tuple-element.61), channel_id=1, source_target_pairs={{0,96},{32,0},{64,32},{96,64},{1,97},{33,1},{65,33},{97,65},{2,98}... | collective-permute-start | bytes 589832 | tf_op jit(solution)/shard_map/ppermute | solution.py:18
  151.3 27.6 %all-to-all-start.1 = ((bf16[16,16,1536]{2,1,0:T(8,128)(2,1)}), bf16[16,16,1536]{2,1,0:T(8,128)(2,1)S(1)}, u32[]{:S(2)}, u32[]{:S(2)}) async-start(bf16[16,16,1536]{2,1,0:T(8,128)(2,1)} %bitcast.39), calls=%async_computation.1 | async-start | bytes 1572864 | tf_op jit(solution)/shard_map/all_to_all | solution.py:211
  156.8 8.4 %copy-start.4 = (bf16[1536,768]{1,0:T(8,128)(2,1)S(1)}, bf16[1536,768]{1,0:T(8,128)(2,1)}, u32[]{:S(2)}) copy-start(bf16[1536,768]{1,0:T(8,128)(2,1)} %copy-done.3) | copy-start | bytes 7077892
  156.9 6.5 %copy-start.6 = (bf16[768,768]{1,0:T(8,128)(2,1)}, bf16[768,768]{1,0:T(8,128)(2,1)S(1)}, u32[]{:S(2)}) copy-start(bf16[768,768]{1,0:T(8,128)(2,1)S(1)} %collective-permute-done.25) | copy-start | bytes 3538948
  160.0 16.8 %collective-permute-start.26 = (bf16[256,768]{1,0:T(8,128)(2,1)}, bf16[256,768]{1,0:T(8,128)(2,1)}, u32[]{:S(2)}, u32[]{:S(2)}) collective-permute-start(bf16[256,768]{1,0:T(8,128)(2,1)} %pad_maximum_fusion.5), channel_id=1, source_target_pairs={{0,32},{32,64},{64,96},{96,0},{1,33},{33,65},{65,97},{97,1},{2,34}... | collective-permute-start | bytes 1179656 | tf_op jit(solution)/shard_map/ppermute | solution.py:18
  163.4 13.4 %collective-permute-start.27 = (bf16[256,768]{1,0:T(8,128)(2,1)S(1)}, bf16[256,768]{1,0:T(8,128)(2,1)S(1)}, u32[]{:S(2)}, u32[]{:S(2)}) collective-permute-start(bf16[256,768]{1,0:T(8,128)(2,1)S(1)} %pad_maximum_fusion.6), channel_id=1, source_target_pairs={{0,96},{32,0},{64,32},{96,64},{1,97},{33,1},{65,33},{97,65},{2,98}... | collective-permute-start | bytes 1179656 | tf_op jit(solution)/shard_map/ppermute | solution.py:18
  167.7 16.2 %collective-permute-start.29 = (bf16[768,384]{1,0:T(8,128)(2,1)}, bf16[768,384]{1,0:T(8,128)(2,1)}, u32[]{:S(2)}, u32[]{:S(2)}) collective-permute-start(bf16[768,384]{1,0:T(8,128)(2,1)} %slice.115), channel_id=1, source_target_pairs={{0,1},{1,0},{2,3},{3,2},{4,5},{5,4},{6,7},{7,6},{8,9},{9,8},{10,11... | collective-permute-start | bytes 1769480 | tf_op jit(solution)/shard_map/ppermute | solution.py:18
  176.8 0.7 copy-start.7
  178.9 8.6 %collective-permute-start.28 = (bf16[256,384]{1,0:T(8,128)(2,1)S(1)}, bf16[256,384]{1,0:T(8,128)(2,1)S(1)}, u32[]{:S(2)}, u32[]{:S(2)}) collective-permute-start(bf16[256,384]{1,0:T(8,128)(2,1)S(1)} %slice.127), channel_id=1, source_target_pairs={{0,1},{1,0},{2,3},{3,2},{4,5},{5,4},{6,7},{7,6},{8,9},{9,8},{10,11... | collective-permute-start | bytes 589832 | tf_op jit(solution)/shard_map/ppermute | solution.py:18

commit v7 on v6

--- a/solution.py
+++ b/solution.py
@@ -102,19 +102,6 @@
         forward_ref[:, here] = (residual_ref[:, here].astype(F32) + jnp.where(section == 0, one, two)).astype(BF16)
         early = early_ref[:, here]
         received_ref[:, here] = jnp.where(section == 0, early, (early.astype(F32) + one).astype(BF16))
-
-
-def send_kernel(at_ref, context_ref, weights_ref, out_ref, done):
-    count, height = context_ref.shape[0], out_ref.shape[0] - context_ref.shape[0]
-    row = pl.multiple_of(at_ref[2] * height, height)
-    copies = [
-        pltpu.make_async_copy(context_ref, out_ref.at[:count], done.at[0]),
-        pltpu.make_async_copy(weights_ref.at[pl.ds(row, height)], out_ref.at[count:], done.at[1]),
-    ]
-    for copy in copies:
-        copy.start()
-    for copy in copies:
-        copy.wait()
 
 
 def local(kernel, at, arrays, shapes):
@@ -143,43 +130,33 @@
     tokens = group_tokens * n_y
     z_tokens = own_count * n_xh
     block_tokens = own_count * group
-    sizes = (n_y, n_core, n_xh, piece)
-    block_at = (y * n_core + core) * n_xh
-    at = jnp.stack([section, core, block_at + 1 - xh]).astype(jnp.int32)
-
+
+    both = jnp.concatenate([contexts, swap(contexts, "xh")], 1)
     def rows(core_at, xh_at):
         return lax.dynamic_slice_in_dim(weights, ((y * n_core + core_at) * n_xh + xh_at) * piece, piece, 0)
 
-    anywhere = pl.BlockSpec(memory_space=pl.ANY)
-    sent = pl.pallas_call(
-        send_kernel,
-        out_shape=jax.ShapeDtypeStruct((group_tokens + piece, width), BF16),
-        in_specs=[pl.BlockSpec(memory_space=pltpu.SMEM), anywhere, anywhere],
-        out_specs=anywhere,
-        scratch_shapes=[pltpu.SemaphoreType.DMA((2,))],
-    )(at, contexts, weights)
-    came = swap(sent, "xh")
-
-    (spread,) = local(functools.partial(spread_kernel, sizes), at, [upstream], [(group, own_count, features)])
-    spread = lax.all_to_all(spread, ("y", "xh"), 0, 0, tiled=True).reshape(block_tokens, features)
-    spread, came = tie(spread, came)
-    both = jnp.concatenate([contexts, came[:group_tokens]], 1)
-    came_rows = came[group_tokens:]
-
+    both, partner_rows = tie(both, rows(core, 1 - xh))
+    came_rows = swap(partner_rows, "xh")
     other_rows = swap(came_rows, "core")
+    outgoing, came_rows = tie(jnp.where(section == 0, residual, upstream), came_rows)
+    early = swap(outgoing, "section")
     block = jnp.concatenate(
         [jnp.concatenate([rows(core, xh), came_rows], 1), jnp.concatenate([rows(1 - core, xh), other_rows], 1)], 0
     )
 
+    ctx_all = jnp.zeros((n_z, n_y, z_tokens, 2 * width), BF16)
     ctx_blocks, across = ring_gather(both, "y")
     ctx_blocks[n_y // 2] = jnp.concatenate(across, 0)
-    ctx_all = jnp.zeros((n_z, n_y, z_tokens, 2 * width), BF16)
     for away, part in ctx_blocks.items():
         ctx_all = place(ctx_all, part.reshape(n_z, 1, z_tokens, 2 * width), (0, wrap(y + away, n_y), 0, 0))
     ctx_flat = ctx_all.reshape(tokens, 2 * width)
 
+    sizes = (n_y, n_core, n_xh, piece)
+    at = jnp.stack([section, core]).astype(jnp.int32)
+    (spread,) = local(functools.partial(spread_kernel, sizes), at, [upstream], [(group, own_count, features)])
+    spread = lax.all_to_all(spread, ("y", "xh"), 0, 0, tiled=True).reshape(block_tokens, features)
+    grad_all = jnp.zeros((n_z, block_tokens, features), BF16)
     grad_blocks, far_blocks = ring_gather(spread, "z")
-    grad_all = jnp.zeros((n_z, block_tokens, features), BF16)
     for away, part in grad_blocks.items():
         grad_all = place(grad_all, part[None], (wrap(z + away, n_z), 0, 0))
 
@@ -187,32 +164,33 @@
         ctx_flat, block, (((1,), (1,)), ((), ())), preferred_element_type=F32
     ).astype(BF16).reshape(n_z, block_tokens, features)
     ring = ring_steps(lambda away: pick(partial_branch, wrap(z + away, n_z)), "z")
-    *step, outgoing = tie(*next(ring), jnp.where(section == 0, residual, upstream))
-    early = swap(outgoing, "section")
+    *step, early = tie(*next(ring), early)
     step = ring.send(step)
-    *step, far_low, far_high = tie(*step, *far_blocks)
+    far = jnp.concatenate(far_blocks, 0)[None]
+    grad_flat = place(grad_all, far, (wrap(z + n_z // 2, n_z), 0, 0)).reshape(tokens, features)
+    partial_ctx = jnp.dot(grad_flat, block, preferred_element_type=F32).astype(BF16)
+    *step, partial_ctx = tie(*step, partial_ctx)
     step = ring.send(step)
-    grad_all = place(grad_all, jnp.concatenate([far_low, far_high], 0)[None], (wrap(z + n_z // 2, n_z), 0, 0))
-    grad_flat = grad_all.reshape(tokens, features)
     norm_factor = 1.0 / math.sqrt(tokens * n_core)
     product = lax.dot_general(grad_flat, ctx_flat, (((0,), (0,)), ((), ())), preferred_element_type=F32)
-    product = (norm_factor * product).astype(BF16)
-    partial_ctx = jnp.dot(grad_flat, block, preferred_element_type=F32).astype(BF16)
-    *step, partial_ctx, product, early = tie(*step, partial_ctx, product, early)
-    other_product = swap(product[piece:], "core")
-    step = ring.send(step)
+    product, partial_ctx = tie((norm_factor * product).astype(BF16), partial_ctx)
     partial_ctx = partial_ctx.reshape(n_z, n_y, z_tokens, 2 * width)
     ctx_ring = ring_steps(lambda away: pick(partial_ctx, wrap(y + away, n_y), 1).reshape(group_tokens, 2 * width), "y")
     ctx_step = next(ctx_ring)
-    ctx_low, ctx_high, other_product = tie(*ctx_step, other_product)
+    *step, product = tie(*step, product)
+    step = ring.send(step)
+    ctx_step = ctx_ring.send(ctx_step)
+    other_product = swap(product[piece:], "core")
+    *ctx_step, other_product = tie(*ctx_step, other_product)
     branch = ring.send(step).astype(BF16)
     branch = branch.reshape(1, group, own_count, features)
     branch = jnp.concatenate([branch, branch], 0).reshape(2 * group, own_count, features)
     branch = lax.all_to_all(branch, ("section", "y", "xh"), 0, 0, tiled=True)
 
-    summed = ctx_ring.send(ctx_ring.send((ctx_low, ctx_high)))
-    branch, summed = tie(branch, summed)
-    ctx_grad = add(summed[:, :width], swap(summed[:, width:].astype(BF16), "xh"))
+    summed = ctx_ring.send(ctx_step)
+    other_ctx = swap(summed[:, width:].astype(BF16), "xh")
+    branch, other_ctx = tie(branch, other_ctx)
+    ctx_grad = add(summed[:, :width], other_ctx)
     forward, received = local(
         functools.partial(finish_kernel, sizes),
         at,

time: 189 us -> 143 us (0.76)
  Pallas kernels: 28.7 us -> 2.98 us
  waiting for transfers between devices: 60.7 us -> 44.7 us
  matrix products: 14.6 us -> 10.3 us
  other arithmetic: 13.5 us -> 10 us
    pallas_call x1 -> x0, Pallas kernels: 25.7 us -> none  [shards(): pl.pallas_call(send_kernel, out_shape=jax.ShapeDtypeStruct((group_tokens...]
    all_to_all x1, waiting for transfers between devices: 17.4 us -> 0.01 us  [shards(): lax.all_to_all(spread, ('y', 'xh'), 0, 0, tiled=True)]
    all_to_all x1, waiting for transfers between devices: 0.01 us -> 17 us  [shards(): branch = lax.all_to_all(branch, ('section', 'y', 'xh'), 0, 0, tiled=True)]
    ppermute x30 -> x31, waiting for transfers between devices: 43.3 us -> 27.7 us  [shift(): return lax.ppermute(value, axis, [(i, (i + by) % n) for i in range(n)])]
    dot_general x1, matrix products: 9.09 us -> 3.71 us  [shards(): lax.dot_general(ctx_flat, block, (((1,), (1,)), ((), ())), preferred_elem...]
    ppermute x30 -> x31, starting transfers between devices: 50.4 us -> 51.5 us  [shift(): return lax.ppermute(value, axis, [(i, (i + by) % n) for i in range(n)])]
  transfers between devices with their start and end apart: 32 -> 33, of which waited for: 12 -> 11; matrix products, arithmetic and copies ran while one was open for 18% -> 18% of each run, Pallas kernels for 2% -> 2%
where the time goes in v7:
time: 143 us; the launch traced here: 141 us
  starting transfers between devices  62.9 us (44%)
  waiting for transfers between devices  44.7 us (31%)
  matrix products  10.3 us (7%)
  other arithmetic  10 us (7%)
  local copies, waits for them, and re-layouts  9.31 us (7%)
  Pallas kernels  2.98 us (2%)
    ppermute x31, starting transfers between devices, shift(): return lax.ppermute(value, axis, [(i, (i + by) % n) for i in range(n)])  51.5 us
    ppermute x31, waiting for transfers between devices, shift(): return lax.ppermute(value, axis, [(i, (i + by) % n) for i in range(n)])  27.7 us
    all_to_all x1, waiting for transfers between devices, shards(): branch = lax.all_to_all(branch, ('section', 'y', 'xh'), 0, 0, tiled=True)  17 us
    all_to_all x1, starting transfers between devices, shards(): branch = lax.all_to_all(branch, ('section', 'y', 'xh'), 0, 0, tiled=True)  6.16 us
    all_to_all x1, starting transfers between devices, shards(): lax.all_to_all(spread, ('y', 'xh'), 0, 0, tiled=True)  5.31 us
    dot_general x1, matrix products, shards(): lax.dot_general(ctx_flat, block, (((1,), (1,)), ((), ())), preferred_elem...  3.71 us
    dot_general x1, matrix products, shards(): jnp.dot(grad_flat, block, preferred_element_type=F32).astype(BF16)  3.66 us
    pallas_call x2, Pallas kernels, local(): pl.pallas_call(kernel, out_shape=[jax.ShapeDtypeStruct(shape, BF16) for s...  2.98 us
  transfers between devices with their start and end apart: 33, of which 11 were waited for; matrix products, arithmetic and copies ran while one was open for 18% of the time, Pallas kernels for 2%

profile of v7, /device:TPU:2, one launch (start us, length us, event | category | flops | bytes accessed | tf_op | source)
XLA Modules:
  0.0 141.4 jit_solution(3951345112235332361)
XLA Ops:
  0.6 2.2 %collective-permute-start = (bf16[256,384]{1,0:T(8,128)(2,1)}, bf16[256,384]{1,0:T(8,128)(2,1)S(1)}, u32[]{:S(2)}, u32[]{:S(2)}) collective-permute-start(bf16[256,384]{1,0:T(8,128)(2,1)} %bitcast.105), channel_id=1, source_target_pairs={{0,1},{1,0},{2,3},{3,2},{4,5},{5,4},{6,7},{7,6},{8,9},{9,8},{10,11... | collective-permute-start | bytes 589832 | tf_op jit(solution)/shard_map/ppermute | solution.py:18
  2.9 1.0 copy-done
  3.9 1.3 shard_map.75
  5.2 5.3 %all-to-all-start = ((bf16[8,16,1536]{2,1,0:T(8,128)(2,1)}), bf16[8,16,1536]{2,1,0:T(8,128)(2,1)S(1)}, u32[]{:S(2)}, u32[]{:S(2)}) async-start(bf16[8,16,1536]{2,1,0:T(8,128)(2,1)} %shard_map.75), calls=%async_computation | async-start | bytes 786432 | tf_op jit(solution)/shard_map/all_to_all | solution.py:157
  10.5 2.7 %dynamic-slice_bitcast_fusion.1 = (bf16[768,384]{1,0:T(8,128)(2,1)}, bf16[768,384]{1,0:T(8,128)(2,1)}, bf16[768,384]{1,0:T(8,128)(2,1)}) fusion(bf16[1,12288,384]{2,1,0:T(8,128)(2,1)} %param.6, s32[]{:T(128)S(6)} %select_n.84, s32[]{:T(128)S(6)} %select_n.79, s32[]{:T(128)S(6)} %select_n.87), kind=kLoop, calls=%fused_computation.21 | loop fusion | bytes 3538956 | tf_op jit(solution)/shard_map/dynamic_slice | solution.py:136
  13.3 2.1 %collective-permute-start.1 = (bf16[256,768]{1,0:T(8,128)(2,1)S(1)}, bf16[256,768]{1,0:T(8,128)(2,1)S(1)}, u32[]{:S(2)}, u32[]{:S(2)}) collective-permute-start(bf16[256,768]{1,0:T(8,128)(2,1)S(1)} %pad_maximum_fusion.1), channel_id=1, source_target_pairs={{0,32},{32,64},{64,96},{96,0},{1,33},{33,65},{65,97},{97,1},{2,34}... | collective-permute-start | bytes 1179656 | tf_op jit(solution)/shard_map/ppermute | solution.py:18
  15.4 1.3 collective-permute-start.2
  16.7 0.8 broadcast_select_fusion.2
  17.5 3.4 %collective-permute-start.5 = (bf16[768,384]{1,0:T(8,128)(2,1)}, bf16[768,384]{1,0:T(8,128)(2,1)}, u32[]{:S(2)}, u32[]{:S(2)}) collective-permute-start(bf16[768,384]{1,0:T(8,128)(2,1)} %get-tuple-element.27), channel_id=1, source_target_pairs={{0,1},{1,0},{2,3},{3,2},{4,5},{5,4},{6,7},{7,6},{8,9},{9,8},{10,11... | collective-permute-start | bytes 1769480 | tf_op jit(solution)/shard_map/ppermute | solution.py:18
  20.9 0.2 broadcast_in_dim.39
  21.2 2.0 %collective-permute-start.12 = (bf16[128,1536]{1,0:T(8,128)(2,1)S(1)}, bf16[128,1536]{1,0:T(8,128)(2,1)S(1)}, u32[]{:S(2)}, u32[]{:S(2)}) collective-permute-start(bf16[128,1536]{1,0:T(8,128)(2,1)S(1)} %bitcast.92), channel_id=1, source_target_pairs={{0,2},{2,4},{4,6},{6,8},{8,10},{10,12},{12,14},{14,0},{1,3},{3,5},... | collective-permute-start | bytes 1179656 | tf_op jit(solution)/shard_map/ppermute | solution.py:18
  23.1 4.0 %collective-permute-start.13 = (bf16[128,1536]{1,0:T(8,128)(2,1)S(1)}, bf16[128,1536]{1,0:T(8,128)(2,1)S(1)}, u32[]{:S(2)}, u32[]{:S(2)}) collective-permute-start(bf16[128,1536]{1,0:T(8,128)(2,1)S(1)} %bitcast.93), channel_id=1, source_target_pairs={{0,14},{2,0},{4,2},{6,4},{8,6},{10,8},{12,10},{14,12},{1,15},{3,1}... | collective-permute-start | bytes 1179656 | tf_op jit(solution)/shard_map/ppermute | solution.py:18
  27.2 0.3 broadcast_in_dim.40
  27.5 0.3 collective-permute-start.3
  27.9 0.9 slice.90
  28.8 3.1 %collective-permute-start.4 = (bf16[128,768]{1,0:T(8,128)(2,1)S(1)}, bf16[128,768]{1,0:T(8,128)(2,1)S(1)}, u32[]{:S(2)}, u32[]{:S(2)}) collective-permute-start(bf16[128,768]{1,0:T(8,128)(2,1)S(1)} %slice.90), channel_id=1, source_target_pairs={{0,96},{32,0},{64,32},{96,64},{1,97},{33,1},{65,33},{97,65},{2,98}... | collective-permute-start | bytes 589832 | tf_op jit(solution)/shard_map/ppermute | solution.py:18
  31.9 1.1 constant_dynamic-update-slice_fusion.1
  33.0 1.5 %collective-permute-done.12 = bf16[128,1536]{1,0:T(8,128)(2,1)S(1)} collective-permute-done((bf16[128,1536]{1,0:T(8,128)(2,1)S(1)}, bf16[128,1536]{1,0:T(8,128)(2,1)S(1)}, u32[]{:S(2)}, u32[]{:S(2)}) %collective-permute-start.12) | collective-permute-done | bytes 393248 | tf_op jit(solution)/shard_map/ppermute | solution.py:18
  34.5 0.4 collective-permute-start.14
  34.9 4.0 %collective-permute-start.15 = (bf16[128,1536]{1,0:T(8,128)(2,1)S(1)}, bf16[128,1536]{1,0:T(8,128)(2,1)S(1)}, u32[]{:S(2)}, u32[]{:S(2)}) collective-permute-start(bf16[128,1536]{1,0:T(8,128)(2,1)S(1)} %collective-permute-done.13), channel_id=1, source_target_pairs={{0,14},{2,0},{4,2},{6,4},{8,6},{10,8},{12,10},{14,12},{1,15},{3,1}... | collective-permute-start | bytes 1179656 | tf_op jit(solution)/shard_map/ppermute | solution.py:18
  39.1 0.7 collective-permute-start.9
  39.8 7.3 %collective-permute-done.14 = bf16[128,1536]{1,0:T(8,128)(2,1)S(1)} collective-permute-done((bf16[128,1536]{1,0:T(8,128)(2,1)S(1)}, bf16[128,1536]{1,0:T(8,128)(2,1)S(1)}, u32[]{:S(2)}, u32[]{:S(2)}) %collective-permute-start.14) | collective-permute-done | bytes 393248 | tf_op jit(solution)/shard_map/ppermute | solution.py:18
  47.2 3.2 %collective-permute-start.17 = (bf16[128,1536]{1,0:T(8,128)(2,1)S(1)}, bf16[128,1536]{1,0:T(8,128)(2,1)S(1)}, u32[]{:S(2)}, u32[]{:S(2)}) collective-permute-start(bf16[128,1536]{1,0:T(8,128)(2,1)S(1)} %collective-permute-done.15), channel_id=1, source_target_pairs={{0,14},{2,0},{4,2},{6,4},{8,6},{10,8},{12,10},{14,12},{1,15},{3,1}... | collective-permute-start | bytes 1179656 | tf_op jit(solution)/shard_map/ppermute | solution.py:18
  50.5 3.7 %convolution_convert_fusion = bf16[1024,1536]{1,0:T(8,128)(2,1)S(1)} fusion(bf16[1024,768]{1,0:T(8,128)(2,1)S(1)} %bitcast.90, bf16[768,384]{1,0:T(8,128)(2,1)S(1)} %collective-permute-done.6, bf16[768,384]{1,0:T(8,128)(2,1)S(1)} %copy-done.6, bf16[768,384]{1,0:T(8,128)(2,1)} %collective-permute-done.5, bf16[768,384]{1,0:T(8,128)(2,1)S(1)} %copy-done.5), kind=kOutput, calls=%fused_computation.1 | convolution fusion | flops 2426929152 | bytes 7077888 | tf_op jit(solution)/shard_map/dot_general | solution.py:163
  54.2 0.1 dynamic-slice_bitcast_fusion.3
  54.3 0.1 collective-permute-start.7
  54.4 3.2 %collective-permute-start.8 = (bf16[128,768]{1,0:T(8,128)(2,1)S(1)}, bf16[128,768]{1,0:T(8,128)(2,1)S(1)}, u32[]{:S(2)}, u32[]{:S(2)}) collective-permute-start(bf16[128,768]{1,0:T(8,128)(2,1)S(1)} %get-tuple-element.66), channel_id=1, source_target_pairs={{0,14},{2,0},{4,2},{6,4},{8,6},{10,8},{12,10},{14,12},{1,15},{3,1}... | collective-permute-start | bytes 589832 | tf_op jit(solution)/shard_map/ppermute | solution.py:18
  57.7 1.7 %collective-permute-done.16 = bf16[128,1536]{1,0:T(8,128)(2,1)S(1)} collective-permute-done((bf16[128,1536]{1,0:T(8,128)(2,1)S(1)}, bf16[128,1536]{1,0:T(8,128)(2,1)S(1)}, u32[]{:S(2)}, u32[]{:S(2)}) %collective-permute-start.16) | collective-permute-done | bytes 393248 | tf_op jit(solution)/shard_map/ppermute | solution.py:18
  59.5 3.3 %collective-permute-start.19 = (bf16[64,1536]{1,0:T(8,128)(2,1)S(1)}, bf16[64,1536]{1,0:T(8,128)(2,1)S(1)}, u32[]{:S(2)}, u32[]{:S(2)}) collective-permute-start(bf16[64,1536]{1,0:T(8,128)(2,1)S(1)} %slice.98), channel_id=1, source_target_pairs={{0,14},{2,0},{4,2},{6,4},{8,6},{10,8},{12,10},{14,12},{1,15},{3,1}... | collective-permute-start | bytes 589832 | tf_op jit(solution)/shard_map/ppermute | solution.py:18
  62.9 0.7 collective-permute-done.7
  63.7 3.2 %collective-permute-start.11 = (bf16[128,1536]{1,0:T(8,128)(2,1)S(1)}, bf16[128,1536]{1,0:T(8,128)(2,1)S(1)}, u32[]{:S(2)}, u32[]{:S(2)}) collective-permute-start(bf16[128,1536]{1,0:T(8,128)(2,1)S(1)} %pad_maximum_fusion.4), channel_id=1, source_target_pairs={{0,14},{2,0},{4,2},{6,4},{8,6},{10,8},{12,10},{14,12},{1,15},{3,1}... | collective-permute-start | bytes 1179656 | tf_op jit(solution)/shard_map/ppermute | solution.py:18
  67.1 0.9 collective-permute-done.19
  68.1 3.7 %convolution_convert_fusion.1 = bf16[1024,768]{1,0:T(8,128)(2,1)S(1)} fusion(bf16[1024,1536]{1,0:T(8,128)(2,1)S(1)} %bitcast.84, bf16[768,384]{1,0:T(8,128)(2,1)S(1)} %collective-permute-done.6, bf16[768,384]{1,0:T(8,128)(2,1)S(1)} %copy-done.6, bf16[768,384]{1,0:T(8,128)(2,1)} %collective-permute-done.5, bf16[768,384]{1,0:T(8,128)(2,1)S(1)} %copy-done.5), kind=kOutput, calls=%fused_computation.4 | convolution fusion | flops 2426142720 | bytes 7077888 | tf_op jit(solution)/shard_map/dot_general | solution.py:171
  71.7 3.0 %multiply_convert_fusion = bf16[1536,768]{1,0:T(8,128)(2,1)S(1)} fusion(bf16[1024,1536]{1,0:T(8,128)(2,1)S(1)} %bitcast.85, bf16[1024,768]{1,0:T(8,128)(2,1)S(1)} %bitcast.91), kind=kOutput, calls=%fused_computation | convolution fusion | flops 2418278400 | bytes 7077888 | tf_op jit(solution)/shard_map/dot_general | solution.py:175
  74.7 1.3 collective-permute-done.10
  76.0 0.8 constant_dynamic-slice_fusion.3
  76.9 0.4 collective-permute-start.26
  77.3 0.2 fusion.2
  77.6 3.2 %collective-permute-start.21 = (bf16[128,1536]{1,0:T(8,128)(2,1)S(1)}, bf16[128,1536]{1,0:T(8,128)(2,1)S(1)}, u32[]{:S(2)}, u32[]{:S(2)}) collective-permute-start(bf16[128,1536]{1,0:T(8,128)(2,1)S(1)} %get-tuple-element.53), channel_id=1, source_target_pairs={{0,14},{2,0},{4,2},{6,4},{8,6},{10,8},{12,10},{14,12},{1,15},{3,1}... | collective-permute-start | bytes 1179656 | tf_op jit(solution)/shard_map/ppermute | solution.py:18
  80.9 1.8 %collective-permute-start.24 = (bf16[256,384]{1,0:T(8,128)(2,1)S(1)}, bf16[256,384]{1,0:T(8,128)(2,1)S(1)}, u32[]{:S(2)}, u32[]{:S(2)}) collective-permute-start(bf16[256,384]{1,0:T(8,128)(2,1)S(1)} %get-tuple-element.65), channel_id=1, source_target_pairs={{0,32},{32,64},{64,96},{96,0},{1,33},{33,65},{65,97},{97,1},{2,34}... | collective-permute-start | bytes 589832 | tf_op jit(solution)/shard_map/ppermute | solution.py:18
  82.8 3.8 %collective-permute-done.20 = bf16[128,1536]{1,0:T(8,128)(2,1)S(1)} collective-permute-done((bf16[128,1536]{1,0:T(8,128)(2,1)S(1)}, bf16[128,1536]{1,0:T(8,128)(2,1)S(1)}, u32[]{:S(2)}, u32[]{:S(2)}) %collective-permute-start.20) | collective-permute-done | bytes 393248 | tf_op jit(solution)/shard_map/ppermute | solution.py:18
  86.7 0.1 collective-permute-start.28
  86.8 0.3 fusion.4
  87.0 2.1 %collective-permute-start.22 = (bf16[128,1536]{1,0:T(8,128)(2,1)S(1)}, bf16[128,1536]{1,0:T(8,128)(2,1)S(1)}, u32[]{:S(2)}, u32[]{:S(2)}) collective-permute-start(bf16[128,1536]{1,0:T(8,128)(2,1)S(1)} %get-tuple-element.51), channel_id=1, source_target_pairs={{0,2},{2,4},{4,6},{6,8},{8,10},{10,12},{12,14},{14,0},{1,3},{3,5},... | collective-permute-start | bytes 1179656 | tf_op jit(solution)/shard_map/ppermute | solution.py:18
  89.1 1.3 collective-permute-start.23
  90.5 0.1 collective-permute-start.27
  90.7 2.1 %collective-permute-start.25 = (bf16[256,768]{1,0:T(8,128)(2,1)S(1)}, bf16[256,768]{1,0:T(8,128)(2,1)}, u32[]{:S(2)}, u32[]{:S(2)}) collective-permute-start(bf16[256,768]{1,0:T(8,128)(2,1)S(1)} %pad_maximum_fusion.5), channel_id=1, source_target_pairs={{0,32},{32,64},{64,96},{96,0},{1,33},{33,65},{65,97},{97,1},{2,34}... | collective-permute-start | bytes 1179656 | tf_op jit(solution)/shard_map/ppermute | solution.py:18
  92.8 7.4 %collective-permute-done.22 = bf16[128,1536]{1,0:T(8,128)(2,1)S(1)} collective-permute-done((bf16[128,1536]{1,0:T(8,128)(2,1)S(1)}, bf16[128,1536]{1,0:T(8,128)(2,1)S(1)}, u32[]{:S(2)}, u32[]{:S(2)}) %collective-permute-start.22) | collective-permute-done | bytes 393248 | tf_op jit(solution)/shard_map/ppermute | solution.py:18
  100.1 0.5 collective-permute-done.23
  100.6 0.2 fusion.6
  100.8 0.9 pad_maximum_fusion
  101.7 6.2 %all-to-all-start.1 = ((bf16[16,16,1536]{2,1,0:T(8,128)(2,1)}), bf16[16,16,1536]{2,1,0:T(8,128)(2,1)S(1)}, u32[]{:S(2)}, u32[]{:S(2)}) async-start(bf16[16,16,1536]{2,1,0:T(8,128)(2,1)} %bitcast.33), calls=%async_computation.1 | async-start | bytes 1572864 | tf_op jit(solution)/shard_map/all_to_all | solution.py:188
  107.9 2.0 %add_convert_fusion = bf16[768,768]{1,0:T(8,128)(2,1)S(1)} fusion(bf16[768,768]{1,0:T(8,128)(2,1)} %collective-permute-done.28, bf16[1536,768]{1,0:T(8,128)(2,1)} %copy-done.3), kind=kLoop, calls=%fused_computation.3 | loop fusion | flops 2359296 | bytes 3538944 | tf_op jit(solution)/shard_map/convert_element_type | solution.py:26
  109.9 0.9 slice.108
  110.8 2.1 %collective-permute-start.30 = (bf16[768,384]{1,0:T(8,128)(2,1)}, bf16[768,384]{1,0:T(8,128)(2,1)}, u32[]{:S(2)}, u32[]{:S(2)}) collective-permute-start(bf16[768,384]{1,0:T(8,128)(2,1)} %slice.108), channel_id=1, source_target_pairs={{0,1},{1,0},{2,3},{3,2},{4,5},{5,4},{6,7},{7,6},{8,9},{9,8},{10,11... | collective-permute-start | bytes 1769480 | tf_op jit(solution)/shard_map/ppermute | solution.py:18
  112.9 1.2 fusion
  114.1 0.7 slice.122
  114.8 1.5 %collective-permute-start.29 = (bf16[256,384]{1,0:T(8,128)(2,1)}, bf16[256,384]{1,0:T(8,128)(2,1)}, u32[]{:S(2)}, u32[]{:S(2)}) collective-permute-start(bf16[256,384]{1,0:T(8,128)(2,1)} %slice.122), channel_id=1, source_target_pairs={{0,1},{1,0},{2,3},{3,2},{4,5},{5,4},{6,7},{7,6},{8,9},{9,8},{10,11... | collective-permute-start | bytes 589832 | tf_op jit(solution)/shard_map/ppermute | solution.py:18
  116.3 17.0 %all-to-all-done.1 = bf16[16,16,1536]{2,1,0:T(8,128)(2,1)S(1)} async-done(((bf16[16,16,1536]{2,1,0:T(8,128)(2,1)}), bf16[16,16,1536]{2,1,0:T(8,128)(2,1)S(1)}, u32[]{:S(2)}, u32[]{:S(2)}) %all-to-all-start.1) | async-done | bytes 786464 | tf_op jit(solution)/shard_map/all_to_all | solution.py:188
  133.2 2.5 %collective-permute-done.29 = bf16[256,384]{1,0:T(8,128)(2,1)} collective-permute-done((bf16[256,384]{1,0:T(8,128)(2,1)}, bf16[256,384]{1,0:T(8,128)(2,1)}, u32[]{:S(2)}, u32[]{:S(2)}) %collective-permute-start.29) | collective-permute-done | bytes 196640 | tf_op jit(solution)/shard_map/ppermute | solution.py:18
  135.7 1.7 %shard_map.76 = (bf16[16,12288]{1,0:T(8,128)(2,1)}, bf16[16,12288]{1,0:T(8,128)(2,1)}) custom-call(s32[2]{0:T(128)S(1)} %pad_add_fusion.at_ref, bf16[2,8,16,1536]{3,2,1,0:T(8,128)(2,1)S(1)} %bitcast.81, bf16[16,12288]{1,0:T(8,128)(2,1)S(1)} %bitcast.83, bf16[16,12288]{1,0:T(8,128)(2,1)S(1)} %collective-permute-done.9.early_ref), custom_call_target="tpu_custom_call" | custom-call | tf_op jit(solution)/shard_map/pallas_call | solution.py:109
  137.4 1.6 %fusion.9 = bf16[1,256,384]{2,1,0:T(8,128)(2,1)} fusion(bf16[256,384]{1,0:T(8,128)(2,1)} %collective-permute-done.29, f32[256,768]{1,0:T(8,128)S(1)} %fusion), kind=kLoop, calls=%fused_computation.51 | loop fusion | flops 294912 | bytes 786432 | tf_op jit(solution)/shard_map/broadcast_in_dim | solution.py:206
  139.0 1.2 broadcast_select_fusion.1
  140.2 1.1 maximum_bitcast_fusion
  (76 shorter events, 1.4 us)
Async XLA Ops:
  0.6 12.6 %collective-permute-start = (bf16[256,384]{1,0:T(8,128)(2,1)}, bf16[256,384]{1,0:T(8,128)(2,1)S(1)}, u32[]{:S(2)}, u32[]{:S(2)}) collective-permute-start(bf16[256,384]{1,0:T(8,128)(2,1)} %bitcast.105), channel_id=1, source_target_pairs={{0,1},{1,0},{2,3},{3,2},{4,5},{5,4},{6,7},{7,6},{8,9},{9,8},{10,11... | collective-permute-start | bytes 589832 | tf_op jit(solution)/shard_map/ppermute | solution.py:18
  2.9 1.0 copy-start
  3.9 9.3 %copy-start.8 = (bf16[1,256,384]{2,1,0:T(8,128)(2,1)S(1)}, bf16[1,256,384]{2,1,0:T(8,128)(2,1)}, u32[]{:S(2)}) copy-start(bf16[1,256,384]{2,1,0:T(8,128)(2,1)} %param.5) | copy-start | bytes 589828
  3.9 12.8 %copy-start.1 = (bf16[1,16,12288]{2,1,0:T(8,128)(2,1)S(1)}, bf16[1,16,12288]{2,1,0:T(8,128)(2,1)}, u32[]{:S(2)}) copy-start(bf16[1,16,12288]{2,1,0:T(8,128)(2,1)} %param.7) | copy-start | bytes 1179652
  3.9 12.8 %copy-start.2 = (bf16[1,16,12288]{2,1,0:T(8,128)(2,1)S(1)}, bf16[1,16,12288]{2,1,0:T(8,128)(2,1)}, u32[]{:S(2)}) copy-start(bf16[1,16,12288]{2,1,0:T(8,128)(2,1)} %param.4) | copy-start | bytes 1179652
  5.2 15.9 %all-to-all-start = ((bf16[8,16,1536]{2,1,0:T(8,128)(2,1)}), bf16[8,16,1536]{2,1,0:T(8,128)(2,1)S(1)}, u32[]{:S(2)}, u32[]{:S(2)}) async-start(bf16[8,16,1536]{2,1,0:T(8,128)(2,1)} %shard_map.75), calls=%async_computation | async-start | bytes 786432 | tf_op jit(solution)/shard_map/all_to_all | solution.py:157
  13.3 14.2 %collective-permute-start.1 = (bf16[256,768]{1,0:T(8,128)(2,1)S(1)}, bf16[256,768]{1,0:T(8,128)(2,1)S(1)}, u32[]{:S(2)}, u32[]{:S(2)}) collective-permute-start(bf16[256,768]{1,0:T(8,128)(2,1)S(1)} %pad_maximum_fusion.1), channel_id=1, source_target_pairs={{0,32},{32,64},{64,96},{96,0},{1,33},{33,65},{65,97},{97,1},{2,34}... | collective-permute-start | bytes 1179656 | tf_op jit(solution)/shard_map/ppermute | solution.py:18
  15.4 12.5 %collective-permute-start.2 = (bf16[256,768]{1,0:T(8,128)(2,1)S(1)}, bf16[256,768]{1,0:T(8,128)(2,1)}, u32[]{:S(2)}, u32[]{:S(2)}) collective-permute-start(bf16[256,768]{1,0:T(8,128)(2,1)S(1)} %pad_maximum_fusion.1), channel_id=1, source_target_pairs={{0,96},{32,0},{64,32},{96,64},{1,97},{33,1},{65,33},{97,65},{2,98}... | collective-permute-start | bytes 1179656 | tf_op jit(solution)/shard_map/ppermute | solution.py:18
  17.5 21.6 %collective-permute-start.5 = (bf16[768,384]{1,0:T(8,128)(2,1)}, bf16[768,384]{1,0:T(8,128)(2,1)}, u32[]{:S(2)}, u32[]{:S(2)}) collective-permute-start(bf16[768,384]{1,0:T(8,128)(2,1)} %get-tuple-element.27), channel_id=1, source_target_pairs={{0,1},{1,0},{2,3},{3,2},{4,5},{5,4},{6,7},{7,6},{8,9},{9,8},{10,11... | collective-permute-start | bytes 1769480 | tf_op jit(solution)/shard_map/ppermute | solution.py:18
  21.2 13.4 %collective-permute-start.12 = (bf16[128,1536]{1,0:T(8,128)(2,1)S(1)}, bf16[128,1536]{1,0:T(8,128)(2,1)S(1)}, u32[]{:S(2)}, u32[]{:S(2)}) collective-permute-start(bf16[128,1536]{1,0:T(8,128)(2,1)S(1)} %bitcast.92), channel_id=1, source_target_pairs={{0,2},{2,4},{4,6},{6,8},{8,10},{10,12},{12,14},{14,0},{1,3},{3,5},... | collective-permute-start | bytes 1179656 | tf_op jit(solution)/shard_map/ppermute | solution.py:18
  23.1 11.8 %collective-permute-start.13 = (bf16[128,1536]{1,0:T(8,128)(2,1)S(1)}, bf16[128,1536]{1,0:T(8,128)(2,1)S(1)}, u32[]{:S(2)}, u32[]{:S(2)}) collective-permute-start(bf16[128,1536]{1,0:T(8,128)(2,1)S(1)} %bitcast.93), channel_id=1, source_target_pairs={{0,14},{2,0},{4,2},{6,4},{8,6},{10,8},{12,10},{14,12},{1,15},{3,1}... | collective-permute-start | bytes 1179656 | tf_op jit(solution)/shard_map/ppermute | solution.py:18
  27.4 11.6 %copy-start.7 = (bf16[16,12288]{1,0:T(8,128)(2,1)S(1)}, bf16[16,12288]{1,0:T(8,128)(2,1)}, u32[]{:S(2)}) copy-start(bf16[16,12288]{1,0:T(8,128)(2,1)} %broadcast_select_fusion.2) | copy-start | bytes 1179652
  27.5 12.2 %collective-permute-start.3 = (bf16[128,768]{1,0:T(8,128)(2,1)S(1)}, bf16[128,768]{1,0:T(8,128)(2,1)S(1)}, u32[]{:S(2)}, u32[]{:S(2)}) collective-permute-start(bf16[128,768]{1,0:T(8,128)(2,1)S(1)} %slice.89), channel_id=1, source_target_pairs={{0,32},{32,64},{64,96},{96,0},{1,33},{33,65},{65,97},{97,1},{2,34}... | collective-permute-start | bytes 589832 | tf_op jit(solution)/shard_map/ppermute | solution.py:18
  28.8 10.9 %collective-permute-start.4 = (bf16[128,768]{1,0:T(8,128)(2,1)S(1)}, bf16[128,768]{1,0:T(8,128)(2,1)S(1)}, u32[]{:S(2)}, u32[]{:S(2)}) collective-permute-start(bf16[128,768]{1,0:T(8,128)(2,1)S(1)} %slice.90), channel_id=1, source_target_pairs={{0,96},{32,0},{64,32},{96,64},{1,97},{33,1},{65,33},{97,65},{2,98}... | collective-permute-start | bytes 589832 | tf_op jit(solution)/shard_map/ppermute | solution.py:18
  31.9 18.6 %copy-start.5 = (bf16[768,384]{1,0:T(8,128)(2,1)S(1)}, bf16[768,384]{1,0:T(8,128)(2,1)}, u32[]{:S(2)}) copy-start(bf16[768,384]{1,0:T(8,128)(2,1)} %get-tuple-element.48) | copy-start | bytes 1769476
  31.9 18.6 %copy-start.6 = (bf16[768,384]{1,0:T(8,128)(2,1)S(1)}, bf16[768,384]{1,0:T(8,128)(2,1)}, u32[]{:S(2)}) copy-start(bf16[768,384]{1,0:T(8,128)(2,1)} %get-tuple-element.50) | copy-start | bytes 1769476
  34.5 12.6 %collective-permute-start.14 = (bf16[128,1536]{1,0:T(8,128)(2,1)S(1)}, bf16[128,1536]{1,0:T(8,128)(2,1)S(1)}, u32[]{:S(2)}, u32[]{:S(2)}) collective-permute-start(bf16[128,1536]{1,0:T(8,128)(2,1)S(1)} %collective-permute-done.12), channel_id=1, source_target_pairs={{0,2},{2,4},{4,6},{6,8},{8,10},{10,12},{12,14},{14,0},{1,3},{3,5},... | collective-permute-start | bytes 1179656 | tf_op jit(solution)/shard_map/ppermute | solution.py:18
  34.9 12.2 %collective-permute-start.15 = (bf16[128,1536]{1,0:T(8,128)(2,1)S(1)}, bf16[128,1536]{1,0:T(8,128)(2,1)S(1)}, u32[]{:S(2)}, u32[]{:S(2)}) collective-permute-start(bf16[128,1536]{1,0:T(8,128)(2,1)S(1)} %collective-permute-done.13), channel_id=1, source_target_pairs={{0,14},{2,0},{4,2},{6,4},{8,6},{10,8},{12,10},{14,12},{1,15},{3,1}... | collective-permute-start | bytes 1179656 | tf_op jit(solution)/shard_map/ppermute | solution.py:18
  39.1 23.8 %collective-permute-start.9 = (bf16[16,12288]{1,0:T(8,128)(2,1)S(1)}, bf16[16,12288]{1,0:T(8,128)(2,1)S(1)}, u32[]{:S(2)}, u32[]{:S(2)}) collective-permute-start(bf16[16,12288]{1,0:T(8,128)(2,1)S(1)} %copy-done.7), channel_id=1, source_target_pairs={{0,128},{128,0},{1,129},{129,1},{2,130},{130,2},{3,131},{131,3},{4... | collective-permute-start | bytes 1179656 | tf_op jit(solution)/shard_map/ppermute | solution.py:18
  39.7 10.7 %collective-permute-start.6 = (bf16[768,384]{1,0:T(8,128)(2,1)}, bf16[768,384]{1,0:T(8,128)(2,1)S(1)}, u32[]{:S(2)}, u32[]{:S(2)}) collective-permute-start(bf16[768,384]{1,0:T(8,128)(2,1)} %collective-permute-done.5), channel_id=1, source_target_pairs={{0,16},{16,0},{1,17},{17,1},{2,18},{18,2},{3,19},{19,3},{4,20},{20... | collective-permute-start | bytes 1769480 | tf_op jit(solution)/shard_map/ppermute | solution.py:18
  47.2 12.2 %collective-permute-start.16 = (bf16[128,1536]{1,0:T(8,128)(2,1)S(1)}, bf16[128,1536]{1,0:T(8,128)(2,1)S(1)}, u32[]{:S(2)}, u32[]{:S(2)}) collective-permute-start(bf16[128,1536]{1,0:T(8,128)(2,1)S(1)} %collective-permute-done.14), channel_id=1, source_target_pairs={{0,2},{2,4},{4,6},{6,8},{8,10},{10,12},{12,14},{14,0},{1,3},{3,5},... | collective-permute-start | bytes 1179656 | tf_op jit(solution)/shard_map/ppermute | solution.py:18
  47.2 12.3 %collective-permute-start.17 = (bf16[128,1536]{1,0:T(8,128)(2,1)S(1)}, bf16[128,1536]{1,0:T(8,128)(2,1)S(1)}, u32[]{:S(2)}, u32[]{:S(2)}) collective-permute-start(bf16[128,1536]{1,0:T(8,128)(2,1)S(1)} %collective-permute-done.15), channel_id=1, source_target_pairs={{0,14},{2,0},{4,2},{6,4},{8,6},{10,8},{12,10},{14,12},{1,15},{3,1}... | collective-permute-start | bytes 1179656 | tf_op jit(solution)/shard_map/ppermute | solution.py:18
  54.3 9.2 %collective-permute-start.7 = (bf16[128,768]{1,0:T(8,128)(2,1)S(1)}, bf16[128,768]{1,0:T(8,128)(2,1)S(1)}, u32[]{:S(2)}, u32[]{:S(2)}) collective-permute-start(bf16[128,768]{1,0:T(8,128)(2,1)S(1)} %get-tuple-element.67), channel_id=1, source_target_pairs={{0,2},{2,4},{4,6},{6,8},{8,10},{10,12},{12,14},{14,0},{1,3},{3,5},... | collective-permute-start | bytes 589832 | tf_op jit(solution)/shard_map/ppermute | solution.py:18
  54.4 9.2 %collective-permute-start.8 = (bf16[128,768]{1,0:T(8,128)(2,1)S(1)}, bf16[128,768]{1,0:T(8,128)(2,1)S(1)}, u32[]{:S(2)}, u32[]{:S(2)}) collective-permute-start(bf16[128,768]{1,0:T(8,128)(2,1)S(1)} %get-tuple-element.66), channel_id=1, source_target_pairs={{0,14},{2,0},{4,2},{6,4},{8,6},{10,8},{12,10},{14,12},{1,15},{3,1}... | collective-permute-start | bytes 589832 | tf_op jit(solution)/shard_map/ppermute | solution.py:18
  59.4 7.7 %collective-permute-start.18 = (bf16[64,1536]{1,0:T(8,128)(2,1)S(1)}, bf16[64,1536]{1,0:T(8,128)(2,1)S(1)}, u32[]{:S(2)}, u32[]{:S(2)}) collective-permute-start(bf16[64,1536]{1,0:T(8,128)(2,1)S(1)} %slice.97), channel_id=1, source_target_pairs={{0,2},{2,4},{4,6},{6,8},{8,10},{10,12},{12,14},{14,0},{1,3},{3,5},... | collective-permute-start | bytes 589832 | tf_op jit(solution)/shard_map/ppermute | solution.py:18
  59.5 8.5 %collective-permute-start.19 = (bf16[64,1536]{1,0:T(8,128)(2,1)S(1)}, bf16[64,1536]{1,0:T(8,128)(2,1)S(1)}, u32[]{:S(2)}, u32[]{:S(2)}) collective-permute-start(bf16[64,1536]{1,0:T(8,128)(2,1)S(1)} %slice.98), channel_id=1, source_target_pairs={{0,14},{2,0},{4,2},{6,4},{8,6},{10,8},{12,10},{14,12},{1,15},{3,1}... | collective-permute-start | bytes 589832 | tf_op jit(solution)/shard_map/ppermute | solution.py:18
  63.7 11.0 %collective-permute-start.11 = (bf16[128,1536]{1,0:T(8,128)(2,1)S(1)}, bf16[128,1536]{1,0:T(8,128)(2,1)S(1)}, u32[]{:S(2)}, u32[]{:S(2)}) collective-permute-start(bf16[128,1536]{1,0:T(8,128)(2,1)S(1)} %pad_maximum_fusion.4), channel_id=1, source_target_pairs={{0,14},{2,0},{4,2},{6,4},{8,6},{10,8},{12,10},{14,12},{1,15},{3,1}... | collective-permute-start | bytes 1179656 | tf_op jit(solution)/shard_map/ppermute | solution.py:18
  67.0 9.1 %collective-permute-start.10 = (bf16[128,1536]{1,0:T(8,128)(2,1)S(1)}, bf16[128,1536]{1,0:T(8,128)(2,1)S(1)}, u32[]{:S(2)}, u32[]{:S(2)}) collective-permute-start(bf16[128,1536]{1,0:T(8,128)(2,1)S(1)} %pad_maximum_fusion.3), channel_id=1, source_target_pairs={{0,2},{2,4},{4,6},{6,8},{8,10},{10,12},{12,14},{14,0},{1,3},{3,5},... | collective-permute-start | bytes 1179656 | tf_op jit(solution)/shard_map/ppermute | solution.py:18
  74.7 11.9 %copy-start.3 = (bf16[1536,768]{1,0:T(8,128)(2,1)}, bf16[1536,768]{1,0:T(8,128)(2,1)S(1)}, u32[]{:S(2)}) copy-start(bf16[1536,768]{1,0:T(8,128)(2,1)S(1)} %multiply_convert_fusion) | copy-start | bytes 7077892
  76.9 5.7 %collective-permute-start.26 = (bf16[256,384]{1,0:T(8,128)(2,1)S(1)}, bf16[256,384]{1,0:T(8,128)(2,1)S(1)}, u32[]{:S(2)}, u32[]{:S(2)}) collective-permute-start(bf16[256,384]{1,0:T(8,128)(2,1)S(1)} %get-tuple-element.64), channel_id=1, source_target_pairs={{0,96},{32,0},{64,32},{96,64},{1,97},{33,1},{65,33},{97,65},{2,98}... | collective-permute-start | bytes 589832 | tf_op jit(solution)/shard_map/ppermute | solution.py:18
  77.5 9.1 %collective-permute-start.20 = (bf16[128,1536]{1,0:T(8,128)(2,1)S(1)}, bf16[128,1536]{1,0:T(8,128)(2,1)S(1)}, u32[]{:S(2)}, u32[]{:S(2)}) collective-permute-start(bf16[128,1536]{1,0:T(8,128)(2,1)S(1)} %get-tuple-element.54), channel_id=1, source_target_pairs={{0,2},{2,4},{4,6},{6,8},{8,10},{10,12},{12,14},{14,0},{1,3},{3,5},... | collective-permute-start | bytes 1179656 | tf_op jit(solution)/shard_map/ppermute | solution.py:18
  77.6 9.0 %collective-permute-start.21 = (bf16[128,1536]{1,0:T(8,128)(2,1)S(1)}, bf16[128,1536]{1,0:T(8,128)(2,1)S(1)}, u32[]{:S(2)}, u32[]{:S(2)}) collective-permute-start(bf16[128,1536]{1,0:T(8,128)(2,1)S(1)} %get-tuple-element.53), channel_id=1, source_target_pairs={{0,14},{2,0},{4,2},{6,4},{8,6},{10,8},{12,10},{14,12},{1,15},{3,1}... | collective-permute-start | bytes 1179656 | tf_op jit(solution)/shard_map/ppermute | solution.py:18
  80.9 9.7 %collective-permute-start.24 = (bf16[256,384]{1,0:T(8,128)(2,1)S(1)}, bf16[256,384]{1,0:T(8,128)(2,1)S(1)}, u32[]{:S(2)}, u32[]{:S(2)}) collective-permute-start(bf16[256,384]{1,0:T(8,128)(2,1)S(1)} %get-tuple-element.65), channel_id=1, source_target_pairs={{0,32},{32,64},{64,96},{96,0},{1,33},{33,65},{65,97},{97,1},{2,34}... | collective-permute-start | bytes 589832 | tf_op jit(solution)/shard_map/ppermute | solution.py:18
  86.7 21.3 %collective-permute-start.28 = (bf16[768,768]{1,0:T(8,128)(2,1)S(1)}, bf16[768,768]{1,0:T(8,128)(2,1)}, u32[]{:S(2)}, u32[]{:S(2)}) collective-permute-start(bf16[768,768]{1,0:T(8,128)(2,1)S(1)} %slice.83), channel_id=1, source_target_pairs={{0,16},{16,0},{1,17},{17,1},{2,18},{18,2},{3,19},{19,3},{4,20},{20... | collective-permute-start | bytes 3538952 | tf_op jit(solution)/shard_map/ppermute | solution.py:18
  87.0 13.1 %collective-permute-start.22 = (bf16[128,1536]{1,0:T(8,128)(2,1)S(1)}, bf16[128,1536]{1,0:T(8,128)(2,1)S(1)}, u32[]{:S(2)}, u32[]{:S(2)}) collective-permute-start(bf16[128,1536]{1,0:T(8,128)(2,1)S(1)} %get-tuple-element.51), channel_id=1, source_target_pairs={{0,2},{2,4},{4,6},{6,8},{8,10},{10,12},{12,14},{14,0},{1,3},{3,5},... | collective-permute-start | bytes 1179656 | tf_op jit(solution)/shard_map/ppermute | solution.py:18
  89.1 11.5 %collective-permute-start.23 = (bf16[128,1536]{1,0:T(8,128)(2,1)S(1)}, bf16[128,1536]{1,0:T(8,128)(2,1)S(1)}, u32[]{:S(2)}, u32[]{:S(2)}) collective-permute-start(bf16[128,1536]{1,0:T(8,128)(2,1)S(1)} %get-tuple-element.52), channel_id=1, source_target_pairs={{0,14},{2,0},{4,2},{6,4},{8,6},{10,8},{12,10},{14,12},{1,15},{3,1}... | collective-permute-start | bytes 1179656 | tf_op jit(solution)/shard_map/ppermute | solution.py:18
  90.5 17.5 %collective-permute-start.27 = (bf16[256,768]{1,0:T(8,128)(2,1)S(1)}, bf16[256,768]{1,0:T(8,128)(2,1)}, u32[]{:S(2)}, u32[]{:S(2)}) collective-permute-start(bf16[256,768]{1,0:T(8,128)(2,1)S(1)} %pad_maximum_fusion.6), channel_id=1, source_target_pairs={{0,96},{32,0},{64,32},{96,64},{1,97},{33,1},{65,33},{97,65},{2,98}... | collective-permute-start | bytes 1179656 | tf_op jit(solution)/shard_map/ppermute | solution.py:18
  90.7 17.3 %collective-permute-start.25 = (bf16[256,768]{1,0:T(8,128)(2,1)S(1)}, bf16[256,768]{1,0:T(8,128)(2,1)}, u32[]{:S(2)}, u32[]{:S(2)}) collective-permute-start(bf16[256,768]{1,0:T(8,128)(2,1)S(1)} %pad_maximum_fusion.5), channel_id=1, source_target_pairs={{0,32},{32,64},{64,96},{96,0},{1,33},{33,65},{65,97},{97,1},{2,34}... | collective-permute-start | bytes 1179656 | tf_op jit(solution)/shard_map/ppermute | solution.py:18
  101.7 31.5 %all-to-all-start.1 = ((bf16[16,16,1536]{2,1,0:T(8,128)(2,1)}), bf16[16,16,1536]{2,1,0:T(8,128)(2,1)S(1)}, u32[]{:S(2)}, u32[]{:S(2)}) async-start(bf16[16,16,1536]{2,1,0:T(8,128)(2,1)} %bitcast.33), calls=%async_computation.1 | async-start | bytes 1572864 | tf_op jit(solution)/shard_map/all_to_all | solution.py:188
  107.9 5.0 %copy-start.4 = (bf16[8,1,32,768]{3,2,1,0:T(8,128)(2,1)S(1)}, bf16[8,1,32,768]{3,2,1,0:T(8,128)(2,1)}, u32[]{:S(2)}) copy-start(bf16[8,1,32,768]{3,2,1,0:T(8,128)(2,1)} %get-tuple-element.60) | copy-start | bytes 1179652
  110.8 28.3 %collective-permute-start.30 = (bf16[768,384]{1,0:T(8,128)(2,1)}, bf16[768,384]{1,0:T(8,128)(2,1)}, u32[]{:S(2)}, u32[]{:S(2)}) collective-permute-start(bf16[768,384]{1,0:T(8,128)(2,1)} %slice.108), channel_id=1, source_target_pairs={{0,1},{1,0},{2,3},{3,2},{4,5},{5,4},{6,7},{7,6},{8,9},{9,8},{10,11... | collective-permute-start | bytes 1769480 | tf_op jit(solution)/shard_map/ppermute | solution.py:18
  114.8 20.9 %collective-permute-start.29 = (bf16[256,384]{1,0:T(8,128)(2,1)}, bf16[256,384]{1,0:T(8,128)(2,1)}, u32[]{:S(2)}, u32[]{:S(2)}) collective-permute-start(bf16[256,384]{1,0:T(8,128)(2,1)} %slice.122), channel_id=1, source_target_pairs={{0,1},{1,0},{2,3},{3,2},{4,5},{5,4},{6,7},{7,6},{8,9},{9,8},{10,11... | collective-permute-start | bytes 589832 | tf_op jit(solution)/shard_map/ppermute | solution.py:18

commit v8 on v7

--- a/solution.py
+++ b/solution.py
@@ -138,8 +138,6 @@
     both, partner_rows = tie(both, rows(core, 1 - xh))
     came_rows = swap(partner_rows, "xh")
     other_rows = swap(came_rows, "core")
-    outgoing, came_rows = tie(jnp.where(section == 0, residual, upstream), came_rows)
-    early = swap(outgoing, "section")
     block = jnp.concatenate(
         [jnp.concatenate([rows(core, xh), came_rows], 1), jnp.concatenate([rows(1 - core, xh), other_rows], 1)], 0
     )
@@ -164,7 +162,8 @@
         ctx_flat, block, (((1,), (1,)), ((), ())), preferred_element_type=F32
     ).astype(BF16).reshape(n_z, block_tokens, features)
     ring = ring_steps(lambda away: pick(partial_branch, wrap(z + away, n_z)), "z")
-    *step, early = tie(*next(ring), early)
+    *step, outgoing = tie(*next(ring), jnp.where(section == 0, residual, upstream))
+    early = swap(outgoing, "section")
     step = ring.send(step)
     far = jnp.concatenate(far_blocks, 0)[None]
     grad_flat = place(grad_all, far, (wrap(z + n_z // 2, n_z), 0, 0)).reshape(tokens, features)
@@ -177,11 +176,13 @@
     partial_ctx = partial_ctx.reshape(n_z, n_y, z_tokens, 2 * width)
     ctx_ring = ring_steps(lambda away: pick(partial_ctx, wrap(y + away, n_y), 1).reshape(group_tokens, 2 * width), "y")
     ctx_step = next(ctx_ring)
-    *step, product = tie(*step, product)
+    other_product = swap(product[piece:], "core")
+    *step, other_product, early = tie(*step, other_product, early)
     step = ring.send(step)
     ctx_step = ctx_ring.send(ctx_step)
-    other_product = swap(product[piece:], "core")
-    *ctx_step, other_product = tie(*ctx_step, other_product)
+    own_rows = add(product[:piece], other_product)
+    came = swap(own_rows[:, width:], "xh")
+    *ctx_step, came = tie(*ctx_step, came)
     branch = ring.send(step).astype(BF16)
     branch = branch.reshape(1, group, own_count, features)
     branch = jnp.concatenate([branch, branch], 0).reshape(2 * group, own_count, features)
@@ -198,9 +199,7 @@
         [residual.shape, residual.shape],
     )
 
-    own_rows = add(product[:piece], other_product)
     kept = own_rows[:, :width]
-    came = swap(own_rows[:, width:], "xh")
     first = xh == 0
     weight_grad = jnp.concatenate([jnp.where(first, kept, came), jnp.where(first, came, kept)], 0)
     return (forward[None], received[None], ctx_grad[None], weight_grad[None])

time: 143 us -> 130 us (0.909)
  waiting for transfers between devices: 44.7 us -> 34 us
  local copies, waits for them, and re-layouts: 9.31 us -> 7.44 us
    all_to_all x1, waiting for transfers between devices: 17 us -> 0.01 us  [shards(): branch = lax.all_to_all(branch, ('section', 'y', 'xh'), 0, 0, tiled=True)]
    ppermute x31, waiting for transfers between devices: 27.7 us -> 34 us  [shift(): return lax.ppermute(value, axis, [(i, (i + by) % n) for i in range(n)])]
    convert_element_type x7, other arithmetic: 2.63 us -> 0.95 us  [add(): return (a.astype(F32) + b.astype(F32)).astype(BF16)]
  transfers between devices with their start and end apart: 33 -> 33, of which waited for: 11 -> 10; matrix products, arithmetic and copies ran while one was open for 18% -> 19% of each run, Pallas kernels for 2% -> 1%
where the time goes in v8:
time: 130 us; the launch traced here: 129 us
  starting transfers between devices  62.7 us (48%)
  waiting for transfers between devices  34 us (26%)
  matrix products  10.3 us (8%)
  other arithmetic  9.96 us (8%)
  local copies, waits for them, and re-layouts  7.44 us (6%)
  Pallas kernels  2.98 us (2%)
    ppermute x31, starting transfers between devices, shift(): return lax.ppermute(value, axis, [(i, (i + by) % n) for i in range(n)])  51.3 us
    ppermute x31, waiting for transfers between devices, shift(): return lax.ppermute(value, axis, [(i, (i + by) % n) for i in range(n)])  34 us
    all_to_all x1, starting transfers between devices, shards(): branch = lax.all_to_all(branch, ('section', 'y', 'xh'), 0, 0, tiled=True)  6.07 us
    all_to_all x1, starting transfers between devices, shards(): lax.all_to_all(spread, ('y', 'xh'), 0, 0, tiled=True)  5.31 us
    dot_general x1, matrix products, shards(): lax.dot_general(ctx_flat, block, (((1,), (1,)), ((), ())), preferred_elem...  3.71 us
    dot_general x1, matrix products, shards(): jnp.dot(grad_flat, block, preferred_element_type=F32).astype(BF16)  3.66 us
    pallas_call x2, Pallas kernels, local(): pl.pallas_call(kernel, out_shape=[jax.ShapeDtypeStruct(shape, BF16) for s...  2.98 us
    dot_general x1, matrix products, shards(): lax.dot_general(grad_flat, ctx_flat, (((0,), (0,)), ((), ())), preferred_...  2.97 us
  transfers between devices with their start and end apart: 33, of which 10 were waited for; matrix products, arithmetic and copies ran while one was open for 19% of the time, Pallas kernels for 1%

profile of v8, /device:TPU:2, one launch (start us, length us, event | category | flops | bytes accessed | tf_op | source)
XLA Modules:
  0.0 128.5 jit_solution(14714299346959024083)
XLA Ops:
  0.6 2.2 %collective-permute-start = (bf16[256,384]{1,0:T(8,128)(2,1)}, bf16[256,384]{1,0:T(8,128)(2,1)S(1)}, u32[]{:S(2)}, u32[]{:S(2)}) collective-permute-start(bf16[256,384]{1,0:T(8,128)(2,1)} %bitcast.106), channel_id=1, source_target_pairs={{0,1},{1,0},{2,3},{3,2},{4,5},{5,4},{6,7},{7,6},{8,9},{9,8},{10,11... | collective-permute-start | bytes 589832 | tf_op jit(solution)/shard_map/ppermute | solution.py:18
  2.9 1.0 copy-done
  3.9 1.3 %shard_map.75 = bf16[8,16,1536]{2,1,0:T(8,128)(2,1)} custom-call(s32[2]{0:T(128)S(1)} %pad_add_fusion.at_ref, bf16[16,12288]{1,0:T(8,128)(2,1)S(1)} %bitcast.82), custom_call_target="tpu_custom_call" | custom-call | tf_op jit(solution)/shard_map/pallas_call | solution.py:109
  5.2 5.3 %all-to-all-start = ((bf16[8,16,1536]{2,1,0:T(8,128)(2,1)}), bf16[8,16,1536]{2,1,0:T(8,128)(2,1)S(1)}, u32[]{:S(2)}, u32[]{:S(2)}) async-start(bf16[8,16,1536]{2,1,0:T(8,128)(2,1)} %shard_map.75), calls=%async_computation | async-start | bytes 786432 | tf_op jit(solution)/shard_map/all_to_all | solution.py:155
  10.5 2.7 %dynamic-slice_bitcast_fusion.1 = (bf16[768,384]{1,0:T(8,128)(2,1)}, bf16[768,384]{1,0:T(8,128)(2,1)}, bf16[768,384]{1,0:T(8,128)(2,1)}) fusion(bf16[1,12288,384]{2,1,0:T(8,128)(2,1)} %param.6, s32[]{:T(128)S(6)} %select_n.84, s32[]{:T(128)S(6)} %select_n.79, s32[]{:T(128)S(6)} %select_n.85), kind=kLoop, calls=%fused_computation.21 | loop fusion | bytes 3538956 | tf_op jit(solution)/shard_map/dynamic_slice | solution.py:136
  13.3 2.1 %collective-permute-start.1 = (bf16[256,768]{1,0:T(8,128)(2,1)S(1)}, bf16[256,768]{1,0:T(8,128)(2,1)S(1)}, u32[]{:S(2)}, u32[]{:S(2)}) collective-permute-start(bf16[256,768]{1,0:T(8,128)(2,1)S(1)} %pad_maximum_fusion.1), channel_id=1, source_target_pairs={{0,32},{32,64},{64,96},{96,0},{1,33},{33,65},{65,97},{97,1},{2,34}... | collective-permute-start | bytes 1179656 | tf_op jit(solution)/shard_map/ppermute | solution.py:18
  15.4 1.3 %collective-permute-start.2 = (bf16[256,768]{1,0:T(8,128)(2,1)S(1)}, bf16[256,768]{1,0:T(8,128)(2,1)S(1)}, u32[]{:S(2)}, u32[]{:S(2)}) collective-permute-start(bf16[256,768]{1,0:T(8,128)(2,1)S(1)} %pad_maximum_fusion.1), channel_id=1, source_target_pairs={{0,96},{32,0},{64,32},{96,64},{1,97},{33,1},{65,33},{97,65},{2,98}... | collective-permute-start | bytes 1179656 | tf_op jit(solution)/shard_map/ppermute | solution.py:18
  16.7 0.8 broadcast_select_fusion.2
  17.5 3.4 %collective-permute-start.5 = (bf16[768,384]{1,0:T(8,128)(2,1)}, bf16[768,384]{1,0:T(8,128)(2,1)}, u32[]{:S(2)}, u32[]{:S(2)}) collective-permute-start(bf16[768,384]{1,0:T(8,128)(2,1)} %get-tuple-element.26), channel_id=1, source_target_pairs={{0,1},{1,0},{2,3},{3,2},{4,5},{5,4},{6,7},{7,6},{8,9},{9,8},{10,11... | collective-permute-start | bytes 1769480 | tf_op jit(solution)/shard_map/ppermute | solution.py:18
  20.9 0.2 broadcast_in_dim.39
  21.2 2.0 %collective-permute-start.11 = (bf16[128,1536]{1,0:T(8,128)(2,1)S(1)}, bf16[128,1536]{1,0:T(8,128)(2,1)S(1)}, u32[]{:S(2)}, u32[]{:S(2)}) collective-permute-start(bf16[128,1536]{1,0:T(8,128)(2,1)S(1)} %bitcast.92), channel_id=1, source_target_pairs={{0,2},{2,4},{4,6},{6,8},{8,10},{10,12},{12,14},{14,0},{1,3},{3,5},... | collective-permute-start | bytes 1179656 | tf_op jit(solution)/shard_map/ppermute | solution.py:18
  23.2 4.0 %collective-permute-start.12 = (bf16[128,1536]{1,0:T(8,128)(2,1)S(1)}, bf16[128,1536]{1,0:T(8,128)(2,1)S(1)}, u32[]{:S(2)}, u32[]{:S(2)}) collective-permute-start(bf16[128,1536]{1,0:T(8,128)(2,1)S(1)} %bitcast.93), channel_id=1, source_target_pairs={{0,14},{2,0},{4,2},{6,4},{8,6},{10,8},{12,10},{14,12},{1,15},{3,1}... | collective-permute-start | bytes 1179656 | tf_op jit(solution)/shard_map/ppermute | solution.py:18
  27.2 0.3 broadcast_in_dim.40
  27.5 0.3 collective-permute-start.3
  27.9 3.1 %collective-permute-start.4 = (bf16[128,768]{1,0:T(8,128)(2,1)S(1)}, bf16[128,768]{1,0:T(8,128)(2,1)S(1)}, u32[]{:S(2)}, u32[]{:S(2)}) collective-permute-start(bf16[128,768]{1,0:T(8,128)(2,1)S(1)} %slice.90), channel_id=1, source_target_pairs={{0,96},{32,0},{64,32},{96,64},{1,97},{33,1},{65,33},{97,65},{2,98}... | collective-permute-start | bytes 589832 | tf_op jit(solution)/shard_map/ppermute | solution.py:18
  31.0 3.5 %collective-permute-done.11 = bf16[128,1536]{1,0:T(8,128)(2,1)S(1)} collective-permute-done((bf16[128,1536]{1,0:T(8,128)(2,1)S(1)}, bf16[128,1536]{1,0:T(8,128)(2,1)S(1)}, u32[]{:S(2)}, u32[]{:S(2)}) %collective-permute-start.11) | collective-permute-done | bytes 393248 | tf_op jit(solution)/shard_map/ppermute | solution.py:18
  34.5 3.2 %collective-permute-start.14 = (bf16[128,1536]{1,0:T(8,128)(2,1)S(1)}, bf16[128,1536]{1,0:T(8,128)(2,1)S(1)}, u32[]{:S(2)}, u32[]{:S(2)}) collective-permute-start(bf16[128,1536]{1,0:T(8,128)(2,1)S(1)} %collective-permute-done.12), channel_id=1, source_target_pairs={{0,14},{2,0},{4,2},{6,4},{8,6},{10,8},{12,10},{14,12},{1,15},{3,1}... | collective-permute-start | bytes 1179656 | tf_op jit(solution)/shard_map/ppermute | solution.py:18
  37.9 0.1 collective-permute-start.6
  38.1 7.1 %collective-permute-done.13 = bf16[128,1536]{1,0:T(8,128)(2,1)S(1)} collective-permute-done((bf16[128,1536]{1,0:T(8,128)(2,1)S(1)}, bf16[128,1536]{1,0:T(8,128)(2,1)S(1)}, u32[]{:S(2)}, u32[]{:S(2)}) %collective-permute-start.13) | collective-permute-done | bytes 393248 | tf_op jit(solution)/shard_map/ppermute | solution.py:18
  45.1 3.2 %collective-permute-start.16 = (bf16[128,1536]{1,0:T(8,128)(2,1)S(1)}, bf16[128,1536]{1,0:T(8,128)(2,1)S(1)}, u32[]{:S(2)}, u32[]{:S(2)}) collective-permute-start(bf16[128,1536]{1,0:T(8,128)(2,1)S(1)} %collective-permute-done.14), channel_id=1, source_target_pairs={{0,14},{2,0},{4,2},{6,4},{8,6},{10,8},{12,10},{14,12},{1,15},{3,1}... | collective-permute-start | bytes 1179656 | tf_op jit(solution)/shard_map/ppermute | solution.py:18
  48.5 3.7 %convolution_convert_fusion = bf16[1024,1536]{1,0:T(8,128)(2,1)S(1)} fusion(bf16[1024,768]{1,0:T(8,128)(2,1)S(1)} %bitcast.90, bf16[768,384]{1,0:T(8,128)(2,1)S(1)} %collective-permute-done.6, bf16[768,384]{1,0:T(8,128)(2,1)S(1)} %copy-done.5, bf16[768,384]{1,0:T(8,128)(2,1)} %collective-permute-done.5, bf16[768,384]{1,0:T(8,128)(2,1)S(1)} %copy-done.4), kind=kOutput, calls=%fused_computation.1 | convolution fusion | flops 2426929152 | bytes 7077888 | tf_op jit(solution)/shard_map/dot_general | solution.py:161
  52.2 0.1 dynamic-slice_bitcast_fusion.3
  52.3 0.1 collective-permute-start.7
  52.4 3.2 %collective-permute-start.8 = (bf16[128,768]{1,0:T(8,128)(2,1)S(1)}, bf16[128,768]{1,0:T(8,128)(2,1)S(1)}, u32[]{:S(2)}, u32[]{:S(2)}) collective-permute-start(bf16[128,768]{1,0:T(8,128)(2,1)S(1)} %get-tuple-element.64), channel_id=1, source_target_pairs={{0,14},{2,0},{4,2},{6,4},{8,6},{10,8},{12,10},{14,12},{1,15},{3,1}... | collective-permute-start | bytes 589832 | tf_op jit(solution)/shard_map/ppermute | solution.py:18
  55.7 0.8 collective-permute-done.15
  56.5 0.1 collective-permute-start.17
  56.6 3.3 %collective-permute-start.18 = (bf16[64,1536]{1,0:T(8,128)(2,1)S(1)}, bf16[64,1536]{1,0:T(8,128)(2,1)S(1)}, u32[]{:S(2)}, u32[]{:S(2)}) collective-permute-start(bf16[64,1536]{1,0:T(8,128)(2,1)S(1)} %slice.98), channel_id=1, source_target_pairs={{0,14},{2,0},{4,2},{6,4},{8,6},{10,8},{12,10},{14,12},{1,15},{3,1}... | collective-permute-start | bytes 589832 | tf_op jit(solution)/shard_map/ppermute | solution.py:18
  60.0 1.2 collective-permute-done.7
  61.2 3.4 %collective-permute-start.10 = (bf16[128,1536]{1,0:T(8,128)(2,1)S(1)}, bf16[128,1536]{1,0:T(8,128)(2,1)S(1)}, u32[]{:S(2)}, u32[]{:S(2)}) collective-permute-start(bf16[128,1536]{1,0:T(8,128)(2,1)S(1)} %pad_maximum_fusion.4), channel_id=1, source_target_pairs={{0,14},{2,0},{4,2},{6,4},{8,6},{10,8},{12,10},{14,12},{1,15},{3,1}... | collective-permute-start | bytes 1179656 | tf_op jit(solution)/shard_map/ppermute | solution.py:18
  64.7 0.1 collective-permute-start.9
  64.8 0.9 collective-permute-start.22
  65.8 3.7 %convolution_convert_fusion.1 = bf16[1024,768]{1,0:T(8,128)(2,1)S(1)} fusion(bf16[1024,1536]{1,0:T(8,128)(2,1)S(1)} %bitcast.84, bf16[768,384]{1,0:T(8,128)(2,1)S(1)} %collective-permute-done.6, bf16[768,384]{1,0:T(8,128)(2,1)S(1)} %copy-done.5, bf16[768,384]{1,0:T(8,128)(2,1)} %collective-permute-done.5, bf16[768,384]{1,0:T(8,128)(2,1)S(1)} %copy-done.4), kind=kOutput, calls=%fused_computation.4 | convolution fusion | flops 2426142720 | bytes 7077888 | tf_op jit(solution)/shard_map/dot_general | solution.py:170
  69.4 3.0 %multiply_convert_fusion = bf16[1536,768]{1,0:T(8,128)(2,1)S(1)} fusion(bf16[1024,1536]{1,0:T(8,128)(2,1)S(1)} %bitcast.85, bf16[1024,768]{1,0:T(8,128)(2,1)S(1)} %bitcast.91), kind=kOutput, calls=%fused_computation | convolution fusion | flops 2418278400 | bytes 7077888 | tf_op jit(solution)/shard_map/dot_general | solution.py:174
  72.4 1.4 %collective-permute-done.9 = bf16[128,1536]{1,0:T(8,128)(2,1)S(1)} collective-permute-done((bf16[128,1536]{1,0:T(8,128)(2,1)S(1)}, bf16[128,1536]{1,0:T(8,128)(2,1)S(1)}, u32[]{:S(2)}, u32[]{:S(2)}) %collective-permute-start.9) | collective-permute-done | bytes 393248 | tf_op jit(solution)/shard_map/ppermute | solution.py:18
  73.9 0.1 collective-permute-start.21
  74.0 0.9 constant_dynamic-slice_fusion.3
  74.9 0.3 collective-permute-start.27
  75.2 0.2 fusion.2
  75.4 0.1 collective-permute-start.19
  75.5 3.2 %collective-permute-start.20 = (bf16[128,1536]{1,0:T(8,128)(2,1)S(1)}, bf16[128,1536]{1,0:T(8,128)(2,1)S(1)}, u32[]{:S(2)}, u32[]{:S(2)}) collective-permute-start(bf16[128,1536]{1,0:T(8,128)(2,1)S(1)} %get-tuple-element.51), channel_id=1, source_target_pairs={{0,14},{2,0},{4,2},{6,4},{8,6},{10,8},{12,10},{14,12},{1,15},{3,1}... | collective-permute-start | bytes 1179656 | tf_op jit(solution)/shard_map/ppermute | solution.py:18
  78.8 3.7 %collective-permute-done.27 = bf16[256,384]{1,0:T(8,128)(2,1)S(1)} collective-permute-done((bf16[256,384]{1,0:T(8,128)(2,1)S(1)}, bf16[256,384]{1,0:T(8,128)(2,1)S(1)}, u32[]{:S(2)}, u32[]{:S(2)}) %collective-permute-start.27) | collective-permute-done | bytes 196640 | tf_op jit(solution)/shard_map/ppermute | solution.py:18
  82.5 0.8 pad_maximum_fusion.6
  83.3 6.9 %collective-permute-done.25 = bf16[256,384]{1,0:T(8,128)(2,1)S(1)} collective-permute-done((bf16[256,384]{1,0:T(8,128)(2,1)S(1)}, bf16[256,384]{1,0:T(8,128)(2,1)S(1)}, u32[]{:S(2)}, u32[]{:S(2)}) %collective-permute-start.25) | collective-permute-done | bytes 196640 | tf_op jit(solution)/shard_map/ppermute | solution.py:18
  90.2 0.5 collective-permute-start.28
  90.8 0.2 fusion.4
  91.1 3.2 %collective-permute-start.24 = (bf16[128,1536]{1,0:T(8,128)(2,1)S(1)}, bf16[128,1536]{1,0:T(8,128)(2,1)S(1)}, u32[]{:S(2)}, u32[]{:S(2)}) collective-permute-start(bf16[128,1536]{1,0:T(8,128)(2,1)S(1)} %get-tuple-element.50), channel_id=1, source_target_pairs={{0,14},{2,0},{4,2},{6,4},{8,6},{10,8},{12,10},{14,12},{1,15},{3,1}... | collective-permute-start | bytes 1179656 | tf_op jit(solution)/shard_map/ppermute | solution.py:18
  94.3 0.8 pad_maximum_fusion.5
  95.1 1.5 %collective-permute-start.26 = (bf16[256,768]{1,0:T(8,128)(2,1)}, bf16[256,768]{1,0:T(8,128)(2,1)}, u32[]{:S(2)}, u32[]{:S(2)}) collective-permute-start(bf16[256,768]{1,0:T(8,128)(2,1)} %pad_maximum_fusion.5), channel_id=1, source_target_pairs={{0,32},{32,64},{64,96},{96,0},{1,33},{33,65},{65,97},{97,1},{2,34}... | collective-permute-start | bytes 1179656 | tf_op jit(solution)/shard_map/ppermute | solution.py:18
  96.6 0.3 add_convert_fusion
  96.9 0.9 slice.105
  97.8 2.9 %collective-permute-start.29 = (bf16[768,384]{1,0:T(8,128)(2,1)}, bf16[768,384]{1,0:T(8,128)(2,1)S(1)}, u32[]{:S(2)}, u32[]{:S(2)}) collective-permute-start(bf16[768,384]{1,0:T(8,128)(2,1)} %slice.105), channel_id=1, source_target_pairs={{0,1},{1,0},{2,3},{3,2},{4,5},{5,4},{6,7},{7,6},{8,9},{9,8},{10,11... | collective-permute-start | bytes 1769480 | tf_op jit(solution)/shard_map/ppermute | solution.py:18
  100.7 1.4 %collective-permute-done.23 = bf16[128,1536]{1,0:T(8,128)(2,1)S(1)} collective-permute-done((bf16[128,1536]{1,0:T(8,128)(2,1)S(1)}, bf16[128,1536]{1,0:T(8,128)(2,1)S(1)}, u32[]{:S(2)}, u32[]{:S(2)}) %collective-permute-start.23) | collective-permute-done | bytes 393248 | tf_op jit(solution)/shard_map/ppermute | solution.py:18
  102.1 0.2 fusion.6
  102.2 0.9 pad_maximum_fusion
  103.2 6.1 %all-to-all-start.1 = ((bf16[16,16,1536]{2,1,0:T(8,128)(2,1)}), bf16[16,16,1536]{2,1,0:T(8,128)(2,1)S(1)}, u32[]{:S(2)}, u32[]{:S(2)}) async-start(bf16[16,16,1536]{2,1,0:T(8,128)(2,1)} %bitcast.33), calls=%async_computation.1 | async-start | bytes 1572864 | tf_op jit(solution)/shard_map/all_to_all | solution.py:189
  109.2 6.2 %collective-permute-done.29 = bf16[768,384]{1,0:T(8,128)(2,1)S(1)} collective-permute-done((bf16[768,384]{1,0:T(8,128)(2,1)}, bf16[768,384]{1,0:T(8,128)(2,1)S(1)}, u32[]{:S(2)}, u32[]{:S(2)}) %collective-permute-start.29) | collective-permute-done | bytes 589856 | tf_op jit(solution)/shard_map/ppermute | solution.py:18
  115.5 0.8 copy-done.3
  116.3 1.4 %fusion = f32[256,768]{1,0:T(8,128)S(1)} fusion(bf16[256,768]{1,0:T(8,128)(2,1)} %collective-permute-done.28, bf16[256,768]{1,0:T(8,128)(2,1)} %collective-permute-done.26, bf16[8,1,32,768]{3,2,1,0:T(8,128)(2,1)} %get-tuple-element.58), kind=kLoop, calls=%fused_computation.8 | loop fusion | flops 983040 | bytes 1966080 | tf_op jit(solution)/shard_map/add | solution.py:72
  117.7 3.3 %collective-permute-start.30 = (bf16[256,384]{1,0:T(8,128)(2,1)S(1)}, bf16[256,384]{1,0:T(8,128)(2,1)}, u32[]{:S(2)}, u32[]{:S(2)}) collective-permute-start(bf16[256,384]{1,0:T(8,128)(2,1)S(1)} %slice.122), channel_id=1, source_target_pairs={{0,1},{1,0},{2,3},{3,2},{4,5},{5,4},{6,7},{7,6},{8,9},{9,8},{10,11... | collective-permute-start | bytes 589832 | tf_op jit(solution)/shard_map/ppermute | solution.py:18
  121.0 1.2 broadcast_select_fusion.1
  122.2 1.1 maximum_bitcast_fusion
  123.4 1.9 %collective-permute-done.30 = bf16[256,384]{1,0:T(8,128)(2,1)} collective-permute-done((bf16[256,384]{1,0:T(8,128)(2,1)S(1)}, bf16[256,384]{1,0:T(8,128)(2,1)}, u32[]{:S(2)}, u32[]{:S(2)}) %collective-permute-start.30) | collective-permute-done | bytes 196640 | tf_op jit(solution)/shard_map/ppermute | solution.py:18
  125.2 1.7 %fusion.9 = bf16[1,256,384]{2,1,0:T(8,128)(2,1)} fusion(bf16[256,384]{1,0:T(8,128)(2,1)} %collective-permute-done.30, f32[256,768]{1,0:T(8,128)S(1)} %fusion), kind=kLoop, calls=%fused_computation.51 | loop fusion | flops 294912 | bytes 786432 | tf_op jit(solution)/shard_map/broadcast_in_dim | solution.py:205
  126.9 1.7 %shard_map.76 = (bf16[16,12288]{1,0:T(8,128)(2,1)}, bf16[16,12288]{1,0:T(8,128)(2,1)}) custom-call(s32[2]{0:T(128)S(1)} %pad_add_fusion.at_ref, bf16[2,8,16,1536]{3,2,1,0:T(8,128)(2,1)S(1)} %bitcast.81, bf16[16,12288]{1,0:T(8,128)(2,1)S(1)} %bitcast.83, bf16[16,12288]{1,0:T(8,128)(2,1)S(1)} %collective-permute-done.22.early_ref), custom_call_target="tpu_custom_call" | custom-call | tf_op jit(solution)/shard_map/pallas_call | solution.py:109
  (74 shorter events, 1.3 us)
Async XLA Ops:
  0.6 12.6 %collective-permute-start = (bf16[256,384]{1,0:T(8,128)(2,1)}, bf16[256,384]{1,0:T(8,128)(2,1)S(1)}, u32[]{:S(2)}, u32[]{:S(2)}) collective-permute-start(bf16[256,384]{1,0:T(8,128)(2,1)} %bitcast.106), channel_id=1, source_target_pairs={{0,1},{1,0},{2,3},{3,2},{4,5},{5,4},{6,7},{7,6},{8,9},{9,8},{10,11... | collective-permute-start | bytes 589832 | tf_op jit(solution)/shard_map/ppermute | solution.py:18
  2.9 1.0 copy-start
  3.9 9.3 %copy-start.7 = (bf16[1,256,384]{2,1,0:T(8,128)(2,1)S(1)}, bf16[1,256,384]{2,1,0:T(8,128)(2,1)}, u32[]{:S(2)}) copy-start(bf16[1,256,384]{2,1,0:T(8,128)(2,1)} %param.5) | copy-start | bytes 589828
  3.9 12.8 %copy-start.1 = (bf16[1,16,12288]{2,1,0:T(8,128)(2,1)S(1)}, bf16[1,16,12288]{2,1,0:T(8,128)(2,1)}, u32[]{:S(2)}) copy-start(bf16[1,16,12288]{2,1,0:T(8,128)(2,1)} %param.7) | copy-start | bytes 1179652
  3.9 12.8 %copy-start.2 = (bf16[1,16,12288]{2,1,0:T(8,128)(2,1)S(1)}, bf16[1,16,12288]{2,1,0:T(8,128)(2,1)}, u32[]{:S(2)}) copy-start(bf16[1,16,12288]{2,1,0:T(8,128)(2,1)} %param.4) | copy-start | bytes 1179652
  5.2 15.9 %all-to-all-start = ((bf16[8,16,1536]{2,1,0:T(8,128)(2,1)}), bf16[8,16,1536]{2,1,0:T(8,128)(2,1)S(1)}, u32[]{:S(2)}, u32[]{:S(2)}) async-start(bf16[8,16,1536]{2,1,0:T(8,128)(2,1)} %shard_map.75), calls=%async_computation | async-start | bytes 786432 | tf_op jit(solution)/shard_map/all_to_all | solution.py:155
  13.3 14.2 %collective-permute-start.1 = (bf16[256,768]{1,0:T(8,128)(2,1)S(1)}, bf16[256,768]{1,0:T(8,128)(2,1)S(1)}, u32[]{:S(2)}, u32[]{:S(2)}) collective-permute-start(bf16[256,768]{1,0:T(8,128)(2,1)S(1)} %pad_maximum_fusion.1), channel_id=1, source_target_pairs={{0,32},{32,64},{64,96},{96,0},{1,33},{33,65},{65,97},{97,1},{2,34}... | collective-permute-start | bytes 1179656 | tf_op jit(solution)/shard_map/ppermute | solution.py:18
  15.4 12.5 %collective-permute-start.2 = (bf16[256,768]{1,0:T(8,128)(2,1)S(1)}, bf16[256,768]{1,0:T(8,128)(2,1)S(1)}, u32[]{:S(2)}, u32[]{:S(2)}) collective-permute-start(bf16[256,768]{1,0:T(8,128)(2,1)S(1)} %pad_maximum_fusion.1), channel_id=1, source_target_pairs={{0,96},{32,0},{64,32},{96,64},{1,97},{33,1},{65,33},{97,65},{2,98}... | collective-permute-start | bytes 1179656 | tf_op jit(solution)/shard_map/ppermute | solution.py:18
  17.5 20.4 %collective-permute-start.5 = (bf16[768,384]{1,0:T(8,128)(2,1)}, bf16[768,384]{1,0:T(8,128)(2,1)}, u32[]{:S(2)}, u32[]{:S(2)}) collective-permute-start(bf16[768,384]{1,0:T(8,128)(2,1)} %get-tuple-element.26), channel_id=1, source_target_pairs={{0,1},{1,0},{2,3},{3,2},{4,5},{5,4},{6,7},{7,6},{8,9},{9,8},{10,11... | collective-permute-start | bytes 1769480 | tf_op jit(solution)/shard_map/ppermute | solution.py:18
  21.2 13.4 %collective-permute-start.11 = (bf16[128,1536]{1,0:T(8,128)(2,1)S(1)}, bf16[128,1536]{1,0:T(8,128)(2,1)S(1)}, u32[]{:S(2)}, u32[]{:S(2)}) collective-permute-start(bf16[128,1536]{1,0:T(8,128)(2,1)S(1)} %bitcast.92), channel_id=1, source_target_pairs={{0,2},{2,4},{4,6},{6,8},{8,10},{10,12},{12,14},{14,0},{1,3},{3,5},... | collective-permute-start | bytes 1179656 | tf_op jit(solution)/shard_map/ppermute | solution.py:18
  23.2 11.4 %collective-permute-start.12 = (bf16[128,1536]{1,0:T(8,128)(2,1)S(1)}, bf16[128,1536]{1,0:T(8,128)(2,1)S(1)}, u32[]{:S(2)}, u32[]{:S(2)}) collective-permute-start(bf16[128,1536]{1,0:T(8,128)(2,1)S(1)} %bitcast.93), channel_id=1, source_target_pairs={{0,14},{2,0},{4,2},{6,4},{8,6},{10,8},{12,10},{14,12},{1,15},{3,1}... | collective-permute-start | bytes 1179656 | tf_op jit(solution)/shard_map/ppermute | solution.py:18
  27.5 10.4 %collective-permute-start.3 = (bf16[128,768]{1,0:T(8,128)(2,1)S(1)}, bf16[128,768]{1,0:T(8,128)(2,1)S(1)}, u32[]{:S(2)}, u32[]{:S(2)}) collective-permute-start(bf16[128,768]{1,0:T(8,128)(2,1)S(1)} %slice.89), channel_id=1, source_target_pairs={{0,32},{32,64},{64,96},{96,0},{1,33},{33,65},{65,97},{97,1},{2,34}... | collective-permute-start | bytes 589832 | tf_op jit(solution)/shard_map/ppermute | solution.py:18
  27.9 10.1 %collective-permute-start.4 = (bf16[128,768]{1,0:T(8,128)(2,1)S(1)}, bf16[128,768]{1,0:T(8,128)(2,1)S(1)}, u32[]{:S(2)}, u32[]{:S(2)}) collective-permute-start(bf16[128,768]{1,0:T(8,128)(2,1)S(1)} %slice.90), channel_id=1, source_target_pairs={{0,96},{32,0},{64,32},{96,64},{1,97},{33,1},{65,33},{97,65},{2,98}... | collective-permute-start | bytes 589832 | tf_op jit(solution)/shard_map/ppermute | solution.py:18
  30.9 17.5 %copy-start.4 = (bf16[768,384]{1,0:T(8,128)(2,1)S(1)}, bf16[768,384]{1,0:T(8,128)(2,1)}, u32[]{:S(2)}) copy-start(bf16[768,384]{1,0:T(8,128)(2,1)} %get-tuple-element.46) | copy-start | bytes 1769476
  30.9 17.5 %copy-start.5 = (bf16[768,384]{1,0:T(8,128)(2,1)S(1)}, bf16[768,384]{1,0:T(8,128)(2,1)}, u32[]{:S(2)}) copy-start(bf16[768,384]{1,0:T(8,128)(2,1)} %get-tuple-element.48) | copy-start | bytes 1769476
  34.5 10.6 %collective-permute-start.13 = (bf16[128,1536]{1,0:T(8,128)(2,1)S(1)}, bf16[128,1536]{1,0:T(8,128)(2,1)S(1)}, u32[]{:S(2)}, u32[]{:S(2)}) collective-permute-start(bf16[128,1536]{1,0:T(8,128)(2,1)S(1)} %collective-permute-done.11), channel_id=1, source_target_pairs={{0,2},{2,4},{4,6},{6,8},{8,10},{10,12},{12,14},{14,0},{1,3},{3,5},... | collective-permute-start | bytes 1179656 | tf_op jit(solution)/shard_map/ppermute | solution.py:18
  34.5 10.6 %collective-permute-start.14 = (bf16[128,1536]{1,0:T(8,128)(2,1)S(1)}, bf16[128,1536]{1,0:T(8,128)(2,1)S(1)}, u32[]{:S(2)}, u32[]{:S(2)}) collective-permute-start(bf16[128,1536]{1,0:T(8,128)(2,1)S(1)} %collective-permute-done.12), channel_id=1, source_target_pairs={{0,14},{2,0},{4,2},{6,4},{8,6},{10,8},{12,10},{14,12},{1,15},{3,1}... | collective-permute-start | bytes 1179656 | tf_op jit(solution)/shard_map/ppermute | solution.py:18
  37.9 10.6 %collective-permute-start.6 = (bf16[768,384]{1,0:T(8,128)(2,1)}, bf16[768,384]{1,0:T(8,128)(2,1)S(1)}, u32[]{:S(2)}, u32[]{:S(2)}) collective-permute-start(bf16[768,384]{1,0:T(8,128)(2,1)} %collective-permute-done.5), channel_id=1, source_target_pairs={{0,16},{16,0},{1,17},{17,1},{2,18},{18,2},{3,19},{19,3},{4,20},{20... | collective-permute-start | bytes 1769480 | tf_op jit(solution)/shard_map/ppermute | solution.py:18
  45.1 11.3 %collective-permute-start.15 = (bf16[128,1536]{1,0:T(8,128)(2,1)S(1)}, bf16[128,1536]{1,0:T(8,128)(2,1)S(1)}, u32[]{:S(2)}, u32[]{:S(2)}) collective-permute-start(bf16[128,1536]{1,0:T(8,128)(2,1)S(1)} %collective-permute-done.13), channel_id=1, source_target_pairs={{0,2},{2,4},{4,6},{6,8},{8,10},{10,12},{12,14},{14,0},{1,3},{3,5},... | collective-permute-start | bytes 1179656 | tf_op jit(solution)/shard_map/ppermute | solution.py:18
  45.1 11.4 %collective-permute-start.16 = (bf16[128,1536]{1,0:T(8,128)(2,1)S(1)}, bf16[128,1536]{1,0:T(8,128)(2,1)S(1)}, u32[]{:S(2)}, u32[]{:S(2)}) collective-permute-start(bf16[128,1536]{1,0:T(8,128)(2,1)S(1)} %collective-permute-done.14), channel_id=1, source_target_pairs={{0,14},{2,0},{4,2},{6,4},{8,6},{10,8},{12,10},{14,12},{1,15},{3,1}... | collective-permute-start | bytes 1179656 | tf_op jit(solution)/shard_map/ppermute | solution.py:18
  52.3 12.5 %copy-start.6 = (bf16[16,12288]{1,0:T(8,128)(2,1)S(1)}, bf16[16,12288]{1,0:T(8,128)(2,1)}, u32[]{:S(2)}) copy-start(bf16[16,12288]{1,0:T(8,128)(2,1)} %broadcast_select_fusion.2) | copy-start | bytes 1179652
  52.3 8.8 %collective-permute-start.7 = (bf16[128,768]{1,0:T(8,128)(2,1)S(1)}, bf16[128,768]{1,0:T(8,128)(2,1)S(1)}, u32[]{:S(2)}, u32[]{:S(2)}) collective-permute-start(bf16[128,768]{1,0:T(8,128)(2,1)S(1)} %get-tuple-element.65), channel_id=1, source_target_pairs={{0,2},{2,4},{4,6},{6,8},{8,10},{10,12},{12,14},{14,0},{1,3},{3,5},... | collective-permute-start | bytes 589832 | tf_op jit(solution)/shard_map/ppermute | solution.py:18
  52.4 8.7 %collective-permute-start.8 = (bf16[128,768]{1,0:T(8,128)(2,1)S(1)}, bf16[128,768]{1,0:T(8,128)(2,1)S(1)}, u32[]{:S(2)}, u32[]{:S(2)}) collective-permute-start(bf16[128,768]{1,0:T(8,128)(2,1)S(1)} %get-tuple-element.64), channel_id=1, source_target_pairs={{0,14},{2,0},{4,2},{6,4},{8,6},{10,8},{12,10},{14,12},{1,15},{3,1}... | collective-permute-start | bytes 589832 | tf_op jit(solution)/shard_map/ppermute | solution.py:18
  56.5 9.2 %collective-permute-start.17 = (bf16[64,1536]{1,0:T(8,128)(2,1)S(1)}, bf16[64,1536]{1,0:T(8,128)(2,1)S(1)}, u32[]{:S(2)}, u32[]{:S(2)}) collective-permute-start(bf16[64,1536]{1,0:T(8,128)(2,1)S(1)} %slice.97), channel_id=1, source_target_pairs={{0,2},{2,4},{4,6},{6,8},{8,10},{10,12},{12,14},{14,0},{1,3},{3,5},... | collective-permute-start | bytes 589832 | tf_op jit(solution)/shard_map/ppermute | solution.py:18
  56.6 9.1 %collective-permute-start.18 = (bf16[64,1536]{1,0:T(8,128)(2,1)S(1)}, bf16[64,1536]{1,0:T(8,128)(2,1)S(1)}, u32[]{:S(2)}, u32[]{:S(2)}) collective-permute-start(bf16[64,1536]{1,0:T(8,128)(2,1)S(1)} %slice.98), channel_id=1, source_target_pairs={{0,14},{2,0},{4,2},{6,4},{8,6},{10,8},{12,10},{14,12},{1,15},{3,1}... | collective-permute-start | bytes 589832 | tf_op jit(solution)/shard_map/ppermute | solution.py:18
  61.2 11.2 %collective-permute-start.10 = (bf16[128,1536]{1,0:T(8,128)(2,1)S(1)}, bf16[128,1536]{1,0:T(8,128)(2,1)S(1)}, u32[]{:S(2)}, u32[]{:S(2)}) collective-permute-start(bf16[128,1536]{1,0:T(8,128)(2,1)S(1)} %pad_maximum_fusion.4), channel_id=1, source_target_pairs={{0,14},{2,0},{4,2},{6,4},{8,6},{10,8},{12,10},{14,12},{1,15},{3,1}... | collective-permute-start | bytes 1179656 | tf_op jit(solution)/shard_map/ppermute | solution.py:18
  64.7 9.1 %collective-permute-start.9 = (bf16[128,1536]{1,0:T(8,128)(2,1)S(1)}, bf16[128,1536]{1,0:T(8,128)(2,1)S(1)}, u32[]{:S(2)}, u32[]{:S(2)}) collective-permute-start(bf16[128,1536]{1,0:T(8,128)(2,1)S(1)} %pad_maximum_fusion.3), channel_id=1, source_target_pairs={{0,2},{2,4},{4,6},{6,8},{8,10},{10,12},{12,14},{14,0},{1,3},{3,5},... | collective-permute-start | bytes 1179656 | tf_op jit(solution)/shard_map/ppermute | solution.py:18
  64.8 25.9 %collective-permute-start.22 = (bf16[16,12288]{1,0:T(8,128)(2,1)S(1)}, bf16[16,12288]{1,0:T(8,128)(2,1)S(1)}, u32[]{:S(2)}, u32[]{:S(2)}) collective-permute-start(bf16[16,12288]{1,0:T(8,128)(2,1)S(1)} %copy-done.6), channel_id=1, source_target_pairs={{0,128},{128,0},{1,129},{129,1},{2,130},{130,2},{3,131},{131,3},{4... | collective-permute-start | bytes 1179656 | tf_op jit(solution)/shard_map/ppermute | solution.py:18
  73.9 16.9 %collective-permute-start.21 = (bf16[768,768]{1,0:T(8,128)(2,1)S(1)}, bf16[768,768]{1,0:T(8,128)(2,1)S(1)}, u32[]{:S(2)}, u32[]{:S(2)}) collective-permute-start(bf16[768,768]{1,0:T(8,128)(2,1)S(1)} %slice.77), channel_id=1, source_target_pairs={{0,16},{16,0},{1,17},{17,1},{2,18},{18,2},{3,19},{19,3},{4,20},{20... | collective-permute-start | bytes 3538952 | tf_op jit(solution)/shard_map/ppermute | solution.py:18
  74.9 7.6 %collective-permute-start.27 = (bf16[256,384]{1,0:T(8,128)(2,1)S(1)}, bf16[256,384]{1,0:T(8,128)(2,1)S(1)}, u32[]{:S(2)}, u32[]{:S(2)}) collective-permute-start(bf16[256,384]{1,0:T(8,128)(2,1)S(1)} %get-tuple-element.62), channel_id=1, source_target_pairs={{0,96},{32,0},{64,32},{96,64},{1,97},{33,1},{65,33},{97,65},{2,98}... | collective-permute-start | bytes 589832 | tf_op jit(solution)/shard_map/ppermute | solution.py:18
  75.4 15.3 %collective-permute-start.19 = (bf16[128,1536]{1,0:T(8,128)(2,1)S(1)}, bf16[128,1536]{1,0:T(8,128)(2,1)S(1)}, u32[]{:S(2)}, u32[]{:S(2)}) collective-permute-start(bf16[128,1536]{1,0:T(8,128)(2,1)S(1)} %get-tuple-element.52), channel_id=1, source_target_pairs={{0,2},{2,4},{4,6},{6,8},{8,10},{10,12},{12,14},{14,0},{1,3},{3,5},... | collective-permute-start | bytes 1179656 | tf_op jit(solution)/shard_map/ppermute | solution.py:18
  75.5 15.3 %collective-permute-start.20 = (bf16[128,1536]{1,0:T(8,128)(2,1)S(1)}, bf16[128,1536]{1,0:T(8,128)(2,1)S(1)}, u32[]{:S(2)}, u32[]{:S(2)}) collective-permute-start(bf16[128,1536]{1,0:T(8,128)(2,1)S(1)} %get-tuple-element.51), channel_id=1, source_target_pairs={{0,14},{2,0},{4,2},{6,4},{8,6},{10,8},{12,10},{14,12},{1,15},{3,1}... | collective-permute-start | bytes 1179656 | tf_op jit(solution)/shard_map/ppermute | solution.py:18
  82.5 7.7 %collective-permute-start.25 = (bf16[256,384]{1,0:T(8,128)(2,1)S(1)}, bf16[256,384]{1,0:T(8,128)(2,1)S(1)}, u32[]{:S(2)}, u32[]{:S(2)}) collective-permute-start(bf16[256,384]{1,0:T(8,128)(2,1)S(1)} %get-tuple-element.63), channel_id=1, source_target_pairs={{0,32},{32,64},{64,96},{96,0},{1,33},{33,65},{65,97},{97,1},{2,34}... | collective-permute-start | bytes 589832 | tf_op jit(solution)/shard_map/ppermute | solution.py:18
  90.2 19.0 %collective-permute-start.28 = (bf16[256,768]{1,0:T(8,128)(2,1)}, bf16[256,768]{1,0:T(8,128)(2,1)}, u32[]{:S(2)}, u32[]{:S(2)}) collective-permute-start(bf16[256,768]{1,0:T(8,128)(2,1)} %pad_maximum_fusion.6), channel_id=1, source_target_pairs={{0,96},{32,0},{64,32},{96,64},{1,97},{33,1},{65,33},{97,65},{2,98}... | collective-permute-start | bytes 1179656 | tf_op jit(solution)/shard_map/ppermute | solution.py:18
  91.0 11.1 %collective-permute-start.23 = (bf16[128,1536]{1,0:T(8,128)(2,1)S(1)}, bf16[128,1536]{1,0:T(8,128)(2,1)S(1)}, u32[]{:S(2)}, u32[]{:S(2)}) collective-permute-start(bf16[128,1536]{1,0:T(8,128)(2,1)S(1)} %get-tuple-element.49), channel_id=1, source_target_pairs={{0,2},{2,4},{4,6},{6,8},{8,10},{10,12},{12,14},{14,0},{1,3},{3,5},... | collective-permute-start | bytes 1179656 | tf_op jit(solution)/shard_map/ppermute | solution.py:18
  91.1 11.0 %collective-permute-start.24 = (bf16[128,1536]{1,0:T(8,128)(2,1)S(1)}, bf16[128,1536]{1,0:T(8,128)(2,1)S(1)}, u32[]{:S(2)}, u32[]{:S(2)}) collective-permute-start(bf16[128,1536]{1,0:T(8,128)(2,1)S(1)} %get-tuple-element.50), channel_id=1, source_target_pairs={{0,14},{2,0},{4,2},{6,4},{8,6},{10,8},{12,10},{14,12},{1,15},{3,1}... | collective-permute-start | bytes 1179656 | tf_op jit(solution)/shard_map/ppermute | solution.py:18
  95.1 14.2 %collective-permute-start.26 = (bf16[256,768]{1,0:T(8,128)(2,1)}, bf16[256,768]{1,0:T(8,128)(2,1)}, u32[]{:S(2)}, u32[]{:S(2)}) collective-permute-start(bf16[256,768]{1,0:T(8,128)(2,1)} %pad_maximum_fusion.5), channel_id=1, source_target_pairs={{0,32},{32,64},{64,96},{96,0},{1,33},{33,65},{65,97},{97,1},{2,34}... | collective-permute-start | bytes 1179656 | tf_op jit(solution)/shard_map/ppermute | solution.py:18
  97.8 17.6 %collective-permute-start.29 = (bf16[768,384]{1,0:T(8,128)(2,1)}, bf16[768,384]{1,0:T(8,128)(2,1)S(1)}, u32[]{:S(2)}, u32[]{:S(2)}) collective-permute-start(bf16[768,384]{1,0:T(8,128)(2,1)} %slice.105), channel_id=1, source_target_pairs={{0,1},{1,0},{2,3},{3,2},{4,5},{5,4},{6,7},{7,6},{8,9},{9,8},{10,11... | collective-permute-start | bytes 1769480 | tf_op jit(solution)/shard_map/ppermute | solution.py:18
  103.2 22.1 %all-to-all-start.1 = ((bf16[16,16,1536]{2,1,0:T(8,128)(2,1)}), bf16[16,16,1536]{2,1,0:T(8,128)(2,1)S(1)}, u32[]{:S(2)}, u32[]{:S(2)}) async-start(bf16[16,16,1536]{2,1,0:T(8,128)(2,1)} %bitcast.33), calls=%async_computation.1 | async-start | bytes 1572864 | tf_op jit(solution)/shard_map/all_to_all | solution.py:189
  115.5 0.8 copy-start.3
  117.7 7.5 %collective-permute-start.30 = (bf16[256,384]{1,0:T(8,128)(2,1)S(1)}, bf16[256,384]{1,0:T(8,128)(2,1)}, u32[]{:S(2)}, u32[]{:S(2)}) collective-permute-start(bf16[256,384]{1,0:T(8,128)(2,1)S(1)} %slice.122), channel_id=1, source_target_pairs={{0,1},{1,0},{2,3},{3,2},{4,5},{5,4},{6,7},{7,6},{8,9},{9,8},{10,11... | collective-permute-start | bytes 589832 | tf_op jit(solution)/shard_map/ppermute | solution.py:18

commit v9 on v8

--- a/solution.py
+++ b/solution.py
@@ -171,18 +171,20 @@
     *step, partial_ctx = tie(*step, partial_ctx)
     step = ring.send(step)
     norm_factor = 1.0 / math.sqrt(tokens * n_core)
-    product = lax.dot_general(grad_flat, ctx_flat, (((0,), (0,)), ((), ())), preferred_element_type=F32)
-    product, partial_ctx = tie((norm_factor * product).astype(BF16), partial_ctx)
+
+    def for_features(features_of):
+        product = lax.dot_general(grad_flat, features_of, (((0,), (0,)), ((), ())), preferred_element_type=F32)
+        return (norm_factor * product).astype(BF16)
+
+    own_product = for_features(ctx_flat[:, :width])
+    partner_product = swap(for_features(ctx_flat[:, width:]), "xh")
+    other_product = swap(own_product[piece:], "core")
     partial_ctx = partial_ctx.reshape(n_z, n_y, z_tokens, 2 * width)
     ctx_ring = ring_steps(lambda away: pick(partial_ctx, wrap(y + away, n_y), 1).reshape(group_tokens, 2 * width), "y")
-    ctx_step = next(ctx_ring)
-    other_product = swap(product[piece:], "core")
-    *step, other_product, early = tie(*step, other_product, early)
+    *step, ctx_low, ctx_high, other_product, early = tie(*step, *next(ctx_ring), other_product, early)
     step = ring.send(step)
-    ctx_step = ctx_ring.send(ctx_step)
-    own_rows = add(product[:piece], other_product)
-    came = swap(own_rows[:, width:], "xh")
-    *ctx_step, came = tie(*ctx_step, came)
+    ctx_step = ctx_ring.send((ctx_low, ctx_high))
+    *ctx_step, partner_product = tie(*ctx_step, partner_product)
     branch = ring.send(step).astype(BF16)
     branch = branch.reshape(1, group, own_count, features)
     branch = jnp.concatenate([branch, branch], 0).reshape(2 * group, own_count, features)
@@ -190,7 +192,8 @@
 
     summed = ctx_ring.send(ctx_step)
     other_ctx = swap(summed[:, width:].astype(BF16), "xh")
-    branch, other_ctx = tie(branch, other_ctx)
+    other_partner = swap(partner_product[piece:], "core")
+    branch, other_ctx, other_partner = tie(branch, other_ctx, other_partner)
     ctx_grad = add(summed[:, :width], other_ctx)
     forward, received = local(
         functools.partial(finish_kernel, sizes),
@@ -199,7 +202,8 @@
         [residual.shape, residual.shape],
     )
 
-    kept = own_rows[:, :width]
+    kept = add(own_product[:piece], other_product)
+    came = add(partner_product[:piece], other_partner)
     first = xh == 0
     weight_grad = jnp.concatenate([jnp.where(first, kept, came), jnp.where(first, came, kept)], 0)
     return (forward[None], received[None], ctx_grad[None], weight_grad[None])

time: 130 us -> 133 us (1.023)
  starting transfers between devices: 62.7 us -> 65.9 us
  other arithmetic: 9.96 us -> 7.82 us
  matrix products: 10.3 us -> 12.1 us
    ppermute x31 -> x32, starting transfers between devices: 51.3 us -> 54.4 us  [shift(): return lax.ppermute(value, axis, [(i, (i + by) % n) for i in range(n)])]
    dot_general x1 -> x2, matrix products: 2.97 us -> 4.71 us  [for_features(): lax.dot_general(grad_flat, features_of, (((0,), (0,)), ((), ())), preferr...]
    unnamed x16 -> x22, local copies, waits for them, and re-layouts: 1.83 us -> 2.76 us
    ppermute x31 -> x32, waiting for transfers between devices: 34 us -> 33.7 us  [shift(): return lax.ppermute(value, axis, [(i, (i + by) % n) for i in range(n)])]
  transfers between devices with their start and end apart: 33 -> 34, of which waited for: 10 -> 10; matrix products, arithmetic and copies ran while one was open for 19% -> 16% of each run, Pallas kernels for 1% -> 1%
where the time goes in v9:
time: 133 us; the launch traced here: 132 us
  starting transfers between devices  65.9 us (50%)
  waiting for transfers between devices  33.7 us (25%)
  matrix products  12.1 us (9%)
  local copies, waits for them, and re-layouts  7.93 us (6%)
  other arithmetic  7.82 us (6%)
  Pallas kernels  2.98 us (2%)
    ppermute x32, starting transfers between devices, shift(): return lax.ppermute(value, axis, [(i, (i + by) % n) for i in range(n)])  54.4 us
    ppermute x32, waiting for transfers between devices, shift(): return lax.ppermute(value, axis, [(i, (i + by) % n) for i in range(n)])  33.7 us
    all_to_all x1, starting transfers between devices, shards(): branch = lax.all_to_all(branch, ('section', 'y', 'xh'), 0, 0, tiled=True)  6 us
    all_to_all x1, starting transfers between devices, shards(): lax.all_to_all(spread, ('y', 'xh'), 0, 0, tiled=True)  5.44 us
    dot_general x2, matrix products, for_features(): lax.dot_general(grad_flat, features_of, (((0,), (0,)), ((), ())), preferr...  4.71 us
    dot_general x1, matrix products, shards(): lax.dot_general(ctx_flat, block, (((1,), (1,)), ((), ())), preferred_elem...  3.71 us
    dot_general x1, matrix products, shards(): jnp.dot(grad_flat, block, preferred_element_type=F32).astype(BF16)  3.66 us
    pallas_call x2, Pallas kernels, local(): pl.pallas_call(kernel, out_shape=[jax.ShapeDtypeStruct(shape, BF16) for s...  2.98 us
  transfers between devices with their start and end apart: 34, of which 10 were waited for; matrix products, arithmetic and copies ran while one was open for 16% of the time, Pallas kernels for 1%

profile of v9, /device:TPU:2, one launch (start us, length us, event | category | flops | bytes accessed | tf_op | source)
XLA Modules:
  0.0 131.6 jit_solution(4567468388234915744)
XLA Ops:
  0.6 2.2 %collective-permute-start = (bf16[256,384]{1,0:T(8,128)(2,1)}, bf16[256,384]{1,0:T(8,128)(2,1)S(1)}, u32[]{:S(2)}, u32[]{:S(2)}) collective-permute-start(bf16[256,384]{1,0:T(8,128)(2,1)} %bitcast.108), channel_id=1, source_target_pairs={{0,1},{1,0},{2,3},{3,2},{4,5},{5,4},{6,7},{7,6},{8,9},{9,8},{10,11... | collective-permute-start | bytes 589832 | tf_op jit(solution)/shard_map/ppermute | solution.py:18
  2.9 1.0 copy-done
  3.9 1.3 %shard_map.75 = bf16[8,16,1536]{2,1,0:T(8,128)(2,1)} custom-call(s32[2]{0:T(128)S(1)} %pad_add_fusion.at_ref, bf16[16,12288]{1,0:T(8,128)(2,1)S(1)} %bitcast.82), custom_call_target="tpu_custom_call" | custom-call | tf_op jit(solution)/shard_map/pallas_call | solution.py:109
  5.2 5.4 %all-to-all-start = ((bf16[8,16,1536]{2,1,0:T(8,128)(2,1)}), bf16[8,16,1536]{2,1,0:T(8,128)(2,1)S(1)}, u32[]{:S(2)}, u32[]{:S(2)}) async-start(bf16[8,16,1536]{2,1,0:T(8,128)(2,1)} %shard_map.75), calls=%async_computation | async-start | bytes 786432 | tf_op jit(solution)/shard_map/all_to_all | solution.py:155
  10.7 2.8 %dynamic-slice_bitcast_fusion.1 = (bf16[768,384]{1,0:T(8,128)(2,1)}, bf16[768,384]{1,0:T(8,128)(2,1)}, bf16[768,384]{1,0:T(8,128)(2,1)}) fusion(bf16[1,12288,384]{2,1,0:T(8,128)(2,1)} %param.6, s32[]{:T(128)S(6)} %select_n.84, s32[]{:T(128)S(6)} %select_n.79, s32[]{:T(128)S(6)} %select_n.85), kind=kLoop, calls=%fused_computation.27 | loop fusion | bytes 3538956 | tf_op jit(solution)/shard_map/dynamic_slice | solution.py:136
  13.5 2.1 %collective-permute-start.1 = (bf16[256,768]{1,0:T(8,128)(2,1)S(1)}, bf16[256,768]{1,0:T(8,128)(2,1)S(1)}, u32[]{:S(2)}, u32[]{:S(2)}) collective-permute-start(bf16[256,768]{1,0:T(8,128)(2,1)S(1)} %pad_maximum_fusion.1), channel_id=1, source_target_pairs={{0,32},{32,64},{64,96},{96,0},{1,33},{33,65},{65,97},{97,1},{2,34}... | collective-permute-start | bytes 1179656 | tf_op jit(solution)/shard_map/ppermute | solution.py:18
  15.6 1.3 collective-permute-start.2
  16.9 0.8 broadcast_select_fusion.2
  17.7 3.4 %collective-permute-start.5 = (bf16[768,384]{1,0:T(8,128)(2,1)}, bf16[768,384]{1,0:T(8,128)(2,1)}, u32[]{:S(2)}, u32[]{:S(2)}) collective-permute-start(bf16[768,384]{1,0:T(8,128)(2,1)} %get-tuple-element.27), channel_id=1, source_target_pairs={{0,1},{1,0},{2,3},{3,2},{4,5},{5,4},{6,7},{7,6},{8,9},{9,8},{10,11... | collective-permute-start | bytes 1769480 | tf_op jit(solution)/shard_map/ppermute | solution.py:18
  21.1 0.2 broadcast_in_dim.39
  21.4 2.0 %collective-permute-start.11 = (bf16[128,1536]{1,0:T(8,128)(2,1)S(1)}, bf16[128,1536]{1,0:T(8,128)(2,1)S(1)}, u32[]{:S(2)}, u32[]{:S(2)}) collective-permute-start(bf16[128,1536]{1,0:T(8,128)(2,1)S(1)} %bitcast.94), channel_id=1, source_target_pairs={{0,2},{2,4},{4,6},{6,8},{8,10},{10,12},{12,14},{14,0},{1,3},{3,5},... | collective-permute-start | bytes 1179656 | tf_op jit(solution)/shard_map/ppermute | solution.py:18
  23.4 4.0 %collective-permute-start.12 = (bf16[128,1536]{1,0:T(8,128)(2,1)S(1)}, bf16[128,1536]{1,0:T(8,128)(2,1)S(1)}, u32[]{:S(2)}, u32[]{:S(2)}) collective-permute-start(bf16[128,1536]{1,0:T(8,128)(2,1)S(1)} %bitcast.95), channel_id=1, source_target_pairs={{0,14},{2,0},{4,2},{6,4},{8,6},{10,8},{12,10},{14,12},{1,15},{3,1}... | collective-permute-start | bytes 1179656 | tf_op jit(solution)/shard_map/ppermute | solution.py:18
  27.4 0.3 broadcast_in_dim.40
  27.7 0.3 collective-permute-start.3
  28.1 3.1 %collective-permute-start.4 = (bf16[128,768]{1,0:T(8,128)(2,1)S(1)}, bf16[128,768]{1,0:T(8,128)(2,1)S(1)}, u32[]{:S(2)}, u32[]{:S(2)}) collective-permute-start(bf16[128,768]{1,0:T(8,128)(2,1)S(1)} %slice.98), channel_id=1, source_target_pairs={{0,96},{32,0},{64,32},{96,64},{1,97},{33,1},{65,33},{97,65},{2,98}... | collective-permute-start | bytes 589832 | tf_op jit(solution)/shard_map/ppermute | solution.py:18
  31.2 3.5 %collective-permute-done.11 = bf16[128,1536]{1,0:T(8,128)(2,1)S(1)} collective-permute-done((bf16[128,1536]{1,0:T(8,128)(2,1)S(1)}, bf16[128,1536]{1,0:T(8,128)(2,1)S(1)}, u32[]{:S(2)}, u32[]{:S(2)}) %collective-permute-start.11) | collective-permute-done | bytes 393248 | tf_op jit(solution)/shard_map/ppermute | solution.py:18
  34.7 3.2 %collective-permute-start.14 = (bf16[128,1536]{1,0:T(8,128)(2,1)S(1)}, bf16[128,1536]{1,0:T(8,128)(2,1)S(1)}, u32[]{:S(2)}, u32[]{:S(2)}) collective-permute-start(bf16[128,1536]{1,0:T(8,128)(2,1)S(1)} %collective-permute-done.12), channel_id=1, source_target_pairs={{0,14},{2,0},{4,2},{6,4},{8,6},{10,8},{12,10},{14,12},{1,15},{3,1}... | collective-permute-start | bytes 1179656 | tf_op jit(solution)/shard_map/ppermute | solution.py:18
  38.1 0.1 collective-permute-start.6
  38.3 7.0 %collective-permute-done.13 = bf16[128,1536]{1,0:T(8,128)(2,1)S(1)} collective-permute-done((bf16[128,1536]{1,0:T(8,128)(2,1)S(1)}, bf16[128,1536]{1,0:T(8,128)(2,1)S(1)}, u32[]{:S(2)}, u32[]{:S(2)}) %collective-permute-start.13) | collective-permute-done | bytes 393248 | tf_op jit(solution)/shard_map/ppermute | solution.py:18
  45.2 3.2 %collective-permute-start.16 = (bf16[128,1536]{1,0:T(8,128)(2,1)S(1)}, bf16[128,1536]{1,0:T(8,128)(2,1)S(1)}, u32[]{:S(2)}, u32[]{:S(2)}) collective-permute-start(bf16[128,1536]{1,0:T(8,128)(2,1)S(1)} %collective-permute-done.14), channel_id=1, source_target_pairs={{0,14},{2,0},{4,2},{6,4},{8,6},{10,8},{12,10},{14,12},{1,15},{3,1}... | collective-permute-start | bytes 1179656 | tf_op jit(solution)/shard_map/ppermute | solution.py:18
  48.6 3.7 %convolution_convert_fusion = bf16[1024,1536]{1,0:T(8,128)(2,1)S(1)} fusion(bf16[1024,768]{1,0:T(8,128)(2,1)S(1)} %bitcast.91, bf16[768,384]{1,0:T(8,128)(2,1)S(1)} %collective-permute-done.6, bf16[768,384]{1,0:T(8,128)(2,1)S(1)} %copy-done.5, bf16[768,384]{1,0:T(8,128)(2,1)} %collective-permute-done.5, bf16[768,384]{1,0:T(8,128)(2,1)S(1)} %copy-done.4), kind=kOutput, calls=%fused_computation | convolution fusion | flops 2426929152 | bytes 7077888 | tf_op jit(solution)/shard_map/dot_general | solution.py:161
  52.3 0.1 dynamic-slice_bitcast_fusion.3
  52.4 0.1 collective-permute-start.7
  52.5 3.2 %collective-permute-start.8 = (bf16[128,768]{1,0:T(8,128)(2,1)S(1)}, bf16[128,768]{1,0:T(8,128)(2,1)S(1)}, u32[]{:S(2)}, u32[]{:S(2)}) collective-permute-start(bf16[128,768]{1,0:T(8,128)(2,1)S(1)} %get-tuple-element.66), channel_id=1, source_target_pairs={{0,14},{2,0},{4,2},{6,4},{8,6},{10,8},{12,10},{14,12},{1,15},{3,1}... | collective-permute-start | bytes 589832 | tf_op jit(solution)/shard_map/ppermute | solution.py:18
  55.8 0.7 collective-permute-done.15
  56.5 0.1 collective-permute-start.17
  56.6 3.3 %collective-permute-start.18 = (bf16[64,1536]{1,0:T(8,128)(2,1)S(1)}, bf16[64,1536]{1,0:T(8,128)(2,1)S(1)}, u32[]{:S(2)}, u32[]{:S(2)}) collective-permute-start(bf16[64,1536]{1,0:T(8,128)(2,1)S(1)} %slice.106), channel_id=1, source_target_pairs={{0,14},{2,0},{4,2},{6,4},{8,6},{10,8},{12,10},{14,12},{1,15},{3,1}... | collective-permute-start | bytes 589832 | tf_op jit(solution)/shard_map/ppermute | solution.py:18
  60.0 1.2 collective-permute-done.7
  61.2 3.4 %collective-permute-start.10 = (bf16[128,1536]{1,0:T(8,128)(2,1)S(1)}, bf16[128,1536]{1,0:T(8,128)(2,1)S(1)}, u32[]{:S(2)}, u32[]{:S(2)}) collective-permute-start(bf16[128,1536]{1,0:T(8,128)(2,1)S(1)} %pad_maximum_fusion.4), channel_id=1, source_target_pairs={{0,14},{2,0},{4,2},{6,4},{8,6},{10,8},{12,10},{14,12},{1,15},{3,1}... | collective-permute-start | bytes 1179656 | tf_op jit(solution)/shard_map/ppermute | solution.py:18
  64.7 0.1 collective-permute-start.9
  64.8 0.9 collective-permute-start.24
  65.7 1.8 %fusion = bf16[1536,384]{1,0:T(8,128)(2,1)S(1)} fusion(bf16[1024,1536]{1,0:T(8,128)(2,1)S(1)} %bitcast.84, bf16[1024,768]{1,0:T(8,128)(2,1)S(1)} %bitcast.92), kind=kOutput, calls=%fused_computation.3 | convolution fusion | flops 1209139200 | bytes 5111808 | tf_op jit(solution)/shard_map/dot_general | solution.py:176
  67.6 0.9 copy-done.3
  68.6 3.7 %convolution_convert_fusion.1 = bf16[1024,768]{1,0:T(8,128)(2,1)S(1)} fusion(bf16[1024,1536]{1,0:T(8,128)(2,1)S(1)} %bitcast.85, bf16[768,384]{1,0:T(8,128)(2,1)S(1)} %collective-permute-done.6, bf16[768,384]{1,0:T(8,128)(2,1)S(1)} %copy-done.5, bf16[768,384]{1,0:T(8,128)(2,1)} %collective-permute-done.5, bf16[768,384]{1,0:T(8,128)(2,1)S(1)} %copy-done.4), kind=kOutput, calls=%fused_computation.6 | convolution fusion | flops 2426142720 | bytes 7077888 | tf_op jit(solution)/shard_map/dot_general | solution.py:170
  72.3 1.5 %collective-permute-done.9 = bf16[128,1536]{1,0:T(8,128)(2,1)S(1)} collective-permute-done((bf16[128,1536]{1,0:T(8,128)(2,1)S(1)}, bf16[128,1536]{1,0:T(8,128)(2,1)S(1)}, u32[]{:S(2)}, u32[]{:S(2)}) %collective-permute-start.9) | collective-permute-done | bytes 393248 | tf_op jit(solution)/shard_map/ppermute | solution.py:18
  73.8 0.1 constant_dynamic-slice_fusion.2
  73.9 0.3 collective-permute-start.21
  74.2 3.2 %collective-permute-start.22 = (bf16[256,384]{1,0:T(8,128)(2,1)S(1)}, bf16[256,384]{1,0:T(8,128)(2,1)S(1)}, u32[]{:S(2)}, u32[]{:S(2)}) collective-permute-start(bf16[256,384]{1,0:T(8,128)(2,1)S(1)} %get-tuple-element.64), channel_id=1, source_target_pairs={{0,96},{32,0},{64,32},{96,64},{1,97},{33,1},{65,33},{97,65},{2,98}... | collective-permute-start | bytes 589832 | tf_op jit(solution)/shard_map/ppermute | solution.py:18
  77.5 0.2 fusion.6
  77.8 3.2 %collective-permute-start.20 = (bf16[128,1536]{1,0:T(8,128)(2,1)S(1)}, bf16[128,1536]{1,0:T(8,128)(2,1)S(1)}, u32[]{:S(2)}, u32[]{:S(2)}) collective-permute-start(bf16[128,1536]{1,0:T(8,128)(2,1)S(1)} %get-tuple-element.55), channel_id=1, source_target_pairs={{0,14},{2,0},{4,2},{6,4},{8,6},{10,8},{12,10},{14,12},{1,15},{3,1}... | collective-permute-start | bytes 1179656 | tf_op jit(solution)/shard_map/ppermute | solution.py:18
  81.0 2.9 %fusion.1 = bf16[1536,384]{1,0:T(8,128)(2,1)} fusion(bf16[1024,1536]{1,0:T(8,128)(2,1)S(1)} %bitcast.86, bf16[1024,768]{1,0:T(8,128)(2,1)S(1)} %bitcast.93), kind=kOutput, calls=%fused_computation.4 | convolution fusion | flops 1209139200 | bytes 5111808 | tf_op jit(solution)/shard_map/dot_general | solution.py:176
  83.9 3.0 %collective-permute-start.29 = (bf16[1536,384]{1,0:T(8,128)(2,1)}, bf16[1536,384]{1,0:T(8,128)(2,1)}, u32[]{:S(2)}, u32[]{:S(2)}) collective-permute-start(bf16[1536,384]{1,0:T(8,128)(2,1)} %fusion.1), channel_id=1, source_target_pairs={{0,1},{1,0},{2,3},{3,2},{4,5},{5,4},{6,7},{7,6},{8,9},{9,8},{10,11... | collective-permute-start | bytes 3538952 | tf_op jit(solution)/shard_map/ppermute | solution.py:18
  86.9 1.8 %collective-permute-done.19 = bf16[128,1536]{1,0:T(8,128)(2,1)S(1)} collective-permute-done((bf16[128,1536]{1,0:T(8,128)(2,1)S(1)}, bf16[128,1536]{1,0:T(8,128)(2,1)S(1)}, u32[]{:S(2)}, u32[]{:S(2)}) %collective-permute-start.19) | collective-permute-done | bytes 393248 | tf_op jit(solution)/shard_map/ppermute | solution.py:18
  88.7 0.2 fusion.8
  88.9 2.5 %collective-permute-start.25 = (bf16[128,1536]{1,0:T(8,128)(2,1)S(1)}, bf16[128,1536]{1,0:T(8,128)(2,1)S(1)}, u32[]{:S(2)}, u32[]{:S(2)}) collective-permute-start(bf16[128,1536]{1,0:T(8,128)(2,1)S(1)} %get-tuple-element.53), channel_id=1, source_target_pairs={{0,2},{2,4},{4,6},{6,8},{8,10},{10,12},{12,14},{14,0},{1,3},{3,5},... | collective-permute-start | bytes 1179656 | tf_op jit(solution)/shard_map/ppermute | solution.py:18
  91.5 0.8 collective-permute-start.26
  92.3 0.4 collective-permute-start.28
  92.8 1.8 %collective-permute-start.27 = (bf16[256,768]{1,0:T(8,128)(2,1)S(1)}, bf16[256,768]{1,0:T(8,128)(2,1)S(1)}, u32[]{:S(2)}, u32[]{:S(2)}) collective-permute-start(bf16[256,768]{1,0:T(8,128)(2,1)S(1)} %pad_maximum_fusion.5), channel_id=1, source_target_pairs={{0,32},{32,64},{64,96},{96,0},{1,33},{33,65},{65,97},{97,1},{2,34}... | collective-permute-start | bytes 1179656 | tf_op jit(solution)/shard_map/ppermute | solution.py:18
  94.6 4.6 %collective-permute-done.25 = bf16[128,1536]{1,0:T(8,128)(2,1)S(1)} collective-permute-done((bf16[128,1536]{1,0:T(8,128)(2,1)S(1)}, bf16[128,1536]{1,0:T(8,128)(2,1)S(1)}, u32[]{:S(2)}, u32[]{:S(2)}) %collective-permute-start.25) | collective-permute-done | bytes 393248 | tf_op jit(solution)/shard_map/ppermute | solution.py:18
  99.2 2.2 %collective-permute-done.26 = bf16[128,1536]{1,0:T(8,128)(2,1)S(1)} collective-permute-done((bf16[128,1536]{1,0:T(8,128)(2,1)S(1)}, bf16[128,1536]{1,0:T(8,128)(2,1)S(1)}, u32[]{:S(2)}, u32[]{:S(2)}) %collective-permute-start.26) | collective-permute-done | bytes 393248 | tf_op jit(solution)/shard_map/ppermute | solution.py:18
  101.4 0.2 fusion.10
  101.6 0.9 pad_maximum_fusion
  102.5 6.0 %all-to-all-start.1 = ((bf16[16,16,1536]{2,1,0:T(8,128)(2,1)}), bf16[16,16,1536]{2,1,0:T(8,128)(2,1)S(1)}, u32[]{:S(2)}, u32[]{:S(2)}) async-start(bf16[16,16,1536]{2,1,0:T(8,128)(2,1)} %bitcast.35), calls=%async_computation.1 | async-start | bytes 1572864 | tf_op jit(solution)/shard_map/all_to_all | solution.py:191
  108.5 0.8 copy-done.9
  109.3 5.4 %collective-permute-done.29 = bf16[1536,384]{1,0:T(8,128)(2,1)} collective-permute-done((bf16[1536,384]{1,0:T(8,128)(2,1)}, bf16[1536,384]{1,0:T(8,128)(2,1)}, u32[]{:S(2)}, u32[]{:S(2)}) %collective-permute-start.29) | collective-permute-done | bytes 1179680 | tf_op jit(solution)/shard_map/ppermute | solution.py:18
  114.7 1.1 slice.93
  115.9 0.1 collective-permute-start.31
  116.0 1.2 fusion.4
  117.3 3.0 %collective-permute-start.30 = (bf16[256,384]{1,0:T(8,128)(2,1)S(1)}, bf16[256,384]{1,0:T(8,128)(2,1)S(1)}, u32[]{:S(2)}, u32[]{:S(2)}) collective-permute-start(bf16[256,384]{1,0:T(8,128)(2,1)S(1)} %slice.143), channel_id=1, source_target_pairs={{0,1},{1,0},{2,3},{3,2},{4,5},{5,4},{6,7},{7,6},{8,9},{9,8},{10,11... | collective-permute-start | bytes 589832 | tf_op jit(solution)/shard_map/ppermute | solution.py:18
  120.3 5.9 %collective-permute-done.30 = bf16[256,384]{1,0:T(8,128)(2,1)S(1)} collective-permute-done((bf16[256,384]{1,0:T(8,128)(2,1)S(1)}, bf16[256,384]{1,0:T(8,128)(2,1)S(1)}, u32[]{:S(2)}, u32[]{:S(2)}) %collective-permute-start.30) | collective-permute-done | bytes 196640 | tf_op jit(solution)/shard_map/ppermute | solution.py:18
  126.1 0.7 fusion.13
  126.9 2.0 %broadcast_select_fusion.1 = (bf16[768,384]{1,0:T(8,128)(2,1)S(1)}, bf16[768,384]{1,0:T(8,128)(2,1)S(1)}) fusion(pred[]{:T(512)S(6)} %eq.7, bf16[768,384]{1,0:T(8,128)(2,1)} %copy-done.6, bf16[1536,384]{1,0:T(8,128)(2,1)} %copy-done.3, bf16[768,384]{1,0:T(8,128)(2,1)} %collective-permute-done.31, bf16[1536,384]{1,0:T(8,128)(2,1)} %collective-permute-done.29), kind=kLoop, calls=%fused_computation.30 | loop fusion | flops 2949120 | bytes 3538945 | tf_op jit(solution)/shard_map/jit(_where)/select_n | solution.py:208
  128.8 1.1 maximum_bitcast_fusion
  130.0 1.7 %shard_map.76 = (bf16[16,12288]{1,0:T(8,128)(2,1)}, bf16[16,12288]{1,0:T(8,128)(2,1)}) custom-call(s32[2]{0:T(128)S(1)} %pad_add_fusion.at_ref, bf16[2,8,16,1536]{3,2,1,0:T(8,128)(2,1)S(1)} %bitcast.81, bf16[16,12288]{1,0:T(8,128)(2,1)S(1)} %bitcast.83, bf16[16,12288]{1,0:T(8,128)(2,1)S(1)} %collective-permute-done.24.early_ref), custom_call_target="tpu_custom_call" | custom-call | tf_op jit(solution)/shard_map/pallas_call | solution.py:109
  (82 shorter events, 1.3 us)
Async XLA Ops:
  0.6 12.9 %collective-permute-start = (bf16[256,384]{1,0:T(8,128)(2,1)}, bf16[256,384]{1,0:T(8,128)(2,1)S(1)}, u32[]{:S(2)}, u32[]{:S(2)}) collective-permute-start(bf16[256,384]{1,0:T(8,128)(2,1)} %bitcast.108), channel_id=1, source_target_pairs={{0,1},{1,0},{2,3},{3,2},{4,5},{5,4},{6,7},{7,6},{8,9},{9,8},{10,11... | collective-permute-start | bytes 589832 | tf_op jit(solution)/shard_map/ppermute | solution.py:18
  2.9 1.0 copy-start
  5.2 8.3 %copy-start.10 = (bf16[1,256,384]{2,1,0:T(8,128)(2,1)S(1)}, bf16[1,256,384]{2,1,0:T(8,128)(2,1)}, u32[]{:S(2)}) copy-start(bf16[1,256,384]{2,1,0:T(8,128)(2,1)} %param.5) | copy-start | bytes 589828
  5.2 16.1 %all-to-all-start = ((bf16[8,16,1536]{2,1,0:T(8,128)(2,1)}), bf16[8,16,1536]{2,1,0:T(8,128)(2,1)S(1)}, u32[]{:S(2)}, u32[]{:S(2)}) async-start(bf16[8,16,1536]{2,1,0:T(8,128)(2,1)} %shard_map.75), calls=%async_computation | async-start | bytes 786432 | tf_op jit(solution)/shard_map/all_to_all | solution.py:155
  10.7 6.2 %copy-start.1 = (bf16[1,16,12288]{2,1,0:T(8,128)(2,1)S(1)}, bf16[1,16,12288]{2,1,0:T(8,128)(2,1)}, u32[]{:S(2)}) copy-start(bf16[1,16,12288]{2,1,0:T(8,128)(2,1)} %param.7) | copy-start | bytes 1179652
  10.7 6.2 %copy-start.2 = (bf16[1,16,12288]{2,1,0:T(8,128)(2,1)S(1)}, bf16[1,16,12288]{2,1,0:T(8,128)(2,1)}, u32[]{:S(2)}) copy-start(bf16[1,16,12288]{2,1,0:T(8,128)(2,1)} %param.4) | copy-start | bytes 1179652
  13.5 14.2 %collective-permute-start.1 = (bf16[256,768]{1,0:T(8,128)(2,1)S(1)}, bf16[256,768]{1,0:T(8,128)(2,1)S(1)}, u32[]{:S(2)}, u32[]{:S(2)}) collective-permute-start(bf16[256,768]{1,0:T(8,128)(2,1)S(1)} %pad_maximum_fusion.1), channel_id=1, source_target_pairs={{0,32},{32,64},{64,96},{96,0},{1,33},{33,65},{65,97},{97,1},{2,34}... | collective-permute-start | bytes 1179656 | tf_op jit(solution)/shard_map/ppermute | solution.py:18
  15.6 12.5 %collective-permute-start.2 = (bf16[256,768]{1,0:T(8,128)(2,1)S(1)}, bf16[256,768]{1,0:T(8,128)(2,1)S(1)}, u32[]{:S(2)}, u32[]{:S(2)}) collective-permute-start(bf16[256,768]{1,0:T(8,128)(2,1)S(1)} %pad_maximum_fusion.1), channel_id=1, source_target_pairs={{0,96},{32,0},{64,32},{96,64},{1,97},{33,1},{65,33},{97,65},{2,98}... | collective-permute-start | bytes 1179656 | tf_op jit(solution)/shard_map/ppermute | solution.py:18
  17.7 20.4 %collective-permute-start.5 = (bf16[768,384]{1,0:T(8,128)(2,1)}, bf16[768,384]{1,0:T(8,128)(2,1)}, u32[]{:S(2)}, u32[]{:S(2)}) collective-permute-start(bf16[768,384]{1,0:T(8,128)(2,1)} %get-tuple-element.27), channel_id=1, source_target_pairs={{0,1},{1,0},{2,3},{3,2},{4,5},{5,4},{6,7},{7,6},{8,9},{9,8},{10,11... | collective-permute-start | bytes 1769480 | tf_op jit(solution)/shard_map/ppermute | solution.py:18
  21.4 13.4 %collective-permute-start.11 = (bf16[128,1536]{1,0:T(8,128)(2,1)S(1)}, bf16[128,1536]{1,0:T(8,128)(2,1)S(1)}, u32[]{:S(2)}, u32[]{:S(2)}) collective-permute-start(bf16[128,1536]{1,0:T(8,128)(2,1)S(1)} %bitcast.94), channel_id=1, source_target_pairs={{0,2},{2,4},{4,6},{6,8},{8,10},{10,12},{12,14},{14,0},{1,3},{3,5},... | collective-permute-start | bytes 1179656 | tf_op jit(solution)/shard_map/ppermute | solution.py:18
  23.4 11.4 %collective-permute-start.12 = (bf16[128,1536]{1,0:T(8,128)(2,1)S(1)}, bf16[128,1536]{1,0:T(8,128)(2,1)S(1)}, u32[]{:S(2)}, u32[]{:S(2)}) collective-permute-start(bf16[128,1536]{1,0:T(8,128)(2,1)S(1)} %bitcast.95), channel_id=1, source_target_pairs={{0,14},{2,0},{4,2},{6,4},{8,6},{10,8},{12,10},{14,12},{1,15},{3,1}... | collective-permute-start | bytes 1179656 | tf_op jit(solution)/shard_map/ppermute | solution.py:18
  27.7 10.4 %collective-permute-start.3 = (bf16[128,768]{1,0:T(8,128)(2,1)S(1)}, bf16[128,768]{1,0:T(8,128)(2,1)S(1)}, u32[]{:S(2)}, u32[]{:S(2)}) collective-permute-start(bf16[128,768]{1,0:T(8,128)(2,1)S(1)} %slice.97), channel_id=1, source_target_pairs={{0,32},{32,64},{64,96},{96,0},{1,33},{33,65},{65,97},{97,1},{2,34}... | collective-permute-start | bytes 589832 | tf_op jit(solution)/shard_map/ppermute | solution.py:18
  28.1 10.1 %collective-permute-start.4 = (bf16[128,768]{1,0:T(8,128)(2,1)S(1)}, bf16[128,768]{1,0:T(8,128)(2,1)S(1)}, u32[]{:S(2)}, u32[]{:S(2)}) collective-permute-start(bf16[128,768]{1,0:T(8,128)(2,1)S(1)} %slice.98), channel_id=1, source_target_pairs={{0,96},{32,0},{64,32},{96,64},{1,97},{33,1},{65,33},{97,65},{2,98}... | collective-permute-start | bytes 589832 | tf_op jit(solution)/shard_map/ppermute | solution.py:18
  31.2 17.3 %copy-start.4 = (bf16[768,384]{1,0:T(8,128)(2,1)S(1)}, bf16[768,384]{1,0:T(8,128)(2,1)}, u32[]{:S(2)}) copy-start(bf16[768,384]{1,0:T(8,128)(2,1)} %get-tuple-element.48) | copy-start | bytes 1769476
  31.2 17.3 %copy-start.5 = (bf16[768,384]{1,0:T(8,128)(2,1)S(1)}, bf16[768,384]{1,0:T(8,128)(2,1)}, u32[]{:S(2)}) copy-start(bf16[768,384]{1,0:T(8,128)(2,1)} %get-tuple-element.50) | copy-start | bytes 1769476
  34.7 10.5 %collective-permute-start.13 = (bf16[128,1536]{1,0:T(8,128)(2,1)S(1)}, bf16[128,1536]{1,0:T(8,128)(2,1)S(1)}, u32[]{:S(2)}, u32[]{:S(2)}) collective-permute-start(bf16[128,1536]{1,0:T(8,128)(2,1)S(1)} %collective-permute-done.11), channel_id=1, source_target_pairs={{0,2},{2,4},{4,6},{6,8},{8,10},{10,12},{12,14},{14,0},{1,3},{3,5},... | collective-permute-start | bytes 1179656 | tf_op jit(solution)/shard_map/ppermute | solution.py:18
  34.7 10.5 %collective-permute-start.14 = (bf16[128,1536]{1,0:T(8,128)(2,1)S(1)}, bf16[128,1536]{1,0:T(8,128)(2,1)S(1)}, u32[]{:S(2)}, u32[]{:S(2)}) collective-permute-start(bf16[128,1536]{1,0:T(8,128)(2,1)S(1)} %collective-permute-done.12), channel_id=1, source_target_pairs={{0,14},{2,0},{4,2},{6,4},{8,6},{10,8},{12,10},{14,12},{1,15},{3,1}... | collective-permute-start | bytes 1179656 | tf_op jit(solution)/shard_map/ppermute | solution.py:18
  38.1 10.5 %collective-permute-start.6 = (bf16[768,384]{1,0:T(8,128)(2,1)}, bf16[768,384]{1,0:T(8,128)(2,1)S(1)}, u32[]{:S(2)}, u32[]{:S(2)}) collective-permute-start(bf16[768,384]{1,0:T(8,128)(2,1)} %collective-permute-done.5), channel_id=1, source_target_pairs={{0,16},{16,0},{1,17},{17,1},{2,18},{18,2},{3,19},{19,3},{4,20},{20... | collective-permute-start | bytes 1769480 | tf_op jit(solution)/shard_map/ppermute | solution.py:18
  45.2 11.2 %collective-permute-start.15 = (bf16[128,1536]{1,0:T(8,128)(2,1)S(1)}, bf16[128,1536]{1,0:T(8,128)(2,1)S(1)}, u32[]{:S(2)}, u32[]{:S(2)}) collective-permute-start(bf16[128,1536]{1,0:T(8,128)(2,1)S(1)} %collective-permute-done.13), channel_id=1, source_target_pairs={{0,2},{2,4},{4,6},{6,8},{8,10},{10,12},{12,14},{14,0},{1,3},{3,5},... | collective-permute-start | bytes 1179656 | tf_op jit(solution)/shard_map/ppermute | solution.py:18
  45.2 11.3 %collective-permute-start.16 = (bf16[128,1536]{1,0:T(8,128)(2,1)S(1)}, bf16[128,1536]{1,0:T(8,128)(2,1)S(1)}, u32[]{:S(2)}, u32[]{:S(2)}) collective-permute-start(bf16[128,1536]{1,0:T(8,128)(2,1)S(1)} %collective-permute-done.14), channel_id=1, source_target_pairs={{0,14},{2,0},{4,2},{6,4},{8,6},{10,8},{12,10},{14,12},{1,15},{3,1}... | collective-permute-start | bytes 1179656 | tf_op jit(solution)/shard_map/ppermute | solution.py:18
  52.4 8.7 %collective-permute-start.7 = (bf16[128,768]{1,0:T(8,128)(2,1)S(1)}, bf16[128,768]{1,0:T(8,128)(2,1)S(1)}, u32[]{:S(2)}, u32[]{:S(2)}) collective-permute-start(bf16[128,768]{1,0:T(8,128)(2,1)S(1)} %get-tuple-element.67), channel_id=1, source_target_pairs={{0,2},{2,4},{4,6},{6,8},{8,10},{10,12},{12,14},{14,0},{1,3},{3,5},... | collective-permute-start | bytes 589832 | tf_op jit(solution)/shard_map/ppermute | solution.py:18
  52.5 8.6 %collective-permute-start.8 = (bf16[128,768]{1,0:T(8,128)(2,1)S(1)}, bf16[128,768]{1,0:T(8,128)(2,1)S(1)}, u32[]{:S(2)}, u32[]{:S(2)}) collective-permute-start(bf16[128,768]{1,0:T(8,128)(2,1)S(1)} %get-tuple-element.66), channel_id=1, source_target_pairs={{0,14},{2,0},{4,2},{6,4},{8,6},{10,8},{12,10},{14,12},{1,15},{3,1}... | collective-permute-start | bytes 589832 | tf_op jit(solution)/shard_map/ppermute | solution.py:18
  56.5 8.3 %copy-start.7 = (bf16[16,12288]{1,0:T(8,128)(2,1)S(1)}, bf16[16,12288]{1,0:T(8,128)(2,1)}, u32[]{:S(2)}) copy-start(bf16[16,12288]{1,0:T(8,128)(2,1)} %broadcast_select_fusion.2) | copy-start | bytes 1179652
  56.5 9.2 %collective-permute-start.17 = (bf16[64,1536]{1,0:T(8,128)(2,1)S(1)}, bf16[64,1536]{1,0:T(8,128)(2,1)S(1)}, u32[]{:S(2)}, u32[]{:S(2)}) collective-permute-start(bf16[64,1536]{1,0:T(8,128)(2,1)S(1)} %slice.105), channel_id=1, source_target_pairs={{0,2},{2,4},{4,6},{6,8},{8,10},{10,12},{12,14},{14,0},{1,3},{3,5},... | collective-permute-start | bytes 589832 | tf_op jit(solution)/shard_map/ppermute | solution.py:18
  56.6 9.1 %collective-permute-start.18 = (bf16[64,1536]{1,0:T(8,128)(2,1)S(1)}, bf16[64,1536]{1,0:T(8,128)(2,1)S(1)}, u32[]{:S(2)}, u32[]{:S(2)}) collective-permute-start(bf16[64,1536]{1,0:T(8,128)(2,1)S(1)} %slice.106), channel_id=1, source_target_pairs={{0,14},{2,0},{4,2},{6,4},{8,6},{10,8},{12,10},{14,12},{1,15},{3,1}... | collective-permute-start | bytes 589832 | tf_op jit(solution)/shard_map/ppermute | solution.py:18
  61.2 11.0 %collective-permute-start.10 = (bf16[128,1536]{1,0:T(8,128)(2,1)S(1)}, bf16[128,1536]{1,0:T(8,128)(2,1)S(1)}, u32[]{:S(2)}, u32[]{:S(2)}) collective-permute-start(bf16[128,1536]{1,0:T(8,128)(2,1)S(1)} %pad_maximum_fusion.4), channel_id=1, source_target_pairs={{0,14},{2,0},{4,2},{6,4},{8,6},{10,8},{12,10},{14,12},{1,15},{3,1}... | collective-permute-start | bytes 1179656 | tf_op jit(solution)/shard_map/ppermute | solution.py:18
  64.7 9.1 %collective-permute-start.9 = (bf16[128,1536]{1,0:T(8,128)(2,1)S(1)}, bf16[128,1536]{1,0:T(8,128)(2,1)S(1)}, u32[]{:S(2)}, u32[]{:S(2)}) collective-permute-start(bf16[128,1536]{1,0:T(8,128)(2,1)S(1)} %pad_maximum_fusion.3), channel_id=1, source_target_pairs={{0,2},{2,4},{4,6},{6,8},{8,10},{10,12},{12,14},{14,0},{1,3},{3,5},... | collective-permute-start | bytes 1179656 | tf_op jit(solution)/shard_map/ppermute | solution.py:18
  64.8 13.0 %collective-permute-start.24 = (bf16[16,12288]{1,0:T(8,128)(2,1)S(1)}, bf16[16,12288]{1,0:T(8,128)(2,1)S(1)}, u32[]{:S(2)}, u32[]{:S(2)}) collective-permute-start(bf16[16,12288]{1,0:T(8,128)(2,1)S(1)} %copy-done.7), channel_id=1, source_target_pairs={{0,128},{128,0},{1,129},{129,1},{2,130},{130,2},{3,131},{131,3},{4... | collective-permute-start | bytes 1179656 | tf_op jit(solution)/shard_map/ppermute | solution.py:18
  67.6 1.0 copy-start.3
  68.6 18.3 %collective-permute-start.23 = (bf16[768,384]{1,0:T(8,128)(2,1)S(1)}, bf16[768,384]{1,0:T(8,128)(2,1)S(1)}, u32[]{:S(2)}, u32[]{:S(2)}) collective-permute-start(bf16[768,384]{1,0:T(8,128)(2,1)S(1)} %slice.110), channel_id=1, source_target_pairs={{0,16},{16,0},{1,17},{17,1},{2,18},{18,2},{3,19},{19,3},{4,20},{20... | collective-permute-start | bytes 1769480 | tf_op jit(solution)/shard_map/ppermute | solution.py:18
  73.9 10.0 %collective-permute-start.21 = (bf16[256,384]{1,0:T(8,128)(2,1)S(1)}, bf16[256,384]{1,0:T(8,128)(2,1)S(1)}, u32[]{:S(2)}, u32[]{:S(2)}) collective-permute-start(bf16[256,384]{1,0:T(8,128)(2,1)S(1)} %get-tuple-element.65), channel_id=1, source_target_pairs={{0,32},{32,64},{64,96},{96,0},{1,33},{33,65},{65,97},{97,1},{2,34}... | collective-permute-start | bytes 589832 | tf_op jit(solution)/shard_map/ppermute | solution.py:18
  74.2 12.7 %collective-permute-start.22 = (bf16[256,384]{1,0:T(8,128)(2,1)S(1)}, bf16[256,384]{1,0:T(8,128)(2,1)S(1)}, u32[]{:S(2)}, u32[]{:S(2)}) collective-permute-start(bf16[256,384]{1,0:T(8,128)(2,1)S(1)} %get-tuple-element.64), channel_id=1, source_target_pairs={{0,96},{32,0},{64,32},{96,64},{1,97},{33,1},{65,33},{97,65},{2,98}... | collective-permute-start | bytes 589832 | tf_op jit(solution)/shard_map/ppermute | solution.py:18
  77.7 11.0 %collective-permute-start.19 = (bf16[128,1536]{1,0:T(8,128)(2,1)S(1)}, bf16[128,1536]{1,0:T(8,128)(2,1)S(1)}, u32[]{:S(2)}, u32[]{:S(2)}) collective-permute-start(bf16[128,1536]{1,0:T(8,128)(2,1)S(1)} %get-tuple-element.56), channel_id=1, source_target_pairs={{0,2},{2,4},{4,6},{6,8},{8,10},{10,12},{12,14},{14,0},{1,3},{3,5},... | collective-permute-start | bytes 1179656 | tf_op jit(solution)/shard_map/ppermute | solution.py:18
  77.8 10.9 %collective-permute-start.20 = (bf16[128,1536]{1,0:T(8,128)(2,1)S(1)}, bf16[128,1536]{1,0:T(8,128)(2,1)S(1)}, u32[]{:S(2)}, u32[]{:S(2)}) collective-permute-start(bf16[128,1536]{1,0:T(8,128)(2,1)S(1)} %get-tuple-element.55), channel_id=1, source_target_pairs={{0,14},{2,0},{4,2},{6,4},{8,6},{10,8},{12,10},{14,12},{1,15},{3,1}... | collective-permute-start | bytes 1179656 | tf_op jit(solution)/shard_map/ppermute | solution.py:18
  83.9 30.8 %collective-permute-start.29 = (bf16[1536,384]{1,0:T(8,128)(2,1)}, bf16[1536,384]{1,0:T(8,128)(2,1)}, u32[]{:S(2)}, u32[]{:S(2)}) collective-permute-start(bf16[1536,384]{1,0:T(8,128)(2,1)} %fusion.1), channel_id=1, source_target_pairs={{0,1},{1,0},{2,3},{3,2},{4,5},{5,4},{6,7},{7,6},{8,9},{9,8},{10,11... | collective-permute-start | bytes 3538952 | tf_op jit(solution)/shard_map/ppermute | solution.py:18
  86.9 5.9 %copy-start.6 = (bf16[768,384]{1,0:T(8,128)(2,1)}, bf16[768,384]{1,0:T(8,128)(2,1)S(1)}, u32[]{:S(2)}) copy-start(bf16[768,384]{1,0:T(8,128)(2,1)S(1)} %collective-permute-done.23) | copy-start | bytes 1769476
  88.9 10.3 %collective-permute-start.25 = (bf16[128,1536]{1,0:T(8,128)(2,1)S(1)}, bf16[128,1536]{1,0:T(8,128)(2,1)S(1)}, u32[]{:S(2)}, u32[]{:S(2)}) collective-permute-start(bf16[128,1536]{1,0:T(8,128)(2,1)S(1)} %get-tuple-element.53), channel_id=1, source_target_pairs={{0,2},{2,4},{4,6},{6,8},{8,10},{10,12},{12,14},{14,0},{1,3},{3,5},... | collective-permute-start | bytes 1179656 | tf_op jit(solution)/shard_map/ppermute | solution.py:18
  91.5 9.9 %collective-permute-start.26 = (bf16[128,1536]{1,0:T(8,128)(2,1)S(1)}, bf16[128,1536]{1,0:T(8,128)(2,1)S(1)}, u32[]{:S(2)}, u32[]{:S(2)}) collective-permute-start(bf16[128,1536]{1,0:T(8,128)(2,1)S(1)} %get-tuple-element.54), channel_id=1, source_target_pairs={{0,14},{2,0},{4,2},{6,4},{8,6},{10,8},{12,10},{14,12},{1,15},{3,1}... | collective-permute-start | bytes 1179656 | tf_op jit(solution)/shard_map/ppermute | solution.py:18
  92.3 16.2 %collective-permute-start.28 = (bf16[256,768]{1,0:T(8,128)(2,1)S(1)}, bf16[256,768]{1,0:T(8,128)(2,1)S(1)}, u32[]{:S(2)}, u32[]{:S(2)}) collective-permute-start(bf16[256,768]{1,0:T(8,128)(2,1)S(1)} %pad_maximum_fusion.6), channel_id=1, source_target_pairs={{0,96},{32,0},{64,32},{96,64},{1,97},{33,1},{65,33},{97,65},{2,98}... | collective-permute-start | bytes 1179656 | tf_op jit(solution)/shard_map/ppermute | solution.py:18
  92.8 15.8 %collective-permute-start.27 = (bf16[256,768]{1,0:T(8,128)(2,1)S(1)}, bf16[256,768]{1,0:T(8,128)(2,1)S(1)}, u32[]{:S(2)}, u32[]{:S(2)}) collective-permute-start(bf16[256,768]{1,0:T(8,128)(2,1)S(1)} %pad_maximum_fusion.5), channel_id=1, source_target_pairs={{0,32},{32,64},{64,96},{96,0},{1,33},{33,65},{65,97},{97,1},{2,34}... | collective-permute-start | bytes 1179656 | tf_op jit(solution)/shard_map/ppermute | solution.py:18
  102.5 23.6 %all-to-all-start.1 = ((bf16[16,16,1536]{2,1,0:T(8,128)(2,1)}), bf16[16,16,1536]{2,1,0:T(8,128)(2,1)S(1)}, u32[]{:S(2)}, u32[]{:S(2)}) async-start(bf16[16,16,1536]{2,1,0:T(8,128)(2,1)} %bitcast.35), calls=%async_computation.1 | async-start | bytes 1572864 | tf_op jit(solution)/shard_map/all_to_all | solution.py:191
  108.5 7.5 %copy-start.8 = (bf16[256,768]{1,0:T(8,128)(2,1)}, bf16[256,768]{1,0:T(8,128)(2,1)S(1)}, u32[]{:S(2)}) copy-start(bf16[256,768]{1,0:T(8,128)(2,1)S(1)} %collective-permute-done.28) | copy-start | bytes 1179652
  108.5 0.8 copy-start.9
  115.9 10.3 %collective-permute-start.31 = (bf16[768,384]{1,0:T(8,128)(2,1)S(1)}, bf16[768,384]{1,0:T(8,128)(2,1)}, u32[]{:S(2)}, u32[]{:S(2)}) collective-permute-start(bf16[768,384]{1,0:T(8,128)(2,1)S(1)} %slice.93), channel_id=1, source_target_pairs={{0,16},{16,0},{1,17},{17,1},{2,18},{18,2},{3,19},{19,3},{4,20},{20... | collective-permute-start | bytes 1769480 | tf_op jit(solution)/shard_map/ppermute | solution.py:18
  117.3 8.9 %collective-permute-start.30 = (bf16[256,384]{1,0:T(8,128)(2,1)S(1)}, bf16[256,384]{1,0:T(8,128)(2,1)S(1)}, u32[]{:S(2)}, u32[]{:S(2)}) collective-permute-start(bf16[256,384]{1,0:T(8,128)(2,1)S(1)} %slice.143), channel_id=1, source_target_pairs={{0,1},{1,0},{2,3},{3,2},{4,5},{5,4},{6,7},{7,6},{8,9},{9,8},{10,11... | collective-permute-start | bytes 589832 | tf_op jit(solution)/shard_map/ppermute | solution.py:18

commit v10 on v9

--- a/solution.py
+++ b/solution.py
@@ -138,6 +138,8 @@
     both, partner_rows = tie(both, rows(core, 1 - xh))
     came_rows = swap(partner_rows, "xh")
     other_rows = swap(came_rows, "core")
+    outgoing, came_rows = tie(jnp.where(section == 0, residual, upstream), came_rows)
+    early = swap(outgoing, "section")
     block = jnp.concatenate(
         [jnp.concatenate([rows(core, xh), came_rows], 1), jnp.concatenate([rows(1 - core, xh), other_rows], 1)], 0
     )
@@ -162,8 +164,7 @@
         ctx_flat, block, (((1,), (1,)), ((), ())), preferred_element_type=F32
     ).astype(BF16).reshape(n_z, block_tokens, features)
     ring = ring_steps(lambda away: pick(partial_branch, wrap(z + away, n_z)), "z")
-    *step, outgoing = tie(*next(ring), jnp.where(section == 0, residual, upstream))
-    early = swap(outgoing, "section")
+    *step, early = tie(*next(ring), early)
     step = ring.send(step)
     far = jnp.concatenate(far_blocks, 0)[None]
     grad_flat = place(grad_all, far, (wrap(z + n_z // 2, n_z), 0, 0)).reshape(tokens, features)
@@ -177,14 +178,15 @@
         return (norm_factor * product).astype(BF16)
 
     own_product = for_features(ctx_flat[:, :width])
-    partner_product = swap(for_features(ctx_flat[:, width:]), "xh")
+    partner_product = lax.all_gather(for_features(ctx_flat[:, width:]), "xh")
     other_product = swap(own_product[piece:], "core")
     partial_ctx = partial_ctx.reshape(n_z, n_y, z_tokens, 2 * width)
     ctx_ring = ring_steps(lambda away: pick(partial_ctx, wrap(y + away, n_y), 1).reshape(group_tokens, 2 * width), "y")
-    *step, ctx_low, ctx_high, other_product, early = tie(*step, *next(ctx_ring), other_product, early)
+    *step, ctx_low, ctx_high, other_product = tie(*step, *next(ctx_ring), other_product)
     step = ring.send(step)
     ctx_step = ctx_ring.send((ctx_low, ctx_high))
     *ctx_step, partner_product = tie(*ctx_step, partner_product)
+    partner_product = pick(partner_product, 1 - xh)
     branch = ring.send(step).astype(BF16)
     branch = branch.reshape(1, group, own_count, features)
     branch = jnp.concatenate([branch, branch], 0).reshape(2 * group, own_count, features)
@@ -204,8 +206,8 @@
 
     kept = add(own_product[:piece], other_product)
     came = add(partner_product[:piece], other_partner)
-    first = xh == 0
-    weight_grad = jnp.concatenate([jnp.where(first, kept, came), jnp.where(first, came, kept)], 0)
+    weight_grad = place(jnp.zeros((n_xh * piece, width), BF16), kept, (xh * piece, 0))
+    weight_grad = place(weight_grad, came, ((1 - xh) * piece, 0))
     return (forward[None], received[None], ctx_grad[None], weight_grad[None])
 
 

time: 133 us -> 147 us (1.11)
  between operations: 1.22 us -> 14.6 us
  starting transfers between devices: 65.9 us -> 61.1 us
  local copies, waits for them, and re-layouts: 7.93 us -> 10.4 us
  other arithmetic: 7.82 us -> 10.2 us
  waiting for transfers between devices: 33.7 us -> 31.6 us
  matrix products: 12.1 us -> 13.7 us
    ppermute x32 -> x31, waiting for transfers between devices: 33.7 us -> 26 us  [shift(): return lax.ppermute(value, axis, [(i, (i + by) % n) for i in range(n)])]
    ppermute x32 -> x31, starting transfers between devices: 54.4 us -> 50.5 us  [shift(): return lax.ppermute(value, axis, [(i, (i + by) % n) for i in range(n)])]
    all_to_all x1, waiting for transfers between devices: 0.01 us -> 3.16 us  [shards(): branch = lax.all_to_all(branch, ('section', 'y', 'xh'), 0, 0, tiled=True)]
    dynamic_update_slice x1 -> x3, other arithmetic: 0.03 us -> 2.9 us  [place(): return lax.dynamic_update_slice(buffer, block, starts)]
    all_gather x0 -> x1, waiting for transfers between devices: none -> 2.41 us  [shards(): partner_product = lax.all_gather(for_features(ctx_flat[:, width:]), 'xh')]
    select_n x1 -> x0, other arithmetic: 1.96 us -> none  [shards(): jnp.where(first, kept, came)]
  transfers between devices with their start and end apart: 34 -> 34, of which waited for: 10 -> 11; matrix products, arithmetic and copies ran while one was open for 16% -> 20% of each run, Pallas kernels for 1% -> 1%
where the time goes in v10:
time: 147 us; the launch traced here: 145 us
  starting transfers between devices  61.1 us (42%)
  waiting for transfers between devices  31.6 us (21%)
  between operations  14.6 us (10%)
  matrix products  13.7 us (9%)
  local copies, waits for them, and re-layouts  10.4 us (7%)
  other arithmetic  10.2 us (7%)
  Pallas kernels  3 us (2%)
    ppermute x31, starting transfers between devices, shift(): return lax.ppermute(value, axis, [(i, (i + by) % n) for i in range(n)])  50.5 us
    ppermute x31, waiting for transfers between devices, shift(): return lax.ppermute(value, axis, [(i, (i + by) % n) for i in range(n)])  26 us
    all_to_all x1, starting transfers between devices, shards(): lax.all_to_all(spread, ('y', 'xh'), 0, 0, tiled=True)  5.44 us
    dot_general x1, matrix products, shards(): jnp.dot(grad_flat, block, preferred_element_type=F32).astype(BF16)  5.13 us
    all_to_all x1, starting transfers between devices, shards(): branch = lax.all_to_all(branch, ('section', 'y', 'xh'), 0, 0, tiled=True)  5.13 us
    dot_general x2, matrix products, for_features(): lax.dot_general(grad_flat, features_of, (((0,), (0,)), ((), ())), preferr...  4.69 us
    dot_general x1, matrix products, shards(): lax.dot_general(ctx_flat, block, (((1,), (1,)), ((), ())), preferred_elem...  3.91 us
    all_to_all x1, waiting for transfers between devices, shards(): branch = lax.all_to_all(branch, ('section', 'y', 'xh'), 0, 0, tiled=True)  3.16 us
  transfers between devices with their start and end apart: 34, of which 11 were waited for; matrix products, arithmetic and copies ran while one was open for 20% of the time, Pallas kernels for 1%

profile of v10, /device:TPU:2, one launch (start us, length us, event | category | flops | bytes accessed | tf_op | source)
XLA Modules:
  0.0 144.5 jit_solution(9497066718979146408)
XLA Ops:
  7.2 2.2 %collective-permute-start = (bf16[256,384]{1,0:T(8,128)(2,1)}, bf16[256,384]{1,0:T(8,128)(2,1)S(1)}, u32[]{:S(2)}, u32[]{:S(2)}) collective-permute-start(bf16[256,384]{1,0:T(8,128)(2,1)} %bitcast.123), channel_id=1, source_target_pairs={{0,1},{1,0},{2,3},{3,2},{4,5},{5,4},{6,7},{7,6},{8,9},{9,8},{10,11... | collective-permute-start | bytes 589832 | tf_op jit(solution)/shard_map/ppermute | solution.py:18
  9.5 1.0 copy-done
  10.4 1.3 shard_map.75
  11.8 5.4 %all-to-all-start = ((bf16[8,16,1536]{2,1,0:T(8,128)(2,1)}), bf16[8,16,1536]{2,1,0:T(8,128)(2,1)S(1)}, u32[]{:S(2)}, u32[]{:S(2)}) async-start(bf16[8,16,1536]{2,1,0:T(8,128)(2,1)} %shard_map.75), calls=%async_computation | async-start | bytes 786432 | tf_op jit(solution)/shard_map/all_to_all | solution.py:157
  17.3 2.8 %dynamic-slice_bitcast_fusion.3 = (bf16[768,384]{1,0:T(8,128)(2,1)}, bf16[768,384]{1,0:T(8,128)(2,1)}, bf16[768,384]{1,0:T(8,128)(2,1)}) fusion(bf16[1,12288,384]{2,1,0:T(8,128)(2,1)} %param.6, s32[]{:T(128)S(6)} %select_n.82, s32[]{:T(128)S(6)} %select_n.77, s32[]{:T(128)S(6)} %select_n.85), kind=kLoop, calls=%fused_computation.33 | loop fusion | bytes 3538956 | tf_op jit(solution)/shard_map/dynamic_slice | solution.py:136
  20.1 2.1 %collective-permute-start.1 = (bf16[256,768]{1,0:T(8,128)(2,1)S(1)}, bf16[256,768]{1,0:T(8,128)(2,1)S(1)}, u32[]{:S(2)}, u32[]{:S(2)}) collective-permute-start(bf16[256,768]{1,0:T(8,128)(2,1)S(1)} %pad_maximum_fusion.1), channel_id=1, source_target_pairs={{0,32},{32,64},{64,96},{96,0},{1,33},{33,65},{65,97},{97,1},{2,34}... | collective-permute-start | bytes 1179656 | tf_op jit(solution)/shard_map/ppermute | solution.py:18
  22.2 1.3 collective-permute-start.2
  23.5 0.8 broadcast_select_fusion
  24.3 3.4 %collective-permute-start.5 = (bf16[768,384]{1,0:T(8,128)(2,1)}, bf16[768,384]{1,0:T(8,128)(2,1)}, u32[]{:S(2)}, u32[]{:S(2)}) collective-permute-start(bf16[768,384]{1,0:T(8,128)(2,1)} %get-tuple-element.28), channel_id=1, source_target_pairs={{0,1},{1,0},{2,3},{3,2},{4,5},{5,4},{6,7},{7,6},{8,9},{9,8},{10,11... | collective-permute-start | bytes 1769480 | tf_op jit(solution)/shard_map/ppermute | solution.py:18
  27.7 0.2 broadcast_in_dim.44
  28.0 2.0 %collective-permute-start.12 = (bf16[128,1536]{1,0:T(8,128)(2,1)S(1)}, bf16[128,1536]{1,0:T(8,128)(2,1)S(1)}, u32[]{:S(2)}, u32[]{:S(2)}) collective-permute-start(bf16[128,1536]{1,0:T(8,128)(2,1)S(1)} %bitcast.108), channel_id=1, source_target_pairs={{0,2},{2,4},{4,6},{6,8},{8,10},{10,12},{12,14},{14,0},{1,3},{3,5},... | collective-permute-start | bytes 1179656 | tf_op jit(solution)/shard_map/ppermute | solution.py:18
  30.0 4.0 %collective-permute-start.13 = (bf16[128,1536]{1,0:T(8,128)(2,1)S(1)}, bf16[128,1536]{1,0:T(8,128)(2,1)S(1)}, u32[]{:S(2)}, u32[]{:S(2)}) collective-permute-start(bf16[128,1536]{1,0:T(8,128)(2,1)S(1)} %bitcast.109), channel_id=1, source_target_pairs={{0,14},{2,0},{4,2},{6,4},{8,6},{10,8},{12,10},{14,12},{1,15},{3,1}... | collective-permute-start | bytes 1179656 | tf_op jit(solution)/shard_map/ppermute | solution.py:18
  34.0 0.3 broadcast_in_dim.45
  34.3 0.3 collective-permute-start.3
  34.7 0.9 slice.103
  35.6 3.1 %collective-permute-start.4 = (bf16[128,768]{1,0:T(8,128)(2,1)S(1)}, bf16[128,768]{1,0:T(8,128)(2,1)S(1)}, u32[]{:S(2)}, u32[]{:S(2)}) collective-permute-start(bf16[128,768]{1,0:T(8,128)(2,1)S(1)} %slice.103), channel_id=1, source_target_pairs={{0,96},{32,0},{64,32},{96,64},{1,97},{33,1},{65,33},{97,65},{2,98}... | collective-permute-start | bytes 589832 | tf_op jit(solution)/shard_map/ppermute | solution.py:18
  38.7 1.0 constant_dynamic-update-slice_fusion.1
  39.8 1.6 %collective-permute-done.12 = bf16[128,1536]{1,0:T(8,128)(2,1)S(1)} collective-permute-done((bf16[128,1536]{1,0:T(8,128)(2,1)S(1)}, bf16[128,1536]{1,0:T(8,128)(2,1)S(1)}, u32[]{:S(2)}, u32[]{:S(2)}) %collective-permute-start.12) | collective-permute-done | bytes 393248 | tf_op jit(solution)/shard_map/ppermute | solution.py:18
  41.3 0.2 collective-permute-start.14
  41.5 4.0 %collective-permute-start.15 = (bf16[128,1536]{1,0:T(8,128)(2,1)S(1)}, bf16[128,1536]{1,0:T(8,128)(2,1)S(1)}, u32[]{:S(2)}, u32[]{:S(2)}) collective-permute-start(bf16[128,1536]{1,0:T(8,128)(2,1)S(1)} %collective-permute-done.13), channel_id=1, source_target_pairs={{0,14},{2,0},{4,2},{6,4},{8,6},{10,8},{12,10},{14,12},{1,15},{3,1}... | collective-permute-start | bytes 1179656 | tf_op jit(solution)/shard_map/ppermute | solution.py:18
  45.7 0.7 collective-permute-start.9
  46.4 7.2 %collective-permute-done.14 = bf16[128,1536]{1,0:T(8,128)(2,1)S(1)} collective-permute-done((bf16[128,1536]{1,0:T(8,128)(2,1)S(1)}, bf16[128,1536]{1,0:T(8,128)(2,1)S(1)}, u32[]{:S(2)}, u32[]{:S(2)}) %collective-permute-start.14) | collective-permute-done | bytes 393248 | tf_op jit(solution)/shard_map/ppermute | solution.py:18
  53.7 3.2 %collective-permute-start.17 = (bf16[128,1536]{1,0:T(8,128)(2,1)S(1)}, bf16[128,1536]{1,0:T(8,128)(2,1)S(1)}, u32[]{:S(2)}, u32[]{:S(2)}) collective-permute-start(bf16[128,1536]{1,0:T(8,128)(2,1)S(1)} %collective-permute-done.15), channel_id=1, source_target_pairs={{0,14},{2,0},{4,2},{6,4},{8,6},{10,8},{12,10},{14,12},{1,15},{3,1}... | collective-permute-start | bytes 1179656 | tf_op jit(solution)/shard_map/ppermute | solution.py:18
  57.0 3.9 %convolution_convert_fusion = bf16[1024,1536]{1,0:T(8,128)(2,1)S(1)} fusion(bf16[1024,768]{1,0:T(8,128)(2,1)S(1)} %bitcast.105, bf16[768,384]{1,0:T(8,128)(2,1)S(1)} %collective-permute-done.6, bf16[768,384]{1,0:T(8,128)(2,1)S(1)} %copy-done.10, bf16[768,384]{1,0:T(8,128)(2,1)} %collective-permute-done.5, bf16[768,384]{1,0:T(8,128)(2,1)S(1)} %copy-done.8), kind=kOutput, calls=%fused_computation | convolution fusion | flops 2426929152 | bytes 7077888 | tf_op jit(solution)/shard_map/dot_general | solution.py:163
  61.2 3.2 %collective-permute-start.8 = (bf16[128,768]{1,0:T(8,128)(2,1)S(1)}, bf16[128,768]{1,0:T(8,128)(2,1)S(1)}, u32[]{:S(2)}, u32[]{:S(2)}) collective-permute-start(bf16[128,768]{1,0:T(8,128)(2,1)S(1)} %get-tuple-element.66), channel_id=1, source_target_pairs={{0,14},{2,0},{4,2},{6,4},{8,6},{10,8},{12,10},{14,12},{1,15},{3,1}... | collective-permute-start | bytes 589832 | tf_op jit(solution)/shard_map/ppermute | solution.py:18
  64.5 1.1 collective-permute-done.16
  65.7 3.3 %collective-permute-start.19 = (bf16[64,1536]{1,0:T(8,128)(2,1)S(1)}, bf16[64,1536]{1,0:T(8,128)(2,1)S(1)}, u32[]{:S(2)}, u32[]{:S(2)}) collective-permute-start(bf16[64,1536]{1,0:T(8,128)(2,1)S(1)} %slice.111), channel_id=1, source_target_pairs={{0,14},{2,0},{4,2},{6,4},{8,6},{10,8},{12,10},{14,12},{1,15},{3,1}... | collective-permute-start | bytes 589832 | tf_op jit(solution)/shard_map/ppermute | solution.py:18
  69.1 1.1 collective-permute-done.7
  70.3 0.8 pad_maximum_fusion.4
  71.1 3.2 %collective-permute-start.11 = (bf16[128,1536]{1,0:T(8,128)(2,1)}, bf16[128,1536]{1,0:T(8,128)(2,1)}, u32[]{:S(2)}, u32[]{:S(2)}) collective-permute-start(bf16[128,1536]{1,0:T(8,128)(2,1)} %pad_maximum_fusion.4), channel_id=1, source_target_pairs={{0,14},{2,0},{4,2},{6,4},{8,6},{10,8},{12,10},{14,12},{1,15},{3,1}... | collective-permute-start | bytes 1179656 | tf_op jit(solution)/shard_map/ppermute | solution.py:18
  74.3 0.8 pad_maximum_fusion.3
  75.2 1.8 %fusion = bf16[1536,384]{1,0:T(8,128)(2,1)S(1)} fusion(bf16[1024,1536]{1,0:T(8,128)(2,1)S(1)} %bitcast.98, bf16[1024,768]{1,0:T(8,128)(2,1)S(1)} %bitcast.106), kind=kOutput, calls=%fused_computation.3 | convolution fusion | flops 1209139200 | bytes 5111808 | tf_op jit(solution)/shard_map/dot_general | solution.py:177
  77.0 2.9 %fusion.1 = bf16[1536,384]{1,0:T(8,128)(2,1)} fusion(bf16[1024,1536]{1,0:T(8,128)(2,1)S(1)} %bitcast.99, bf16[1024,768]{1,0:T(8,128)(2,1)S(1)} %bitcast.107), kind=kOutput, calls=%fused_computation.4 | convolution fusion | flops 1209139200 | bytes 5111808 | tf_op jit(solution)/shard_map/dot_general | solution.py:177
  80.0 0.3 collective-permute-start.24
  80.3 0.7 copy-done.9
  81.0 5.1 %convolution_convert_fusion.1 = bf16[1024,768]{1,0:T(8,128)(2,1)S(1)} fusion(bf16[1024,1536]{1,0:T(8,128)(2,1)} %bitcast.100, bf16[768,384]{1,0:T(8,128)(2,1)} %copy-done.13, bf16[768,384]{1,0:T(8,128)(2,1)} %get-tuple-element.52, bf16[768,384]{1,0:T(8,128)(2,1)} %collective-permute-done.5, bf16[768,384]{1,0:T(8,128)(2,1)S(1)} %copy-done.9), kind=kOutput, calls=%fused_computation.6 | convolution fusion | flops 2426142720 | bytes 7077888 | tf_op jit(solution)/shard_map/dot_general | solution.py:171
  86.1 1.4 fusion.7
  87.6 3.3 %collective-permute-start.21 = (bf16[128,1536]{1,0:T(8,128)(2,1)S(1)}, bf16[128,1536]{1,0:T(8,128)(2,1)S(1)}, u32[]{:S(2)}, u32[]{:S(2)}) collective-permute-start(bf16[128,1536]{1,0:T(8,128)(2,1)S(1)} %get-tuple-element.55), channel_id=1, source_target_pairs={{0,14},{2,0},{4,2},{6,4},{8,6},{10,8},{12,10},{14,12},{1,15},{3,1}... | collective-permute-start | bytes 1179656 | tf_op jit(solution)/shard_map/ppermute | solution.py:18
  90.9 0.1 constant_dynamic-slice_fusion.2
  91.2 3.2 %collective-permute-start.23 = (bf16[256,384]{1,0:T(8,128)(2,1)S(1)}, bf16[256,384]{1,0:T(8,128)(2,1)S(1)}, u32[]{:S(2)}, u32[]{:S(2)}) collective-permute-start(bf16[256,384]{1,0:T(8,128)(2,1)S(1)} %get-tuple-element.64), channel_id=1, source_target_pairs={{0,96},{32,0},{64,32},{96,64},{1,97},{33,1},{65,33},{97,65},{2,98}... | collective-permute-start | bytes 589832 | tf_op jit(solution)/shard_map/ppermute | solution.py:18
  94.4 4.3 %collective-permute-done.22 = bf16[256,384]{1,0:T(8,128)(2,1)S(1)} collective-permute-done((bf16[256,384]{1,0:T(8,128)(2,1)S(1)}, bf16[256,384]{1,0:T(8,128)(2,1)S(1)}, u32[]{:S(2)}, u32[]{:S(2)}) %collective-permute-start.22) | collective-permute-done | bytes 196640 | tf_op jit(solution)/shard_map/ppermute | solution.py:18
  98.8 1.2 collective-permute-done.20
  100.0 0.2 fusion.9
  100.2 2.3 %collective-permute-start.25 = (bf16[128,1536]{1,0:T(8,128)(2,1)S(1)}, bf16[128,1536]{1,0:T(8,128)(2,1)S(1)}, u32[]{:S(2)}, u32[]{:S(2)}) collective-permute-start(bf16[128,1536]{1,0:T(8,128)(2,1)S(1)} %get-tuple-element.53), channel_id=1, source_target_pairs={{0,2},{2,4},{4,6},{6,8},{8,10},{10,12},{12,14},{14,0},{1,3},{3,5},... | collective-permute-start | bytes 1179656 | tf_op jit(solution)/shard_map/ppermute | solution.py:18
  102.4 1.1 collective-permute-start.26
  103.6 1.8 %collective-permute-start.28 = (bf16[256,768]{1,0:T(8,128)(2,1)S(1)}, bf16[256,768]{1,0:T(8,128)(2,1)S(1)}, u32[]{:S(2)}, u32[]{:S(2)}) collective-permute-start(bf16[256,768]{1,0:T(8,128)(2,1)S(1)} %pad_maximum_fusion.6), channel_id=1, source_target_pairs={{0,96},{32,0},{64,32},{96,64},{1,97},{33,1},{65,33},{97,65},{2,98}... | collective-permute-start | bytes 1179656 | tf_op jit(solution)/shard_map/ppermute | solution.py:18
  105.5 0.3 collective-permute-start.27
  105.9 5.9 %collective-permute-done.25 = bf16[128,1536]{1,0:T(8,128)(2,1)S(1)} collective-permute-done((bf16[128,1536]{1,0:T(8,128)(2,1)S(1)}, bf16[128,1536]{1,0:T(8,128)(2,1)S(1)}, u32[]{:S(2)}, u32[]{:S(2)}) %collective-permute-start.25) | collective-permute-done | bytes 393248 | tf_op jit(solution)/shard_map/ppermute | solution.py:18
  111.8 0.5 collective-permute-done.26
  112.3 0.2 fusion.11
  112.4 1.0 pad_maximum_fusion
  113.4 5.1 %all-to-all-start.1 = ((bf16[16,16,1536]{2,1,0:T(8,128)(2,1)}), bf16[16,16,1536]{2,1,0:T(8,128)(2,1)S(1)}, u32[]{:S(2)}, u32[]{:S(2)}) async-start(bf16[16,16,1536]{2,1,0:T(8,128)(2,1)} %bitcast.35), calls=%async_computation.1 | async-start | bytes 1572864 | tf_op jit(solution)/shard_map/all_to_all | solution.py:193
  118.5 2.4 %all-gather.3.cloned.1.call-done = bf16[3072,384]{1,0:T(8,128)(2,1)} async-done(((bf16[1536,384]{1,0:T(8,128)(2,1)}), bf16[3072,384]{1,0:T(8,128)(2,1)}) %all-gather.3.cloned.1.call-update) | async-done | bytes 2359312 | tf_op jit(solution)/shard_map/all_gather | solution.py:181
  120.9 2.0 %dynamic-slice_bitcast_fusion.1 = bf16[768,384]{1,0:T(8,128)(2,1)} fusion(bf16[2,1536,384]{2,1,0:T(8,128)(2,1)} %bitcast.121, s32[]{:T(128)S(6)} %select_n.94, s32[]{:T(128)S(6)} %add.220), kind=kLoop, calls=%fused_computation.31 | loop fusion | bytes 1179656 | tf_op jit(solution)/shard_map/slice | solution.py:197
  122.9 0.2 fusion.5
  123.1 0.7 slice.139
  123.8 1.4 collective-permute-start.29
  125.2 0.1 broadcast_in_dim.56
  125.3 1.4 fusion.13
  126.8 3.2 %all-to-all-done.1 = bf16[16,16,1536]{2,1,0:T(8,128)(2,1)S(1)} async-done(((bf16[16,16,1536]{2,1,0:T(8,128)(2,1)}), bf16[16,16,1536]{2,1,0:T(8,128)(2,1)S(1)}, u32[]{:S(2)}, u32[]{:S(2)}) %all-to-all-start.1) | async-done | bytes 786464 | tf_op jit(solution)/shard_map/all_to_all | solution.py:193
  129.9 3.0 %collective-permute-done.29 = bf16[256,384]{1,0:T(8,128)(2,1)} collective-permute-done((bf16[256,384]{1,0:T(8,128)(2,1)}, bf16[256,384]{1,0:T(8,128)(2,1)}, u32[]{:S(2)}, u32[]{:S(2)}) %collective-permute-start.29) | collective-permute-done | bytes 196640 | tf_op jit(solution)/shard_map/ppermute | solution.py:18
  132.9 1.7 %fusion.18 = bf16[1,256,384]{2,1,0:T(8,128)(2,1)} fusion(bf16[256,384]{1,0:T(8,128)(2,1)} %collective-permute-done.29, f32[256,768]{1,0:T(8,128)S(1)} %fusion.5), kind=kLoop, calls=%fused_computation.61 | loop fusion | flops 294912 | bytes 786432 | tf_op jit(solution)/shard_map/broadcast_in_dim | solution.py:211
  134.5 1.4 fusion.15
  136.0 1.7 %shard_map.76 = (bf16[16,12288]{1,0:T(8,128)(2,1)}, bf16[16,12288]{1,0:T(8,128)(2,1)}) custom-call(s32[2]{0:T(128)S(1)} %pad_add_fusion.at_ref, bf16[2,8,16,1536]{3,2,1,0:T(8,128)(2,1)S(1)} %bitcast.95, bf16[16,12288]{1,0:T(8,128)(2,1)S(1)} %bitcast.97, bf16[16,12288]{1,0:T(8,128)(2,1)S(1)} %collective-permute-done.9.early_ref), custom_call_target="tpu_custom_call" | custom-call | tf_op jit(solution)/shard_map/pallas_call | solution.py:109
  (90 shorter events, 1.6 us)
Async XLA Ops:
  7.2 12.9 %collective-permute-start = (bf16[256,384]{1,0:T(8,128)(2,1)}, bf16[256,384]{1,0:T(8,128)(2,1)S(1)}, u32[]{:S(2)}, u32[]{:S(2)}) collective-permute-start(bf16[256,384]{1,0:T(8,128)(2,1)} %bitcast.123), channel_id=1, source_target_pairs={{0,1},{1,0},{2,3},{3,2},{4,5},{5,4},{6,7},{7,6},{8,9},{9,8},{10,11... | collective-permute-start | bytes 589832 | tf_op jit(solution)/shard_map/ppermute | solution.py:18
  9.5 1.0 copy-start
  11.8 8.3 %copy-start.12 = (bf16[1,256,384]{2,1,0:T(8,128)(2,1)S(1)}, bf16[1,256,384]{2,1,0:T(8,128)(2,1)}, u32[]{:S(2)}) copy-start(bf16[1,256,384]{2,1,0:T(8,128)(2,1)} %param.5) | copy-start | bytes 589828
  11.8 16.2 %all-to-all-start = ((bf16[8,16,1536]{2,1,0:T(8,128)(2,1)}), bf16[8,16,1536]{2,1,0:T(8,128)(2,1)S(1)}, u32[]{:S(2)}, u32[]{:S(2)}) async-start(bf16[8,16,1536]{2,1,0:T(8,128)(2,1)} %shard_map.75), calls=%async_computation | async-start | bytes 786432 | tf_op jit(solution)/shard_map/all_to_all | solution.py:157
  17.2 6.3 %copy-start.1 = (bf16[1,16,12288]{2,1,0:T(8,128)(2,1)S(1)}, bf16[1,16,12288]{2,1,0:T(8,128)(2,1)}, u32[]{:S(2)}) copy-start(bf16[1,16,12288]{2,1,0:T(8,128)(2,1)} %param.7) | copy-start | bytes 1179652
  17.2 6.3 %copy-start.2 = (bf16[1,16,12288]{2,1,0:T(8,128)(2,1)S(1)}, bf16[1,16,12288]{2,1,0:T(8,128)(2,1)}, u32[]{:S(2)}) copy-start(bf16[1,16,12288]{2,1,0:T(8,128)(2,1)} %param.4) | copy-start | bytes 1179652
  17.2 103.7 %all-gather.3.cloned.1.call-start = ((), (), s32[]{:S(2)}) async-start(), calls=%async_computation.2 | async-start | bytes 3538944 | tf_op jit(solution)/shard_map/all_gather | solution.py:181
  20.1 14.2 %collective-permute-start.1 = (bf16[256,768]{1,0:T(8,128)(2,1)S(1)}, bf16[256,768]{1,0:T(8,128)(2,1)S(1)}, u32[]{:S(2)}, u32[]{:S(2)}) collective-permute-start(bf16[256,768]{1,0:T(8,128)(2,1)S(1)} %pad_maximum_fusion.1), channel_id=1, source_target_pairs={{0,32},{32,64},{64,96},{96,0},{1,33},{33,65},{65,97},{97,1},{2,34}... | collective-permute-start | bytes 1179656 | tf_op jit(solution)/shard_map/ppermute | solution.py:18
  22.2 12.5 %collective-permute-start.2 = (bf16[256,768]{1,0:T(8,128)(2,1)S(1)}, bf16[256,768]{1,0:T(8,128)(2,1)}, u32[]{:S(2)}, u32[]{:S(2)}) collective-permute-start(bf16[256,768]{1,0:T(8,128)(2,1)S(1)} %pad_maximum_fusion.1), channel_id=1, source_target_pairs={{0,96},{32,0},{64,32},{96,64},{1,97},{33,1},{65,33},{97,65},{2,98}... | collective-permute-start | bytes 1179656 | tf_op jit(solution)/shard_map/ppermute | solution.py:18
  24.3 21.3 %collective-permute-start.5 = (bf16[768,384]{1,0:T(8,128)(2,1)}, bf16[768,384]{1,0:T(8,128)(2,1)}, u32[]{:S(2)}, u32[]{:S(2)}) collective-permute-start(bf16[768,384]{1,0:T(8,128)(2,1)} %get-tuple-element.28), channel_id=1, source_target_pairs={{0,1},{1,0},{2,3},{3,2},{4,5},{5,4},{6,7},{7,6},{8,9},{9,8},{10,11... | collective-permute-start | bytes 1769480 | tf_op jit(solution)/shard_map/ppermute | solution.py:18
  28.0 13.4 %collective-permute-start.12 = (bf16[128,1536]{1,0:T(8,128)(2,1)S(1)}, bf16[128,1536]{1,0:T(8,128)(2,1)S(1)}, u32[]{:S(2)}, u32[]{:S(2)}) collective-permute-start(bf16[128,1536]{1,0:T(8,128)(2,1)S(1)} %bitcast.108), channel_id=1, source_target_pairs={{0,2},{2,4},{4,6},{6,8},{8,10},{10,12},{12,14},{14,0},{1,3},{3,5},... | collective-permute-start | bytes 1179656 | tf_op jit(solution)/shard_map/ppermute | solution.py:18
  30.0 11.6 %collective-permute-start.13 = (bf16[128,1536]{1,0:T(8,128)(2,1)S(1)}, bf16[128,1536]{1,0:T(8,128)(2,1)S(1)}, u32[]{:S(2)}, u32[]{:S(2)}) collective-permute-start(bf16[128,1536]{1,0:T(8,128)(2,1)S(1)} %bitcast.109), channel_id=1, source_target_pairs={{0,14},{2,0},{4,2},{6,4},{8,6},{10,8},{12,10},{14,12},{1,15},{3,1}... | collective-permute-start | bytes 1179656 | tf_op jit(solution)/shard_map/ppermute | solution.py:18
  34.2 11.4 %copy-start.11 = (bf16[16,12288]{1,0:T(8,128)(2,1)S(1)}, bf16[16,12288]{1,0:T(8,128)(2,1)}, u32[]{:S(2)}) copy-start(bf16[16,12288]{1,0:T(8,128)(2,1)} %broadcast_select_fusion) | copy-start | bytes 1179652
  34.3 12.0 %collective-permute-start.3 = (bf16[128,768]{1,0:T(8,128)(2,1)S(1)}, bf16[128,768]{1,0:T(8,128)(2,1)S(1)}, u32[]{:S(2)}, u32[]{:S(2)}) collective-permute-start(bf16[128,768]{1,0:T(8,128)(2,1)S(1)} %slice.102), channel_id=1, source_target_pairs={{0,32},{32,64},{64,96},{96,0},{1,33},{33,65},{65,97},{97,1},{2,34}... | collective-permute-start | bytes 589832 | tf_op jit(solution)/shard_map/ppermute | solution.py:18
  35.6 10.7 %collective-permute-start.4 = (bf16[128,768]{1,0:T(8,128)(2,1)S(1)}, bf16[128,768]{1,0:T(8,128)(2,1)S(1)}, u32[]{:S(2)}, u32[]{:S(2)}) collective-permute-start(bf16[128,768]{1,0:T(8,128)(2,1)S(1)} %slice.103), channel_id=1, source_target_pairs={{0,96},{32,0},{64,32},{96,64},{1,97},{33,1},{65,33},{97,65},{2,98}... | collective-permute-start | bytes 589832 | tf_op jit(solution)/shard_map/ppermute | solution.py:18
  39.7 17.3 %copy-start.8 = (bf16[768,384]{1,0:T(8,128)(2,1)S(1)}, bf16[768,384]{1,0:T(8,128)(2,1)}, u32[]{:S(2)}) copy-start(bf16[768,384]{1,0:T(8,128)(2,1)} %get-tuple-element.50) | copy-start | bytes 1769476
  39.8 17.3 %copy-start.10 = (bf16[768,384]{1,0:T(8,128)(2,1)S(1)}, bf16[768,384]{1,0:T(8,128)(2,1)}, u32[]{:S(2)}) copy-start(bf16[768,384]{1,0:T(8,128)(2,1)} %get-tuple-element.52) | copy-start | bytes 1769476
  41.3 12.3 %collective-permute-start.14 = (bf16[128,1536]{1,0:T(8,128)(2,1)S(1)}, bf16[128,1536]{1,0:T(8,128)(2,1)S(1)}, u32[]{:S(2)}, u32[]{:S(2)}) collective-permute-start(bf16[128,1536]{1,0:T(8,128)(2,1)S(1)} %collective-permute-done.12), channel_id=1, source_target_pairs={{0,2},{2,4},{4,6},{6,8},{8,10},{10,12},{12,14},{14,0},{1,3},{3,5},... | collective-permute-start | bytes 1179656 | tf_op jit(solution)/shard_map/ppermute | solution.py:18
  41.5 12.1 %collective-permute-start.15 = (bf16[128,1536]{1,0:T(8,128)(2,1)S(1)}, bf16[128,1536]{1,0:T(8,128)(2,1)S(1)}, u32[]{:S(2)}, u32[]{:S(2)}) collective-permute-start(bf16[128,1536]{1,0:T(8,128)(2,1)S(1)} %collective-permute-done.13), channel_id=1, source_target_pairs={{0,14},{2,0},{4,2},{6,4},{8,6},{10,8},{12,10},{14,12},{1,15},{3,1}... | collective-permute-start | bytes 1179656 | tf_op jit(solution)/shard_map/ppermute | solution.py:18
  45.7 23.5 %collective-permute-start.9 = (bf16[16,12288]{1,0:T(8,128)(2,1)S(1)}, bf16[16,12288]{1,0:T(8,128)(2,1)S(1)}, u32[]{:S(2)}, u32[]{:S(2)}) collective-permute-start(bf16[16,12288]{1,0:T(8,128)(2,1)S(1)} %copy-done.11), channel_id=1, source_target_pairs={{0,128},{128,0},{1,129},{129,1},{2,130},{130,2},{3,131},{131,3},{4... | collective-permute-start | bytes 1179656 | tf_op jit(solution)/shard_map/ppermute | solution.py:18
  46.3 10.6 %collective-permute-start.6 = (bf16[768,384]{1,0:T(8,128)(2,1)}, bf16[768,384]{1,0:T(8,128)(2,1)S(1)}, u32[]{:S(2)}, u32[]{:S(2)}) collective-permute-start(bf16[768,384]{1,0:T(8,128)(2,1)} %collective-permute-done.5), channel_id=1, source_target_pairs={{0,16},{16,0},{1,17},{17,1},{2,18},{18,2},{3,19},{19,3},{4,20},{20... | collective-permute-start | bytes 1769480 | tf_op jit(solution)/shard_map/ppermute | solution.py:18
  53.7 11.9 %collective-permute-start.16 = (bf16[128,1536]{1,0:T(8,128)(2,1)S(1)}, bf16[128,1536]{1,0:T(8,128)(2,1)S(1)}, u32[]{:S(2)}, u32[]{:S(2)}) collective-permute-start(bf16[128,1536]{1,0:T(8,128)(2,1)S(1)} %collective-permute-done.14), channel_id=1, source_target_pairs={{0,2},{2,4},{4,6},{6,8},{8,10},{10,12},{12,14},{14,0},{1,3},{3,5},... | collective-permute-start | bytes 1179656 | tf_op jit(solution)/shard_map/ppermute | solution.py:18
  53.7 12.0 %collective-permute-start.17 = (bf16[128,1536]{1,0:T(8,128)(2,1)S(1)}, bf16[128,1536]{1,0:T(8,128)(2,1)S(1)}, u32[]{:S(2)}, u32[]{:S(2)}) collective-permute-start(bf16[128,1536]{1,0:T(8,128)(2,1)S(1)} %collective-permute-done.15), channel_id=1, source_target_pairs={{0,14},{2,0},{4,2},{6,4},{8,6},{10,8},{12,10},{14,12},{1,15},{3,1}... | collective-permute-start | bytes 1179656 | tf_op jit(solution)/shard_map/ppermute | solution.py:18
  57.0 3.9 %copy-start.13 = (bf16[768,384]{1,0:T(8,128)(2,1)}, bf16[768,384]{1,0:T(8,128)(2,1)S(1)}, u32[]{:S(2)}) copy-start(bf16[768,384]{1,0:T(8,128)(2,1)S(1)} %collective-permute-done.6) | copy-start | bytes 1769476
  60.9 4.8 %copy-start.4 = (bf16[1024,1536]{1,0:T(8,128)(2,1)}, bf16[1024,1536]{1,0:T(8,128)(2,1)S(1)}, u32[]{:S(2)}) copy-start(bf16[1024,1536]{1,0:T(8,128)(2,1)S(1)} %convolution_convert_fusion) | copy-start | bytes 9437188
  61.1 9.1 %collective-permute-start.7 = (bf16[128,768]{1,0:T(8,128)(2,1)S(1)}, bf16[128,768]{1,0:T(8,128)(2,1)S(1)}, u32[]{:S(2)}, u32[]{:S(2)}) collective-permute-start(bf16[128,768]{1,0:T(8,128)(2,1)S(1)} %get-tuple-element.67), channel_id=1, source_target_pairs={{0,2},{2,4},{4,6},{6,8},{8,10},{10,12},{12,14},{14,0},{1,3},{3,5},... | collective-permute-start | bytes 589832 | tf_op jit(solution)/shard_map/ppermute | solution.py:18
  61.2 9.0 %collective-permute-start.8 = (bf16[128,768]{1,0:T(8,128)(2,1)S(1)}, bf16[128,768]{1,0:T(8,128)(2,1)S(1)}, u32[]{:S(2)}, u32[]{:S(2)}) collective-permute-start(bf16[128,768]{1,0:T(8,128)(2,1)S(1)} %get-tuple-element.66), channel_id=1, source_target_pairs={{0,14},{2,0},{4,2},{6,4},{8,6},{10,8},{12,10},{14,12},{1,15},{3,1}... | collective-permute-start | bytes 589832 | tf_op jit(solution)/shard_map/ppermute | solution.py:18
  65.6 9.5 %collective-permute-start.18 = (bf16[64,1536]{1,0:T(8,128)(2,1)S(1)}, bf16[64,1536]{1,0:T(8,128)(2,1)S(1)}, u32[]{:S(2)}, u32[]{:S(2)}) collective-permute-start(bf16[64,1536]{1,0:T(8,128)(2,1)S(1)} %slice.110), channel_id=1, source_target_pairs={{0,2},{2,4},{4,6},{6,8},{8,10},{10,12},{12,14},{14,0},{1,3},{3,5},... | collective-permute-start | bytes 589832 | tf_op jit(solution)/shard_map/ppermute | solution.py:18
  65.7 9.4 %collective-permute-start.19 = (bf16[64,1536]{1,0:T(8,128)(2,1)S(1)}, bf16[64,1536]{1,0:T(8,128)(2,1)S(1)}, u32[]{:S(2)}, u32[]{:S(2)}) collective-permute-start(bf16[64,1536]{1,0:T(8,128)(2,1)S(1)} %slice.111), channel_id=1, source_target_pairs={{0,14},{2,0},{4,2},{6,4},{8,6},{10,8},{12,10},{14,12},{1,15},{3,1}... | collective-permute-start | bytes 589832 | tf_op jit(solution)/shard_map/ppermute | solution.py:18
  71.1 15.1 %collective-permute-start.11 = (bf16[128,1536]{1,0:T(8,128)(2,1)}, bf16[128,1536]{1,0:T(8,128)(2,1)}, u32[]{:S(2)}, u32[]{:S(2)}) collective-permute-start(bf16[128,1536]{1,0:T(8,128)(2,1)} %pad_maximum_fusion.4), channel_id=1, source_target_pairs={{0,14},{2,0},{4,2},{6,4},{8,6},{10,8},{12,10},{14,12},{1,15},{3,1}... | collective-permute-start | bytes 1179656 | tf_op jit(solution)/shard_map/ppermute | solution.py:18
  75.1 11.0 %collective-permute-start.10 = (bf16[128,1536]{1,0:T(8,128)(2,1)}, bf16[128,1536]{1,0:T(8,128)(2,1)}, u32[]{:S(2)}, u32[]{:S(2)}) collective-permute-start(bf16[128,1536]{1,0:T(8,128)(2,1)} %pad_maximum_fusion.3), channel_id=1, source_target_pairs={{0,2},{2,4},{4,6},{6,8},{8,10},{10,12},{12,14},{14,0},{1,3},{3,5},... | collective-permute-start | bytes 1179656 | tf_op jit(solution)/shard_map/ppermute | solution.py:18
  75.2 1.9 %copy-start.3 = (bf16[8,128,1536]{2,1,0:T(8,128)(2,1)}, bf16[8,128,1536]{2,1,0:T(8,128)(2,1)S(1)}, u32[]{:S(2)}) copy-start(bf16[8,128,1536]{2,1,0:T(8,128)(2,1)S(1)} %fusion.17) | copy-start | bytes 9437188
  77.0 9.1 %copy-start.7 = (bf16[1536,384]{1,0:T(8,128)(2,1)}, bf16[1536,384]{1,0:T(8,128)(2,1)S(1)}, u32[]{:S(2)}) copy-start(bf16[1536,384]{1,0:T(8,128)(2,1)S(1)} %fusion) | copy-start | bytes 3538948
  79.9 1.1 copy-start.9
  80.0 18.8 %collective-permute-start.24 = (bf16[768,384]{1,0:T(8,128)(2,1)S(1)}, bf16[768,384]{1,0:T(8,128)(2,1)}, u32[]{:S(2)}, u32[]{:S(2)}) collective-permute-start(bf16[768,384]{1,0:T(8,128)(2,1)S(1)} %slice.115), channel_id=1, source_target_pairs={{0,16},{16,0},{1,17},{17,1},{2,18},{18,2},{3,19},{19,3},{4,20},{20... | collective-permute-start | bytes 1769480 | tf_op jit(solution)/shard_map/ppermute | solution.py:18
  81.0 5.2 %copy-start.5 = (bf16[1024,1536]{1,0:T(8,128)(2,1)S(1)}, bf16[1024,1536]{1,0:T(8,128)(2,1)}, u32[]{:S(2)}) copy-start(bf16[1024,1536]{1,0:T(8,128)(2,1)} %copy-done.4) | copy-start | bytes 9437188
  87.5 12.4 %collective-permute-start.20 = (bf16[128,1536]{1,0:T(8,128)(2,1)S(1)}, bf16[128,1536]{1,0:T(8,128)(2,1)S(1)}, u32[]{:S(2)}, u32[]{:S(2)}) collective-permute-start(bf16[128,1536]{1,0:T(8,128)(2,1)S(1)} %get-tuple-element.56), channel_id=1, source_target_pairs={{0,2},{2,4},{4,6},{6,8},{8,10},{10,12},{12,14},{14,0},{1,3},{3,5},... | collective-permute-start | bytes 1179656 | tf_op jit(solution)/shard_map/ppermute | solution.py:18
  87.6 12.4 %collective-permute-start.21 = (bf16[128,1536]{1,0:T(8,128)(2,1)S(1)}, bf16[128,1536]{1,0:T(8,128)(2,1)S(1)}, u32[]{:S(2)}, u32[]{:S(2)}) collective-permute-start(bf16[128,1536]{1,0:T(8,128)(2,1)S(1)} %get-tuple-element.55), channel_id=1, source_target_pairs={{0,14},{2,0},{4,2},{6,4},{8,6},{10,8},{12,10},{14,12},{1,15},{3,1}... | collective-permute-start | bytes 1179656 | tf_op jit(solution)/shard_map/ppermute | solution.py:18
  91.1 7.7 %collective-permute-start.22 = (bf16[256,384]{1,0:T(8,128)(2,1)S(1)}, bf16[256,384]{1,0:T(8,128)(2,1)S(1)}, u32[]{:S(2)}, u32[]{:S(2)}) collective-permute-start(bf16[256,384]{1,0:T(8,128)(2,1)S(1)} %get-tuple-element.65), channel_id=1, source_target_pairs={{0,32},{32,64},{64,96},{96,0},{1,33},{33,65},{65,97},{97,1},{2,34}... | collective-permute-start | bytes 589832 | tf_op jit(solution)/shard_map/ppermute | solution.py:18
  91.2 7.6 %collective-permute-start.23 = (bf16[256,384]{1,0:T(8,128)(2,1)S(1)}, bf16[256,384]{1,0:T(8,128)(2,1)S(1)}, u32[]{:S(2)}, u32[]{:S(2)}) collective-permute-start(bf16[256,384]{1,0:T(8,128)(2,1)S(1)} %get-tuple-element.64), channel_id=1, source_target_pairs={{0,96},{32,0},{64,32},{96,64},{1,97},{33,1},{65,33},{97,65},{2,98}... | collective-permute-start | bytes 589832 | tf_op jit(solution)/shard_map/ppermute | solution.py:18
  100.2 11.6 %collective-permute-start.25 = (bf16[128,1536]{1,0:T(8,128)(2,1)S(1)}, bf16[128,1536]{1,0:T(8,128)(2,1)S(1)}, u32[]{:S(2)}, u32[]{:S(2)}) collective-permute-start(bf16[128,1536]{1,0:T(8,128)(2,1)S(1)} %get-tuple-element.53), channel_id=1, source_target_pairs={{0,2},{2,4},{4,6},{6,8},{8,10},{10,12},{12,14},{14,0},{1,3},{3,5},... | collective-permute-start | bytes 1179656 | tf_op jit(solution)/shard_map/ppermute | solution.py:18
  102.4 9.8 %collective-permute-start.26 = (bf16[128,1536]{1,0:T(8,128)(2,1)S(1)}, bf16[128,1536]{1,0:T(8,128)(2,1)S(1)}, u32[]{:S(2)}, u32[]{:S(2)}) collective-permute-start(bf16[128,1536]{1,0:T(8,128)(2,1)S(1)} %get-tuple-element.54), channel_id=1, source_target_pairs={{0,14},{2,0},{4,2},{6,4},{8,6},{10,8},{12,10},{14,12},{1,15},{3,1}... | collective-permute-start | bytes 1179656 | tf_op jit(solution)/shard_map/ppermute | solution.py:18
  103.6 14.9 %collective-permute-start.28 = (bf16[256,768]{1,0:T(8,128)(2,1)S(1)}, bf16[256,768]{1,0:T(8,128)(2,1)S(1)}, u32[]{:S(2)}, u32[]{:S(2)}) collective-permute-start(bf16[256,768]{1,0:T(8,128)(2,1)S(1)} %pad_maximum_fusion.6), channel_id=1, source_target_pairs={{0,96},{32,0},{64,32},{96,64},{1,97},{33,1},{65,33},{97,65},{2,98}... | collective-permute-start | bytes 1179656 | tf_op jit(solution)/shard_map/ppermute | solution.py:18
  105.5 13.0 %collective-permute-start.27 = (bf16[256,768]{1,0:T(8,128)(2,1)S(1)}, bf16[256,768]{1,0:T(8,128)(2,1)S(1)}, u32[]{:S(2)}, u32[]{:S(2)}) collective-permute-start(bf16[256,768]{1,0:T(8,128)(2,1)S(1)} %pad_maximum_fusion.5), channel_id=1, source_target_pairs={{0,32},{32,64},{64,96},{96,0},{1,33},{33,65},{65,97},{97,1},{2,34}... | collective-permute-start | bytes 1179656 | tf_op jit(solution)/shard_map/ppermute | solution.py:18
  113.4 16.5 %all-to-all-start.1 = ((bf16[16,16,1536]{2,1,0:T(8,128)(2,1)}), bf16[16,16,1536]{2,1,0:T(8,128)(2,1)S(1)}, u32[]{:S(2)}, u32[]{:S(2)}) async-start(bf16[16,16,1536]{2,1,0:T(8,128)(2,1)} %bitcast.35), calls=%async_computation.1 | async-start | bytes 1572864 | tf_op jit(solution)/shard_map/all_to_all | solution.py:193
  122.9 10.0 %collective-permute-start.30 = (bf16[768,384]{1,0:T(8,128)(2,1)}, bf16[768,384]{1,0:T(8,128)(2,1)}, u32[]{:S(2)}, u32[]{:S(2)}) collective-permute-start(bf16[768,384]{1,0:T(8,128)(2,1)} %dynamic-slice_bitcast_fusion.1), channel_id=1, source_target_pairs={{0,16},{16,0},{1,17},{17,1},{2,18},{18,2},{3,19},{19,3},{4,20},{20... | collective-permute-start | bytes 1769480 | tf_op jit(solution)/shard_map/ppermute | solution.py:18
  123.8 9.1 %collective-permute-start.29 = (bf16[256,384]{1,0:T(8,128)(2,1)}, bf16[256,384]{1,0:T(8,128)(2,1)}, u32[]{:S(2)}, u32[]{:S(2)}) collective-permute-start(bf16[256,384]{1,0:T(8,128)(2,1)} %slice.139), channel_id=1, source_target_pairs={{0,1},{1,0},{2,3},{3,2},{4,5},{5,4},{6,7},{7,6},{8,9},{9,8},{10,11... | collective-permute-start | bytes 589832 | tf_op jit(solution)/shard_map/ppermute | solution.py:18
  136.0 1.7 %copy-start.6 = (bf16[1,1536,384]{2,1,0:T(8,128)(2,1)}, bf16[1,1536,384]{2,1,0:T(8,128)(2,1)S(1)}, u32[]{:S(2)}) copy-start(bf16[1,1536,384]{2,1,0:T(8,128)(2,1)S(1)} %fusion.15) | copy-start | bytes 3538948
Sparse Core Ops, SparseCore 0:
  80.4 40.4 all-gather.2

commit v11 on v9

--- a/solution.py
+++ b/solution.py
@@ -176,15 +176,22 @@
         product = lax.dot_general(grad_flat, features_of, (((0,), (0,)), ((), ())), preferred_element_type=F32)
         return (norm_factor * product).astype(BF16)
 
+    partner_product = for_features(ctx_flat[:, width:])
+    partner_rows = add(partner_product[:piece], swap(partner_product[piece:], "core"))
     own_product = for_features(ctx_flat[:, :width])
-    partner_product = swap(for_features(ctx_flat[:, width:]), "xh")
-    other_product = swap(own_product[piece:], "core")
     partial_ctx = partial_ctx.reshape(n_z, n_y, z_tokens, 2 * width)
     ctx_ring = ring_steps(lambda away: pick(partial_ctx, wrap(y + away, n_y), 1).reshape(group_tokens, 2 * width), "y")
-    *step, ctx_low, ctx_high, other_product, early = tie(*step, *next(ctx_ring), other_product, early)
+    half = piece // 2
+    came_first = swap(partner_rows[:half], "xh")
+    *step, ctx_low, ctx_high, came_first, partner_rows, own_product, early = tie(
+        *step, *next(ctx_ring), came_first, partner_rows, own_product, early
+    )
     step = ring.send(step)
     ctx_step = ctx_ring.send((ctx_low, ctx_high))
-    *ctx_step, partner_product = tie(*ctx_step, partner_product)
+    came_last = swap(partner_rows[half:], "xh")
+    other_product = swap(own_product[piece:], "core")
+    *ctx_step, other_product = tie(*ctx_step, other_product)
+    *step, came_last = tie(*step, came_last)
     branch = ring.send(step).astype(BF16)
     branch = branch.reshape(1, group, own_count, features)
     branch = jnp.concatenate([branch, branch], 0).reshape(2 * group, own_count, features)
@@ -192,8 +199,7 @@
 
     summed = ctx_ring.send(ctx_step)
     other_ctx = swap(summed[:, width:].astype(BF16), "xh")
-    other_partner = swap(partner_product[piece:], "core")
-    branch, other_ctx, other_partner = tie(branch, other_ctx, other_partner)
+    branch, other_ctx = tie(branch, other_ctx)
     ctx_grad = add(summed[:, :width], other_ctx)
     forward, received = local(
         functools.partial(finish_kernel, sizes),
@@ -203,9 +209,9 @@
     )
 
     kept = add(own_product[:piece], other_product)
-    came = add(partner_product[:piece], other_partner)
-    first = xh == 0
-    weight_grad = jnp.concatenate([jnp.where(first, kept, came), jnp.where(first, came, kept)], 0)
+    weight_grad = place(jnp.zeros((n_xh * piece, width), BF16), kept, (xh * piece, 0))
+    weight_grad = place(weight_grad, came_first, ((1 - xh) * piece, 0))
+    weight_grad = place(weight_grad, came_last, ((1 - xh) * piece + half, 0))
     return (forward[None], received[None], ctx_grad[None], weight_grad[None])
 
 

time: 133 us -> 134 us (level)
  starting transfers between devices: 65.9 us -> 68.9 us
  waiting for transfers between devices: 33.7 us -> 31.8 us
    ppermute x32 -> x33, starting transfers between devices: 54.4 us -> 56.9 us  [shift(): return lax.ppermute(value, axis, [(i, (i + by) % n) for i in range(n)])]
    select_n x1 -> x0, other arithmetic: 1.96 us -> none  [shards(): jnp.where(first, kept, came)]
    ppermute x32 -> x33, waiting for transfers between devices: 33.7 us -> 31.8 us  [shift(): return lax.ppermute(value, axis, [(i, (i + by) % n) for i in range(n)])]
    unnamed x22 -> x32, local copies, waits for them, and re-layouts: 2.76 us -> 2.61 us
  transfers between devices with their start and end apart: 34 -> 35, of which waited for: 10 -> 11; matrix products, arithmetic and copies ran while one was open for 16% -> 17% of each run, Pallas kernels for 1% -> 1%
where the time goes in v11:
time: 134 us; the launch traced here: 132 us
  starting transfers between devices  68.9 us (51%)
  waiting for transfers between devices  31.8 us (24%)
  matrix products  11.1 us (8%)
  local copies, waits for them, and re-layouts  8.88 us (7%)
  other arithmetic  6.87 us (5%)
  Pallas kernels  2.98 us (2%)
    ppermute x33, starting transfers between devices, shift(): return lax.ppermute(value, axis, [(i, (i + by) % n) for i in range(n)])  56.9 us
    ppermute x33, waiting for transfers between devices, shift(): return lax.ppermute(value, axis, [(i, (i + by) % n) for i in range(n)])  31.8 us
    all_to_all x1, starting transfers between devices, shards(): branch = lax.all_to_all(branch, ('section', 'y', 'xh'), 0, 0, tiled=True)  6.49 us
    all_to_all x1, starting transfers between devices, shards(): lax.all_to_all(spread, ('y', 'xh'), 0, 0, tiled=True)  5.44 us
    dot_general x1, matrix products, shards(): lax.dot_general(ctx_flat, block, (((1,), (1,)), ((), ())), preferred_elem...  3.72 us
    dot_general x2, matrix products, for_features(): lax.dot_general(grad_flat, features_of, (((0,), (0,)), ((), ())), preferr...  3.69 us
    dot_general x1, matrix products, shards(): jnp.dot(grad_flat, block, preferred_element_type=F32).astype(BF16)  3.66 us
    pallas_call x2, Pallas kernels, local(): pl.pallas_call(kernel, out_shape=[jax.ShapeDtypeStruct(shape, BF16) for s...  2.98 us
  transfers between devices with their start and end apart: 35, of which 11 were waited for; matrix products, arithmetic and copies ran while one was open for 17% of the time, Pallas kernels for 1%

profile of v11, /device:TPU:2, one launch (start us, length us, event | category | flops | bytes accessed | tf_op | source)
XLA Modules:
  0.0 131.7 jit_solution(16508599515080704946)
XLA Ops:
  0.6 2.2 %collective-permute-start = (bf16[256,384]{1,0:T(8,128)(2,1)}, bf16[256,384]{1,0:T(8,128)(2,1)S(1)}, u32[]{:S(2)}, u32[]{:S(2)}) collective-permute-start(bf16[256,384]{1,0:T(8,128)(2,1)} %bitcast.113), channel_id=1, source_target_pairs={{0,1},{1,0},{2,3},{3,2},{4,5},{5,4},{6,7},{7,6},{8,9},{9,8},{10,11... | collective-permute-start | bytes 589832 | tf_op jit(solution)/shard_map/ppermute | solution.py:18
  2.9 1.0 copy-done
  3.9 1.3 shard_map.75
  5.2 5.4 %all-to-all-start = ((bf16[8,16,1536]{2,1,0:T(8,128)(2,1)}), bf16[8,16,1536]{2,1,0:T(8,128)(2,1)S(1)}, u32[]{:S(2)}, u32[]{:S(2)}) async-start(bf16[8,16,1536]{2,1,0:T(8,128)(2,1)} %shard_map.75), calls=%async_computation | async-start | bytes 786432 | tf_op jit(solution)/shard_map/all_to_all | solution.py:155
  10.7 2.7 %dynamic-slice_bitcast_fusion.1 = (bf16[768,384]{1,0:T(8,128)(2,1)}, bf16[768,384]{1,0:T(8,128)(2,1)}, bf16[768,384]{1,0:T(8,128)(2,1)}) fusion(bf16[1,12288,384]{2,1,0:T(8,128)(2,1)} %param.6, s32[]{:T(128)S(6)} %select_n.81, s32[]{:T(128)S(6)} %select_n.76, s32[]{:T(128)S(6)} %select_n.82), kind=kLoop, calls=%fused_computation.28 | loop fusion | bytes 3538956 | tf_op jit(solution)/shard_map/dynamic_slice | solution.py:136
  13.5 2.1 %collective-permute-start.1 = (bf16[256,768]{1,0:T(8,128)(2,1)S(1)}, bf16[256,768]{1,0:T(8,128)(2,1)S(1)}, u32[]{:S(2)}, u32[]{:S(2)}) collective-permute-start(bf16[256,768]{1,0:T(8,128)(2,1)S(1)} %pad_maximum_fusion.1), channel_id=1, source_target_pairs={{0,32},{32,64},{64,96},{96,0},{1,33},{33,65},{65,97},{97,1},{2,34}... | collective-permute-start | bytes 1179656 | tf_op jit(solution)/shard_map/ppermute | solution.py:18
  15.6 1.3 collective-permute-start.2
  16.9 0.8 broadcast_select_fusion
  17.7 3.4 %collective-permute-start.5 = (bf16[768,384]{1,0:T(8,128)(2,1)}, bf16[768,384]{1,0:T(8,128)(2,1)}, u32[]{:S(2)}, u32[]{:S(2)}) collective-permute-start(bf16[768,384]{1,0:T(8,128)(2,1)} %get-tuple-element.31), channel_id=1, source_target_pairs={{0,1},{1,0},{2,3},{3,2},{4,5},{5,4},{6,7},{7,6},{8,9},{9,8},{10,11... | collective-permute-start | bytes 1769480 | tf_op jit(solution)/shard_map/ppermute | solution.py:18
  21.1 0.2 broadcast_in_dim.46
  21.3 2.0 %collective-permute-start.11 = (bf16[128,1536]{1,0:T(8,128)(2,1)S(1)}, bf16[128,1536]{1,0:T(8,128)(2,1)S(1)}, u32[]{:S(2)}, u32[]{:S(2)}) collective-permute-start(bf16[128,1536]{1,0:T(8,128)(2,1)S(1)} %bitcast.100), channel_id=1, source_target_pairs={{0,2},{2,4},{4,6},{6,8},{8,10},{10,12},{12,14},{14,0},{1,3},{3,5},... | collective-permute-start | bytes 1179656 | tf_op jit(solution)/shard_map/ppermute | solution.py:18
  23.3 4.0 %collective-permute-start.12 = (bf16[128,1536]{1,0:T(8,128)(2,1)S(1)}, bf16[128,1536]{1,0:T(8,128)(2,1)S(1)}, u32[]{:S(2)}, u32[]{:S(2)}) collective-permute-start(bf16[128,1536]{1,0:T(8,128)(2,1)S(1)} %bitcast.101), channel_id=1, source_target_pairs={{0,14},{2,0},{4,2},{6,4},{8,6},{10,8},{12,10},{14,12},{1,15},{3,1}... | collective-permute-start | bytes 1179656 | tf_op jit(solution)/shard_map/ppermute | solution.py:18
  27.4 0.3 broadcast_in_dim.47
  27.7 0.3 collective-permute-start.3
  28.0 0.9 slice.106
  29.0 3.1 %collective-permute-start.4 = (bf16[128,768]{1,0:T(8,128)(2,1)S(1)}, bf16[128,768]{1,0:T(8,128)(2,1)S(1)}, u32[]{:S(2)}, u32[]{:S(2)}) collective-permute-start(bf16[128,768]{1,0:T(8,128)(2,1)S(1)} %slice.106), channel_id=1, source_target_pairs={{0,96},{32,0},{64,32},{96,64},{1,97},{33,1},{65,33},{97,65},{2,98}... | collective-permute-start | bytes 589832 | tf_op jit(solution)/shard_map/ppermute | solution.py:18
  32.1 1.0 constant_dynamic-update-slice_fusion.1
  33.1 1.6 %collective-permute-done.11 = bf16[128,1536]{1,0:T(8,128)(2,1)S(1)} collective-permute-done((bf16[128,1536]{1,0:T(8,128)(2,1)S(1)}, bf16[128,1536]{1,0:T(8,128)(2,1)S(1)}, u32[]{:S(2)}, u32[]{:S(2)}) %collective-permute-start.11) | collective-permute-done | bytes 393248 | tf_op jit(solution)/shard_map/ppermute | solution.py:18
  34.7 0.3 collective-permute-start.13
  35.0 4.0 %collective-permute-start.14 = (bf16[128,1536]{1,0:T(8,128)(2,1)S(1)}, bf16[128,1536]{1,0:T(8,128)(2,1)S(1)}, u32[]{:S(2)}, u32[]{:S(2)}) collective-permute-start(bf16[128,1536]{1,0:T(8,128)(2,1)S(1)} %collective-permute-done.12), channel_id=1, source_target_pairs={{0,14},{2,0},{4,2},{6,4},{8,6},{10,8},{12,10},{14,12},{1,15},{3,1}... | collective-permute-start | bytes 1179656 | tf_op jit(solution)/shard_map/ppermute | solution.py:18
  39.3 7.9 %collective-permute-done.13 = bf16[128,1536]{1,0:T(8,128)(2,1)S(1)} collective-permute-done((bf16[128,1536]{1,0:T(8,128)(2,1)S(1)}, bf16[128,1536]{1,0:T(8,128)(2,1)S(1)}, u32[]{:S(2)}, u32[]{:S(2)}) %collective-permute-start.13) | collective-permute-done | bytes 393248 | tf_op jit(solution)/shard_map/ppermute | solution.py:18
  47.2 3.2 %collective-permute-start.16 = (bf16[128,1536]{1,0:T(8,128)(2,1)S(1)}, bf16[128,1536]{1,0:T(8,128)(2,1)S(1)}, u32[]{:S(2)}, u32[]{:S(2)}) collective-permute-start(bf16[128,1536]{1,0:T(8,128)(2,1)S(1)} %collective-permute-done.14), channel_id=1, source_target_pairs={{0,14},{2,0},{4,2},{6,4},{8,6},{10,8},{12,10},{14,12},{1,15},{3,1}... | collective-permute-start | bytes 1179656 | tf_op jit(solution)/shard_map/ppermute | solution.py:18
  50.5 3.7 %convolution_convert_fusion = bf16[1024,1536]{1,0:T(8,128)(2,1)S(1)} fusion(bf16[1024,768]{1,0:T(8,128)(2,1)S(1)} %bitcast.97, bf16[768,384]{1,0:T(8,128)(2,1)S(1)} %collective-permute-done.6, bf16[768,384]{1,0:T(8,128)(2,1)S(1)} %copy-done.7, bf16[768,384]{1,0:T(8,128)(2,1)} %collective-permute-done.5, bf16[768,384]{1,0:T(8,128)(2,1)S(1)} %copy-done.6), kind=kOutput, calls=%fused_computation | convolution fusion | flops 2426929152 | bytes 7077888 | tf_op jit(solution)/shard_map/dot_general | solution.py:161
  54.5 3.2 %collective-permute-start.8 = (bf16[128,768]{1,0:T(8,128)(2,1)S(1)}, bf16[128,768]{1,0:T(8,128)(2,1)S(1)}, u32[]{:S(2)}, u32[]{:S(2)}) collective-permute-start(bf16[128,768]{1,0:T(8,128)(2,1)S(1)} %get-tuple-element.72), channel_id=1, source_target_pairs={{0,14},{2,0},{4,2},{6,4},{8,6},{10,8},{12,10},{14,12},{1,15},{3,1}... | collective-permute-start | bytes 589832 | tf_op jit(solution)/shard_map/ppermute | solution.py:18
  57.7 1.6 %collective-permute-done.15 = bf16[128,1536]{1,0:T(8,128)(2,1)S(1)} collective-permute-done((bf16[128,1536]{1,0:T(8,128)(2,1)S(1)}, bf16[128,1536]{1,0:T(8,128)(2,1)S(1)}, u32[]{:S(2)}, u32[]{:S(2)}) %collective-permute-start.15) | collective-permute-done | bytes 393248 | tf_op jit(solution)/shard_map/ppermute | solution.py:18
  59.5 3.3 %collective-permute-start.18 = (bf16[64,1536]{1,0:T(8,128)(2,1)S(1)}, bf16[64,1536]{1,0:T(8,128)(2,1)S(1)}, u32[]{:S(2)}, u32[]{:S(2)}) collective-permute-start(bf16[64,1536]{1,0:T(8,128)(2,1)S(1)} %slice.114), channel_id=1, source_target_pairs={{0,14},{2,0},{4,2},{6,4},{8,6},{10,8},{12,10},{14,12},{1,15},{3,1}... | collective-permute-start | bytes 589832 | tf_op jit(solution)/shard_map/ppermute | solution.py:18
  62.9 0.7 collective-permute-done.7
  63.7 3.2 %collective-permute-start.10 = (bf16[128,1536]{1,0:T(8,128)(2,1)S(1)}, bf16[128,1536]{1,0:T(8,128)(2,1)S(1)}, u32[]{:S(2)}, u32[]{:S(2)}) collective-permute-start(bf16[128,1536]{1,0:T(8,128)(2,1)S(1)} %pad_maximum_fusion.4), channel_id=1, source_target_pairs={{0,14},{2,0},{4,2},{6,4},{8,6},{10,8},{12,10},{14,12},{1,15},{3,1}... | collective-permute-start | bytes 1179656 | tf_op jit(solution)/shard_map/ppermute | solution.py:18
  67.1 0.8 collective-permute-start.25
  67.9 0.1 collective-permute-done.18
  68.0 1.8 %fusion = bf16[1536,384]{1,0:T(8,128)(2,1)S(1)} fusion(bf16[1024,1536]{1,0:T(8,128)(2,1)S(1)} %bitcast.90, bf16[1024,768]{1,0:T(8,128)(2,1)S(1)} %bitcast.98), kind=kOutput, calls=%fused_computation.3 | convolution fusion | flops 1209139200 | bytes 5111808 | tf_op jit(solution)/shard_map/dot_general | solution.py:176
  70.1 3.7 %convolution_convert_fusion.1 = bf16[1024,768]{1,0:T(8,128)(2,1)S(1)} fusion(bf16[1024,1536]{1,0:T(8,128)(2,1)S(1)} %bitcast.91, bf16[768,384]{1,0:T(8,128)(2,1)S(1)} %collective-permute-done.6, bf16[768,384]{1,0:T(8,128)(2,1)S(1)} %copy-done.7, bf16[768,384]{1,0:T(8,128)(2,1)} %collective-permute-done.5, bf16[768,384]{1,0:T(8,128)(2,1)S(1)} %copy-done.6), kind=kOutput, calls=%fused_computation.6 | convolution fusion | flops 2426142720 | bytes 7077888 | tf_op jit(solution)/shard_map/dot_general | solution.py:170
  73.7 0.2 collective-permute-done.10
  74.0 2.1 %collective-permute-done.9 = bf16[128,1536]{1,0:T(8,128)(2,1)S(1)} collective-permute-done((bf16[128,1536]{1,0:T(8,128)(2,1)S(1)}, bf16[128,1536]{1,0:T(8,128)(2,1)S(1)}, u32[]{:S(2)}, u32[]{:S(2)}) %collective-permute-start.9) | collective-permute-done | bytes 393248 | tf_op jit(solution)/shard_map/ppermute | solution.py:18
  76.1 0.1 constant_dynamic-slice_fusion.2
  76.2 0.3 collective-permute-start.21
  76.5 3.2 %collective-permute-start.22 = (bf16[256,384]{1,0:T(8,128)(2,1)S(1)}, bf16[256,384]{1,0:T(8,128)(2,1)S(1)}, u32[]{:S(2)}, u32[]{:S(2)}) collective-permute-start(bf16[256,384]{1,0:T(8,128)(2,1)S(1)} %get-tuple-element.70), channel_id=1, source_target_pairs={{0,96},{32,0},{64,32},{96,64},{1,97},{33,1},{65,33},{97,65},{2,98}... | collective-permute-start | bytes 589832 | tf_op jit(solution)/shard_map/ppermute | solution.py:18
  79.8 0.2 fusion.6
  80.1 3.2 %collective-permute-start.20 = (bf16[128,1536]{1,0:T(8,128)(2,1)S(1)}, bf16[128,1536]{1,0:T(8,128)(2,1)S(1)}, u32[]{:S(2)}, u32[]{:S(2)}) collective-permute-start(bf16[128,1536]{1,0:T(8,128)(2,1)S(1)} %get-tuple-element.61), channel_id=1, source_target_pairs={{0,14},{2,0},{4,2},{6,4},{8,6},{10,8},{12,10},{14,12},{1,15},{3,1}... | collective-permute-start | bytes 1179656 | tf_op jit(solution)/shard_map/ppermute | solution.py:18
  83.3 0.1 add_convert_fusion.1
  83.5 2.6 %collective-permute-start.24 = (bf16[384,384]{1,0:T(8,128)(2,1)S(1)}, bf16[384,384]{1,0:T(8,128)(2,1)S(1)}, u32[]{:S(2)}, u32[]{:S(2)}) collective-permute-start(bf16[384,384]{1,0:T(8,128)(2,1)S(1)} %slice.120), channel_id=1, source_target_pairs={{0,1},{1,0},{2,3},{3,2},{4,5},{5,4},{6,7},{7,6},{8,9},{9,8},{10,11... | collective-permute-start | bytes 884744 | tf_op jit(solution)/shard_map/ppermute | solution.py:18
  86.1 1.8 %fusion.1 = bf16[1536,384]{1,0:T(8,128)(2,1)S(1)} fusion(bf16[1024,1536]{1,0:T(8,128)(2,1)S(1)} %bitcast.92, bf16[1024,768]{1,0:T(8,128)(2,1)S(1)} %bitcast.99), kind=kOutput, calls=%fused_computation.4 | convolution fusion | flops 1209139200 | bytes 5111808 | tf_op jit(solution)/shard_map/dot_general | solution.py:176
  88.1 2.6 %collective-permute-done.19 = bf16[128,1536]{1,0:T(8,128)(2,1)S(1)} collective-permute-done((bf16[128,1536]{1,0:T(8,128)(2,1)S(1)}, bf16[128,1536]{1,0:T(8,128)(2,1)S(1)}, u32[]{:S(2)}, u32[]{:S(2)}) %collective-permute-start.19) | collective-permute-done | bytes 393248 | tf_op jit(solution)/shard_map/ppermute | solution.py:18
  90.7 1.2 collective-permute-done.24
  91.9 0.7 copy-done.11
  92.7 0.2 fusion.5
  92.9 1.2 collective-permute-start.26
  94.0 2.1 %collective-permute-start.27 = (bf16[128,1536]{1,0:T(8,128)(2,1)S(1)}, bf16[128,1536]{1,0:T(8,128)(2,1)S(1)}, u32[]{:S(2)}, u32[]{:S(2)}) collective-permute-start(bf16[128,1536]{1,0:T(8,128)(2,1)S(1)} %get-tuple-element.59), channel_id=1, source_target_pairs={{0,14},{2,0},{4,2},{6,4},{8,6},{10,8},{12,10},{14,12},{1,15},{3,1}... | collective-permute-start | bytes 1179656 | tf_op jit(solution)/shard_map/ppermute | solution.py:18
  96.2 0.4 collective-permute-start.30
  96.6 2.9 %collective-permute-start.28 = (bf16[384,384]{1,0:T(8,128)(2,1)S(1)}, bf16[384,384]{1,0:T(8,128)(2,1)S(1)}, u32[]{:S(2)}, u32[]{:S(2)}) collective-permute-start(bf16[384,384]{1,0:T(8,128)(2,1)S(1)} %slice.96), channel_id=1, source_target_pairs={{0,1},{1,0},{2,3},{3,2},{4,5},{5,4},{6,7},{7,6},{8,9},{9,8},{10,11... | collective-permute-start | bytes 884744 | tf_op jit(solution)/shard_map/ppermute | solution.py:18
  99.6 0.8 pad_maximum_fusion.5
  100.4 1.7 %collective-permute-start.29 = (bf16[256,768]{1,0:T(8,128)(2,1)}, bf16[256,768]{1,0:T(8,128)(2,1)}, u32[]{:S(2)}, u32[]{:S(2)}) collective-permute-start(bf16[256,768]{1,0:T(8,128)(2,1)} %pad_maximum_fusion.5), channel_id=1, source_target_pairs={{0,32},{32,64},{64,96},{96,0},{1,33},{33,65},{65,97},{97,1},{2,34}... | collective-permute-start | bytes 1179656 | tf_op jit(solution)/shard_map/ppermute | solution.py:18
  102.2 2.7 %collective-permute-done.28 = bf16[384,384]{1,0:T(8,128)(2,1)S(1)} collective-permute-done((bf16[384,384]{1,0:T(8,128)(2,1)S(1)}, bf16[384,384]{1,0:T(8,128)(2,1)S(1)}, u32[]{:S(2)}, u32[]{:S(2)}) %collective-permute-start.28) | collective-permute-done | bytes 294944 | tf_op jit(solution)/shard_map/ppermute | solution.py:18
  105.0 0.2 fusion.10
  105.1 1.0 pad_maximum_fusion
  106.1 6.5 %all-to-all-start.1 = ((bf16[16,16,1536]{2,1,0:T(8,128)(2,1)}), bf16[16,16,1536]{2,1,0:T(8,128)(2,1)S(1)}, u32[]{:S(2)}, u32[]{:S(2)}) async-start(bf16[16,16,1536]{2,1,0:T(8,128)(2,1)} %bitcast.35), calls=%async_computation.1 | async-start | bytes 1572864 | tf_op jit(solution)/shard_map/all_to_all | solution.py:198
  112.6 0.8 copy-done.8
  113.5 1.3 %fusion.4 = f32[256,768]{1,0:T(8,128)S(1)} fusion(bf16[256,768]{1,0:T(8,128)(2,1)} %collective-permute-done.30, bf16[256,768]{1,0:T(8,128)(2,1)} %collective-permute-done.29, bf16[8,1,32,768]{3,2,1,0:T(8,128)(2,1)S(1)} %get-tuple-element.66), kind=kLoop, calls=%fused_computation.13 | loop fusion | flops 983040 | bytes 1966080 | tf_op jit(solution)/shard_map/add | solution.py:72
  114.8 2.2 %collective-permute-start.32 = (bf16[256,384]{1,0:T(8,128)(2,1)S(1)}, bf16[256,384]{1,0:T(8,128)(2,1)}, u32[]{:S(2)}, u32[]{:S(2)}) collective-permute-start(bf16[256,384]{1,0:T(8,128)(2,1)S(1)} %slice.144), channel_id=1, source_target_pairs={{0,1},{1,0},{2,3},{3,2},{4,5},{5,4},{6,7},{7,6},{8,9},{9,8},{10,11... | collective-permute-start | bytes 589832 | tf_op jit(solution)/shard_map/ppermute | solution.py:18
  117.0 0.1 broadcast_in_dim.58
  117.1 0.2 fusion.12
  117.5 11.0 %collective-permute-done.32 = bf16[256,384]{1,0:T(8,128)(2,1)} collective-permute-done((bf16[256,384]{1,0:T(8,128)(2,1)S(1)}, bf16[256,384]{1,0:T(8,128)(2,1)}, u32[]{:S(2)}, u32[]{:S(2)}) %collective-permute-start.32) | collective-permute-done | bytes 196640 | tf_op jit(solution)/shard_map/ppermute | solution.py:18
  128.4 1.7 %fusion.15 = bf16[1,256,384]{2,1,0:T(8,128)(2,1)} fusion(bf16[256,384]{1,0:T(8,128)(2,1)} %collective-permute-done.32, f32[256,768]{1,0:T(8,128)S(1)} %fusion.4), kind=kLoop, calls=%fused_computation.58 | loop fusion | flops 294912 | bytes 786432 | tf_op jit(solution)/shard_map/broadcast_in_dim | solution.py:215
  130.1 1.7 %shard_map.76 = (bf16[16,12288]{1,0:T(8,128)(2,1)}, bf16[16,12288]{1,0:T(8,128)(2,1)}) custom-call(s32[2]{0:T(128)S(1)} %pad_add_fusion.at_ref, bf16[2,8,16,1536]{3,2,1,0:T(8,128)(2,1)S(1)} %bitcast.87, bf16[16,12288]{1,0:T(8,128)(2,1)S(1)} %bitcast.89, bf16[16,12288]{1,0:T(8,128)(2,1)S(1)} %collective-permute-done.25.early_ref), custom_call_target="tpu_custom_call" | custom-call | tf_op jit(solution)/shard_map/pallas_call | solution.py:109
  (99 shorter events, 2.0 us)
Async XLA Ops:
  0.6 12.8 %collective-permute-start = (bf16[256,384]{1,0:T(8,128)(2,1)}, bf16[256,384]{1,0:T(8,128)(2,1)S(1)}, u32[]{:S(2)}, u32[]{:S(2)}) collective-permute-start(bf16[256,384]{1,0:T(8,128)(2,1)} %bitcast.113), channel_id=1, source_target_pairs={{0,1},{1,0},{2,3},{3,2},{4,5},{5,4},{6,7},{7,6},{8,9},{9,8},{10,11... | collective-permute-start | bytes 589832 | tf_op jit(solution)/shard_map/ppermute | solution.py:18
  2.9 1.0 copy-start
  5.2 8.2 %copy-start.15 = (bf16[1,256,384]{2,1,0:T(8,128)(2,1)S(1)}, bf16[1,256,384]{2,1,0:T(8,128)(2,1)}, u32[]{:S(2)}) copy-start(bf16[1,256,384]{2,1,0:T(8,128)(2,1)} %param.5) | copy-start | bytes 589828
  5.2 16.1 %all-to-all-start = ((bf16[8,16,1536]{2,1,0:T(8,128)(2,1)}), bf16[8,16,1536]{2,1,0:T(8,128)(2,1)S(1)}, u32[]{:S(2)}, u32[]{:S(2)}) async-start(bf16[8,16,1536]{2,1,0:T(8,128)(2,1)} %shard_map.75), calls=%async_computation | async-start | bytes 786432 | tf_op jit(solution)/shard_map/all_to_all | solution.py:155
  10.7 6.2 %copy-start.1 = (bf16[1,16,12288]{2,1,0:T(8,128)(2,1)S(1)}, bf16[1,16,12288]{2,1,0:T(8,128)(2,1)}, u32[]{:S(2)}) copy-start(bf16[1,16,12288]{2,1,0:T(8,128)(2,1)} %param.7) | copy-start | bytes 1179652
  10.7 6.2 %copy-start.2 = (bf16[1,16,12288]{2,1,0:T(8,128)(2,1)S(1)}, bf16[1,16,12288]{2,1,0:T(8,128)(2,1)}, u32[]{:S(2)}) copy-start(bf16[1,16,12288]{2,1,0:T(8,128)(2,1)} %param.4) | copy-start | bytes 1179652
  13.5 14.2 %collective-permute-start.1 = (bf16[256,768]{1,0:T(8,128)(2,1)S(1)}, bf16[256,768]{1,0:T(8,128)(2,1)S(1)}, u32[]{:S(2)}, u32[]{:S(2)}) collective-permute-start(bf16[256,768]{1,0:T(8,128)(2,1)S(1)} %pad_maximum_fusion.1), channel_id=1, source_target_pairs={{0,32},{32,64},{64,96},{96,0},{1,33},{33,65},{65,97},{97,1},{2,34}... | collective-permute-start | bytes 1179656 | tf_op jit(solution)/shard_map/ppermute | solution.py:18
  15.6 12.5 %collective-permute-start.2 = (bf16[256,768]{1,0:T(8,128)(2,1)S(1)}, bf16[256,768]{1,0:T(8,128)(2,1)}, u32[]{:S(2)}, u32[]{:S(2)}) collective-permute-start(bf16[256,768]{1,0:T(8,128)(2,1)S(1)} %pad_maximum_fusion.1), channel_id=1, source_target_pairs={{0,96},{32,0},{64,32},{96,64},{1,97},{33,1},{65,33},{97,65},{2,98}... | collective-permute-start | bytes 1179656 | tf_op jit(solution)/shard_map/ppermute | solution.py:18
  17.7 21.4 %collective-permute-start.5 = (bf16[768,384]{1,0:T(8,128)(2,1)}, bf16[768,384]{1,0:T(8,128)(2,1)}, u32[]{:S(2)}, u32[]{:S(2)}) collective-permute-start(bf16[768,384]{1,0:T(8,128)(2,1)} %get-tuple-element.31), channel_id=1, source_target_pairs={{0,1},{1,0},{2,3},{3,2},{4,5},{5,4},{6,7},{7,6},{8,9},{9,8},{10,11... | collective-permute-start | bytes 1769480 | tf_op jit(solution)/shard_map/ppermute | solution.py:18
  21.3 13.4 %collective-permute-start.11 = (bf16[128,1536]{1,0:T(8,128)(2,1)S(1)}, bf16[128,1536]{1,0:T(8,128)(2,1)S(1)}, u32[]{:S(2)}, u32[]{:S(2)}) collective-permute-start(bf16[128,1536]{1,0:T(8,128)(2,1)S(1)} %bitcast.100), channel_id=1, source_target_pairs={{0,2},{2,4},{4,6},{6,8},{8,10},{10,12},{12,14},{14,0},{1,3},{3,5},... | collective-permute-start | bytes 1179656 | tf_op jit(solution)/shard_map/ppermute | solution.py:18
  23.3 11.7 %collective-permute-start.12 = (bf16[128,1536]{1,0:T(8,128)(2,1)S(1)}, bf16[128,1536]{1,0:T(8,128)(2,1)S(1)}, u32[]{:S(2)}, u32[]{:S(2)}) collective-permute-start(bf16[128,1536]{1,0:T(8,128)(2,1)S(1)} %bitcast.101), channel_id=1, source_target_pairs={{0,14},{2,0},{4,2},{6,4},{8,6},{10,8},{12,10},{14,12},{1,15},{3,1}... | collective-permute-start | bytes 1179656 | tf_op jit(solution)/shard_map/ppermute | solution.py:18
  27.7 11.5 %collective-permute-start.3 = (bf16[128,768]{1,0:T(8,128)(2,1)S(1)}, bf16[128,768]{1,0:T(8,128)(2,1)S(1)}, u32[]{:S(2)}, u32[]{:S(2)}) collective-permute-start(bf16[128,768]{1,0:T(8,128)(2,1)S(1)} %slice.105), channel_id=1, source_target_pairs={{0,32},{32,64},{64,96},{96,0},{1,33},{33,65},{65,97},{97,1},{2,34}... | collective-permute-start | bytes 589832 | tf_op jit(solution)/shard_map/ppermute | solution.py:18
  29.0 10.2 %collective-permute-start.4 = (bf16[128,768]{1,0:T(8,128)(2,1)S(1)}, bf16[128,768]{1,0:T(8,128)(2,1)S(1)}, u32[]{:S(2)}, u32[]{:S(2)}) collective-permute-start(bf16[128,768]{1,0:T(8,128)(2,1)S(1)} %slice.106), channel_id=1, source_target_pairs={{0,96},{32,0},{64,32},{96,64},{1,97},{33,1},{65,33},{97,65},{2,98}... | collective-permute-start | bytes 589832 | tf_op jit(solution)/shard_map/ppermute | solution.py:18
  33.1 17.4 %copy-start.6 = (bf16[768,384]{1,0:T(8,128)(2,1)S(1)}, bf16[768,384]{1,0:T(8,128)(2,1)}, u32[]{:S(2)}) copy-start(bf16[768,384]{1,0:T(8,128)(2,1)} %get-tuple-element.56) | copy-start | bytes 1769476
  33.1 17.4 %copy-start.7 = (bf16[768,384]{1,0:T(8,128)(2,1)S(1)}, bf16[768,384]{1,0:T(8,128)(2,1)}, u32[]{:S(2)}) copy-start(bf16[768,384]{1,0:T(8,128)(2,1)} %get-tuple-element.58) | copy-start | bytes 1769476
  34.7 12.5 %collective-permute-start.13 = (bf16[128,1536]{1,0:T(8,128)(2,1)S(1)}, bf16[128,1536]{1,0:T(8,128)(2,1)S(1)}, u32[]{:S(2)}, u32[]{:S(2)}) collective-permute-start(bf16[128,1536]{1,0:T(8,128)(2,1)S(1)} %collective-permute-done.11), channel_id=1, source_target_pairs={{0,2},{2,4},{4,6},{6,8},{8,10},{10,12},{12,14},{14,0},{1,3},{3,5},... | collective-permute-start | bytes 1179656 | tf_op jit(solution)/shard_map/ppermute | solution.py:18
  35.0 12.2 %collective-permute-start.14 = (bf16[128,1536]{1,0:T(8,128)(2,1)S(1)}, bf16[128,1536]{1,0:T(8,128)(2,1)S(1)}, u32[]{:S(2)}, u32[]{:S(2)}) collective-permute-start(bf16[128,1536]{1,0:T(8,128)(2,1)S(1)} %collective-permute-done.12), channel_id=1, source_target_pairs={{0,14},{2,0},{4,2},{6,4},{8,6},{10,8},{12,10},{14,12},{1,15},{3,1}... | collective-permute-start | bytes 1179656 | tf_op jit(solution)/shard_map/ppermute | solution.py:18
  39.1 11.4 %collective-permute-start.6 = (bf16[768,384]{1,0:T(8,128)(2,1)}, bf16[768,384]{1,0:T(8,128)(2,1)S(1)}, u32[]{:S(2)}, u32[]{:S(2)}) collective-permute-start(bf16[768,384]{1,0:T(8,128)(2,1)} %collective-permute-done.5), channel_id=1, source_target_pairs={{0,16},{16,0},{1,17},{17,1},{2,18},{18,2},{3,19},{19,3},{4,20},{20... | collective-permute-start | bytes 1769480 | tf_op jit(solution)/shard_map/ppermute | solution.py:18
  47.2 12.2 %collective-permute-start.15 = (bf16[128,1536]{1,0:T(8,128)(2,1)S(1)}, bf16[128,1536]{1,0:T(8,128)(2,1)S(1)}, u32[]{:S(2)}, u32[]{:S(2)}) collective-permute-start(bf16[128,1536]{1,0:T(8,128)(2,1)S(1)} %collective-permute-done.13), channel_id=1, source_target_pairs={{0,2},{2,4},{4,6},{6,8},{8,10},{10,12},{12,14},{14,0},{1,3},{3,5},... | collective-permute-start | bytes 1179656 | tf_op jit(solution)/shard_map/ppermute | solution.py:18
  47.2 12.3 %collective-permute-start.16 = (bf16[128,1536]{1,0:T(8,128)(2,1)S(1)}, bf16[128,1536]{1,0:T(8,128)(2,1)S(1)}, u32[]{:S(2)}, u32[]{:S(2)}) collective-permute-start(bf16[128,1536]{1,0:T(8,128)(2,1)S(1)} %collective-permute-done.14), channel_id=1, source_target_pairs={{0,14},{2,0},{4,2},{6,4},{8,6},{10,8},{12,10},{14,12},{1,15},{3,1}... | collective-permute-start | bytes 1179656 | tf_op jit(solution)/shard_map/ppermute | solution.py:18
  54.4 9.2 %collective-permute-start.7 = (bf16[128,768]{1,0:T(8,128)(2,1)S(1)}, bf16[128,768]{1,0:T(8,128)(2,1)S(1)}, u32[]{:S(2)}, u32[]{:S(2)}) collective-permute-start(bf16[128,768]{1,0:T(8,128)(2,1)S(1)} %get-tuple-element.73), channel_id=1, source_target_pairs={{0,2},{2,4},{4,6},{6,8},{8,10},{10,12},{12,14},{14,0},{1,3},{3,5},... | collective-permute-start | bytes 589832 | tf_op jit(solution)/shard_map/ppermute | solution.py:18
  54.5 9.1 %collective-permute-start.8 = (bf16[128,768]{1,0:T(8,128)(2,1)S(1)}, bf16[128,768]{1,0:T(8,128)(2,1)S(1)}, u32[]{:S(2)}, u32[]{:S(2)}) collective-permute-start(bf16[128,768]{1,0:T(8,128)(2,1)S(1)} %get-tuple-element.72), channel_id=1, source_target_pairs={{0,14},{2,0},{4,2},{6,4},{8,6},{10,8},{12,10},{14,12},{1,15},{3,1}... | collective-permute-start | bytes 589832 | tf_op jit(solution)/shard_map/ppermute | solution.py:18
  59.4 7.7 %copy-start.10 = (bf16[16,12288]{1,0:T(8,128)(2,1)S(1)}, bf16[16,12288]{1,0:T(8,128)(2,1)}, u32[]{:S(2)}) copy-start(bf16[16,12288]{1,0:T(8,128)(2,1)} %broadcast_select_fusion) | copy-start | bytes 1179652
  59.4 8.5 %collective-permute-start.17 = (bf16[64,1536]{1,0:T(8,128)(2,1)S(1)}, bf16[64,1536]{1,0:T(8,128)(2,1)S(1)}, u32[]{:S(2)}, u32[]{:S(2)}) collective-permute-start(bf16[64,1536]{1,0:T(8,128)(2,1)S(1)} %slice.113), channel_id=1, source_target_pairs={{0,2},{2,4},{4,6},{6,8},{8,10},{10,12},{12,14},{14,0},{1,3},{3,5},... | collective-permute-start | bytes 589832 | tf_op jit(solution)/shard_map/ppermute | solution.py:18
  59.5 8.5 %collective-permute-start.18 = (bf16[64,1536]{1,0:T(8,128)(2,1)S(1)}, bf16[64,1536]{1,0:T(8,128)(2,1)S(1)}, u32[]{:S(2)}, u32[]{:S(2)}) collective-permute-start(bf16[64,1536]{1,0:T(8,128)(2,1)S(1)} %slice.114), channel_id=1, source_target_pairs={{0,14},{2,0},{4,2},{6,4},{8,6},{10,8},{12,10},{14,12},{1,15},{3,1}... | collective-permute-start | bytes 589832 | tf_op jit(solution)/shard_map/ppermute | solution.py:18
  63.7 10.3 %collective-permute-start.10 = (bf16[128,1536]{1,0:T(8,128)(2,1)S(1)}, bf16[128,1536]{1,0:T(8,128)(2,1)S(1)}, u32[]{:S(2)}, u32[]{:S(2)}) collective-permute-start(bf16[128,1536]{1,0:T(8,128)(2,1)S(1)} %pad_maximum_fusion.4), channel_id=1, source_target_pairs={{0,14},{2,0},{4,2},{6,4},{8,6},{10,8},{12,10},{14,12},{1,15},{3,1}... | collective-permute-start | bytes 1179656 | tf_op jit(solution)/shard_map/ppermute | solution.py:18
  67.0 9.1 %collective-permute-start.9 = (bf16[128,1536]{1,0:T(8,128)(2,1)S(1)}, bf16[128,1536]{1,0:T(8,128)(2,1)S(1)}, u32[]{:S(2)}, u32[]{:S(2)}) collective-permute-start(bf16[128,1536]{1,0:T(8,128)(2,1)S(1)} %pad_maximum_fusion.3), channel_id=1, source_target_pairs={{0,2},{2,4},{4,6},{6,8},{8,10},{10,12},{12,14},{14,0},{1,3},{3,5},... | collective-permute-start | bytes 1179656 | tf_op jit(solution)/shard_map/ppermute | solution.py:18
  67.1 16.4 %collective-permute-start.25 = (bf16[16,12288]{1,0:T(8,128)(2,1)S(1)}, bf16[16,12288]{1,0:T(8,128)(2,1)S(1)}, u32[]{:S(2)}, u32[]{:S(2)}) collective-permute-start(bf16[16,12288]{1,0:T(8,128)(2,1)S(1)} %copy-done.10), channel_id=1, source_target_pairs={{0,128},{128,0},{1,129},{129,1},{2,130},{130,2},{3,131},{131,3},{4... | collective-permute-start | bytes 1179656 | tf_op jit(solution)/shard_map/ppermute | solution.py:18
  70.0 10.1 %collective-permute-start.23 = (bf16[768,384]{1,0:T(8,128)(2,1)S(1)}, bf16[768,384]{1,0:T(8,128)(2,1)S(1)}, u32[]{:S(2)}, u32[]{:S(2)}) collective-permute-start(bf16[768,384]{1,0:T(8,128)(2,1)S(1)} %slice.119), channel_id=1, source_target_pairs={{0,16},{16,0},{1,17},{17,1},{2,18},{18,2},{3,19},{19,3},{4,20},{20... | collective-permute-start | bytes 1769480 | tf_op jit(solution)/shard_map/ppermute | solution.py:18
  76.2 11.8 %collective-permute-start.21 = (bf16[256,384]{1,0:T(8,128)(2,1)S(1)}, bf16[256,384]{1,0:T(8,128)(2,1)S(1)}, u32[]{:S(2)}, u32[]{:S(2)}) collective-permute-start(bf16[256,384]{1,0:T(8,128)(2,1)S(1)} %get-tuple-element.71), channel_id=1, source_target_pairs={{0,32},{32,64},{64,96},{96,0},{1,33},{33,65},{65,97},{97,1},{2,34}... | collective-permute-start | bytes 589832 | tf_op jit(solution)/shard_map/ppermute | solution.py:18
  76.5 11.5 %collective-permute-start.22 = (bf16[256,384]{1,0:T(8,128)(2,1)S(1)}, bf16[256,384]{1,0:T(8,128)(2,1)S(1)}, u32[]{:S(2)}, u32[]{:S(2)}) collective-permute-start(bf16[256,384]{1,0:T(8,128)(2,1)S(1)} %get-tuple-element.70), channel_id=1, source_target_pairs={{0,96},{32,0},{64,32},{96,64},{1,97},{33,1},{65,33},{97,65},{2,98}... | collective-permute-start | bytes 589832 | tf_op jit(solution)/shard_map/ppermute | solution.py:18
  80.0 10.7 %collective-permute-start.19 = (bf16[128,1536]{1,0:T(8,128)(2,1)S(1)}, bf16[128,1536]{1,0:T(8,128)(2,1)S(1)}, u32[]{:S(2)}, u32[]{:S(2)}) collective-permute-start(bf16[128,1536]{1,0:T(8,128)(2,1)S(1)} %get-tuple-element.62), channel_id=1, source_target_pairs={{0,2},{2,4},{4,6},{6,8},{8,10},{10,12},{12,14},{14,0},{1,3},{3,5},... | collective-permute-start | bytes 1179656 | tf_op jit(solution)/shard_map/ppermute | solution.py:18
  80.1 10.6 %collective-permute-start.20 = (bf16[128,1536]{1,0:T(8,128)(2,1)S(1)}, bf16[128,1536]{1,0:T(8,128)(2,1)S(1)}, u32[]{:S(2)}, u32[]{:S(2)}) collective-permute-start(bf16[128,1536]{1,0:T(8,128)(2,1)S(1)} %get-tuple-element.61), channel_id=1, source_target_pairs={{0,14},{2,0},{4,2},{6,4},{8,6},{10,8},{12,10},{14,12},{1,15},{3,1}... | collective-permute-start | bytes 1179656 | tf_op jit(solution)/shard_map/ppermute | solution.py:18
  83.5 8.4 %collective-permute-start.24 = (bf16[384,384]{1,0:T(8,128)(2,1)S(1)}, bf16[384,384]{1,0:T(8,128)(2,1)S(1)}, u32[]{:S(2)}, u32[]{:S(2)}) collective-permute-start(bf16[384,384]{1,0:T(8,128)(2,1)S(1)} %slice.120), channel_id=1, source_target_pairs={{0,1},{1,0},{2,3},{3,2},{4,5},{5,4},{6,7},{7,6},{8,9},{9,8},{10,11... | collective-permute-start | bytes 884744 | tf_op jit(solution)/shard_map/ppermute | solution.py:18
  88.0 14.2 %copy-start.4 = (bf16[1536,384]{1,0:T(8,128)(2,1)}, bf16[1536,384]{1,0:T(8,128)(2,1)S(1)}, u32[]{:S(2)}) copy-start(bf16[1536,384]{1,0:T(8,128)(2,1)S(1)} %fusion.1) | copy-start | bytes 3538948
  91.9 0.7 copy-start.11
  92.9 12.1 %collective-permute-start.26 = (bf16[128,1536]{1,0:T(8,128)(2,1)S(1)}, bf16[128,1536]{1,0:T(8,128)(2,1)S(1)}, u32[]{:S(2)}, u32[]{:S(2)}) collective-permute-start(bf16[128,1536]{1,0:T(8,128)(2,1)S(1)} %get-tuple-element.60), channel_id=1, source_target_pairs={{0,2},{2,4},{4,6},{6,8},{8,10},{10,12},{12,14},{14,0},{1,3},{3,5},... | collective-permute-start | bytes 1179656 | tf_op jit(solution)/shard_map/ppermute | solution.py:18
  94.0 10.9 %collective-permute-start.27 = (bf16[128,1536]{1,0:T(8,128)(2,1)S(1)}, bf16[128,1536]{1,0:T(8,128)(2,1)S(1)}, u32[]{:S(2)}, u32[]{:S(2)}) collective-permute-start(bf16[128,1536]{1,0:T(8,128)(2,1)S(1)} %get-tuple-element.59), channel_id=1, source_target_pairs={{0,14},{2,0},{4,2},{6,4},{8,6},{10,8},{12,10},{14,12},{1,15},{3,1}... | collective-permute-start | bytes 1179656 | tf_op jit(solution)/shard_map/ppermute | solution.py:18
  96.2 16.4 %collective-permute-start.30 = (bf16[256,768]{1,0:T(8,128)(2,1)S(1)}, bf16[256,768]{1,0:T(8,128)(2,1)}, u32[]{:S(2)}, u32[]{:S(2)}) collective-permute-start(bf16[256,768]{1,0:T(8,128)(2,1)S(1)} %pad_maximum_fusion.6), channel_id=1, source_target_pairs={{0,96},{32,0},{64,32},{96,64},{1,97},{33,1},{65,33},{97,65},{2,98}... | collective-permute-start | bytes 1179656 | tf_op jit(solution)/shard_map/ppermute | solution.py:18
  96.6 8.3 %collective-permute-start.28 = (bf16[384,384]{1,0:T(8,128)(2,1)S(1)}, bf16[384,384]{1,0:T(8,128)(2,1)S(1)}, u32[]{:S(2)}, u32[]{:S(2)}) collective-permute-start(bf16[384,384]{1,0:T(8,128)(2,1)S(1)} %slice.96), channel_id=1, source_target_pairs={{0,1},{1,0},{2,3},{3,2},{4,5},{5,4},{6,7},{7,6},{8,9},{9,8},{10,11... | collective-permute-start | bytes 884744 | tf_op jit(solution)/shard_map/ppermute | solution.py:18
  100.4 12.2 %collective-permute-start.29 = (bf16[256,768]{1,0:T(8,128)(2,1)}, bf16[256,768]{1,0:T(8,128)(2,1)}, u32[]{:S(2)}, u32[]{:S(2)}) collective-permute-start(bf16[256,768]{1,0:T(8,128)(2,1)} %pad_maximum_fusion.5), channel_id=1, source_target_pairs={{0,32},{32,64},{64,96},{96,0},{1,33},{33,65},{65,97},{97,1},{2,34}... | collective-permute-start | bytes 1179656 | tf_op jit(solution)/shard_map/ppermute | solution.py:18
  104.9 1.1 copy-start.13
  104.9 7.7 %collective-permute-start.31 = (bf16[768,384]{1,0:T(8,128)(2,1)S(1)}, bf16[768,384]{1,0:T(8,128)(2,1)S(1)}, u32[]{:S(2)}, u32[]{:S(2)}) collective-permute-start(bf16[768,384]{1,0:T(8,128)(2,1)S(1)} %slice.101), channel_id=1, source_target_pairs={{0,16},{16,0},{1,17},{17,1},{2,18},{18,2},{3,19},{19,3},{4,20},{20... | collective-permute-start | bytes 1769480 | tf_op jit(solution)/shard_map/ppermute | solution.py:18
  106.1 22.4 %all-to-all-start.1 = ((bf16[16,16,1536]{2,1,0:T(8,128)(2,1)}), bf16[16,16,1536]{2,1,0:T(8,128)(2,1)S(1)}, u32[]{:S(2)}, u32[]{:S(2)}) async-start(bf16[16,16,1536]{2,1,0:T(8,128)(2,1)} %bitcast.35), calls=%async_computation.1 | async-start | bytes 1572864 | tf_op jit(solution)/shard_map/all_to_all | solution.py:198
  112.6 4.5 %copy-start.5 = (bf16[1536,384]{1,0:T(8,128)(2,1)S(1)}, bf16[1536,384]{1,0:T(8,128)(2,1)}, u32[]{:S(2)}) copy-start(bf16[1536,384]{1,0:T(8,128)(2,1)} %copy-done.4) | copy-start | bytes 3538948
  112.6 0.8 copy-start.8
  113.4 3.6 %copy-start.9 = (bf16[768,384]{1,0:T(8,128)(2,1)S(1)}, bf16[768,384]{1,0:T(8,128)(2,1)}, u32[]{:S(2)}) copy-start(bf16[768,384]{1,0:T(8,128)(2,1)} %copy-done.8) | copy-start | bytes 1769476
  113.5 3.9 %copy-start.12 = (bf16[384,384]{1,0:T(8,128)(2,1)S(1)}, bf16[384,384]{1,0:T(8,128)(2,1)}, u32[]{:S(2)}) copy-start(bf16[384,384]{1,0:T(8,128)(2,1)} %copy-done.11) | copy-start | bytes 884740
  114.8 2.6 %copy-start.14 = (bf16[384,384]{1,0:T(8,128)(2,1)S(1)}, bf16[384,384]{1,0:T(8,128)(2,1)}, u32[]{:S(2)}) copy-start(bf16[384,384]{1,0:T(8,128)(2,1)} %copy-done.13) | copy-start | bytes 884740
  114.8 13.6 %collective-permute-start.32 = (bf16[256,384]{1,0:T(8,128)(2,1)S(1)}, bf16[256,384]{1,0:T(8,128)(2,1)}, u32[]{:S(2)}, u32[]{:S(2)}) collective-permute-start(bf16[256,384]{1,0:T(8,128)(2,1)S(1)} %slice.144), channel_id=1, source_target_pairs={{0,1},{1,0},{2,3},{3,2},{4,5},{5,4},{6,7},{7,6},{8,9},{9,8},{10,11... | collective-permute-start | bytes 589832 | tf_op jit(solution)/shard_map/ppermute | solution.py:18
  117.5 14.3 %copy-start.3 = (bf16[1,1536,384]{2,1,0:T(8,128)(2,1)}, bf16[1,1536,384]{2,1,0:T(8,128)(2,1)S(1)}, u32[]{:S(2)}) copy-start(bf16[1,1536,384]{2,1,0:T(8,128)(2,1)S(1)} %bitcast_dynamic-update-slice_fusion.7) | copy-start | bytes 3538948

commit v12 on v8

--- a/solution.py
+++ b/solution.py
@@ -88,7 +88,10 @@
         out_ref[group, :, at * piece : (at + 1) * piece] = chosen
 
 
-def finish_kernel(sizes, at_ref, branch_ref, residual_ref, early_ref, forward_ref, received_ref):
+def finish_kernel(
+    sizes, at_ref, branch_ref, residual_ref, early_ref, summed_ref, other_ref, forward_ref, received_ref, ctx_ref
+):
+    ctx_ref[...] = (summed_ref[:, : ctx_ref.shape[1]] + other_ref[...].astype(F32)).astype(BF16)
     piece = sizes[-1]
     section, core = at_ref[0], at_ref[1]
     for group, at, first in by_group(*sizes):
@@ -168,7 +171,7 @@
     far = jnp.concatenate(far_blocks, 0)[None]
     grad_flat = place(grad_all, far, (wrap(z + n_z // 2, n_z), 0, 0)).reshape(tokens, features)
     partial_ctx = jnp.dot(grad_flat, block, preferred_element_type=F32).astype(BF16)
-    *step, partial_ctx = tie(*step, partial_ctx)
+    *step, partial_ctx, early = tie(*step, partial_ctx, early)
     step = ring.send(step)
     norm_factor = 1.0 / math.sqrt(tokens * n_core)
     product = lax.dot_general(grad_flat, ctx_flat, (((0,), (0,)), ((), ())), preferred_element_type=F32)
@@ -177,9 +180,9 @@
     ctx_ring = ring_steps(lambda away: pick(partial_ctx, wrap(y + away, n_y), 1).reshape(group_tokens, 2 * width), "y")
     ctx_step = next(ctx_ring)
     other_product = swap(product[piece:], "core")
-    *step, other_product, early = tie(*step, other_product, early)
+    *step, ctx_low, ctx_high, other_product = tie(*step, *ctx_step, other_product)
     step = ring.send(step)
-    ctx_step = ctx_ring.send(ctx_step)
+    ctx_step = ctx_ring.send((ctx_low, ctx_high))
     own_rows = add(product[:piece], other_product)
     came = swap(own_rows[:, width:], "xh")
     *ctx_step, came = tie(*ctx_step, came)
@@ -190,18 +193,15 @@
 
     summed = ctx_ring.send(ctx_step)
     other_ctx = swap(summed[:, width:].astype(BF16), "xh")
-    branch, other_ctx = tie(branch, other_ctx)
-    ctx_grad = add(summed[:, :width], other_ctx)
-    forward, received = local(
+    forward, received, ctx_grad = local(
         functools.partial(finish_kernel, sizes),
         at,
-        [branch.reshape(2, group, own_count, features), residual, early],
-        [residual.shape, residual.shape],
+        [branch.reshape(2, group, own_count, features), residual, early, summed, other_ctx],
+        [residual.shape, residual.shape, other_ctx.shape],
     )
 
-    kept = own_rows[:, :width]
-    first = xh == 0
-    weight_grad = jnp.concatenate([jnp.where(first, kept, came), jnp.where(first, came, kept)], 0)
+    weight_grad = place(jnp.zeros((n_xh * piece, width), BF16), own_rows[:, :width], (xh * piece, 0))
+    weight_grad = place(weight_grad, came, ((1 - xh) * piece, 0))
     return (forward[None], received[None], ctx_grad[None], weight_grad[None])
 
 

time: 130 us -> 133 us (1.023)
  local copies, waits for them, and re-layouts: 7.44 us -> 11 us
  waiting for transfers between devices: 34 us -> 30.5 us
  other arithmetic: 9.96 us -> 11.7 us
  starting transfers between devices: 62.7 us -> 64.2 us
    convert_element_type x7, other arithmetic: 0.95 us -> 6.51 us  [add(): return (a.astype(F32) + b.astype(F32)).astype(BF16)]
    ppermute x31, waiting for transfers between devices: 34 us -> 30.4 us  [shift(): return lax.ppermute(value, axis, [(i, (i + by) % n) for i in range(n)])]
    ppermute x31, starting transfers between devices: 51.3 us -> 54.2 us  [shift(): return lax.ppermute(value, axis, [(i, (i + by) % n) for i in range(n)])]
    broadcast_in_dim x2 -> x0, other arithmetic: 2.78 us -> none  [shards(): return (forward[None], received[None], ctx_grad[None], weight_grad[None])]
    dynamic_update_slice x11 -> x13, local copies, waits for them, and re-layouts: 0.35 us -> 2.69 us  [place(): return lax.dynamic_update_slice(buffer, block, starts)]
    all_to_all x1, starting transfers between devices: 6.07 us -> 4.67 us  [shards(): branch = lax.all_to_all(branch, ('section', 'y', 'xh'), 0, 0, tiled=True)]
  transfers between devices with their start and end apart: 33 -> 33, of which waited for: 10 -> 10; matrix products, arithmetic and copies ran while one was open for 19% -> 21% of each run, Pallas kernels for 1% -> 1%
where the time goes in v12:
time: 133 us; the launch traced here: 132 us
  starting transfers between devices  64.2 us (48%)
  waiting for transfers between devices  30.5 us (23%)
  other arithmetic  11.7 us (9%)
  local copies, waits for them, and re-layouts  11 us (8%)
  matrix products  10.3 us (8%)
  Pallas kernels  2.95 us (2%)
    ppermute x31, starting transfers between devices, shift(): return lax.ppermute(value, axis, [(i, (i + by) % n) for i in range(n)])  54.2 us
    ppermute x31, waiting for transfers between devices, shift(): return lax.ppermute(value, axis, [(i, (i + by) % n) for i in range(n)])  30.4 us
    convert_element_type x7, other arithmetic, add(): return (a.astype(F32) + b.astype(F32)).astype(BF16)  6.51 us
    all_to_all x1, starting transfers between devices, shards(): lax.all_to_all(spread, ('y', 'xh'), 0, 0, tiled=True)  5.31 us
    all_to_all x1, starting transfers between devices, shards(): branch = lax.all_to_all(branch, ('section', 'y', 'xh'), 0, 0, tiled=True)  4.67 us
    dot_general x1, matrix products, shards(): lax.dot_general(ctx_flat, block, (((1,), (1,)), ((), ())), preferred_elem...  3.71 us
    dot_general x1, matrix products, shards(): jnp.dot(grad_flat, block, preferred_element_type=F32).astype(BF16)  3.66 us
    dot_general x1, matrix products, shards(): lax.dot_general(grad_flat, ctx_flat, (((0,), (0,)), ((), ())), preferred_...  2.96 us
  transfers between devices with their start and end apart: 33, of which 10 were waited for; matrix products, arithmetic and copies ran while one was open for 21% of the time, Pallas kernels for 1%

profile of v12, /device:TPU:2, one launch (start us, length us, event | category | flops | bytes accessed | tf_op | source)
XLA Modules:
  0.0 131.7 jit_solution(8244425448120158860)
XLA Ops:
  0.6 2.2 %collective-permute-start = (bf16[256,384]{1,0:T(8,128)(2,1)}, bf16[256,384]{1,0:T(8,128)(2,1)S(1)}, u32[]{:S(2)}, u32[]{:S(2)}) collective-permute-start(bf16[256,384]{1,0:T(8,128)(2,1)} %bitcast.116), channel_id=1, source_target_pairs={{0,1},{1,0},{2,3},{3,2},{4,5},{5,4},{6,7},{7,6},{8,9},{9,8},{10,11... | collective-permute-start | bytes 589832 | tf_op jit(solution)/shard_map/ppermute | solution.py:18
  2.9 1.0 copy-done
  3.9 1.3 shard_map.75
  5.2 5.3 %all-to-all-start = ((bf16[8,16,1536]{2,1,0:T(8,128)(2,1)}), bf16[8,16,1536]{2,1,0:T(8,128)(2,1)S(1)}, u32[]{:S(2)}, u32[]{:S(2)}) async-start(bf16[8,16,1536]{2,1,0:T(8,128)(2,1)} %shard_map.75), calls=%async_computation | async-start | bytes 786432 | tf_op jit(solution)/shard_map/all_to_all | solution.py:158
  10.5 2.7 %dynamic-slice_bitcast_fusion.1 = (bf16[768,384]{1,0:T(8,128)(2,1)}, bf16[768,384]{1,0:T(8,128)(2,1)}, bf16[768,384]{1,0:T(8,128)(2,1)}) fusion(bf16[1,12288,384]{2,1,0:T(8,128)(2,1)} %param.6, s32[]{:T(128)S(6)} %select_n.78, s32[]{:T(128)S(6)} %select_n.73, s32[]{:T(128)S(6)} %select_n.79), kind=kLoop, calls=%fused_computation.23 | loop fusion | bytes 3538956 | tf_op jit(solution)/shard_map/dynamic_slice | solution.py:139
  13.3 2.1 %collective-permute-start.1 = (bf16[256,768]{1,0:T(8,128)(2,1)S(1)}, bf16[256,768]{1,0:T(8,128)(2,1)S(1)}, u32[]{:S(2)}, u32[]{:S(2)}) collective-permute-start(bf16[256,768]{1,0:T(8,128)(2,1)S(1)} %pad_maximum_fusion.1), channel_id=1, source_target_pairs={{0,32},{32,64},{64,96},{96,0},{1,33},{33,65},{65,97},{97,1},{2,34}... | collective-permute-start | bytes 1179656 | tf_op jit(solution)/shard_map/ppermute | solution.py:18
  15.4 1.3 collective-permute-start.2
  16.7 0.8 broadcast_select_fusion
  17.5 3.4 %collective-permute-start.5 = (bf16[768,384]{1,0:T(8,128)(2,1)}, bf16[768,384]{1,0:T(8,128)(2,1)}, u32[]{:S(2)}, u32[]{:S(2)}) collective-permute-start(bf16[768,384]{1,0:T(8,128)(2,1)} %get-tuple-element.27), channel_id=1, source_target_pairs={{0,1},{1,0},{2,3},{3,2},{4,5},{5,4},{6,7},{7,6},{8,9},{9,8},{10,11... | collective-permute-start | bytes 1769480 | tf_op jit(solution)/shard_map/ppermute | solution.py:18
  20.9 0.2 broadcast_in_dim.44
  21.2 2.0 %collective-permute-start.11 = (bf16[128,1536]{1,0:T(8,128)(2,1)S(1)}, bf16[128,1536]{1,0:T(8,128)(2,1)S(1)}, u32[]{:S(2)}, u32[]{:S(2)}) collective-permute-start(bf16[128,1536]{1,0:T(8,128)(2,1)S(1)} %bitcast.103), channel_id=1, source_target_pairs={{0,2},{2,4},{4,6},{6,8},{8,10},{10,12},{12,14},{14,0},{1,3},{3,5},... | collective-permute-start | bytes 1179656 | tf_op jit(solution)/shard_map/ppermute | solution.py:18
  23.1 4.0 %collective-permute-start.12 = (bf16[128,1536]{1,0:T(8,128)(2,1)S(1)}, bf16[128,1536]{1,0:T(8,128)(2,1)S(1)}, u32[]{:S(2)}, u32[]{:S(2)}) collective-permute-start(bf16[128,1536]{1,0:T(8,128)(2,1)S(1)} %bitcast.104), channel_id=1, source_target_pairs={{0,14},{2,0},{4,2},{6,4},{8,6},{10,8},{12,10},{14,12},{1,15},{3,1}... | collective-permute-start | bytes 1179656 | tf_op jit(solution)/shard_map/ppermute | solution.py:18
  27.2 0.3 broadcast_in_dim.45
  27.5 0.3 collective-permute-start.3
  27.9 0.9 slice.86
  28.8 3.1 %collective-permute-start.4 = (bf16[128,768]{1,0:T(8,128)(2,1)S(1)}, bf16[128,768]{1,0:T(8,128)(2,1)S(1)}, u32[]{:S(2)}, u32[]{:S(2)}) collective-permute-start(bf16[128,768]{1,0:T(8,128)(2,1)S(1)} %slice.86), channel_id=1, source_target_pairs={{0,96},{32,0},{64,32},{96,64},{1,97},{33,1},{65,33},{97,65},{2,98}... | collective-permute-start | bytes 589832 | tf_op jit(solution)/shard_map/ppermute | solution.py:18
  31.9 1.1 constant_dynamic-update-slice_fusion.1
  33.0 1.5 %collective-permute-done.11 = bf16[128,1536]{1,0:T(8,128)(2,1)S(1)} collective-permute-done((bf16[128,1536]{1,0:T(8,128)(2,1)S(1)}, bf16[128,1536]{1,0:T(8,128)(2,1)S(1)}, u32[]{:S(2)}, u32[]{:S(2)}) %collective-permute-start.11) | collective-permute-done | bytes 393248 | tf_op jit(solution)/shard_map/ppermute | solution.py:18
  34.5 0.4 collective-permute-start.13
  34.9 4.0 %collective-permute-start.14 = (bf16[128,1536]{1,0:T(8,128)(2,1)S(1)}, bf16[128,1536]{1,0:T(8,128)(2,1)S(1)}, u32[]{:S(2)}, u32[]{:S(2)}) collective-permute-start(bf16[128,1536]{1,0:T(8,128)(2,1)S(1)} %collective-permute-done.12), channel_id=1, source_target_pairs={{0,14},{2,0},{4,2},{6,4},{8,6},{10,8},{12,10},{14,12},{1,15},{3,1}... | collective-permute-start | bytes 1179656 | tf_op jit(solution)/shard_map/ppermute | solution.py:18
  39.1 0.1 collective-permute-start.6
  39.3 7.9 %collective-permute-done.13 = bf16[128,1536]{1,0:T(8,128)(2,1)S(1)} collective-permute-done((bf16[128,1536]{1,0:T(8,128)(2,1)S(1)}, bf16[128,1536]{1,0:T(8,128)(2,1)S(1)}, u32[]{:S(2)}, u32[]{:S(2)}) %collective-permute-start.13) | collective-permute-done | bytes 393248 | tf_op jit(solution)/shard_map/ppermute | solution.py:18
  47.2 3.2 %collective-permute-start.16 = (bf16[128,1536]{1,0:T(8,128)(2,1)S(1)}, bf16[128,1536]{1,0:T(8,128)(2,1)S(1)}, u32[]{:S(2)}, u32[]{:S(2)}) collective-permute-start(bf16[128,1536]{1,0:T(8,128)(2,1)S(1)} %collective-permute-done.14), channel_id=1, source_target_pairs={{0,14},{2,0},{4,2},{6,4},{8,6},{10,8},{12,10},{14,12},{1,15},{3,1}... | collective-permute-start | bytes 1179656 | tf_op jit(solution)/shard_map/ppermute | solution.py:18
  50.5 3.7 %convolution_convert_fusion = bf16[1024,1536]{1,0:T(8,128)(2,1)S(1)} fusion(bf16[1024,768]{1,0:T(8,128)(2,1)S(1)} %bitcast.101, bf16[768,384]{1,0:T(8,128)(2,1)S(1)} %collective-permute-done.6, bf16[768,384]{1,0:T(8,128)(2,1)S(1)} %copy-done.7, bf16[768,384]{1,0:T(8,128)(2,1)} %collective-permute-done.5, bf16[768,384]{1,0:T(8,128)(2,1)S(1)} %copy-done.6), kind=kOutput, calls=%fused_computation.1 | convolution fusion | flops 2426929152 | bytes 7077888 | tf_op jit(solution)/shard_map/dot_general | solution.py:164
  54.5 3.2 %collective-permute-start.8 = (bf16[128,768]{1,0:T(8,128)(2,1)S(1)}, bf16[128,768]{1,0:T(8,128)(2,1)S(1)}, u32[]{:S(2)}, u32[]{:S(2)}) collective-permute-start(bf16[128,768]{1,0:T(8,128)(2,1)S(1)} %get-tuple-element.64), channel_id=1, source_target_pairs={{0,14},{2,0},{4,2},{6,4},{8,6},{10,8},{12,10},{14,12},{1,15},{3,1}... | collective-permute-start | bytes 589832 | tf_op jit(solution)/shard_map/ppermute | solution.py:18
  57.7 1.6 %collective-permute-done.15 = bf16[128,1536]{1,0:T(8,128)(2,1)S(1)} collective-permute-done((bf16[128,1536]{1,0:T(8,128)(2,1)S(1)}, bf16[128,1536]{1,0:T(8,128)(2,1)S(1)}, u32[]{:S(2)}, u32[]{:S(2)}) %collective-permute-start.15) | collective-permute-done | bytes 393248 | tf_op jit(solution)/shard_map/ppermute | solution.py:18
  59.5 3.3 %collective-permute-start.18 = (bf16[64,1536]{1,0:T(8,128)(2,1)S(1)}, bf16[64,1536]{1,0:T(8,128)(2,1)S(1)}, u32[]{:S(2)}, u32[]{:S(2)}) collective-permute-start(bf16[64,1536]{1,0:T(8,128)(2,1)S(1)} %slice.94), channel_id=1, source_target_pairs={{0,14},{2,0},{4,2},{6,4},{8,6},{10,8},{12,10},{14,12},{1,15},{3,1}... | collective-permute-start | bytes 589832 | tf_op jit(solution)/shard_map/ppermute | solution.py:18
  62.9 0.7 collective-permute-done.7
  63.7 3.2 %collective-permute-start.10 = (bf16[128,1536]{1,0:T(8,128)(2,1)S(1)}, bf16[128,1536]{1,0:T(8,128)(2,1)S(1)}, u32[]{:S(2)}, u32[]{:S(2)}) collective-permute-start(bf16[128,1536]{1,0:T(8,128)(2,1)S(1)} %pad_maximum_fusion.4), channel_id=1, source_target_pairs={{0,14},{2,0},{4,2},{6,4},{8,6},{10,8},{12,10},{14,12},{1,15},{3,1}... | collective-permute-start | bytes 1179656 | tf_op jit(solution)/shard_map/ppermute | solution.py:18
  67.1 0.8 collective-permute-start.19
  67.9 0.1 collective-permute-done.18
  68.0 3.7 %convolution_convert_fusion.1 = bf16[1024,768]{1,0:T(8,128)(2,1)S(1)} fusion(bf16[1024,1536]{1,0:T(8,128)(2,1)S(1)} %bitcast.95, bf16[768,384]{1,0:T(8,128)(2,1)S(1)} %collective-permute-done.6, bf16[768,384]{1,0:T(8,128)(2,1)S(1)} %copy-done.7, bf16[768,384]{1,0:T(8,128)(2,1)} %collective-permute-done.5, bf16[768,384]{1,0:T(8,128)(2,1)S(1)} %copy-done.6), kind=kOutput, calls=%fused_computation.4 | convolution fusion | flops 2426142720 | bytes 7077888 | tf_op jit(solution)/shard_map/dot_general | solution.py:173
  71.7 3.0 %multiply_convert_fusion = bf16[1536,768]{1,0:T(8,128)(2,1)S(1)} fusion(bf16[1024,1536]{1,0:T(8,128)(2,1)S(1)} %bitcast.96, bf16[1024,768]{1,0:T(8,128)(2,1)S(1)} %bitcast.102), kind=kOutput, calls=%fused_computation | convolution fusion | flops 2418278400 | bytes 7077888 | tf_op jit(solution)/shard_map/dot_general | solution.py:177
  74.7 1.4 %collective-permute-done.9 = bf16[128,1536]{1,0:T(8,128)(2,1)S(1)} collective-permute-done((bf16[128,1536]{1,0:T(8,128)(2,1)S(1)}, bf16[128,1536]{1,0:T(8,128)(2,1)S(1)}, u32[]{:S(2)}, u32[]{:S(2)}) %collective-permute-start.9) | collective-permute-done | bytes 393248 | tf_op jit(solution)/shard_map/ppermute | solution.py:18
  76.1 0.1 collective-permute-start.24
  76.3 1.1 fusion.2
  77.3 3.2 %collective-permute-start.21 = (bf16[128,1536]{1,0:T(8,128)(2,1)}, bf16[128,1536]{1,0:T(8,128)(2,1)}, u32[]{:S(2)}, u32[]{:S(2)}) collective-permute-start(bf16[128,1536]{1,0:T(8,128)(2,1)} %get-tuple-element.53), channel_id=1, source_target_pairs={{0,14},{2,0},{4,2},{6,4},{8,6},{10,8},{12,10},{14,12},{1,15},{3,1}... | collective-permute-start | bytes 1179656 | tf_op jit(solution)/shard_map/ppermute | solution.py:18
  80.6 0.1 constant_dynamic-slice_fusion.2
  80.7 0.8 fusion.11
  81.5 3.2 %collective-permute-start.23 = (bf16[256,384]{1,0:T(8,128)(2,1)}, bf16[256,384]{1,0:T(8,128)(2,1)}, u32[]{:S(2)}, u32[]{:S(2)}) collective-permute-start(bf16[256,384]{1,0:T(8,128)(2,1)} %get-tuple-element.62), channel_id=1, source_target_pairs={{0,96},{32,0},{64,32},{96,64},{1,97},{33,1},{65,33},{97,65},{2,98}... | collective-permute-start | bytes 589832 | tf_op jit(solution)/shard_map/ppermute | solution.py:18
  84.8 5.0 %collective-permute-done.22 = bf16[256,384]{1,0:T(8,128)(2,1)} collective-permute-done((bf16[256,384]{1,0:T(8,128)(2,1)}, bf16[256,384]{1,0:T(8,128)(2,1)}, u32[]{:S(2)}, u32[]{:S(2)}) %collective-permute-start.22) | collective-permute-done | bytes 196640 | tf_op jit(solution)/shard_map/ppermute | solution.py:18
  89.7 0.5 collective-permute-done.20
  90.3 1.9 %add_convert_fusion = bf16[768,768]{1,0:T(8,128)(2,1)S(1)} fusion(bf16[768,768]{1,0:T(8,128)(2,1)} %collective-permute-done.24, bf16[1536,768]{1,0:T(8,128)(2,1)} %copy-done.4), kind=kLoop, calls=%fused_computation.3 | loop fusion | flops 2359296 | bytes 3538944 | tf_op jit(solution)/shard_map/convert_element_type | solution.py:26
  92.2 0.9 slice.101
  93.0 2.6 %collective-permute-start.29 = (bf16[768,384]{1,0:T(8,128)(2,1)}, bf16[768,384]{1,0:T(8,128)(2,1)}, u32[]{:S(2)}, u32[]{:S(2)}) collective-permute-start(bf16[768,384]{1,0:T(8,128)(2,1)} %slice.101), channel_id=1, source_target_pairs={{0,1},{1,0},{2,3},{3,2},{4,5},{5,4},{6,7},{7,6},{8,9},{9,8},{10,11... | collective-permute-start | bytes 1769480 | tf_op jit(solution)/shard_map/ppermute | solution.py:18
  95.6 1.0 add_convert_fusion.1
  96.6 1.5 %fusion.4 = (bf16[128,1536]{1,0:T(8,128)(2,1)S(1)}, bf16[128,1536]{1,0:T(8,128)(2,1)S(1)}) fusion(bf16[128,1536]{1,0:T(8,128)(2,1)S(1)} %collective-permute-done.20, bf16[8,128,1536]{2,1,0:T(8,128)(2,1)} %bitcast.99, s32[]{:T(128)S(6)} %select_n.81, bf16[128,1536]{1,0:T(8,128)(2,1)} %collective-permute-done.21, s32[]{:T(128)S(6)} %select_n.88), kind=kLoop, calls=%fused_computation.15 | loop fusion | flops 1572864 | bytes 2359304 | tf_op jit(solution)/shard_map/convert_element_type | solution.py:26
  98.1 2.0 %collective-permute-start.25 = (bf16[128,1536]{1,0:T(8,128)(2,1)S(1)}, bf16[128,1536]{1,0:T(8,128)(2,1)S(1)}, u32[]{:S(2)}, u32[]{:S(2)}) collective-permute-start(bf16[128,1536]{1,0:T(8,128)(2,1)S(1)} %get-tuple-element.51), channel_id=1, source_target_pairs={{0,2},{2,4},{4,6},{6,8},{8,10},{10,12},{12,14},{14,0},{1,3},{3,5},... | collective-permute-start | bytes 1179656 | tf_op jit(solution)/shard_map/ppermute | solution.py:18
  100.0 1.4 %collective-permute-start.26 = (bf16[128,1536]{1,0:T(8,128)(2,1)S(1)}, bf16[128,1536]{1,0:T(8,128)(2,1)S(1)}, u32[]{:S(2)}, u32[]{:S(2)}) collective-permute-start(bf16[128,1536]{1,0:T(8,128)(2,1)S(1)} %get-tuple-element.52), channel_id=1, source_target_pairs={{0,14},{2,0},{4,2},{6,4},{8,6},{10,8},{12,10},{14,12},{1,15},{3,1}... | collective-permute-start | bytes 1179656 | tf_op jit(solution)/shard_map/ppermute | solution.py:18
  101.4 2.5 %collective-permute-start.28 = (bf16[256,768]{1,0:T(8,128)(2,1)S(1)}, bf16[256,768]{1,0:T(8,128)(2,1)}, u32[]{:S(2)}, u32[]{:S(2)}) collective-permute-start(bf16[256,768]{1,0:T(8,128)(2,1)S(1)} %pad_maximum_fusion.6), channel_id=1, source_target_pairs={{0,96},{32,0},{64,32},{96,64},{1,97},{33,1},{65,33},{97,65},{2,98}... | collective-permute-start | bytes 1179656 | tf_op jit(solution)/shard_map/ppermute | solution.py:18
  104.0 1.0 add_convert_fusion.2
  104.9 0.8 pad_maximum_fusion.5
  105.7 4.1 %collective-permute-done.25 = bf16[128,1536]{1,0:T(8,128)(2,1)S(1)} collective-permute-done((bf16[128,1536]{1,0:T(8,128)(2,1)S(1)}, bf16[128,1536]{1,0:T(8,128)(2,1)S(1)}, u32[]{:S(2)}, u32[]{:S(2)}) %collective-permute-start.25) | collective-permute-done | bytes 393248 | tf_op jit(solution)/shard_map/ppermute | solution.py:18
  109.8 1.2 fusion.6
  111.0 1.0 pad_maximum_fusion
  111.9 4.7 %all-to-all-start.1 = ((bf16[16,16,1536]{2,1,0:T(8,128)(2,1)}), bf16[16,16,1536]{2,1,0:T(8,128)(2,1)S(1)}, u32[]{:S(2)}, u32[]{:S(2)}) async-start(bf16[16,16,1536]{2,1,0:T(8,128)(2,1)} %bitcast.35), calls=%async_computation.1 | async-start | bytes 1572864 | tf_op jit(solution)/shard_map/all_to_all | solution.py:192
  116.6 0.1 broadcast_in_dim.56
  116.7 0.1 fusion.7
  116.9 1.2 fusion.summed_ref
  118.1 2.2 %collective-permute-start.30 = (bf16[256,384]{1,0:T(8,128)(2,1)S(1)}, bf16[256,384]{1,0:T(8,128)(2,1)S(1)}, u32[]{:S(2)}, u32[]{:S(2)}) collective-permute-start(bf16[256,384]{1,0:T(8,128)(2,1)S(1)} %slice.113), channel_id=1, source_target_pairs={{0,1},{1,0},{2,3},{3,2},{4,5},{5,4},{6,7},{7,6},{8,9},{9,8},{10,11... | collective-permute-start | bytes 589832 | tf_op jit(solution)/shard_map/ppermute | solution.py:18
  120.3 1.2 bitcast_dynamic-update-slice_fusion
  121.5 1.0 copy-done.5
  122.5 7.6 %collective-permute-done.30.other_ref = bf16[256,384]{1,0:T(8,128)(2,1)S(1)} collective-permute-done((bf16[256,384]{1,0:T(8,128)(2,1)S(1)}, bf16[256,384]{1,0:T(8,128)(2,1)S(1)}, u32[]{:S(2)}, u32[]{:S(2)}) %collective-permute-start.30) | collective-permute-done | bytes 196640 | tf_op jit(solution)/shard_map/ppermute | solution.py:18
  130.1 1.6 %shard_map.76 = (bf16[16,12288]{1,0:T(8,128)(2,1)}, bf16[16,12288]{1,0:T(8,128)(2,1)}, bf16[256,384]{1,0:T(8,128)(2,1)}) custom-call(s32[2]{0:T(128)S(1)} %pad_add_fusion.at_ref, bf16[2,8,16,1536]{3,2,1,0:T(8,128)(2,1)S(1)} %bitcast.92, bf16[16,12288]{1,0:T(8,128)(2,1)S(1)} %bitcast.94, bf16[16,12288]{1,0:T(8,128)(2,1)S(1)} %collective-permute-done.19.early_ref, ...), custom_call_target="tpu_custom_call" | custom-call | tf_op jit(solution)/shard_map/pallas_call | solution.py:112
  (78 shorter events, 1.4 us)
Async XLA Ops:
  0.6 12.6 %collective-permute-start = (bf16[256,384]{1,0:T(8,128)(2,1)}, bf16[256,384]{1,0:T(8,128)(2,1)S(1)}, u32[]{:S(2)}, u32[]{:S(2)}) collective-permute-start(bf16[256,384]{1,0:T(8,128)(2,1)} %bitcast.116), channel_id=1, source_target_pairs={{0,1},{1,0},{2,3},{3,2},{4,5},{5,4},{6,7},{7,6},{8,9},{9,8},{10,11... | collective-permute-start | bytes 589832 | tf_op jit(solution)/shard_map/ppermute | solution.py:18
  2.9 1.0 copy-start
  3.9 9.3 %copy-start.9 = (bf16[1,256,384]{2,1,0:T(8,128)(2,1)S(1)}, bf16[1,256,384]{2,1,0:T(8,128)(2,1)}, u32[]{:S(2)}) copy-start(bf16[1,256,384]{2,1,0:T(8,128)(2,1)} %param.5) | copy-start | bytes 589828
  3.9 12.8 %copy-start.1 = (bf16[1,16,12288]{2,1,0:T(8,128)(2,1)S(1)}, bf16[1,16,12288]{2,1,0:T(8,128)(2,1)}, u32[]{:S(2)}) copy-start(bf16[1,16,12288]{2,1,0:T(8,128)(2,1)} %param.7) | copy-start | bytes 1179652
  3.9 12.8 %copy-start.2 = (bf16[1,16,12288]{2,1,0:T(8,128)(2,1)S(1)}, bf16[1,16,12288]{2,1,0:T(8,128)(2,1)}, u32[]{:S(2)}) copy-start(bf16[1,16,12288]{2,1,0:T(8,128)(2,1)} %param.4) | copy-start | bytes 1179652
  5.2 15.9 %all-to-all-start = ((bf16[8,16,1536]{2,1,0:T(8,128)(2,1)}), bf16[8,16,1536]{2,1,0:T(8,128)(2,1)S(1)}, u32[]{:S(2)}, u32[]{:S(2)}) async-start(bf16[8,16,1536]{2,1,0:T(8,128)(2,1)} %shard_map.75), calls=%async_computation | async-start | bytes 786432 | tf_op jit(solution)/shard_map/all_to_all | solution.py:158
  13.3 14.2 %collective-permute-start.1 = (bf16[256,768]{1,0:T(8,128)(2,1)S(1)}, bf16[256,768]{1,0:T(8,128)(2,1)S(1)}, u32[]{:S(2)}, u32[]{:S(2)}) collective-permute-start(bf16[256,768]{1,0:T(8,128)(2,1)S(1)} %pad_maximum_fusion.1), channel_id=1, source_target_pairs={{0,32},{32,64},{64,96},{96,0},{1,33},{33,65},{65,97},{97,1},{2,34}... | collective-permute-start | bytes 1179656 | tf_op jit(solution)/shard_map/ppermute | solution.py:18
  15.4 12.5 %collective-permute-start.2 = (bf16[256,768]{1,0:T(8,128)(2,1)S(1)}, bf16[256,768]{1,0:T(8,128)(2,1)}, u32[]{:S(2)}, u32[]{:S(2)}) collective-permute-start(bf16[256,768]{1,0:T(8,128)(2,1)S(1)} %pad_maximum_fusion.1), channel_id=1, source_target_pairs={{0,96},{32,0},{64,32},{96,64},{1,97},{33,1},{65,33},{97,65},{2,98}... | collective-permute-start | bytes 1179656 | tf_op jit(solution)/shard_map/ppermute | solution.py:18
  17.5 21.6 %collective-permute-start.5 = (bf16[768,384]{1,0:T(8,128)(2,1)}, bf16[768,384]{1,0:T(8,128)(2,1)}, u32[]{:S(2)}, u32[]{:S(2)}) collective-permute-start(bf16[768,384]{1,0:T(8,128)(2,1)} %get-tuple-element.27), channel_id=1, source_target_pairs={{0,1},{1,0},{2,3},{3,2},{4,5},{5,4},{6,7},{7,6},{8,9},{9,8},{10,11... | collective-permute-start | bytes 1769480 | tf_op jit(solution)/shard_map/ppermute | solution.py:18
  21.2 13.4 %collective-permute-start.11 = (bf16[128,1536]{1,0:T(8,128)(2,1)S(1)}, bf16[128,1536]{1,0:T(8,128)(2,1)S(1)}, u32[]{:S(2)}, u32[]{:S(2)}) collective-permute-start(bf16[128,1536]{1,0:T(8,128)(2,1)S(1)} %bitcast.103), channel_id=1, source_target_pairs={{0,2},{2,4},{4,6},{6,8},{8,10},{10,12},{12,14},{14,0},{1,3},{3,5},... | collective-permute-start | bytes 1179656 | tf_op jit(solution)/shard_map/ppermute | solution.py:18
  23.1 11.8 %collective-permute-start.12 = (bf16[128,1536]{1,0:T(8,128)(2,1)S(1)}, bf16[128,1536]{1,0:T(8,128)(2,1)S(1)}, u32[]{:S(2)}, u32[]{:S(2)}) collective-permute-start(bf16[128,1536]{1,0:T(8,128)(2,1)S(1)} %bitcast.104), channel_id=1, source_target_pairs={{0,14},{2,0},{4,2},{6,4},{8,6},{10,8},{12,10},{14,12},{1,15},{3,1}... | collective-permute-start | bytes 1179656 | tf_op jit(solution)/shard_map/ppermute | solution.py:18
  27.5 11.6 %collective-permute-start.3 = (bf16[128,768]{1,0:T(8,128)(2,1)S(1)}, bf16[128,768]{1,0:T(8,128)(2,1)S(1)}, u32[]{:S(2)}, u32[]{:S(2)}) collective-permute-start(bf16[128,768]{1,0:T(8,128)(2,1)S(1)} %slice.85), channel_id=1, source_target_pairs={{0,32},{32,64},{64,96},{96,0},{1,33},{33,65},{65,97},{97,1},{2,34}... | collective-permute-start | bytes 589832 | tf_op jit(solution)/shard_map/ppermute | solution.py:18
  28.8 10.4 %collective-permute-start.4 = (bf16[128,768]{1,0:T(8,128)(2,1)S(1)}, bf16[128,768]{1,0:T(8,128)(2,1)S(1)}, u32[]{:S(2)}, u32[]{:S(2)}) collective-permute-start(bf16[128,768]{1,0:T(8,128)(2,1)S(1)} %slice.86), channel_id=1, source_target_pairs={{0,96},{32,0},{64,32},{96,64},{1,97},{33,1},{65,33},{97,65},{2,98}... | collective-permute-start | bytes 589832 | tf_op jit(solution)/shard_map/ppermute | solution.py:18
  31.9 18.6 %copy-start.6 = (bf16[768,384]{1,0:T(8,128)(2,1)S(1)}, bf16[768,384]{1,0:T(8,128)(2,1)}, u32[]{:S(2)}) copy-start(bf16[768,384]{1,0:T(8,128)(2,1)} %get-tuple-element.48) | copy-start | bytes 1769476
  31.9 18.6 %copy-start.7 = (bf16[768,384]{1,0:T(8,128)(2,1)S(1)}, bf16[768,384]{1,0:T(8,128)(2,1)}, u32[]{:S(2)}) copy-start(bf16[768,384]{1,0:T(8,128)(2,1)} %get-tuple-element.50) | copy-start | bytes 1769476
  34.5 12.6 %collective-permute-start.13 = (bf16[128,1536]{1,0:T(8,128)(2,1)S(1)}, bf16[128,1536]{1,0:T(8,128)(2,1)S(1)}, u32[]{:S(2)}, u32[]{:S(2)}) collective-permute-start(bf16[128,1536]{1,0:T(8,128)(2,1)S(1)} %collective-permute-done.11), channel_id=1, source_target_pairs={{0,2},{2,4},{4,6},{6,8},{8,10},{10,12},{12,14},{14,0},{1,3},{3,5},... | collective-permute-start | bytes 1179656 | tf_op jit(solution)/shard_map/ppermute | solution.py:18
  34.9 12.2 %collective-permute-start.14 = (bf16[128,1536]{1,0:T(8,128)(2,1)S(1)}, bf16[128,1536]{1,0:T(8,128)(2,1)S(1)}, u32[]{:S(2)}, u32[]{:S(2)}) collective-permute-start(bf16[128,1536]{1,0:T(8,128)(2,1)S(1)} %collective-permute-done.12), channel_id=1, source_target_pairs={{0,14},{2,0},{4,2},{6,4},{8,6},{10,8},{12,10},{14,12},{1,15},{3,1}... | collective-permute-start | bytes 1179656 | tf_op jit(solution)/shard_map/ppermute | solution.py:18
  39.1 11.4 %collective-permute-start.6 = (bf16[768,384]{1,0:T(8,128)(2,1)}, bf16[768,384]{1,0:T(8,128)(2,1)S(1)}, u32[]{:S(2)}, u32[]{:S(2)}) collective-permute-start(bf16[768,384]{1,0:T(8,128)(2,1)} %collective-permute-done.5), channel_id=1, source_target_pairs={{0,16},{16,0},{1,17},{17,1},{2,18},{18,2},{3,19},{19,3},{4,20},{20... | collective-permute-start | bytes 1769480 | tf_op jit(solution)/shard_map/ppermute | solution.py:18
  47.2 12.2 %collective-permute-start.15 = (bf16[128,1536]{1,0:T(8,128)(2,1)S(1)}, bf16[128,1536]{1,0:T(8,128)(2,1)S(1)}, u32[]{:S(2)}, u32[]{:S(2)}) collective-permute-start(bf16[128,1536]{1,0:T(8,128)(2,1)S(1)} %collective-permute-done.13), channel_id=1, source_target_pairs={{0,2},{2,4},{4,6},{6,8},{8,10},{10,12},{12,14},{14,0},{1,3},{3,5},... | collective-permute-start | bytes 1179656 | tf_op jit(solution)/shard_map/ppermute | solution.py:18
  47.2 12.3 %collective-permute-start.16 = (bf16[128,1536]{1,0:T(8,128)(2,1)S(1)}, bf16[128,1536]{1,0:T(8,128)(2,1)S(1)}, u32[]{:S(2)}, u32[]{:S(2)}) collective-permute-start(bf16[128,1536]{1,0:T(8,128)(2,1)S(1)} %collective-permute-done.14), channel_id=1, source_target_pairs={{0,14},{2,0},{4,2},{6,4},{8,6},{10,8},{12,10},{14,12},{1,15},{3,1}... | collective-permute-start | bytes 1179656 | tf_op jit(solution)/shard_map/ppermute | solution.py:18
  54.2 22.0 %copy-start.3 = (bf16[1024,1536]{1,0:T(8,128)(2,1)}, bf16[1024,1536]{1,0:T(8,128)(2,1)S(1)}, u32[]{:S(2)}) copy-start(bf16[1024,1536]{1,0:T(8,128)(2,1)S(1)} %convolution_convert_fusion) | copy-start | bytes 9437188
  54.4 12.7 %copy-start.8 = (bf16[16,12288]{1,0:T(8,128)(2,1)S(1)}, bf16[16,12288]{1,0:T(8,128)(2,1)}, u32[]{:S(2)}) copy-start(bf16[16,12288]{1,0:T(8,128)(2,1)} %broadcast_select_fusion) | copy-start | bytes 1179652
  54.4 9.2 %collective-permute-start.7 = (bf16[128,768]{1,0:T(8,128)(2,1)S(1)}, bf16[128,768]{1,0:T(8,128)(2,1)S(1)}, u32[]{:S(2)}, u32[]{:S(2)}) collective-permute-start(bf16[128,768]{1,0:T(8,128)(2,1)S(1)} %get-tuple-element.65), channel_id=1, source_target_pairs={{0,2},{2,4},{4,6},{6,8},{8,10},{10,12},{12,14},{14,0},{1,3},{3,5},... | collective-permute-start | bytes 589832 | tf_op jit(solution)/shard_map/ppermute | solution.py:18
  54.5 9.1 %collective-permute-start.8 = (bf16[128,768]{1,0:T(8,128)(2,1)S(1)}, bf16[128,768]{1,0:T(8,128)(2,1)S(1)}, u32[]{:S(2)}, u32[]{:S(2)}) collective-permute-start(bf16[128,768]{1,0:T(8,128)(2,1)S(1)} %get-tuple-element.64), channel_id=1, source_target_pairs={{0,14},{2,0},{4,2},{6,4},{8,6},{10,8},{12,10},{14,12},{1,15},{3,1}... | collective-permute-start | bytes 589832 | tf_op jit(solution)/shard_map/ppermute | solution.py:18
  59.4 8.5 %collective-permute-start.17 = (bf16[64,1536]{1,0:T(8,128)(2,1)S(1)}, bf16[64,1536]{1,0:T(8,128)(2,1)S(1)}, u32[]{:S(2)}, u32[]{:S(2)}) collective-permute-start(bf16[64,1536]{1,0:T(8,128)(2,1)S(1)} %slice.93), channel_id=1, source_target_pairs={{0,2},{2,4},{4,6},{6,8},{8,10},{10,12},{12,14},{14,0},{1,3},{3,5},... | collective-permute-start | bytes 589832 | tf_op jit(solution)/shard_map/ppermute | solution.py:18
  59.5 8.5 %collective-permute-start.18 = (bf16[64,1536]{1,0:T(8,128)(2,1)S(1)}, bf16[64,1536]{1,0:T(8,128)(2,1)S(1)}, u32[]{:S(2)}, u32[]{:S(2)}) collective-permute-start(bf16[64,1536]{1,0:T(8,128)(2,1)S(1)} %slice.94), channel_id=1, source_target_pairs={{0,14},{2,0},{4,2},{6,4},{8,6},{10,8},{12,10},{14,12},{1,15},{3,1}... | collective-permute-start | bytes 589832 | tf_op jit(solution)/shard_map/ppermute | solution.py:18
  63.7 11.0 %collective-permute-start.10 = (bf16[128,1536]{1,0:T(8,128)(2,1)S(1)}, bf16[128,1536]{1,0:T(8,128)(2,1)S(1)}, u32[]{:S(2)}, u32[]{:S(2)}) collective-permute-start(bf16[128,1536]{1,0:T(8,128)(2,1)S(1)} %pad_maximum_fusion.4), channel_id=1, source_target_pairs={{0,14},{2,0},{4,2},{6,4},{8,6},{10,8},{12,10},{14,12},{1,15},{3,1}... | collective-permute-start | bytes 1179656 | tf_op jit(solution)/shard_map/ppermute | solution.py:18
  67.0 9.1 %collective-permute-start.9 = (bf16[128,1536]{1,0:T(8,128)(2,1)S(1)}, bf16[128,1536]{1,0:T(8,128)(2,1)S(1)}, u32[]{:S(2)}, u32[]{:S(2)}) collective-permute-start(bf16[128,1536]{1,0:T(8,128)(2,1)S(1)} %pad_maximum_fusion.3), channel_id=1, source_target_pairs={{0,2},{2,4},{4,6},{6,8},{8,10},{10,12},{12,14},{14,0},{1,3},{3,5},... | collective-permute-start | bytes 1179656 | tf_op jit(solution)/shard_map/ppermute | solution.py:18
  67.1 9.0 %collective-permute-start.19 = (bf16[16,12288]{1,0:T(8,128)(2,1)S(1)}, bf16[16,12288]{1,0:T(8,128)(2,1)S(1)}, u32[]{:S(2)}, u32[]{:S(2)}) collective-permute-start(bf16[16,12288]{1,0:T(8,128)(2,1)S(1)} %copy-done.8), channel_id=1, source_target_pairs={{0,128},{128,0},{1,129},{129,1},{2,130},{130,2},{3,131},{131,3},{4... | collective-permute-start | bytes 1179656 | tf_op jit(solution)/shard_map/ppermute | solution.py:18
  74.7 6.0 %copy-start.4 = (bf16[1536,768]{1,0:T(8,128)(2,1)}, bf16[1536,768]{1,0:T(8,128)(2,1)S(1)}, u32[]{:S(2)}) copy-start(bf16[1536,768]{1,0:T(8,128)(2,1)S(1)} %multiply_convert_fusion) | copy-start | bytes 7077892
  76.1 14.1 %collective-permute-start.24 = (bf16[768,768]{1,0:T(8,128)(2,1)S(1)}, bf16[768,768]{1,0:T(8,128)(2,1)}, u32[]{:S(2)}, u32[]{:S(2)}) collective-permute-start(bf16[768,768]{1,0:T(8,128)(2,1)S(1)} %slice.76), channel_id=1, source_target_pairs={{0,16},{16,0},{1,17},{17,1},{2,18},{18,2},{3,19},{19,3},{4,20},{20... | collective-permute-start | bytes 3538952 | tf_op jit(solution)/shard_map/ppermute | solution.py:18
  77.3 12.9 %collective-permute-start.20 = (bf16[128,1536]{1,0:T(8,128)(2,1)}, bf16[128,1536]{1,0:T(8,128)(2,1)S(1)}, u32[]{:S(2)}, u32[]{:S(2)}) collective-permute-start(bf16[128,1536]{1,0:T(8,128)(2,1)} %get-tuple-element.54), channel_id=1, source_target_pairs={{0,2},{2,4},{4,6},{6,8},{8,10},{10,12},{12,14},{14,0},{1,3},{3,5},... | collective-permute-start | bytes 1179656 | tf_op jit(solution)/shard_map/ppermute | solution.py:18
  77.3 12.9 %collective-permute-start.21 = (bf16[128,1536]{1,0:T(8,128)(2,1)}, bf16[128,1536]{1,0:T(8,128)(2,1)}, u32[]{:S(2)}, u32[]{:S(2)}) collective-permute-start(bf16[128,1536]{1,0:T(8,128)(2,1)} %get-tuple-element.53), channel_id=1, source_target_pairs={{0,14},{2,0},{4,2},{6,4},{8,6},{10,8},{12,10},{14,12},{1,15},{3,1}... | collective-permute-start | bytes 1179656 | tf_op jit(solution)/shard_map/ppermute | solution.py:18
  81.5 8.3 %collective-permute-start.22 = (bf16[256,384]{1,0:T(8,128)(2,1)}, bf16[256,384]{1,0:T(8,128)(2,1)}, u32[]{:S(2)}, u32[]{:S(2)}) collective-permute-start(bf16[256,384]{1,0:T(8,128)(2,1)} %get-tuple-element.63), channel_id=1, source_target_pairs={{0,32},{32,64},{64,96},{96,0},{1,33},{33,65},{65,97},{97,1},{2,34}... | collective-permute-start | bytes 589832 | tf_op jit(solution)/shard_map/ppermute | solution.py:18
  81.5 8.3 %collective-permute-start.23 = (bf16[256,384]{1,0:T(8,128)(2,1)}, bf16[256,384]{1,0:T(8,128)(2,1)}, u32[]{:S(2)}, u32[]{:S(2)}) collective-permute-start(bf16[256,384]{1,0:T(8,128)(2,1)} %get-tuple-element.62), channel_id=1, source_target_pairs={{0,96},{32,0},{64,32},{96,64},{1,97},{33,1},{65,33},{97,65},{2,98}... | collective-permute-start | bytes 589832 | tf_op jit(solution)/shard_map/ppermute | solution.py:18
  93.0 23.8 %collective-permute-start.29 = (bf16[768,384]{1,0:T(8,128)(2,1)}, bf16[768,384]{1,0:T(8,128)(2,1)}, u32[]{:S(2)}, u32[]{:S(2)}) collective-permute-start(bf16[768,384]{1,0:T(8,128)(2,1)} %slice.101), channel_id=1, source_target_pairs={{0,1},{1,0},{2,3},{3,2},{4,5},{5,4},{6,7},{7,6},{8,9},{9,8},{10,11... | collective-permute-start | bytes 1769480 | tf_op jit(solution)/shard_map/ppermute | solution.py:18
  98.1 11.7 %collective-permute-start.25 = (bf16[128,1536]{1,0:T(8,128)(2,1)S(1)}, bf16[128,1536]{1,0:T(8,128)(2,1)S(1)}, u32[]{:S(2)}, u32[]{:S(2)}) collective-permute-start(bf16[128,1536]{1,0:T(8,128)(2,1)S(1)} %get-tuple-element.51), channel_id=1, source_target_pairs={{0,2},{2,4},{4,6},{6,8},{8,10},{10,12},{12,14},{14,0},{1,3},{3,5},... | collective-permute-start | bytes 1179656 | tf_op jit(solution)/shard_map/ppermute | solution.py:18
  100.0 9.8 %collective-permute-start.26 = (bf16[128,1536]{1,0:T(8,128)(2,1)S(1)}, bf16[128,1536]{1,0:T(8,128)(2,1)S(1)}, u32[]{:S(2)}, u32[]{:S(2)}) collective-permute-start(bf16[128,1536]{1,0:T(8,128)(2,1)S(1)} %get-tuple-element.52), channel_id=1, source_target_pairs={{0,14},{2,0},{4,2},{6,4},{8,6},{10,8},{12,10},{14,12},{1,15},{3,1}... | collective-permute-start | bytes 1179656 | tf_op jit(solution)/shard_map/ppermute | solution.py:18
  101.4 15.4 %collective-permute-start.28 = (bf16[256,768]{1,0:T(8,128)(2,1)S(1)}, bf16[256,768]{1,0:T(8,128)(2,1)}, u32[]{:S(2)}, u32[]{:S(2)}) collective-permute-start(bf16[256,768]{1,0:T(8,128)(2,1)S(1)} %pad_maximum_fusion.6), channel_id=1, source_target_pairs={{0,96},{32,0},{64,32},{96,64},{1,97},{33,1},{65,33},{97,65},{2,98}... | collective-permute-start | bytes 1179656 | tf_op jit(solution)/shard_map/ppermute | solution.py:18
  105.7 11.1 %collective-permute-start.27 = (bf16[256,768]{1,0:T(8,128)(2,1)}, bf16[256,768]{1,0:T(8,128)(2,1)}, u32[]{:S(2)}, u32[]{:S(2)}) collective-permute-start(bf16[256,768]{1,0:T(8,128)(2,1)} %pad_maximum_fusion.5), channel_id=1, source_target_pairs={{0,32},{32,64},{64,96},{96,0},{1,33},{33,65},{65,97},{97,1},{2,34}... | collective-permute-start | bytes 1179656 | tf_op jit(solution)/shard_map/ppermute | solution.py:18
  111.9 18.1 %all-to-all-start.1 = ((bf16[16,16,1536]{2,1,0:T(8,128)(2,1)}), bf16[16,16,1536]{2,1,0:T(8,128)(2,1)S(1)}, u32[]{:S(2)}, u32[]{:S(2)}) async-start(bf16[16,16,1536]{2,1,0:T(8,128)(2,1)} %bitcast.35), calls=%async_computation.1 | async-start | bytes 1572864 | tf_op jit(solution)/shard_map/all_to_all | solution.py:192
  118.1 11.9 %collective-permute-start.30 = (bf16[256,384]{1,0:T(8,128)(2,1)S(1)}, bf16[256,384]{1,0:T(8,128)(2,1)S(1)}, u32[]{:S(2)}, u32[]{:S(2)}) collective-permute-start(bf16[256,384]{1,0:T(8,128)(2,1)S(1)} %slice.113), channel_id=1, source_target_pairs={{0,1},{1,0},{2,3},{3,2},{4,5},{5,4},{6,7},{7,6},{8,9},{9,8},{10,11... | collective-permute-start | bytes 589832 | tf_op jit(solution)/shard_map/ppermute | solution.py:18
  121.5 1.0 copy-start.5

commit v13 on v12

--- a/solution.py
+++ b/solution.py
@@ -171,7 +171,7 @@
     far = jnp.concatenate(far_blocks, 0)[None]
     grad_flat = place(grad_all, far, (wrap(z + n_z // 2, n_z), 0, 0)).reshape(tokens, features)
     partial_ctx = jnp.dot(grad_flat, block, preferred_element_type=F32).astype(BF16)
-    *step, partial_ctx, early = tie(*step, partial_ctx, early)
+    *step, partial_ctx = tie(*step, partial_ctx)
     step = ring.send(step)
     norm_factor = 1.0 / math.sqrt(tokens * n_core)
     product = lax.dot_general(grad_flat, ctx_flat, (((0,), (0,)), ((), ())), preferred_element_type=F32)
@@ -180,12 +180,14 @@
     ctx_ring = ring_steps(lambda away: pick(partial_ctx, wrap(y + away, n_y), 1).reshape(group_tokens, 2 * width), "y")
     ctx_step = next(ctx_ring)
     other_product = swap(product[piece:], "core")
-    *step, ctx_low, ctx_high, other_product = tie(*step, *ctx_step, other_product)
+    *step, other_product, early = tie(*step, other_product, early)
     step = ring.send(step)
-    ctx_step = ctx_ring.send((ctx_low, ctx_high))
+    ctx_step = ctx_ring.send(ctx_step)
     own_rows = add(product[:piece], other_product)
-    came = swap(own_rows[:, width:], "xh")
-    *ctx_step, came = tie(*ctx_step, came)
+    half = piece // 2
+    came_first = swap(own_rows[:half, width:], "xh")
+    *ctx_step, came_first = tie(*ctx_step, came_first)
+    came_last = swap(own_rows[half:, width:], "xh")
     branch = ring.send(step).astype(BF16)
     branch = branch.reshape(1, group, own_count, features)
     branch = jnp.concatenate([branch, branch], 0).reshape(2 * group, own_count, features)
@@ -193,6 +195,7 @@
 
     summed = ctx_ring.send(ctx_step)
     other_ctx = swap(summed[:, width:].astype(BF16), "xh")
+    branch, other_ctx, came_last = tie(branch, other_ctx, came_last)
     forward, received, ctx_grad = local(
         functools.partial(finish_kernel, sizes),
         at,
@@ -201,7 +204,8 @@
     )
 
     weight_grad = place(jnp.zeros((n_xh * piece, width), BF16), own_rows[:, :width], (xh * piece, 0))
-    weight_grad = place(weight_grad, came, ((1 - xh) * piece, 0))
+    weight_grad = place(weight_grad, came_first, ((1 - xh) * piece, 0))
+    weight_grad = place(weight_grad, came_last, ((1 - xh) * piece + half, 0))
     return (forward[None], received[None], ctx_grad[None], weight_grad[None])
 
 

time: 133 us -> 129 us (0.970)
  other arithmetic: 11.7 us -> 5.15 us
  waiting for transfers between devices: 30.5 us -> 35.6 us
  starting transfers between devices: 64.2 us -> 62.8 us
    convert_element_type x7, other arithmetic: 6.51 us -> 0.97 us  [add(): return (a.astype(F32) + b.astype(F32)).astype(BF16)]
    ppermute x31 -> x32, waiting for transfers between devices: 30.4 us -> 35.6 us  [shift(): return lax.ppermute(value, axis, [(i, (i + by) % n) for i in range(n)])]
    ppermute x31 -> x32, starting transfers between devices: 54.2 us -> 53 us  [shift(): return lax.ppermute(value, axis, [(i, (i + by) % n) for i in range(n)])]
    dynamic_update_slice x13 -> x14, local copies, waits for them, and re-layouts: 2.69 us -> 3.16 us  [place(): return lax.dynamic_update_slice(buffer, block, starts)]
  transfers between devices with their start and end apart: 33 -> 34, of which waited for: 10 -> 9; matrix products, arithmetic and copies ran while one was open for 21% -> 17% of each run, Pallas kernels for 1% -> 1%
where the time goes in v13:
time: 129 us; the launch traced here: 128 us
  starting transfers between devices  62.8 us (49%)
  waiting for transfers between devices  35.6 us (28%)
  matrix products  10.3 us (8%)
  local copies, waits for them, and re-layouts  9.79 us (8%)
  other arithmetic  5.15 us (4%)
  Pallas kernels  2.95 us (2%)
    ppermute x32, starting transfers between devices, shift(): return lax.ppermute(value, axis, [(i, (i + by) % n) for i in range(n)])  53 us
    ppermute x32, waiting for transfers between devices, shift(): return lax.ppermute(value, axis, [(i, (i + by) % n) for i in range(n)])  35.6 us
    all_to_all x1, starting transfers between devices, shards(): lax.all_to_all(spread, ('y', 'xh'), 0, 0, tiled=True)  5.31 us
    all_to_all x1, starting transfers between devices, shards(): branch = lax.all_to_all(branch, ('section', 'y', 'xh'), 0, 0, tiled=True)  4.51 us
    dot_general x1, matrix products, shards(): lax.dot_general(ctx_flat, block, (((1,), (1,)), ((), ())), preferred_elem...  3.71 us
    dot_general x1, matrix products, shards(): jnp.dot(grad_flat, block, preferred_element_type=F32).astype(BF16)  3.66 us
    dynamic_update_slice x14, local copies, waits for them, and re-layouts, place(): return lax.dynamic_update_slice(buffer, block, starts)  3.16 us
    dot_general x1, matrix products, shards(): lax.dot_general(grad_flat, ctx_flat, (((0,), (0,)), ((), ())), preferred_...  2.97 us
  transfers between devices with their start and end apart: 34, of which 9 were waited for; matrix products, arithmetic and copies ran while one was open for 17% of the time, Pallas kernels for 1%

profile of v13, /device:TPU:2, one launch (start us, length us, event | category | flops | bytes accessed | tf_op | source)
XLA Modules:
  0.0 127.8 jit_solution(9258692013139563203)
XLA Ops:
  0.6 2.2 %collective-permute-start = (bf16[256,384]{1,0:T(8,128)(2,1)}, bf16[256,384]{1,0:T(8,128)(2,1)S(1)}, u32[]{:S(2)}, u32[]{:S(2)}) collective-permute-start(bf16[256,384]{1,0:T(8,128)(2,1)} %bitcast.119), channel_id=1, source_target_pairs={{0,1},{1,0},{2,3},{3,2},{4,5},{5,4},{6,7},{7,6},{8,9},{9,8},{10,11... | collective-permute-start | bytes 589832 | tf_op jit(solution)/shard_map/ppermute | solution.py:18
  2.9 1.0 copy-done
  3.9 1.3 %shard_map.75 = bf16[8,16,1536]{2,1,0:T(8,128)(2,1)} custom-call(s32[2]{0:T(128)S(1)} %pad_add_fusion.at_ref, bf16[16,12288]{1,0:T(8,128)(2,1)S(1)} %bitcast.95), custom_call_target="tpu_custom_call" | custom-call | tf_op jit(solution)/shard_map/pallas_call | solution.py:112
  5.2 5.3 %all-to-all-start = ((bf16[8,16,1536]{2,1,0:T(8,128)(2,1)}), bf16[8,16,1536]{2,1,0:T(8,128)(2,1)S(1)}, u32[]{:S(2)}, u32[]{:S(2)}) async-start(bf16[8,16,1536]{2,1,0:T(8,128)(2,1)} %shard_map.75), calls=%async_computation | async-start | bytes 786432 | tf_op jit(solution)/shard_map/all_to_all | solution.py:158
  10.5 2.7 %dynamic-slice_bitcast_fusion.1 = (bf16[768,384]{1,0:T(8,128)(2,1)}, bf16[768,384]{1,0:T(8,128)(2,1)}, bf16[768,384]{1,0:T(8,128)(2,1)}) fusion(bf16[1,12288,384]{2,1,0:T(8,128)(2,1)} %param.6, s32[]{:T(128)S(6)} %select_n.81, s32[]{:T(128)S(6)} %select_n.76, s32[]{:T(128)S(6)} %select_n.82), kind=kLoop, calls=%fused_computation.22 | loop fusion | bytes 3538956 | tf_op jit(solution)/shard_map/dynamic_slice | solution.py:139
  13.3 2.1 %collective-permute-start.1 = (bf16[256,768]{1,0:T(8,128)(2,1)S(1)}, bf16[256,768]{1,0:T(8,128)(2,1)S(1)}, u32[]{:S(2)}, u32[]{:S(2)}) collective-permute-start(bf16[256,768]{1,0:T(8,128)(2,1)S(1)} %pad_maximum_fusion.1), channel_id=1, source_target_pairs={{0,32},{32,64},{64,96},{96,0},{1,33},{33,65},{65,97},{97,1},{2,34}... | collective-permute-start | bytes 1179656 | tf_op jit(solution)/shard_map/ppermute | solution.py:18
  15.4 1.3 %collective-permute-start.2 = (bf16[256,768]{1,0:T(8,128)(2,1)S(1)}, bf16[256,768]{1,0:T(8,128)(2,1)S(1)}, u32[]{:S(2)}, u32[]{:S(2)}) collective-permute-start(bf16[256,768]{1,0:T(8,128)(2,1)S(1)} %pad_maximum_fusion.1), channel_id=1, source_target_pairs={{0,96},{32,0},{64,32},{96,64},{1,97},{33,1},{65,33},{97,65},{2,98}... | collective-permute-start | bytes 1179656 | tf_op jit(solution)/shard_map/ppermute | solution.py:18
  16.7 0.8 broadcast_select_fusion
  17.5 3.4 %collective-permute-start.5 = (bf16[768,384]{1,0:T(8,128)(2,1)}, bf16[768,384]{1,0:T(8,128)(2,1)}, u32[]{:S(2)}, u32[]{:S(2)}) collective-permute-start(bf16[768,384]{1,0:T(8,128)(2,1)} %get-tuple-element.28), channel_id=1, source_target_pairs={{0,1},{1,0},{2,3},{3,2},{4,5},{5,4},{6,7},{7,6},{8,9},{9,8},{10,11... | collective-permute-start | bytes 1769480 | tf_op jit(solution)/shard_map/ppermute | solution.py:18
  20.9 0.2 broadcast_in_dim.46
  21.2 2.0 %collective-permute-start.11 = (bf16[128,1536]{1,0:T(8,128)(2,1)S(1)}, bf16[128,1536]{1,0:T(8,128)(2,1)S(1)}, u32[]{:S(2)}, u32[]{:S(2)}) collective-permute-start(bf16[128,1536]{1,0:T(8,128)(2,1)S(1)} %bitcast.105), channel_id=1, source_target_pairs={{0,2},{2,4},{4,6},{6,8},{8,10},{10,12},{12,14},{14,0},{1,3},{3,5},... | collective-permute-start | bytes 1179656 | tf_op jit(solution)/shard_map/ppermute | solution.py:18
  23.1 4.0 %collective-permute-start.12 = (bf16[128,1536]{1,0:T(8,128)(2,1)S(1)}, bf16[128,1536]{1,0:T(8,128)(2,1)S(1)}, u32[]{:S(2)}, u32[]{:S(2)}) collective-permute-start(bf16[128,1536]{1,0:T(8,128)(2,1)S(1)} %bitcast.106), channel_id=1, source_target_pairs={{0,14},{2,0},{4,2},{6,4},{8,6},{10,8},{12,10},{14,12},{1,15},{3,1}... | collective-permute-start | bytes 1179656 | tf_op jit(solution)/shard_map/ppermute | solution.py:18
  27.2 0.3 broadcast_in_dim.47
  27.5 0.3 collective-permute-start.3
  27.9 3.1 %collective-permute-start.4 = (bf16[128,768]{1,0:T(8,128)(2,1)S(1)}, bf16[128,768]{1,0:T(8,128)(2,1)S(1)}, u32[]{:S(2)}, u32[]{:S(2)}) collective-permute-start(bf16[128,768]{1,0:T(8,128)(2,1)S(1)} %slice.90), channel_id=1, source_target_pairs={{0,96},{32,0},{64,32},{96,64},{1,97},{33,1},{65,33},{97,65},{2,98}... | collective-permute-start | bytes 589832 | tf_op jit(solution)/shard_map/ppermute | solution.py:18
  31.0 3.5 %collective-permute-done.11 = bf16[128,1536]{1,0:T(8,128)(2,1)S(1)} collective-permute-done((bf16[128,1536]{1,0:T(8,128)(2,1)S(1)}, bf16[128,1536]{1,0:T(8,128)(2,1)S(1)}, u32[]{:S(2)}, u32[]{:S(2)}) %collective-permute-start.11) | collective-permute-done | bytes 393248 | tf_op jit(solution)/shard_map/ppermute | solution.py:18
  34.5 3.2 %collective-permute-start.14 = (bf16[128,1536]{1,0:T(8,128)(2,1)S(1)}, bf16[128,1536]{1,0:T(8,128)(2,1)S(1)}, u32[]{:S(2)}, u32[]{:S(2)}) collective-permute-start(bf16[128,1536]{1,0:T(8,128)(2,1)S(1)} %collective-permute-done.12), channel_id=1, source_target_pairs={{0,14},{2,0},{4,2},{6,4},{8,6},{10,8},{12,10},{14,12},{1,15},{3,1}... | collective-permute-start | bytes 1179656 | tf_op jit(solution)/shard_map/ppermute | solution.py:18
  37.8 0.1 collective-permute-start.6
  38.0 7.1 %collective-permute-done.13 = bf16[128,1536]{1,0:T(8,128)(2,1)S(1)} collective-permute-done((bf16[128,1536]{1,0:T(8,128)(2,1)S(1)}, bf16[128,1536]{1,0:T(8,128)(2,1)S(1)}, u32[]{:S(2)}, u32[]{:S(2)}) %collective-permute-start.13) | collective-permute-done | bytes 393248 | tf_op jit(solution)/shard_map/ppermute | solution.py:18
  45.2 3.2 %collective-permute-start.16 = (bf16[128,1536]{1,0:T(8,128)(2,1)S(1)}, bf16[128,1536]{1,0:T(8,128)(2,1)S(1)}, u32[]{:S(2)}, u32[]{:S(2)}) collective-permute-start(bf16[128,1536]{1,0:T(8,128)(2,1)S(1)} %collective-permute-done.14), channel_id=1, source_target_pairs={{0,14},{2,0},{4,2},{6,4},{8,6},{10,8},{12,10},{14,12},{1,15},{3,1}... | collective-permute-start | bytes 1179656 | tf_op jit(solution)/shard_map/ppermute | solution.py:18
  48.5 3.7 %convolution_convert_fusion = bf16[1024,1536]{1,0:T(8,128)(2,1)S(1)} fusion(bf16[1024,768]{1,0:T(8,128)(2,1)S(1)} %bitcast.103, bf16[768,384]{1,0:T(8,128)(2,1)S(1)} %collective-permute-done.6, bf16[768,384]{1,0:T(8,128)(2,1)S(1)} %copy-done.5, bf16[768,384]{1,0:T(8,128)(2,1)} %collective-permute-done.5, bf16[768,384]{1,0:T(8,128)(2,1)S(1)} %copy-done.4), kind=kOutput, calls=%fused_computation.1 | convolution fusion | flops 2426929152 | bytes 7077888 | tf_op jit(solution)/shard_map/dot_general | solution.py:164
  52.2 0.1 dynamic-slice_bitcast_fusion.3
  52.4 0.1 collective-permute-start.7
  52.4 3.2 %collective-permute-start.8 = (bf16[128,768]{1,0:T(8,128)(2,1)S(1)}, bf16[128,768]{1,0:T(8,128)(2,1)S(1)}, u32[]{:S(2)}, u32[]{:S(2)}) collective-permute-start(bf16[128,768]{1,0:T(8,128)(2,1)S(1)} %get-tuple-element.68), channel_id=1, source_target_pairs={{0,14},{2,0},{4,2},{6,4},{8,6},{10,8},{12,10},{14,12},{1,15},{3,1}... | collective-permute-start | bytes 589832 | tf_op jit(solution)/shard_map/ppermute | solution.py:18
  55.7 0.8 collective-permute-done.15
  56.5 0.1 collective-permute-start.17
  56.6 3.3 %collective-permute-start.18 = (bf16[64,1536]{1,0:T(8,128)(2,1)S(1)}, bf16[64,1536]{1,0:T(8,128)(2,1)S(1)}, u32[]{:S(2)}, u32[]{:S(2)}) collective-permute-start(bf16[64,1536]{1,0:T(8,128)(2,1)S(1)} %slice.98), channel_id=1, source_target_pairs={{0,14},{2,0},{4,2},{6,4},{8,6},{10,8},{12,10},{14,12},{1,15},{3,1}... | collective-permute-start | bytes 589832 | tf_op jit(solution)/shard_map/ppermute | solution.py:18
  60.0 1.2 collective-permute-done.7
  61.3 3.4 %collective-permute-start.10 = (bf16[128,1536]{1,0:T(8,128)(2,1)S(1)}, bf16[128,1536]{1,0:T(8,128)(2,1)S(1)}, u32[]{:S(2)}, u32[]{:S(2)}) collective-permute-start(bf16[128,1536]{1,0:T(8,128)(2,1)S(1)} %pad_maximum_fusion.4), channel_id=1, source_target_pairs={{0,14},{2,0},{4,2},{6,4},{8,6},{10,8},{12,10},{14,12},{1,15},{3,1}... | collective-permute-start | bytes 1179656 | tf_op jit(solution)/shard_map/ppermute | solution.py:18
  64.7 0.1 collective-permute-start.9
  64.8 0.9 collective-permute-start.22
  65.8 3.7 %convolution_convert_fusion.1 = bf16[1024,768]{1,0:T(8,128)(2,1)S(1)} fusion(bf16[1024,1536]{1,0:T(8,128)(2,1)S(1)} %bitcast.97, bf16[768,384]{1,0:T(8,128)(2,1)S(1)} %collective-permute-done.6, bf16[768,384]{1,0:T(8,128)(2,1)S(1)} %copy-done.5, bf16[768,384]{1,0:T(8,128)(2,1)} %collective-permute-done.5, bf16[768,384]{1,0:T(8,128)(2,1)S(1)} %copy-done.4), kind=kOutput, calls=%fused_computation.4 | convolution fusion | flops 2426142720 | bytes 7077888 | tf_op jit(solution)/shard_map/dot_general | solution.py:173
  69.4 3.0 %multiply_convert_fusion = bf16[1536,768]{1,0:T(8,128)(2,1)S(1)} fusion(bf16[1024,1536]{1,0:T(8,128)(2,1)S(1)} %bitcast.98, bf16[1024,768]{1,0:T(8,128)(2,1)S(1)} %bitcast.104), kind=kOutput, calls=%fused_computation | convolution fusion | flops 2418278400 | bytes 7077888 | tf_op jit(solution)/shard_map/dot_general | solution.py:177
  72.4 1.4 %collective-permute-done.9 = bf16[128,1536]{1,0:T(8,128)(2,1)S(1)} collective-permute-done((bf16[128,1536]{1,0:T(8,128)(2,1)S(1)}, bf16[128,1536]{1,0:T(8,128)(2,1)S(1)}, u32[]{:S(2)}, u32[]{:S(2)}) %collective-permute-start.9) | collective-permute-done | bytes 393248 | tf_op jit(solution)/shard_map/ppermute | solution.py:18
  73.9 0.1 collective-permute-start.21
  74.0 0.1 constant_dynamic-slice_fusion.3
  74.2 0.3 collective-permute-start.27
  74.5 0.2 fusion.2
  74.7 0.1 collective-permute-start.19
  74.8 3.2 %collective-permute-start.20 = (bf16[128,1536]{1,0:T(8,128)(2,1)S(1)}, bf16[128,1536]{1,0:T(8,128)(2,1)S(1)}, u32[]{:S(2)}, u32[]{:S(2)}) collective-permute-start(bf16[128,1536]{1,0:T(8,128)(2,1)S(1)} %get-tuple-element.55), channel_id=1, source_target_pairs={{0,14},{2,0},{4,2},{6,4},{8,6},{10,8},{12,10},{14,12},{1,15},{3,1}... | collective-permute-start | bytes 1179656 | tf_op jit(solution)/shard_map/ppermute | solution.py:18
  78.1 3.7 %collective-permute-done.27 = bf16[256,384]{1,0:T(8,128)(2,1)S(1)} collective-permute-done((bf16[256,384]{1,0:T(8,128)(2,1)S(1)}, bf16[256,384]{1,0:T(8,128)(2,1)S(1)}, u32[]{:S(2)}, u32[]{:S(2)}) %collective-permute-start.27) | collective-permute-done | bytes 196640 | tf_op jit(solution)/shard_map/ppermute | solution.py:18
  81.9 7.6 %collective-permute-done.25 = bf16[256,384]{1,0:T(8,128)(2,1)S(1)} collective-permute-done((bf16[256,384]{1,0:T(8,128)(2,1)S(1)}, bf16[256,384]{1,0:T(8,128)(2,1)S(1)}, u32[]{:S(2)}, u32[]{:S(2)}) %collective-permute-start.25) | collective-permute-done | bytes 196640 | tf_op jit(solution)/shard_map/ppermute | solution.py:18
  89.5 0.5 collective-permute-start.28
  90.0 0.8 pad_maximum_fusion.5
  90.8 1.5 %collective-permute-start.26 = (bf16[256,768]{1,0:T(8,128)(2,1)}, bf16[256,768]{1,0:T(8,128)(2,1)}, u32[]{:S(2)}, u32[]{:S(2)}) collective-permute-start(bf16[256,768]{1,0:T(8,128)(2,1)} %pad_maximum_fusion.5), channel_id=1, source_target_pairs={{0,32},{32,64},{64,96},{96,0},{1,33},{33,65},{65,97},{97,1},{2,34}... | collective-permute-start | bytes 1179656 | tf_op jit(solution)/shard_map/ppermute | solution.py:18
  92.3 0.2 fusion.4
  92.6 3.2 %collective-permute-start.24 = (bf16[128,1536]{1,0:T(8,128)(2,1)S(1)}, bf16[128,1536]{1,0:T(8,128)(2,1)S(1)}, u32[]{:S(2)}, u32[]{:S(2)}) collective-permute-start(bf16[128,1536]{1,0:T(8,128)(2,1)S(1)} %get-tuple-element.54), channel_id=1, source_target_pairs={{0,14},{2,0},{4,2},{6,4},{8,6},{10,8},{12,10},{14,12},{1,15},{3,1}... | collective-permute-start | bytes 1179656 | tf_op jit(solution)/shard_map/ppermute | solution.py:18
  95.9 0.3 add_convert_fusion
  96.2 0.9 fusion.11
  97.1 2.9 %collective-permute-start.29 = (bf16[384,384]{1,0:T(8,128)(2,1)}, bf16[384,384]{1,0:T(8,128)(2,1)}, u32[]{:S(2)}, u32[]{:S(2)}) collective-permute-start(bf16[384,384]{1,0:T(8,128)(2,1)} %get-tuple-element.65), channel_id=1, source_target_pairs={{0,1},{1,0},{2,3},{3,2},{4,5},{5,4},{6,7},{7,6},{8,9},{9,8},{10,11... | collective-permute-start | bytes 884744 | tf_op jit(solution)/shard_map/ppermute | solution.py:18
  99.9 3.2 %collective-permute-done.23 = bf16[128,1536]{1,0:T(8,128)(2,1)S(1)} collective-permute-done((bf16[128,1536]{1,0:T(8,128)(2,1)S(1)}, bf16[128,1536]{1,0:T(8,128)(2,1)S(1)}, u32[]{:S(2)}, u32[]{:S(2)}) %collective-permute-start.23) | collective-permute-done | bytes 393248 | tf_op jit(solution)/shard_map/ppermute | solution.py:18
  103.1 2.9 %collective-permute-start.31 = (bf16[384,384]{1,0:T(8,128)(2,1)}, bf16[384,384]{1,0:T(8,128)(2,1)}, u32[]{:S(2)}, u32[]{:S(2)}) collective-permute-start(bf16[384,384]{1,0:T(8,128)(2,1)} %get-tuple-element.64), channel_id=1, source_target_pairs={{0,1},{1,0},{2,3},{3,2},{4,5},{5,4},{6,7},{7,6},{8,9},{9,8},{10,11... | collective-permute-start | bytes 884744 | tf_op jit(solution)/shard_map/ppermute | solution.py:18
  106.0 0.2 fusion.6
  106.1 1.0 pad_maximum_fusion
  107.1 4.5 %all-to-all-start.1 = ((bf16[16,16,1536]{2,1,0:T(8,128)(2,1)}), bf16[16,16,1536]{2,1,0:T(8,128)(2,1)S(1)}, u32[]{:S(2)}, u32[]{:S(2)}) async-start(bf16[16,16,1536]{2,1,0:T(8,128)(2,1)} %bitcast.33), calls=%async_computation.1 | async-start | bytes 1572864 | tf_op jit(solution)/shard_map/all_to_all | solution.py:194
  111.6 0.1 broadcast_in_dim.58
  111.7 0.1 fusion.7
  111.8 1.2 fusion.summed_ref
  113.1 2.2 %collective-permute-start.30 = (bf16[256,384]{1,0:T(8,128)(2,1)S(1)}, bf16[256,384]{1,0:T(8,128)(2,1)S(1)}, u32[]{:S(2)}, u32[]{:S(2)}) collective-permute-start(bf16[256,384]{1,0:T(8,128)(2,1)S(1)} %slice.118), channel_id=1, source_target_pairs={{0,1},{1,0},{2,3},{3,2},{4,5},{5,4},{6,7},{7,6},{8,9},{9,8},{10,11... | collective-permute-start | bytes 589832 | tf_op jit(solution)/shard_map/ppermute | solution.py:18
  115.3 1.0 bitcast_dynamic-update-slice_fusion.8
  116.3 1.0 copy-done.3
  117.3 7.2 %collective-permute-done.30.other_ref = bf16[256,384]{1,0:T(8,128)(2,1)S(1)} collective-permute-done((bf16[256,384]{1,0:T(8,128)(2,1)S(1)}, bf16[256,384]{1,0:T(8,128)(2,1)S(1)}, u32[]{:S(2)}, u32[]{:S(2)}) %collective-permute-start.30) | collective-permute-done | bytes 196640 | tf_op jit(solution)/shard_map/ppermute | solution.py:18
  124.5 1.7 %bitcast_dynamic-update-slice_fusion.7 = bf16[1,1536,384]{2,1,0:T(8,128)(2,1)} fusion(bf16[1,1536,384]{2,1,0:T(8,128)(2,1)} %copy-done.3, s32[]{:T(128)S(6)} %select_n.95, bf16[384,384]{1,0:T(8,128)(2,1)} %collective-permute-done.31), kind=kLoop, calls=%fused_computation.48 | loop fusion | bytes 589828 | tf_op jit(solution)/shard_map/dynamic_update_slice | solution.py:38
  126.2 1.6 %shard_map.76 = (bf16[16,12288]{1,0:T(8,128)(2,1)}, bf16[16,12288]{1,0:T(8,128)(2,1)}, bf16[256,384]{1,0:T(8,128)(2,1)}) custom-call(s32[2]{0:T(128)S(1)} %pad_add_fusion.at_ref, bf16[2,8,16,1536]{3,2,1,0:T(8,128)(2,1)S(1)} %bitcast.94, bf16[16,12288]{1,0:T(8,128)(2,1)S(1)} %bitcast.96, bf16[16,12288]{1,0:T(8,128)(2,1)S(1)} %collective-permute-done.22.early_ref, ...), custom_call_target="tpu_custom_call" | custom-call | tf_op jit(solution)/shard_map/pallas_call | solution.py:112
  (77 shorter events, 1.3 us)
Async XLA Ops:
  0.6 12.6 %collective-permute-start = (bf16[256,384]{1,0:T(8,128)(2,1)}, bf16[256,384]{1,0:T(8,128)(2,1)S(1)}, u32[]{:S(2)}, u32[]{:S(2)}) collective-permute-start(bf16[256,384]{1,0:T(8,128)(2,1)} %bitcast.119), channel_id=1, source_target_pairs={{0,1},{1,0},{2,3},{3,2},{4,5},{5,4},{6,7},{7,6},{8,9},{9,8},{10,11... | collective-permute-start | bytes 589832 | tf_op jit(solution)/shard_map/ppermute | solution.py:18
  2.9 1.0 copy-start
  3.9 9.3 %copy-start.7 = (bf16[1,256,384]{2,1,0:T(8,128)(2,1)S(1)}, bf16[1,256,384]{2,1,0:T(8,128)(2,1)}, u32[]{:S(2)}) copy-start(bf16[1,256,384]{2,1,0:T(8,128)(2,1)} %param.5) | copy-start | bytes 589828
  3.9 12.8 %copy-start.1 = (bf16[1,16,12288]{2,1,0:T(8,128)(2,1)S(1)}, bf16[1,16,12288]{2,1,0:T(8,128)(2,1)}, u32[]{:S(2)}) copy-start(bf16[1,16,12288]{2,1,0:T(8,128)(2,1)} %param.7) | copy-start | bytes 1179652
  3.9 12.8 %copy-start.2 = (bf16[1,16,12288]{2,1,0:T(8,128)(2,1)S(1)}, bf16[1,16,12288]{2,1,0:T(8,128)(2,1)}, u32[]{:S(2)}) copy-start(bf16[1,16,12288]{2,1,0:T(8,128)(2,1)} %param.4) | copy-start | bytes 1179652
  5.2 15.9 %all-to-all-start = ((bf16[8,16,1536]{2,1,0:T(8,128)(2,1)}), bf16[8,16,1536]{2,1,0:T(8,128)(2,1)S(1)}, u32[]{:S(2)}, u32[]{:S(2)}) async-start(bf16[8,16,1536]{2,1,0:T(8,128)(2,1)} %shard_map.75), calls=%async_computation | async-start | bytes 786432 | tf_op jit(solution)/shard_map/all_to_all | solution.py:158
  13.3 14.2 %collective-permute-start.1 = (bf16[256,768]{1,0:T(8,128)(2,1)S(1)}, bf16[256,768]{1,0:T(8,128)(2,1)S(1)}, u32[]{:S(2)}, u32[]{:S(2)}) collective-permute-start(bf16[256,768]{1,0:T(8,128)(2,1)S(1)} %pad_maximum_fusion.1), channel_id=1, source_target_pairs={{0,32},{32,64},{64,96},{96,0},{1,33},{33,65},{65,97},{97,1},{2,34}... | collective-permute-start | bytes 1179656 | tf_op jit(solution)/shard_map/ppermute | solution.py:18
  15.4 12.5 %collective-permute-start.2 = (bf16[256,768]{1,0:T(8,128)(2,1)S(1)}, bf16[256,768]{1,0:T(8,128)(2,1)S(1)}, u32[]{:S(2)}, u32[]{:S(2)}) collective-permute-start(bf16[256,768]{1,0:T(8,128)(2,1)S(1)} %pad_maximum_fusion.1), channel_id=1, source_target_pairs={{0,96},{32,0},{64,32},{96,64},{1,97},{33,1},{65,33},{97,65},{2,98}... | collective-permute-start | bytes 1179656 | tf_op jit(solution)/shard_map/ppermute | solution.py:18
  17.5 20.4 %collective-permute-start.5 = (bf16[768,384]{1,0:T(8,128)(2,1)}, bf16[768,384]{1,0:T(8,128)(2,1)}, u32[]{:S(2)}, u32[]{:S(2)}) collective-permute-start(bf16[768,384]{1,0:T(8,128)(2,1)} %get-tuple-element.28), channel_id=1, source_target_pairs={{0,1},{1,0},{2,3},{3,2},{4,5},{5,4},{6,7},{7,6},{8,9},{9,8},{10,11... | collective-permute-start | bytes 1769480 | tf_op jit(solution)/shard_map/ppermute | solution.py:18
  21.2 13.4 %collective-permute-start.11 = (bf16[128,1536]{1,0:T(8,128)(2,1)S(1)}, bf16[128,1536]{1,0:T(8,128)(2,1)S(1)}, u32[]{:S(2)}, u32[]{:S(2)}) collective-permute-start(bf16[128,1536]{1,0:T(8,128)(2,1)S(1)} %bitcast.105), channel_id=1, source_target_pairs={{0,2},{2,4},{4,6},{6,8},{8,10},{10,12},{12,14},{14,0},{1,3},{3,5},... | collective-permute-start | bytes 1179656 | tf_op jit(solution)/shard_map/ppermute | solution.py:18
  23.1 11.4 %collective-permute-start.12 = (bf16[128,1536]{1,0:T(8,128)(2,1)S(1)}, bf16[128,1536]{1,0:T(8,128)(2,1)S(1)}, u32[]{:S(2)}, u32[]{:S(2)}) collective-permute-start(bf16[128,1536]{1,0:T(8,128)(2,1)S(1)} %bitcast.106), channel_id=1, source_target_pairs={{0,14},{2,0},{4,2},{6,4},{8,6},{10,8},{12,10},{14,12},{1,15},{3,1}... | collective-permute-start | bytes 1179656 | tf_op jit(solution)/shard_map/ppermute | solution.py:18
  27.5 10.4 %collective-permute-start.3 = (bf16[128,768]{1,0:T(8,128)(2,1)S(1)}, bf16[128,768]{1,0:T(8,128)(2,1)S(1)}, u32[]{:S(2)}, u32[]{:S(2)}) collective-permute-start(bf16[128,768]{1,0:T(8,128)(2,1)S(1)} %slice.89), channel_id=1, source_target_pairs={{0,32},{32,64},{64,96},{96,0},{1,33},{33,65},{65,97},{97,1},{2,34}... | collective-permute-start | bytes 589832 | tf_op jit(solution)/shard_map/ppermute | solution.py:18
  27.9 10.1 %collective-permute-start.4 = (bf16[128,768]{1,0:T(8,128)(2,1)S(1)}, bf16[128,768]{1,0:T(8,128)(2,1)S(1)}, u32[]{:S(2)}, u32[]{:S(2)}) collective-permute-start(bf16[128,768]{1,0:T(8,128)(2,1)S(1)} %slice.90), channel_id=1, source_target_pairs={{0,96},{32,0},{64,32},{96,64},{1,97},{33,1},{65,33},{97,65},{2,98}... | collective-permute-start | bytes 589832 | tf_op jit(solution)/shard_map/ppermute | solution.py:18
  30.9 17.5 %copy-start.4 = (bf16[768,384]{1,0:T(8,128)(2,1)S(1)}, bf16[768,384]{1,0:T(8,128)(2,1)}, u32[]{:S(2)}) copy-start(bf16[768,384]{1,0:T(8,128)(2,1)} %get-tuple-element.50) | copy-start | bytes 1769476
  30.9 17.5 %copy-start.5 = (bf16[768,384]{1,0:T(8,128)(2,1)S(1)}, bf16[768,384]{1,0:T(8,128)(2,1)}, u32[]{:S(2)}) copy-start(bf16[768,384]{1,0:T(8,128)(2,1)} %get-tuple-element.52) | copy-start | bytes 1769476
  34.5 10.6 %collective-permute-start.13 = (bf16[128,1536]{1,0:T(8,128)(2,1)S(1)}, bf16[128,1536]{1,0:T(8,128)(2,1)S(1)}, u32[]{:S(2)}, u32[]{:S(2)}) collective-permute-start(bf16[128,1536]{1,0:T(8,128)(2,1)S(1)} %collective-permute-done.11), channel_id=1, source_target_pairs={{0,2},{2,4},{4,6},{6,8},{8,10},{10,12},{12,14},{14,0},{1,3},{3,5},... | collective-permute-start | bytes 1179656 | tf_op jit(solution)/shard_map/ppermute | solution.py:18
  34.5 10.6 %collective-permute-start.14 = (bf16[128,1536]{1,0:T(8,128)(2,1)S(1)}, bf16[128,1536]{1,0:T(8,128)(2,1)S(1)}, u32[]{:S(2)}, u32[]{:S(2)}) collective-permute-start(bf16[128,1536]{1,0:T(8,128)(2,1)S(1)} %collective-permute-done.12), channel_id=1, source_target_pairs={{0,14},{2,0},{4,2},{6,4},{8,6},{10,8},{12,10},{14,12},{1,15},{3,1}... | collective-permute-start | bytes 1179656 | tf_op jit(solution)/shard_map/ppermute | solution.py:18
  37.8 10.6 %collective-permute-start.6 = (bf16[768,384]{1,0:T(8,128)(2,1)}, bf16[768,384]{1,0:T(8,128)(2,1)S(1)}, u32[]{:S(2)}, u32[]{:S(2)}) collective-permute-start(bf16[768,384]{1,0:T(8,128)(2,1)} %collective-permute-done.5), channel_id=1, source_target_pairs={{0,16},{16,0},{1,17},{17,1},{2,18},{18,2},{3,19},{19,3},{4,20},{20... | collective-permute-start | bytes 1769480 | tf_op jit(solution)/shard_map/ppermute | solution.py:18
  45.1 11.3 %collective-permute-start.15 = (bf16[128,1536]{1,0:T(8,128)(2,1)S(1)}, bf16[128,1536]{1,0:T(8,128)(2,1)S(1)}, u32[]{:S(2)}, u32[]{:S(2)}) collective-permute-start(bf16[128,1536]{1,0:T(8,128)(2,1)S(1)} %collective-permute-done.13), channel_id=1, source_target_pairs={{0,2},{2,4},{4,6},{6,8},{8,10},{10,12},{12,14},{14,0},{1,3},{3,5},... | collective-permute-start | bytes 1179656 | tf_op jit(solution)/shard_map/ppermute | solution.py:18
  45.2 11.4 %collective-permute-start.16 = (bf16[128,1536]{1,0:T(8,128)(2,1)S(1)}, bf16[128,1536]{1,0:T(8,128)(2,1)S(1)}, u32[]{:S(2)}, u32[]{:S(2)}) collective-permute-start(bf16[128,1536]{1,0:T(8,128)(2,1)S(1)} %collective-permute-done.14), channel_id=1, source_target_pairs={{0,14},{2,0},{4,2},{6,4},{8,6},{10,8},{12,10},{14,12},{1,15},{3,1}... | collective-permute-start | bytes 1179656 | tf_op jit(solution)/shard_map/ppermute | solution.py:18
  52.3 12.5 %copy-start.6 = (bf16[16,12288]{1,0:T(8,128)(2,1)S(1)}, bf16[16,12288]{1,0:T(8,128)(2,1)}, u32[]{:S(2)}) copy-start(bf16[16,12288]{1,0:T(8,128)(2,1)} %broadcast_select_fusion) | copy-start | bytes 1179652
  52.4 8.8 %collective-permute-start.7 = (bf16[128,768]{1,0:T(8,128)(2,1)S(1)}, bf16[128,768]{1,0:T(8,128)(2,1)S(1)}, u32[]{:S(2)}, u32[]{:S(2)}) collective-permute-start(bf16[128,768]{1,0:T(8,128)(2,1)S(1)} %get-tuple-element.69), channel_id=1, source_target_pairs={{0,2},{2,4},{4,6},{6,8},{8,10},{10,12},{12,14},{14,0},{1,3},{3,5},... | collective-permute-start | bytes 589832 | tf_op jit(solution)/shard_map/ppermute | solution.py:18
  52.4 8.7 %collective-permute-start.8 = (bf16[128,768]{1,0:T(8,128)(2,1)S(1)}, bf16[128,768]{1,0:T(8,128)(2,1)S(1)}, u32[]{:S(2)}, u32[]{:S(2)}) collective-permute-start(bf16[128,768]{1,0:T(8,128)(2,1)S(1)} %get-tuple-element.68), channel_id=1, source_target_pairs={{0,14},{2,0},{4,2},{6,4},{8,6},{10,8},{12,10},{14,12},{1,15},{3,1}... | collective-permute-start | bytes 589832 | tf_op jit(solution)/shard_map/ppermute | solution.py:18
  56.5 9.2 %collective-permute-start.17 = (bf16[64,1536]{1,0:T(8,128)(2,1)S(1)}, bf16[64,1536]{1,0:T(8,128)(2,1)S(1)}, u32[]{:S(2)}, u32[]{:S(2)}) collective-permute-start(bf16[64,1536]{1,0:T(8,128)(2,1)S(1)} %slice.97), channel_id=1, source_target_pairs={{0,2},{2,4},{4,6},{6,8},{8,10},{10,12},{12,14},{14,0},{1,3},{3,5},... | collective-permute-start | bytes 589832 | tf_op jit(solution)/shard_map/ppermute | solution.py:18
  56.6 9.1 %collective-permute-start.18 = (bf16[64,1536]{1,0:T(8,128)(2,1)S(1)}, bf16[64,1536]{1,0:T(8,128)(2,1)S(1)}, u32[]{:S(2)}, u32[]{:S(2)}) collective-permute-start(bf16[64,1536]{1,0:T(8,128)(2,1)S(1)} %slice.98), channel_id=1, source_target_pairs={{0,14},{2,0},{4,2},{6,4},{8,6},{10,8},{12,10},{14,12},{1,15},{3,1}... | collective-permute-start | bytes 589832 | tf_op jit(solution)/shard_map/ppermute | solution.py:18
  61.3 11.2 %collective-permute-start.10 = (bf16[128,1536]{1,0:T(8,128)(2,1)S(1)}, bf16[128,1536]{1,0:T(8,128)(2,1)S(1)}, u32[]{:S(2)}, u32[]{:S(2)}) collective-permute-start(bf16[128,1536]{1,0:T(8,128)(2,1)S(1)} %pad_maximum_fusion.4), channel_id=1, source_target_pairs={{0,14},{2,0},{4,2},{6,4},{8,6},{10,8},{12,10},{14,12},{1,15},{3,1}... | collective-permute-start | bytes 1179656 | tf_op jit(solution)/shard_map/ppermute | solution.py:18
  64.7 9.1 %collective-permute-start.9 = (bf16[128,1536]{1,0:T(8,128)(2,1)S(1)}, bf16[128,1536]{1,0:T(8,128)(2,1)S(1)}, u32[]{:S(2)}, u32[]{:S(2)}) collective-permute-start(bf16[128,1536]{1,0:T(8,128)(2,1)S(1)} %pad_maximum_fusion.3), channel_id=1, source_target_pairs={{0,2},{2,4},{4,6},{6,8},{8,10},{10,12},{12,14},{14,0},{1,3},{3,5},... | collective-permute-start | bytes 1179656 | tf_op jit(solution)/shard_map/ppermute | solution.py:18
  64.8 26.0 %collective-permute-start.22 = (bf16[16,12288]{1,0:T(8,128)(2,1)S(1)}, bf16[16,12288]{1,0:T(8,128)(2,1)S(1)}, u32[]{:S(2)}, u32[]{:S(2)}) collective-permute-start(bf16[16,12288]{1,0:T(8,128)(2,1)S(1)} %copy-done.6), channel_id=1, source_target_pairs={{0,128},{128,0},{1,129},{129,1},{2,130},{130,2},{3,131},{131,3},{4... | collective-permute-start | bytes 1179656 | tf_op jit(solution)/shard_map/ppermute | solution.py:18
  73.9 18.4 %collective-permute-start.21 = (bf16[768,768]{1,0:T(8,128)(2,1)S(1)}, bf16[768,768]{1,0:T(8,128)(2,1)S(1)}, u32[]{:S(2)}, u32[]{:S(2)}) collective-permute-start(bf16[768,768]{1,0:T(8,128)(2,1)S(1)} %slice.77), channel_id=1, source_target_pairs={{0,16},{16,0},{1,17},{17,1},{2,18},{18,2},{3,19},{19,3},{4,20},{20... | collective-permute-start | bytes 3538952 | tf_op jit(solution)/shard_map/ppermute | solution.py:18
  74.2 7.6 %collective-permute-start.27 = (bf16[256,384]{1,0:T(8,128)(2,1)S(1)}, bf16[256,384]{1,0:T(8,128)(2,1)S(1)}, u32[]{:S(2)}, u32[]{:S(2)}) collective-permute-start(bf16[256,384]{1,0:T(8,128)(2,1)S(1)} %get-tuple-element.66), channel_id=1, source_target_pairs={{0,96},{32,0},{64,32},{96,64},{1,97},{33,1},{65,33},{97,65},{2,98}... | collective-permute-start | bytes 589832 | tf_op jit(solution)/shard_map/ppermute | solution.py:18
  74.7 17.6 %collective-permute-start.19 = (bf16[128,1536]{1,0:T(8,128)(2,1)S(1)}, bf16[128,1536]{1,0:T(8,128)(2,1)S(1)}, u32[]{:S(2)}, u32[]{:S(2)}) collective-permute-start(bf16[128,1536]{1,0:T(8,128)(2,1)S(1)} %get-tuple-element.56), channel_id=1, source_target_pairs={{0,2},{2,4},{4,6},{6,8},{8,10},{10,12},{12,14},{14,0},{1,3},{3,5},... | collective-permute-start | bytes 1179656 | tf_op jit(solution)/shard_map/ppermute | solution.py:18
  74.8 17.6 %collective-permute-start.20 = (bf16[128,1536]{1,0:T(8,128)(2,1)S(1)}, bf16[128,1536]{1,0:T(8,128)(2,1)S(1)}, u32[]{:S(2)}, u32[]{:S(2)}) collective-permute-start(bf16[128,1536]{1,0:T(8,128)(2,1)S(1)} %get-tuple-element.55), channel_id=1, source_target_pairs={{0,14},{2,0},{4,2},{6,4},{8,6},{10,8},{12,10},{14,12},{1,15},{3,1}... | collective-permute-start | bytes 1179656 | tf_op jit(solution)/shard_map/ppermute | solution.py:18
  81.7 7.7 %collective-permute-start.25 = (bf16[256,384]{1,0:T(8,128)(2,1)S(1)}, bf16[256,384]{1,0:T(8,128)(2,1)S(1)}, u32[]{:S(2)}, u32[]{:S(2)}) collective-permute-start(bf16[256,384]{1,0:T(8,128)(2,1)S(1)} %get-tuple-element.67), channel_id=1, source_target_pairs={{0,32},{32,64},{64,96},{96,0},{1,33},{33,65},{65,97},{97,1},{2,34}... | collective-permute-start | bytes 589832 | tf_op jit(solution)/shard_map/ppermute | solution.py:18
  89.5 22.3 %collective-permute-start.28 = (bf16[256,768]{1,0:T(8,128)(2,1)S(1)}, bf16[256,768]{1,0:T(8,128)(2,1)}, u32[]{:S(2)}, u32[]{:S(2)}) collective-permute-start(bf16[256,768]{1,0:T(8,128)(2,1)S(1)} %pad_maximum_fusion.6), channel_id=1, source_target_pairs={{0,96},{32,0},{64,32},{96,64},{1,97},{33,1},{65,33},{97,65},{2,98}... | collective-permute-start | bytes 1179656 | tf_op jit(solution)/shard_map/ppermute | solution.py:18
  90.8 21.0 %collective-permute-start.26 = (bf16[256,768]{1,0:T(8,128)(2,1)}, bf16[256,768]{1,0:T(8,128)(2,1)}, u32[]{:S(2)}, u32[]{:S(2)}) collective-permute-start(bf16[256,768]{1,0:T(8,128)(2,1)} %pad_maximum_fusion.5), channel_id=1, source_target_pairs={{0,32},{32,64},{64,96},{96,0},{1,33},{33,65},{65,97},{97,1},{2,34}... | collective-permute-start | bytes 1179656 | tf_op jit(solution)/shard_map/ppermute | solution.py:18
  92.5 10.5 %collective-permute-start.23 = (bf16[128,1536]{1,0:T(8,128)(2,1)S(1)}, bf16[128,1536]{1,0:T(8,128)(2,1)S(1)}, u32[]{:S(2)}, u32[]{:S(2)}) collective-permute-start(bf16[128,1536]{1,0:T(8,128)(2,1)S(1)} %get-tuple-element.53), channel_id=1, source_target_pairs={{0,2},{2,4},{4,6},{6,8},{8,10},{10,12},{12,14},{14,0},{1,3},{3,5},... | collective-permute-start | bytes 1179656 | tf_op jit(solution)/shard_map/ppermute | solution.py:18
  92.6 13.3 %collective-permute-start.24 = (bf16[128,1536]{1,0:T(8,128)(2,1)S(1)}, bf16[128,1536]{1,0:T(8,128)(2,1)S(1)}, u32[]{:S(2)}, u32[]{:S(2)}) collective-permute-start(bf16[128,1536]{1,0:T(8,128)(2,1)S(1)} %get-tuple-element.54), channel_id=1, source_target_pairs={{0,14},{2,0},{4,2},{6,4},{8,6},{10,8},{12,10},{14,12},{1,15},{3,1}... | collective-permute-start | bytes 1179656 | tf_op jit(solution)/shard_map/ppermute | solution.py:18
  97.1 14.7 %collective-permute-start.29 = (bf16[384,384]{1,0:T(8,128)(2,1)}, bf16[384,384]{1,0:T(8,128)(2,1)}, u32[]{:S(2)}, u32[]{:S(2)}) collective-permute-start(bf16[384,384]{1,0:T(8,128)(2,1)} %get-tuple-element.65), channel_id=1, source_target_pairs={{0,1},{1,0},{2,3},{3,2},{4,5},{5,4},{6,7},{7,6},{8,9},{9,8},{10,11... | collective-permute-start | bytes 884744 | tf_op jit(solution)/shard_map/ppermute | solution.py:18
  103.1 13.2 %collective-permute-start.31 = (bf16[384,384]{1,0:T(8,128)(2,1)}, bf16[384,384]{1,0:T(8,128)(2,1)}, u32[]{:S(2)}, u32[]{:S(2)}) collective-permute-start(bf16[384,384]{1,0:T(8,128)(2,1)} %get-tuple-element.64), channel_id=1, source_target_pairs={{0,1},{1,0},{2,3},{3,2},{4,5},{5,4},{6,7},{7,6},{8,9},{9,8},{10,11... | collective-permute-start | bytes 884744 | tf_op jit(solution)/shard_map/ppermute | solution.py:18
  107.1 17.4 %all-to-all-start.1 = ((bf16[16,16,1536]{2,1,0:T(8,128)(2,1)}), bf16[16,16,1536]{2,1,0:T(8,128)(2,1)S(1)}, u32[]{:S(2)}, u32[]{:S(2)}) async-start(bf16[16,16,1536]{2,1,0:T(8,128)(2,1)} %bitcast.33), calls=%async_computation.1 | async-start | bytes 1572864 | tf_op jit(solution)/shard_map/all_to_all | solution.py:194
  113.1 11.4 %collective-permute-start.30 = (bf16[256,384]{1,0:T(8,128)(2,1)S(1)}, bf16[256,384]{1,0:T(8,128)(2,1)S(1)}, u32[]{:S(2)}, u32[]{:S(2)}) collective-permute-start(bf16[256,384]{1,0:T(8,128)(2,1)S(1)} %slice.118), channel_id=1, source_target_pairs={{0,1},{1,0},{2,3},{3,2},{4,5},{5,4},{6,7},{7,6},{8,9},{9,8},{10,11... | collective-permute-start | bytes 589832 | tf_op jit(solution)/shard_map/ppermute | solution.py:18
  116.3 1.0 copy-start.3

commit v14 on v13

--- a/solution.py
+++ b/solution.py
@@ -195,7 +195,7 @@
 
     summed = ctx_ring.send(ctx_step)
     other_ctx = swap(summed[:, width:].astype(BF16), "xh")
-    branch, other_ctx, came_last = tie(branch, other_ctx, came_last)
+    branch, other_ctx = tie(branch, other_ctx)
     forward, received, ctx_grad = local(
         functools.partial(finish_kernel, sizes),
         at,

time: 129 us -> 131 us (1.016)
    all_to_all x1, starting transfers between devices: 4.51 us -> 6.35 us  [shards(): branch = lax.all_to_all(branch, ('section', 'y', 'xh'), 0, 0, tiled=True)]
  transfers between devices with their start and end apart: 34 -> 34, of which waited for: 9 -> 9; matrix products, arithmetic and copies ran while one was open for 17% -> 19% of each run, Pallas kernels for 1% -> 1%
where the time goes in v14:
time: 131 us; the launch traced here: 129 us
  starting transfers between devices  63.7 us (49%)
  waiting for transfers between devices  36.2 us (28%)
  matrix products  10.3 us (8%)
  local copies, waits for them, and re-layouts  8.57 us (7%)
  other arithmetic  6.41 us (5%)
  Pallas kernels  2.95 us (2%)
    ppermute x32, starting transfers between devices, shift(): return lax.ppermute(value, axis, [(i, (i + by) % n) for i in range(n)])  52.1 us
    ppermute x32, waiting for transfers between devices, shift(): return lax.ppermute(value, axis, [(i, (i + by) % n) for i in range(n)])  36.2 us
    all_to_all x1, starting transfers between devices, shards(): branch = lax.all_to_all(branch, ('section', 'y', 'xh'), 0, 0, tiled=True)  6.35 us
    all_to_all x1, starting transfers between devices, shards(): lax.all_to_all(spread, ('y', 'xh'), 0, 0, tiled=True)  5.31 us
    dot_general x1, matrix products, shards(): lax.dot_general(ctx_flat, block, (((1,), (1,)), ((), ())), preferred_elem...  3.71 us
    dot_general x1, matrix products, shards(): jnp.dot(grad_flat, block, preferred_element_type=F32).astype(BF16)  3.66 us
    dot_general x1, matrix products, shards(): lax.dot_general(grad_flat, ctx_flat, (((0,), (0,)), ((), ())), preferred_...  2.97 us
    pallas_call x2, Pallas kernels, local(): pl.pallas_call(kernel, out_shape=[jax.ShapeDtypeStruct(shape, BF16) for s...  2.95 us
  transfers between devices with their start and end apart: 34, of which 9 were waited for; matrix products, arithmetic and copies ran while one was open for 19% of the time, Pallas kernels for 1%

profile of v14, /device:TPU:2, one launch (start us, length us, event | category | flops | bytes accessed | tf_op | source)
XLA Modules:
  0.0 129.3 jit_solution(10822425553606750189)
XLA Ops:
  0.6 2.2 %collective-permute-start = (bf16[256,384]{1,0:T(8,128)(2,1)}, bf16[256,384]{1,0:T(8,128)(2,1)S(1)}, u32[]{:S(2)}, u32[]{:S(2)}) collective-permute-start(bf16[256,384]{1,0:T(8,128)(2,1)} %bitcast.119), channel_id=1, source_target_pairs={{0,1},{1,0},{2,3},{3,2},{4,5},{5,4},{6,7},{7,6},{8,9},{9,8},{10,11... | collective-permute-start | bytes 589832 | tf_op jit(solution)/shard_map/ppermute | solution.py:18
  2.8 0.1 pad_add_fusion.at_ref
  2.9 1.0 copy-done
  3.9 1.3 %shard_map.75 = bf16[8,16,1536]{2,1,0:T(8,128)(2,1)} custom-call(s32[2]{0:T(128)S(1)} %pad_add_fusion.at_ref, bf16[16,12288]{1,0:T(8,128)(2,1)S(1)} %bitcast.95), custom_call_target="tpu_custom_call" | custom-call | tf_op jit(solution)/shard_map/pallas_call | solution.py:112
  5.2 5.3 %all-to-all-start = ((bf16[8,16,1536]{2,1,0:T(8,128)(2,1)}), bf16[8,16,1536]{2,1,0:T(8,128)(2,1)S(1)}, u32[]{:S(2)}, u32[]{:S(2)}) async-start(bf16[8,16,1536]{2,1,0:T(8,128)(2,1)} %shard_map.75), calls=%async_computation | async-start | bytes 786432 | tf_op jit(solution)/shard_map/all_to_all | solution.py:158
  10.5 2.7 %dynamic-slice_bitcast_fusion.1 = (bf16[768,384]{1,0:T(8,128)(2,1)}, bf16[768,384]{1,0:T(8,128)(2,1)}, bf16[768,384]{1,0:T(8,128)(2,1)}) fusion(bf16[1,12288,384]{2,1,0:T(8,128)(2,1)} %param.6, s32[]{:T(128)S(6)} %select_n.81, s32[]{:T(128)S(6)} %select_n.76, s32[]{:T(128)S(6)} %select_n.82), kind=kLoop, calls=%fused_computation.22 | loop fusion | bytes 3538956 | tf_op jit(solution)/shard_map/dynamic_slice | solution.py:139
  13.3 2.1 %collective-permute-start.1 = (bf16[256,768]{1,0:T(8,128)(2,1)S(1)}, bf16[256,768]{1,0:T(8,128)(2,1)S(1)}, u32[]{:S(2)}, u32[]{:S(2)}) collective-permute-start(bf16[256,768]{1,0:T(8,128)(2,1)S(1)} %pad_maximum_fusion.1), channel_id=1, source_target_pairs={{0,32},{32,64},{64,96},{96,0},{1,33},{33,65},{65,97},{97,1},{2,34}... | collective-permute-start | bytes 1179656 | tf_op jit(solution)/shard_map/ppermute | solution.py:18
  15.4 1.3 %collective-permute-start.2 = (bf16[256,768]{1,0:T(8,128)(2,1)S(1)}, bf16[256,768]{1,0:T(8,128)(2,1)S(1)}, u32[]{:S(2)}, u32[]{:S(2)}) collective-permute-start(bf16[256,768]{1,0:T(8,128)(2,1)S(1)} %pad_maximum_fusion.1), channel_id=1, source_target_pairs={{0,96},{32,0},{64,32},{96,64},{1,97},{33,1},{65,33},{97,65},{2,98}... | collective-permute-start | bytes 1179656 | tf_op jit(solution)/shard_map/ppermute | solution.py:18
  16.7 0.8 broadcast_select_fusion
  17.5 3.4 %collective-permute-start.5 = (bf16[768,384]{1,0:T(8,128)(2,1)}, bf16[768,384]{1,0:T(8,128)(2,1)}, u32[]{:S(2)}, u32[]{:S(2)}) collective-permute-start(bf16[768,384]{1,0:T(8,128)(2,1)} %get-tuple-element.27), channel_id=1, source_target_pairs={{0,1},{1,0},{2,3},{3,2},{4,5},{5,4},{6,7},{7,6},{8,9},{9,8},{10,11... | collective-permute-start | bytes 1769480 | tf_op jit(solution)/shard_map/ppermute | solution.py:18
  20.9 0.2 broadcast_in_dim.46
  21.2 2.0 %collective-permute-start.11 = (bf16[128,1536]{1,0:T(8,128)(2,1)S(1)}, bf16[128,1536]{1,0:T(8,128)(2,1)S(1)}, u32[]{:S(2)}, u32[]{:S(2)}) collective-permute-start(bf16[128,1536]{1,0:T(8,128)(2,1)S(1)} %bitcast.105), channel_id=1, source_target_pairs={{0,2},{2,4},{4,6},{6,8},{8,10},{10,12},{12,14},{14,0},{1,3},{3,5},... | collective-permute-start | bytes 1179656 | tf_op jit(solution)/shard_map/ppermute | solution.py:18
  23.2 4.0 %collective-permute-start.12 = (bf16[128,1536]{1,0:T(8,128)(2,1)S(1)}, bf16[128,1536]{1,0:T(8,128)(2,1)S(1)}, u32[]{:S(2)}, u32[]{:S(2)}) collective-permute-start(bf16[128,1536]{1,0:T(8,128)(2,1)S(1)} %bitcast.106), channel_id=1, source_target_pairs={{0,14},{2,0},{4,2},{6,4},{8,6},{10,8},{12,10},{14,12},{1,15},{3,1}... | collective-permute-start | bytes 1179656 | tf_op jit(solution)/shard_map/ppermute | solution.py:18
  27.2 0.3 broadcast_in_dim.47
  27.5 0.3 collective-permute-start.3
  27.9 3.1 %collective-permute-start.4 = (bf16[128,768]{1,0:T(8,128)(2,1)S(1)}, bf16[128,768]{1,0:T(8,128)(2,1)S(1)}, u32[]{:S(2)}, u32[]{:S(2)}) collective-permute-start(bf16[128,768]{1,0:T(8,128)(2,1)S(1)} %slice.90), channel_id=1, source_target_pairs={{0,96},{32,0},{64,32},{96,64},{1,97},{33,1},{65,33},{97,65},{2,98}... | collective-permute-start | bytes 589832 | tf_op jit(solution)/shard_map/ppermute | solution.py:18
  31.0 3.5 %collective-permute-done.11 = bf16[128,1536]{1,0:T(8,128)(2,1)S(1)} collective-permute-done((bf16[128,1536]{1,0:T(8,128)(2,1)S(1)}, bf16[128,1536]{1,0:T(8,128)(2,1)S(1)}, u32[]{:S(2)}, u32[]{:S(2)}) %collective-permute-start.11) | collective-permute-done | bytes 393248 | tf_op jit(solution)/shard_map/ppermute | solution.py:18
  34.5 3.2 %collective-permute-start.14 = (bf16[128,1536]{1,0:T(8,128)(2,1)S(1)}, bf16[128,1536]{1,0:T(8,128)(2,1)S(1)}, u32[]{:S(2)}, u32[]{:S(2)}) collective-permute-start(bf16[128,1536]{1,0:T(8,128)(2,1)S(1)} %collective-permute-done.12), channel_id=1, source_target_pairs={{0,14},{2,0},{4,2},{6,4},{8,6},{10,8},{12,10},{14,12},{1,15},{3,1}... | collective-permute-start | bytes 1179656 | tf_op jit(solution)/shard_map/ppermute | solution.py:18
  37.9 0.1 collective-permute-start.6
  38.1 7.1 %collective-permute-done.13 = bf16[128,1536]{1,0:T(8,128)(2,1)S(1)} collective-permute-done((bf16[128,1536]{1,0:T(8,128)(2,1)S(1)}, bf16[128,1536]{1,0:T(8,128)(2,1)S(1)}, u32[]{:S(2)}, u32[]{:S(2)}) %collective-permute-start.13) | collective-permute-done | bytes 393248 | tf_op jit(solution)/shard_map/ppermute | solution.py:18
  45.1 3.2 %collective-permute-start.16 = (bf16[128,1536]{1,0:T(8,128)(2,1)S(1)}, bf16[128,1536]{1,0:T(8,128)(2,1)S(1)}, u32[]{:S(2)}, u32[]{:S(2)}) collective-permute-start(bf16[128,1536]{1,0:T(8,128)(2,1)S(1)} %collective-permute-done.14), channel_id=1, source_target_pairs={{0,14},{2,0},{4,2},{6,4},{8,6},{10,8},{12,10},{14,12},{1,15},{3,1}... | collective-permute-start | bytes 1179656 | tf_op jit(solution)/shard_map/ppermute | solution.py:18
  48.5 3.7 %convolution_convert_fusion = bf16[1024,1536]{1,0:T(8,128)(2,1)S(1)} fusion(bf16[1024,768]{1,0:T(8,128)(2,1)S(1)} %bitcast.103, bf16[768,384]{1,0:T(8,128)(2,1)S(1)} %collective-permute-done.6, bf16[768,384]{1,0:T(8,128)(2,1)S(1)} %copy-done.6, bf16[768,384]{1,0:T(8,128)(2,1)} %collective-permute-done.5, bf16[768,384]{1,0:T(8,128)(2,1)S(1)} %copy-done.5), kind=kOutput, calls=%fused_computation.1 | convolution fusion | flops 2426929152 | bytes 7077888 | tf_op jit(solution)/shard_map/dot_general | solution.py:164
  52.2 0.1 dynamic-slice_bitcast_fusion.3
  52.4 0.1 collective-permute-start.7
  52.5 3.2 %collective-permute-start.8 = (bf16[128,768]{1,0:T(8,128)(2,1)S(1)}, bf16[128,768]{1,0:T(8,128)(2,1)S(1)}, u32[]{:S(2)}, u32[]{:S(2)}) collective-permute-start(bf16[128,768]{1,0:T(8,128)(2,1)S(1)} %get-tuple-element.66), channel_id=1, source_target_pairs={{0,14},{2,0},{4,2},{6,4},{8,6},{10,8},{12,10},{14,12},{1,15},{3,1}... | collective-permute-start | bytes 589832 | tf_op jit(solution)/shard_map/ppermute | solution.py:18
  55.7 0.7 collective-permute-done.15
  56.5 0.1 collective-permute-start.17
  56.6 3.3 %collective-permute-start.18 = (bf16[64,1536]{1,0:T(8,128)(2,1)S(1)}, bf16[64,1536]{1,0:T(8,128)(2,1)S(1)}, u32[]{:S(2)}, u32[]{:S(2)}) collective-permute-start(bf16[64,1536]{1,0:T(8,128)(2,1)S(1)} %slice.98), channel_id=1, source_target_pairs={{0,14},{2,0},{4,2},{6,4},{8,6},{10,8},{12,10},{14,12},{1,15},{3,1}... | collective-permute-start | bytes 589832 | tf_op jit(solution)/shard_map/ppermute | solution.py:18
  59.9 1.2 collective-permute-done.7
  61.2 3.4 %collective-permute-start.10 = (bf16[128,1536]{1,0:T(8,128)(2,1)S(1)}, bf16[128,1536]{1,0:T(8,128)(2,1)S(1)}, u32[]{:S(2)}, u32[]{:S(2)}) collective-permute-start(bf16[128,1536]{1,0:T(8,128)(2,1)S(1)} %pad_maximum_fusion.4), channel_id=1, source_target_pairs={{0,14},{2,0},{4,2},{6,4},{8,6},{10,8},{12,10},{14,12},{1,15},{3,1}... | collective-permute-start | bytes 1179656 | tf_op jit(solution)/shard_map/ppermute | solution.py:18
  64.7 0.1 collective-permute-start.9
  64.8 0.9 collective-permute-start.22
  65.8 3.7 %convolution_convert_fusion.1 = bf16[1024,768]{1,0:T(8,128)(2,1)S(1)} fusion(bf16[1024,1536]{1,0:T(8,128)(2,1)S(1)} %bitcast.97, bf16[768,384]{1,0:T(8,128)(2,1)S(1)} %collective-permute-done.6, bf16[768,384]{1,0:T(8,128)(2,1)S(1)} %copy-done.6, bf16[768,384]{1,0:T(8,128)(2,1)} %collective-permute-done.5, bf16[768,384]{1,0:T(8,128)(2,1)S(1)} %copy-done.5), kind=kOutput, calls=%fused_computation.4 | convolution fusion | flops 2426142720 | bytes 7077888 | tf_op jit(solution)/shard_map/dot_general | solution.py:173
  69.4 3.0 %multiply_convert_fusion = bf16[1536,768]{1,0:T(8,128)(2,1)S(1)} fusion(bf16[1024,1536]{1,0:T(8,128)(2,1)S(1)} %bitcast.98, bf16[1024,768]{1,0:T(8,128)(2,1)S(1)} %bitcast.104), kind=kOutput, calls=%fused_computation | convolution fusion | flops 2418278400 | bytes 7077888 | tf_op jit(solution)/shard_map/dot_general | solution.py:177
  72.4 1.4 %collective-permute-done.9 = bf16[128,1536]{1,0:T(8,128)(2,1)S(1)} collective-permute-done((bf16[128,1536]{1,0:T(8,128)(2,1)S(1)}, bf16[128,1536]{1,0:T(8,128)(2,1)S(1)}, u32[]{:S(2)}, u32[]{:S(2)}) %collective-permute-start.9) | collective-permute-done | bytes 393248 | tf_op jit(solution)/shard_map/ppermute | solution.py:18
  73.8 0.1 slice.77
  73.9 0.1 collective-permute-start.21
  74.0 0.1 constant_dynamic-slice_fusion.3
  74.1 0.3 collective-permute-start.27
  74.5 0.2 fusion.2
  74.7 0.1 collective-permute-start.19
  74.8 3.2 %collective-permute-start.20 = (bf16[128,1536]{1,0:T(8,128)(2,1)S(1)}, bf16[128,1536]{1,0:T(8,128)(2,1)S(1)}, u32[]{:S(2)}, u32[]{:S(2)}) collective-permute-start(bf16[128,1536]{1,0:T(8,128)(2,1)S(1)} %get-tuple-element.53), channel_id=1, source_target_pairs={{0,14},{2,0},{4,2},{6,4},{8,6},{10,8},{12,10},{14,12},{1,15},{3,1}... | collective-permute-start | bytes 1179656 | tf_op jit(solution)/shard_map/ppermute | solution.py:18
  78.0 3.7 %collective-permute-done.27 = bf16[256,384]{1,0:T(8,128)(2,1)S(1)} collective-permute-done((bf16[256,384]{1,0:T(8,128)(2,1)S(1)}, bf16[256,384]{1,0:T(8,128)(2,1)S(1)}, u32[]{:S(2)}, u32[]{:S(2)}) %collective-permute-start.27) | collective-permute-done | bytes 196640 | tf_op jit(solution)/shard_map/ppermute | solution.py:18
  81.8 7.6 %collective-permute-done.25 = bf16[256,384]{1,0:T(8,128)(2,1)S(1)} collective-permute-done((bf16[256,384]{1,0:T(8,128)(2,1)S(1)}, bf16[256,384]{1,0:T(8,128)(2,1)S(1)}, u32[]{:S(2)}, u32[]{:S(2)}) %collective-permute-start.25) | collective-permute-done | bytes 196640 | tf_op jit(solution)/shard_map/ppermute | solution.py:18
  89.5 0.5 collective-permute-start.28
  90.1 1.6 %collective-permute-start.26 = (bf16[256,768]{1,0:T(8,128)(2,1)S(1)}, bf16[256,768]{1,0:T(8,128)(2,1)}, u32[]{:S(2)}, u32[]{:S(2)}) collective-permute-start(bf16[256,768]{1,0:T(8,128)(2,1)S(1)} %pad_maximum_fusion.5), channel_id=1, source_target_pairs={{0,32},{32,64},{64,96},{96,0},{1,33},{33,65},{65,97},{97,1},{2,34}... | collective-permute-start | bytes 1179656 | tf_op jit(solution)/shard_map/ppermute | solution.py:18
  91.7 0.3 add_convert_fusion
  92.0 1.1 fusion.4
  93.1 3.2 %collective-permute-start.24 = (bf16[128,1536]{1,0:T(8,128)(2,1)}, bf16[128,1536]{1,0:T(8,128)(2,1)}, u32[]{:S(2)}, u32[]{:S(2)}) collective-permute-start(bf16[128,1536]{1,0:T(8,128)(2,1)} %get-tuple-element.52), channel_id=1, source_target_pairs={{0,14},{2,0},{4,2},{6,4},{8,6},{10,8},{12,10},{14,12},{1,15},{3,1}... | collective-permute-start | bytes 1179656 | tf_op jit(solution)/shard_map/ppermute | solution.py:18
  96.3 0.9 fusion.11
  97.2 2.9 %collective-permute-start.29 = (bf16[384,384]{1,0:T(8,128)(2,1)}, bf16[384,384]{1,0:T(8,128)(2,1)}, u32[]{:S(2)}, u32[]{:S(2)}) collective-permute-start(bf16[384,384]{1,0:T(8,128)(2,1)} %get-tuple-element.63), channel_id=1, source_target_pairs={{0,1},{1,0},{2,3},{3,2},{4,5},{5,4},{6,7},{7,6},{8,9},{9,8},{10,11... | collective-permute-start | bytes 884744 | tf_op jit(solution)/shard_map/ppermute | solution.py:18
  100.1 0.1 broadcast_in_dim.58
  100.2 0.1 fusion.7
  100.3 1.9 %collective-permute-start.31 = (bf16[384,384]{1,0:T(8,128)(2,1)}, bf16[384,384]{1,0:T(8,128)(2,1)S(1)}, u32[]{:S(2)}, u32[]{:S(2)}) collective-permute-start(bf16[384,384]{1,0:T(8,128)(2,1)} %get-tuple-element.62), channel_id=1, source_target_pairs={{0,1},{1,0},{2,3},{3,2},{4,5},{5,4},{6,7},{7,6},{8,9},{9,8},{10,11... | collective-permute-start | bytes 884744 | tf_op jit(solution)/shard_map/ppermute | solution.py:18
  102.3 6.5 %collective-permute-done.29 = bf16[384,384]{1,0:T(8,128)(2,1)} collective-permute-done((bf16[384,384]{1,0:T(8,128)(2,1)}, bf16[384,384]{1,0:T(8,128)(2,1)}, u32[]{:S(2)}, u32[]{:S(2)}) %collective-permute-start.29) | collective-permute-done | bytes 294944 | tf_op jit(solution)/shard_map/ppermute | solution.py:18
  108.8 1.3 %fusion.6 = bf16[128,1536]{1,0:T(8,128)(2,1)S(1)} fusion(bf16[128,1536]{1,0:T(8,128)(2,1)} %collective-permute-done.24, bf16[128,1536]{1,0:T(8,128)(2,1)S(1)} %collective-permute-done.23, bf16[8,128,1536]{2,1,0:T(8,128)(2,1)} %bitcast.102, s32[]{:T(128)S(6)} %select_n.83), kind=kLoop, calls=%fused_computation.18 | loop fusion | flops 1179648 | bytes 1572868 | tf_op jit(solution)/shard_map/convert_element_type | solution.py:191
  110.1 1.0 pad_maximum_fusion
  111.1 6.3 %all-to-all-start.1 = ((bf16[16,16,1536]{2,1,0:T(8,128)(2,1)}), bf16[16,16,1536]{2,1,0:T(8,128)(2,1)S(1)}, u32[]{:S(2)}, u32[]{:S(2)}) async-start(bf16[16,16,1536]{2,1,0:T(8,128)(2,1)} %bitcast.33), calls=%async_computation.1 | async-start | bytes 1572864 | tf_op jit(solution)/shard_map/all_to_all | solution.py:194
  117.4 1.2 fusion.summed_ref
  118.7 2.2 %collective-permute-start.30 = (bf16[256,384]{1,0:T(8,128)(2,1)S(1)}, bf16[256,384]{1,0:T(8,128)(2,1)S(1)}, u32[]{:S(2)}, u32[]{:S(2)}) collective-permute-start(bf16[256,384]{1,0:T(8,128)(2,1)S(1)} %slice.118), channel_id=1, source_target_pairs={{0,1},{1,0},{2,3},{3,2},{4,5},{5,4},{6,7},{7,6},{8,9},{9,8},{10,11... | collective-permute-start | bytes 589832 | tf_op jit(solution)/shard_map/ppermute | solution.py:18
  120.9 1.7 %bitcast_dynamic-update-slice_fusion.8 = bf16[1,1536,384]{2,1,0:T(8,128)(2,1)} fusion(bf16[1,1536,384]{2,1,0:T(8,128)(2,1)} %copy-done.4, s32[]{:T(128)S(6)} %select_n.94, bf16[384,384]{1,0:T(8,128)(2,1)} %collective-permute-done.29), kind=kLoop, calls=%fused_computation.49 | loop fusion | bytes 589828 | tf_op jit(solution)/shard_map/dynamic_update_slice | solution.py:38
  122.6 0.7 bitcast_dynamic-update-slice_fusion.7
  123.3 4.4 %collective-permute-done.30.other_ref = bf16[256,384]{1,0:T(8,128)(2,1)S(1)} collective-permute-done((bf16[256,384]{1,0:T(8,128)(2,1)S(1)}, bf16[256,384]{1,0:T(8,128)(2,1)S(1)}, u32[]{:S(2)}, u32[]{:S(2)}) %collective-permute-start.30) | collective-permute-done | bytes 196640 | tf_op jit(solution)/shard_map/ppermute | solution.py:18
  127.7 1.6 %shard_map.76 = (bf16[16,12288]{1,0:T(8,128)(2,1)}, bf16[16,12288]{1,0:T(8,128)(2,1)}, bf16[256,384]{1,0:T(8,128)(2,1)}) custom-call(s32[2]{0:T(128)S(1)} %pad_add_fusion.at_ref, bf16[2,8,16,1536]{3,2,1,0:T(8,128)(2,1)S(1)} %bitcast.94, bf16[16,12288]{1,0:T(8,128)(2,1)S(1)} %bitcast.96, bf16[16,12288]{1,0:T(8,128)(2,1)S(1)} %collective-permute-done.22.early_ref, ...), custom_call_target="tpu_custom_call" | custom-call | tf_op jit(solution)/shard_map/pallas_call | solution.py:112
  (79 shorter events, 1.1 us)
Async XLA Ops:
  0.6 12.6 %collective-permute-start = (bf16[256,384]{1,0:T(8,128)(2,1)}, bf16[256,384]{1,0:T(8,128)(2,1)S(1)}, u32[]{:S(2)}, u32[]{:S(2)}) collective-permute-start(bf16[256,384]{1,0:T(8,128)(2,1)} %bitcast.119), channel_id=1, source_target_pairs={{0,1},{1,0},{2,3},{3,2},{4,5},{5,4},{6,7},{7,6},{8,9},{9,8},{10,11... | collective-permute-start | bytes 589832 | tf_op jit(solution)/shard_map/ppermute | solution.py:18
  2.9 1.0 copy-start
  3.9 9.3 %copy-start.8 = (bf16[1,256,384]{2,1,0:T(8,128)(2,1)S(1)}, bf16[1,256,384]{2,1,0:T(8,128)(2,1)}, u32[]{:S(2)}) copy-start(bf16[1,256,384]{2,1,0:T(8,128)(2,1)} %param.5) | copy-start | bytes 589828
  3.9 12.8 %copy-start.1 = (bf16[1,16,12288]{2,1,0:T(8,128)(2,1)S(1)}, bf16[1,16,12288]{2,1,0:T(8,128)(2,1)}, u32[]{:S(2)}) copy-start(bf16[1,16,12288]{2,1,0:T(8,128)(2,1)} %param.7) | copy-start | bytes 1179652
  3.9 12.8 %copy-start.2 = (bf16[1,16,12288]{2,1,0:T(8,128)(2,1)S(1)}, bf16[1,16,12288]{2,1,0:T(8,128)(2,1)}, u32[]{:S(2)}) copy-start(bf16[1,16,12288]{2,1,0:T(8,128)(2,1)} %param.4) | copy-start | bytes 1179652
  5.2 15.9 %all-to-all-start = ((bf16[8,16,1536]{2,1,0:T(8,128)(2,1)}), bf16[8,16,1536]{2,1,0:T(8,128)(2,1)S(1)}, u32[]{:S(2)}, u32[]{:S(2)}) async-start(bf16[8,16,1536]{2,1,0:T(8,128)(2,1)} %shard_map.75), calls=%async_computation | async-start | bytes 786432 | tf_op jit(solution)/shard_map/all_to_all | solution.py:158
  13.3 14.2 %collective-permute-start.1 = (bf16[256,768]{1,0:T(8,128)(2,1)S(1)}, bf16[256,768]{1,0:T(8,128)(2,1)S(1)}, u32[]{:S(2)}, u32[]{:S(2)}) collective-permute-start(bf16[256,768]{1,0:T(8,128)(2,1)S(1)} %pad_maximum_fusion.1), channel_id=1, source_target_pairs={{0,32},{32,64},{64,96},{96,0},{1,33},{33,65},{65,97},{97,1},{2,34}... | collective-permute-start | bytes 1179656 | tf_op jit(solution)/shard_map/ppermute | solution.py:18
  15.4 12.5 %collective-permute-start.2 = (bf16[256,768]{1,0:T(8,128)(2,1)S(1)}, bf16[256,768]{1,0:T(8,128)(2,1)S(1)}, u32[]{:S(2)}, u32[]{:S(2)}) collective-permute-start(bf16[256,768]{1,0:T(8,128)(2,1)S(1)} %pad_maximum_fusion.1), channel_id=1, source_target_pairs={{0,96},{32,0},{64,32},{96,64},{1,97},{33,1},{65,33},{97,65},{2,98}... | collective-permute-start | bytes 1179656 | tf_op jit(solution)/shard_map/ppermute | solution.py:18
  17.5 20.4 %collective-permute-start.5 = (bf16[768,384]{1,0:T(8,128)(2,1)}, bf16[768,384]{1,0:T(8,128)(2,1)}, u32[]{:S(2)}, u32[]{:S(2)}) collective-permute-start(bf16[768,384]{1,0:T(8,128)(2,1)} %get-tuple-element.27), channel_id=1, source_target_pairs={{0,1},{1,0},{2,3},{3,2},{4,5},{5,4},{6,7},{7,6},{8,9},{9,8},{10,11... | collective-permute-start | bytes 1769480 | tf_op jit(solution)/shard_map/ppermute | solution.py:18
  21.2 13.4 %collective-permute-start.11 = (bf16[128,1536]{1,0:T(8,128)(2,1)S(1)}, bf16[128,1536]{1,0:T(8,128)(2,1)S(1)}, u32[]{:S(2)}, u32[]{:S(2)}) collective-permute-start(bf16[128,1536]{1,0:T(8,128)(2,1)S(1)} %bitcast.105), channel_id=1, source_target_pairs={{0,2},{2,4},{4,6},{6,8},{8,10},{10,12},{12,14},{14,0},{1,3},{3,5},... | collective-permute-start | bytes 1179656 | tf_op jit(solution)/shard_map/ppermute | solution.py:18
  23.2 11.4 %collective-permute-start.12 = (bf16[128,1536]{1,0:T(8,128)(2,1)S(1)}, bf16[128,1536]{1,0:T(8,128)(2,1)S(1)}, u32[]{:S(2)}, u32[]{:S(2)}) collective-permute-start(bf16[128,1536]{1,0:T(8,128)(2,1)S(1)} %bitcast.106), channel_id=1, source_target_pairs={{0,14},{2,0},{4,2},{6,4},{8,6},{10,8},{12,10},{14,12},{1,15},{3,1}... | collective-permute-start | bytes 1179656 | tf_op jit(solution)/shard_map/ppermute | solution.py:18
  27.5 10.4 %collective-permute-start.3 = (bf16[128,768]{1,0:T(8,128)(2,1)S(1)}, bf16[128,768]{1,0:T(8,128)(2,1)S(1)}, u32[]{:S(2)}, u32[]{:S(2)}) collective-permute-start(bf16[128,768]{1,0:T(8,128)(2,1)S(1)} %slice.89), channel_id=1, source_target_pairs={{0,32},{32,64},{64,96},{96,0},{1,33},{33,65},{65,97},{97,1},{2,34}... | collective-permute-start | bytes 589832 | tf_op jit(solution)/shard_map/ppermute | solution.py:18
  27.9 10.1 %collective-permute-start.4 = (bf16[128,768]{1,0:T(8,128)(2,1)S(1)}, bf16[128,768]{1,0:T(8,128)(2,1)S(1)}, u32[]{:S(2)}, u32[]{:S(2)}) collective-permute-start(bf16[128,768]{1,0:T(8,128)(2,1)S(1)} %slice.90), channel_id=1, source_target_pairs={{0,96},{32,0},{64,32},{96,64},{1,97},{33,1},{65,33},{97,65},{2,98}... | collective-permute-start | bytes 589832 | tf_op jit(solution)/shard_map/ppermute | solution.py:18
  30.9 17.5 %copy-start.5 = (bf16[768,384]{1,0:T(8,128)(2,1)S(1)}, bf16[768,384]{1,0:T(8,128)(2,1)}, u32[]{:S(2)}) copy-start(bf16[768,384]{1,0:T(8,128)(2,1)} %get-tuple-element.48) | copy-start | bytes 1769476
  30.9 17.5 %copy-start.6 = (bf16[768,384]{1,0:T(8,128)(2,1)S(1)}, bf16[768,384]{1,0:T(8,128)(2,1)}, u32[]{:S(2)}) copy-start(bf16[768,384]{1,0:T(8,128)(2,1)} %get-tuple-element.50) | copy-start | bytes 1769476
  34.5 10.6 %collective-permute-start.13 = (bf16[128,1536]{1,0:T(8,128)(2,1)S(1)}, bf16[128,1536]{1,0:T(8,128)(2,1)S(1)}, u32[]{:S(2)}, u32[]{:S(2)}) collective-permute-start(bf16[128,1536]{1,0:T(8,128)(2,1)S(1)} %collective-permute-done.11), channel_id=1, source_target_pairs={{0,2},{2,4},{4,6},{6,8},{8,10},{10,12},{12,14},{14,0},{1,3},{3,5},... | collective-permute-start | bytes 1179656 | tf_op jit(solution)/shard_map/ppermute | solution.py:18
  34.5 10.6 %collective-permute-start.14 = (bf16[128,1536]{1,0:T(8,128)(2,1)S(1)}, bf16[128,1536]{1,0:T(8,128)(2,1)S(1)}, u32[]{:S(2)}, u32[]{:S(2)}) collective-permute-start(bf16[128,1536]{1,0:T(8,128)(2,1)S(1)} %collective-permute-done.12), channel_id=1, source_target_pairs={{0,14},{2,0},{4,2},{6,4},{8,6},{10,8},{12,10},{14,12},{1,15},{3,1}... | collective-permute-start | bytes 1179656 | tf_op jit(solution)/shard_map/ppermute | solution.py:18
  37.9 10.6 %collective-permute-start.6 = (bf16[768,384]{1,0:T(8,128)(2,1)}, bf16[768,384]{1,0:T(8,128)(2,1)S(1)}, u32[]{:S(2)}, u32[]{:S(2)}) collective-permute-start(bf16[768,384]{1,0:T(8,128)(2,1)} %collective-permute-done.5), channel_id=1, source_target_pairs={{0,16},{16,0},{1,17},{17,1},{2,18},{18,2},{3,19},{19,3},{4,20},{20... | collective-permute-start | bytes 1769480 | tf_op jit(solution)/shard_map/ppermute | solution.py:18
  45.1 11.3 %collective-permute-start.15 = (bf16[128,1536]{1,0:T(8,128)(2,1)S(1)}, bf16[128,1536]{1,0:T(8,128)(2,1)S(1)}, u32[]{:S(2)}, u32[]{:S(2)}) collective-permute-start(bf16[128,1536]{1,0:T(8,128)(2,1)S(1)} %collective-permute-done.13), channel_id=1, source_target_pairs={{0,2},{2,4},{4,6},{6,8},{8,10},{10,12},{12,14},{14,0},{1,3},{3,5},... | collective-permute-start | bytes 1179656 | tf_op jit(solution)/shard_map/ppermute | solution.py:18
  45.1 11.4 %collective-permute-start.16 = (bf16[128,1536]{1,0:T(8,128)(2,1)S(1)}, bf16[128,1536]{1,0:T(8,128)(2,1)S(1)}, u32[]{:S(2)}, u32[]{:S(2)}) collective-permute-start(bf16[128,1536]{1,0:T(8,128)(2,1)S(1)} %collective-permute-done.14), channel_id=1, source_target_pairs={{0,14},{2,0},{4,2},{6,4},{8,6},{10,8},{12,10},{14,12},{1,15},{3,1}... | collective-permute-start | bytes 1179656 | tf_op jit(solution)/shard_map/ppermute | solution.py:18
  52.2 39.8 %copy-start.3 = (bf16[1024,1536]{1,0:T(8,128)(2,1)}, bf16[1024,1536]{1,0:T(8,128)(2,1)S(1)}, u32[]{:S(2)}) copy-start(bf16[1024,1536]{1,0:T(8,128)(2,1)S(1)} %convolution_convert_fusion) | copy-start | bytes 9437188
  52.3 12.5 %copy-start.7 = (bf16[16,12288]{1,0:T(8,128)(2,1)S(1)}, bf16[16,12288]{1,0:T(8,128)(2,1)}, u32[]{:S(2)}) copy-start(bf16[16,12288]{1,0:T(8,128)(2,1)} %broadcast_select_fusion) | copy-start | bytes 1179652
  52.4 8.8 %collective-permute-start.7 = (bf16[128,768]{1,0:T(8,128)(2,1)S(1)}, bf16[128,768]{1,0:T(8,128)(2,1)S(1)}, u32[]{:S(2)}, u32[]{:S(2)}) collective-permute-start(bf16[128,768]{1,0:T(8,128)(2,1)S(1)} %get-tuple-element.67), channel_id=1, source_target_pairs={{0,2},{2,4},{4,6},{6,8},{8,10},{10,12},{12,14},{14,0},{1,3},{3,5},... | collective-permute-start | bytes 589832 | tf_op jit(solution)/shard_map/ppermute | solution.py:18
  52.5 8.7 %collective-permute-start.8 = (bf16[128,768]{1,0:T(8,128)(2,1)S(1)}, bf16[128,768]{1,0:T(8,128)(2,1)S(1)}, u32[]{:S(2)}, u32[]{:S(2)}) collective-permute-start(bf16[128,768]{1,0:T(8,128)(2,1)S(1)} %get-tuple-element.66), channel_id=1, source_target_pairs={{0,14},{2,0},{4,2},{6,4},{8,6},{10,8},{12,10},{14,12},{1,15},{3,1}... | collective-permute-start | bytes 589832 | tf_op jit(solution)/shard_map/ppermute | solution.py:18
  56.5 9.3 %collective-permute-start.17 = (bf16[64,1536]{1,0:T(8,128)(2,1)S(1)}, bf16[64,1536]{1,0:T(8,128)(2,1)S(1)}, u32[]{:S(2)}, u32[]{:S(2)}) collective-permute-start(bf16[64,1536]{1,0:T(8,128)(2,1)S(1)} %slice.97), channel_id=1, source_target_pairs={{0,2},{2,4},{4,6},{6,8},{8,10},{10,12},{12,14},{14,0},{1,3},{3,5},... | collective-permute-start | bytes 589832 | tf_op jit(solution)/shard_map/ppermute | solution.py:18
  56.6 9.1 %collective-permute-start.18 = (bf16[64,1536]{1,0:T(8,128)(2,1)S(1)}, bf16[64,1536]{1,0:T(8,128)(2,1)S(1)}, u32[]{:S(2)}, u32[]{:S(2)}) collective-permute-start(bf16[64,1536]{1,0:T(8,128)(2,1)S(1)} %slice.98), channel_id=1, source_target_pairs={{0,14},{2,0},{4,2},{6,4},{8,6},{10,8},{12,10},{14,12},{1,15},{3,1}... | collective-permute-start | bytes 589832 | tf_op jit(solution)/shard_map/ppermute | solution.py:18
  61.2 11.2 %collective-permute-start.10 = (bf16[128,1536]{1,0:T(8,128)(2,1)S(1)}, bf16[128,1536]{1,0:T(8,128)(2,1)S(1)}, u32[]{:S(2)}, u32[]{:S(2)}) collective-permute-start(bf16[128,1536]{1,0:T(8,128)(2,1)S(1)} %pad_maximum_fusion.4), channel_id=1, source_target_pairs={{0,14},{2,0},{4,2},{6,4},{8,6},{10,8},{12,10},{14,12},{1,15},{3,1}... | collective-permute-start | bytes 1179656 | tf_op jit(solution)/shard_map/ppermute | solution.py:18
  64.7 9.1 %collective-permute-start.9 = (bf16[128,1536]{1,0:T(8,128)(2,1)S(1)}, bf16[128,1536]{1,0:T(8,128)(2,1)S(1)}, u32[]{:S(2)}, u32[]{:S(2)}) collective-permute-start(bf16[128,1536]{1,0:T(8,128)(2,1)S(1)} %pad_maximum_fusion.3), channel_id=1, source_target_pairs={{0,2},{2,4},{4,6},{6,8},{8,10},{10,12},{12,14},{14,0},{1,3},{3,5},... | collective-permute-start | bytes 1179656 | tf_op jit(solution)/shard_map/ppermute | solution.py:18
  64.8 25.2 %collective-permute-start.22 = (bf16[16,12288]{1,0:T(8,128)(2,1)S(1)}, bf16[16,12288]{1,0:T(8,128)(2,1)S(1)}, u32[]{:S(2)}, u32[]{:S(2)}) collective-permute-start(bf16[16,12288]{1,0:T(8,128)(2,1)S(1)} %copy-done.7), channel_id=1, source_target_pairs={{0,128},{128,0},{1,129},{129,1},{2,130},{130,2},{3,131},{131,3},{4... | collective-permute-start | bytes 1179656 | tf_op jit(solution)/shard_map/ppermute | solution.py:18
  73.9 17.8 %collective-permute-start.21 = (bf16[768,768]{1,0:T(8,128)(2,1)S(1)}, bf16[768,768]{1,0:T(8,128)(2,1)S(1)}, u32[]{:S(2)}, u32[]{:S(2)}) collective-permute-start(bf16[768,768]{1,0:T(8,128)(2,1)S(1)} %slice.77), channel_id=1, source_target_pairs={{0,16},{16,0},{1,17},{17,1},{2,18},{18,2},{3,19},{19,3},{4,20},{20... | collective-permute-start | bytes 3538952 | tf_op jit(solution)/shard_map/ppermute | solution.py:18
  74.1 7.6 %collective-permute-start.27 = (bf16[256,384]{1,0:T(8,128)(2,1)S(1)}, bf16[256,384]{1,0:T(8,128)(2,1)S(1)}, u32[]{:S(2)}, u32[]{:S(2)}) collective-permute-start(bf16[256,384]{1,0:T(8,128)(2,1)S(1)} %get-tuple-element.64), channel_id=1, source_target_pairs={{0,96},{32,0},{64,32},{96,64},{1,97},{33,1},{65,33},{97,65},{2,98}... | collective-permute-start | bytes 589832 | tf_op jit(solution)/shard_map/ppermute | solution.py:18
  74.7 17.0 %collective-permute-start.19 = (bf16[128,1536]{1,0:T(8,128)(2,1)S(1)}, bf16[128,1536]{1,0:T(8,128)(2,1)S(1)}, u32[]{:S(2)}, u32[]{:S(2)}) collective-permute-start(bf16[128,1536]{1,0:T(8,128)(2,1)S(1)} %get-tuple-element.54), channel_id=1, source_target_pairs={{0,2},{2,4},{4,6},{6,8},{8,10},{10,12},{12,14},{14,0},{1,3},{3,5},... | collective-permute-start | bytes 1179656 | tf_op jit(solution)/shard_map/ppermute | solution.py:18
  74.8 16.9 %collective-permute-start.20 = (bf16[128,1536]{1,0:T(8,128)(2,1)S(1)}, bf16[128,1536]{1,0:T(8,128)(2,1)S(1)}, u32[]{:S(2)}, u32[]{:S(2)}) collective-permute-start(bf16[128,1536]{1,0:T(8,128)(2,1)S(1)} %get-tuple-element.53), channel_id=1, source_target_pairs={{0,14},{2,0},{4,2},{6,4},{8,6},{10,8},{12,10},{14,12},{1,15},{3,1}... | collective-permute-start | bytes 1179656 | tf_op jit(solution)/shard_map/ppermute | solution.py:18
  81.7 7.7 %collective-permute-start.25 = (bf16[256,384]{1,0:T(8,128)(2,1)S(1)}, bf16[256,384]{1,0:T(8,128)(2,1)S(1)}, u32[]{:S(2)}, u32[]{:S(2)}) collective-permute-start(bf16[256,384]{1,0:T(8,128)(2,1)S(1)} %get-tuple-element.65), channel_id=1, source_target_pairs={{0,32},{32,64},{64,96},{96,0},{1,33},{33,65},{65,97},{97,1},{2,34}... | collective-permute-start | bytes 589832 | tf_op jit(solution)/shard_map/ppermute | solution.py:18
  89.5 10.9 %collective-permute-start.28 = (bf16[256,768]{1,0:T(8,128)(2,1)S(1)}, bf16[256,768]{1,0:T(8,128)(2,1)}, u32[]{:S(2)}, u32[]{:S(2)}) collective-permute-start(bf16[256,768]{1,0:T(8,128)(2,1)S(1)} %pad_maximum_fusion.6), channel_id=1, source_target_pairs={{0,96},{32,0},{64,32},{96,64},{1,97},{33,1},{65,33},{97,65},{2,98}... | collective-permute-start | bytes 1179656 | tf_op jit(solution)/shard_map/ppermute | solution.py:18
  90.1 12.2 %collective-permute-start.26 = (bf16[256,768]{1,0:T(8,128)(2,1)S(1)}, bf16[256,768]{1,0:T(8,128)(2,1)}, u32[]{:S(2)}, u32[]{:S(2)}) collective-permute-start(bf16[256,768]{1,0:T(8,128)(2,1)S(1)} %pad_maximum_fusion.5), channel_id=1, source_target_pairs={{0,32},{32,64},{64,96},{96,0},{1,33},{33,65},{65,97},{97,1},{2,34}... | collective-permute-start | bytes 1179656 | tf_op jit(solution)/shard_map/ppermute | solution.py:18
  93.1 15.7 %collective-permute-start.23 = (bf16[128,1536]{1,0:T(8,128)(2,1)}, bf16[128,1536]{1,0:T(8,128)(2,1)S(1)}, u32[]{:S(2)}, u32[]{:S(2)}) collective-permute-start(bf16[128,1536]{1,0:T(8,128)(2,1)} %get-tuple-element.51), channel_id=1, source_target_pairs={{0,2},{2,4},{4,6},{6,8},{8,10},{10,12},{12,14},{14,0},{1,3},{3,5},... | collective-permute-start | bytes 1179656 | tf_op jit(solution)/shard_map/ppermute | solution.py:18
  93.1 15.7 %collective-permute-start.24 = (bf16[128,1536]{1,0:T(8,128)(2,1)}, bf16[128,1536]{1,0:T(8,128)(2,1)}, u32[]{:S(2)}, u32[]{:S(2)}) collective-permute-start(bf16[128,1536]{1,0:T(8,128)(2,1)} %get-tuple-element.52), channel_id=1, source_target_pairs={{0,14},{2,0},{4,2},{6,4},{8,6},{10,8},{12,10},{14,12},{1,15},{3,1}... | collective-permute-start | bytes 1179656 | tf_op jit(solution)/shard_map/ppermute | solution.py:18
  97.2 11.6 %collective-permute-start.29 = (bf16[384,384]{1,0:T(8,128)(2,1)}, bf16[384,384]{1,0:T(8,128)(2,1)}, u32[]{:S(2)}, u32[]{:S(2)}) collective-permute-start(bf16[384,384]{1,0:T(8,128)(2,1)} %get-tuple-element.63), channel_id=1, source_target_pairs={{0,1},{1,0},{2,3},{3,2},{4,5},{5,4},{6,7},{7,6},{8,9},{9,8},{10,11... | collective-permute-start | bytes 884744 | tf_op jit(solution)/shard_map/ppermute | solution.py:18
  100.3 8.5 %copy-start.4 = (bf16[1,1536,384]{2,1,0:T(8,128)(2,1)}, bf16[1,1536,384]{2,1,0:T(8,128)(2,1)S(1)}, u32[]{:S(2)}) copy-start(bf16[1,1536,384]{2,1,0:T(8,128)(2,1)S(1)} %fusion.7) | copy-start | bytes 3538948
  100.3 22.3 %collective-permute-start.31 = (bf16[384,384]{1,0:T(8,128)(2,1)}, bf16[384,384]{1,0:T(8,128)(2,1)S(1)}, u32[]{:S(2)}, u32[]{:S(2)}) collective-permute-start(bf16[384,384]{1,0:T(8,128)(2,1)} %get-tuple-element.62), channel_id=1, source_target_pairs={{0,1},{1,0},{2,3},{3,2},{4,5},{5,4},{6,7},{7,6},{8,9},{9,8},{10,11... | collective-permute-start | bytes 884744 | tf_op jit(solution)/shard_map/ppermute | solution.py:18
  111.1 16.6 %all-to-all-start.1 = ((bf16[16,16,1536]{2,1,0:T(8,128)(2,1)}), bf16[16,16,1536]{2,1,0:T(8,128)(2,1)S(1)}, u32[]{:S(2)}, u32[]{:S(2)}) async-start(bf16[16,16,1536]{2,1,0:T(8,128)(2,1)} %bitcast.33), calls=%async_computation.1 | async-start | bytes 1572864 | tf_op jit(solution)/shard_map/all_to_all | solution.py:194
  118.7 9.0 %collective-permute-start.30 = (bf16[256,384]{1,0:T(8,128)(2,1)S(1)}, bf16[256,384]{1,0:T(8,128)(2,1)S(1)}, u32[]{:S(2)}, u32[]{:S(2)}) collective-permute-start(bf16[256,384]{1,0:T(8,128)(2,1)S(1)} %slice.118), channel_id=1, source_target_pairs={{0,1},{1,0},{2,3},{3,2},{4,5},{5,4},{6,7},{7,6},{8,9},{9,8},{10,11... | collective-permute-start | bytes 589832 | tf_op jit(solution)/shard_map/ppermute | solution.py:18

commit v15 on v14

--- a/solution.py
+++ b/solution.py
@@ -195,7 +195,7 @@
 
     summed = ctx_ring.send(ctx_step)
     other_ctx = swap(summed[:, width:].astype(BF16), "xh")
-    branch, other_ctx = tie(branch, other_ctx)
+    branch, came_last = tie(branch, came_last)
     forward, received, ctx_grad = local(
         functools.partial(finish_kernel, sizes),
         at,

time: 131 us -> 127 us (0.969)
  waiting for transfers between devices: 36.2 us -> 33.8 us
    ppermute x32, waiting for transfers between devices: 36.2 us -> 26.6 us  [shift(): return lax.ppermute(value, axis, [(i, (i + by) % n) for i in range(n)])]
    all_to_all x1, waiting for transfers between devices: 0.01 us -> 7.18 us  [shards(): branch = lax.all_to_all(branch, ('section', 'y', 'xh'), 0, 0, tiled=True)]
    all_to_all x1, starting transfers between devices: 6.35 us -> 4.32 us  [shards(): branch = lax.all_to_all(branch, ('section', 'y', 'xh'), 0, 0, tiled=True)]
    ppermute x32, starting transfers between devices: 52.1 us -> 53.6 us  [shift(): return lax.ppermute(value, axis, [(i, (i + by) % n) for i in range(n)])]
  transfers between devices with their start and end apart: 34 -> 34, of which waited for: 9 -> 9; matrix products, arithmetic and copies ran while one was open for 19% -> 18% of each run, Pallas kernels for 1% -> 1%
where the time goes in v15:
time: 127 us; the launch traced here: 126 us
  starting transfers between devices  63.2 us (50%)
  waiting for transfers between devices  33.8 us (27%)
  matrix products  10.3 us (8%)
  local copies, waits for them, and re-layouts  9.79 us (8%)
  other arithmetic  5.15 us (4%)
  Pallas kernels  2.95 us (2%)
    ppermute x32, starting transfers between devices, shift(): return lax.ppermute(value, axis, [(i, (i + by) % n) for i in range(n)])  53.6 us
    ppermute x32, waiting for transfers between devices, shift(): return lax.ppermute(value, axis, [(i, (i + by) % n) for i in range(n)])  26.6 us
    all_to_all x1, waiting for transfers between devices, shards(): branch = lax.all_to_all(branch, ('section', 'y', 'xh'), 0, 0, tiled=True)  7.18 us
    all_to_all x1, starting transfers between devices, shards(): lax.all_to_all(spread, ('y', 'xh'), 0, 0, tiled=True)  5.31 us
    all_to_all x1, starting transfers between devices, shards(): branch = lax.all_to_all(branch, ('section', 'y', 'xh'), 0, 0, tiled=True)  4.32 us
    dot_general x1, matrix products, shards(): lax.dot_general(ctx_flat, block, (((1,), (1,)), ((), ())), preferred_elem...  3.71 us
    dot_general x1, matrix products, shards(): jnp.dot(grad_flat, block, preferred_element_type=F32).astype(BF16)  3.66 us
    dynamic_update_slice x14, local copies, waits for them, and re-layouts, place(): return lax.dynamic_update_slice(buffer, block, starts)  3.16 us
  transfers between devices with their start and end apart: 34, of which 9 were waited for; matrix products, arithmetic and copies ran while one was open for 18% of the time, Pallas kernels for 1%

profile of v15, /device:TPU:2, one launch (start us, length us, event | category | flops | bytes accessed | tf_op | source)
XLA Modules:
  0.0 126.4 jit_solution(5666235727934019428)
XLA Ops:
  0.6 2.2 %collective-permute-start = (bf16[256,384]{1,0:T(8,128)(2,1)}, bf16[256,384]{1,0:T(8,128)(2,1)S(1)}, u32[]{:S(2)}, u32[]{:S(2)}) collective-permute-start(bf16[256,384]{1,0:T(8,128)(2,1)} %bitcast.119), channel_id=1, source_target_pairs={{0,1},{1,0},{2,3},{3,2},{4,5},{5,4},{6,7},{7,6},{8,9},{9,8},{10,11... | collective-permute-start | bytes 589832 | tf_op jit(solution)/shard_map/ppermute | solution.py:18
  2.9 1.0 copy-done
  3.9 1.3 %shard_map.75 = bf16[8,16,1536]{2,1,0:T(8,128)(2,1)} custom-call(s32[2]{0:T(128)S(1)} %pad_add_fusion.at_ref, bf16[16,12288]{1,0:T(8,128)(2,1)S(1)} %bitcast.95), custom_call_target="tpu_custom_call" | custom-call | tf_op jit(solution)/shard_map/pallas_call | solution.py:112
  5.2 5.3 %all-to-all-start = ((bf16[8,16,1536]{2,1,0:T(8,128)(2,1)}), bf16[8,16,1536]{2,1,0:T(8,128)(2,1)S(1)}, u32[]{:S(2)}, u32[]{:S(2)}) async-start(bf16[8,16,1536]{2,1,0:T(8,128)(2,1)} %shard_map.75), calls=%async_computation | async-start | bytes 786432 | tf_op jit(solution)/shard_map/all_to_all | solution.py:158
  10.5 2.7 %dynamic-slice_bitcast_fusion.1 = (bf16[768,384]{1,0:T(8,128)(2,1)}, bf16[768,384]{1,0:T(8,128)(2,1)}, bf16[768,384]{1,0:T(8,128)(2,1)}) fusion(bf16[1,12288,384]{2,1,0:T(8,128)(2,1)} %param.6, s32[]{:T(128)S(6)} %select_n.81, s32[]{:T(128)S(6)} %select_n.76, s32[]{:T(128)S(6)} %select_n.82), kind=kLoop, calls=%fused_computation.22 | loop fusion | bytes 3538956 | tf_op jit(solution)/shard_map/dynamic_slice | solution.py:139
  13.3 2.1 %collective-permute-start.1 = (bf16[256,768]{1,0:T(8,128)(2,1)S(1)}, bf16[256,768]{1,0:T(8,128)(2,1)S(1)}, u32[]{:S(2)}, u32[]{:S(2)}) collective-permute-start(bf16[256,768]{1,0:T(8,128)(2,1)S(1)} %pad_maximum_fusion.1), channel_id=1, source_target_pairs={{0,32},{32,64},{64,96},{96,0},{1,33},{33,65},{65,97},{97,1},{2,34}... | collective-permute-start | bytes 1179656 | tf_op jit(solution)/shard_map/ppermute | solution.py:18
  15.4 1.3 %collective-permute-start.2 = (bf16[256,768]{1,0:T(8,128)(2,1)S(1)}, bf16[256,768]{1,0:T(8,128)(2,1)S(1)}, u32[]{:S(2)}, u32[]{:S(2)}) collective-permute-start(bf16[256,768]{1,0:T(8,128)(2,1)S(1)} %pad_maximum_fusion.1), channel_id=1, source_target_pairs={{0,96},{32,0},{64,32},{96,64},{1,97},{33,1},{65,33},{97,65},{2,98}... | collective-permute-start | bytes 1179656 | tf_op jit(solution)/shard_map/ppermute | solution.py:18
  16.7 0.8 broadcast_select_fusion
  17.5 3.4 %collective-permute-start.5 = (bf16[768,384]{1,0:T(8,128)(2,1)}, bf16[768,384]{1,0:T(8,128)(2,1)}, u32[]{:S(2)}, u32[]{:S(2)}) collective-permute-start(bf16[768,384]{1,0:T(8,128)(2,1)} %get-tuple-element.27), channel_id=1, source_target_pairs={{0,1},{1,0},{2,3},{3,2},{4,5},{5,4},{6,7},{7,6},{8,9},{9,8},{10,11... | collective-permute-start | bytes 1769480 | tf_op jit(solution)/shard_map/ppermute | solution.py:18
  20.9 0.2 broadcast_in_dim.46
  21.2 2.0 %collective-permute-start.11 = (bf16[128,1536]{1,0:T(8,128)(2,1)S(1)}, bf16[128,1536]{1,0:T(8,128)(2,1)S(1)}, u32[]{:S(2)}, u32[]{:S(2)}) collective-permute-start(bf16[128,1536]{1,0:T(8,128)(2,1)S(1)} %bitcast.105), channel_id=1, source_target_pairs={{0,2},{2,4},{4,6},{6,8},{8,10},{10,12},{12,14},{14,0},{1,3},{3,5},... | collective-permute-start | bytes 1179656 | tf_op jit(solution)/shard_map/ppermute | solution.py:18
  23.1 4.0 %collective-permute-start.12 = (bf16[128,1536]{1,0:T(8,128)(2,1)S(1)}, bf16[128,1536]{1,0:T(8,128)(2,1)S(1)}, u32[]{:S(2)}, u32[]{:S(2)}) collective-permute-start(bf16[128,1536]{1,0:T(8,128)(2,1)S(1)} %bitcast.106), channel_id=1, source_target_pairs={{0,14},{2,0},{4,2},{6,4},{8,6},{10,8},{12,10},{14,12},{1,15},{3,1}... | collective-permute-start | bytes 1179656 | tf_op jit(solution)/shard_map/ppermute | solution.py:18
  27.2 0.3 broadcast_in_dim.47
  27.5 0.3 collective-permute-start.3
  27.9 3.1 %collective-permute-start.4 = (bf16[128,768]{1,0:T(8,128)(2,1)S(1)}, bf16[128,768]{1,0:T(8,128)(2,1)S(1)}, u32[]{:S(2)}, u32[]{:S(2)}) collective-permute-start(bf16[128,768]{1,0:T(8,128)(2,1)S(1)} %slice.90), channel_id=1, source_target_pairs={{0,96},{32,0},{64,32},{96,64},{1,97},{33,1},{65,33},{97,65},{2,98}... | collective-permute-start | bytes 589832 | tf_op jit(solution)/shard_map/ppermute | solution.py:18
  31.0 3.5 %collective-permute-done.11 = bf16[128,1536]{1,0:T(8,128)(2,1)S(1)} collective-permute-done((bf16[128,1536]{1,0:T(8,128)(2,1)S(1)}, bf16[128,1536]{1,0:T(8,128)(2,1)S(1)}, u32[]{:S(2)}, u32[]{:S(2)}) %collective-permute-start.11) | collective-permute-done | bytes 393248 | tf_op jit(solution)/shard_map/ppermute | solution.py:18
  34.5 3.2 %collective-permute-start.14 = (bf16[128,1536]{1,0:T(8,128)(2,1)S(1)}, bf16[128,1536]{1,0:T(8,128)(2,1)S(1)}, u32[]{:S(2)}, u32[]{:S(2)}) collective-permute-start(bf16[128,1536]{1,0:T(8,128)(2,1)S(1)} %collective-permute-done.12), channel_id=1, source_target_pairs={{0,14},{2,0},{4,2},{6,4},{8,6},{10,8},{12,10},{14,12},{1,15},{3,1}... | collective-permute-start | bytes 1179656 | tf_op jit(solution)/shard_map/ppermute | solution.py:18
  37.8 0.1 collective-permute-start.6
  38.0 7.1 %collective-permute-done.13 = bf16[128,1536]{1,0:T(8,128)(2,1)S(1)} collective-permute-done((bf16[128,1536]{1,0:T(8,128)(2,1)S(1)}, bf16[128,1536]{1,0:T(8,128)(2,1)S(1)}, u32[]{:S(2)}, u32[]{:S(2)}) %collective-permute-start.13) | collective-permute-done | bytes 393248 | tf_op jit(solution)/shard_map/ppermute | solution.py:18
  45.2 3.2 %collective-permute-start.16 = (bf16[128,1536]{1,0:T(8,128)(2,1)S(1)}, bf16[128,1536]{1,0:T(8,128)(2,1)S(1)}, u32[]{:S(2)}, u32[]{:S(2)}) collective-permute-start(bf16[128,1536]{1,0:T(8,128)(2,1)S(1)} %collective-permute-done.14), channel_id=1, source_target_pairs={{0,14},{2,0},{4,2},{6,4},{8,6},{10,8},{12,10},{14,12},{1,15},{3,1}... | collective-permute-start | bytes 1179656 | tf_op jit(solution)/shard_map/ppermute | solution.py:18
  48.5 3.7 %convolution_convert_fusion = bf16[1024,1536]{1,0:T(8,128)(2,1)S(1)} fusion(bf16[1024,768]{1,0:T(8,128)(2,1)S(1)} %bitcast.103, bf16[768,384]{1,0:T(8,128)(2,1)S(1)} %collective-permute-done.6, bf16[768,384]{1,0:T(8,128)(2,1)S(1)} %copy-done.5, bf16[768,384]{1,0:T(8,128)(2,1)} %collective-permute-done.5, bf16[768,384]{1,0:T(8,128)(2,1)S(1)} %copy-done.4), kind=kOutput, calls=%fused_computation.1 | convolution fusion | flops 2426929152 | bytes 7077888 | tf_op jit(solution)/shard_map/dot_general | solution.py:164
  52.2 0.1 dynamic-slice_bitcast_fusion.3
  52.4 0.1 collective-permute-start.7
  52.4 3.2 %collective-permute-start.8 = (bf16[128,768]{1,0:T(8,128)(2,1)S(1)}, bf16[128,768]{1,0:T(8,128)(2,1)S(1)}, u32[]{:S(2)}, u32[]{:S(2)}) collective-permute-start(bf16[128,768]{1,0:T(8,128)(2,1)S(1)} %get-tuple-element.66), channel_id=1, source_target_pairs={{0,14},{2,0},{4,2},{6,4},{8,6},{10,8},{12,10},{14,12},{1,15},{3,1}... | collective-permute-start | bytes 589832 | tf_op jit(solution)/shard_map/ppermute | solution.py:18
  55.7 0.8 collective-permute-done.15
  56.5 0.1 collective-permute-start.17
  56.6 3.3 %collective-permute-start.18 = (bf16[64,1536]{1,0:T(8,128)(2,1)S(1)}, bf16[64,1536]{1,0:T(8,128)(2,1)S(1)}, u32[]{:S(2)}, u32[]{:S(2)}) collective-permute-start(bf16[64,1536]{1,0:T(8,128)(2,1)S(1)} %slice.98), channel_id=1, source_target_pairs={{0,14},{2,0},{4,2},{6,4},{8,6},{10,8},{12,10},{14,12},{1,15},{3,1}... | collective-permute-start | bytes 589832 | tf_op jit(solution)/shard_map/ppermute | solution.py:18
  60.0 1.2 collective-permute-done.7
  61.3 3.4 %collective-permute-start.10 = (bf16[128,1536]{1,0:T(8,128)(2,1)S(1)}, bf16[128,1536]{1,0:T(8,128)(2,1)S(1)}, u32[]{:S(2)}, u32[]{:S(2)}) collective-permute-start(bf16[128,1536]{1,0:T(8,128)(2,1)S(1)} %pad_maximum_fusion.4), channel_id=1, source_target_pairs={{0,14},{2,0},{4,2},{6,4},{8,6},{10,8},{12,10},{14,12},{1,15},{3,1}... | collective-permute-start | bytes 1179656 | tf_op jit(solution)/shard_map/ppermute | solution.py:18
  64.7 0.1 collective-permute-start.9
  64.8 0.9 collective-permute-start.22
  65.8 3.7 %convolution_convert_fusion.1 = bf16[1024,768]{1,0:T(8,128)(2,1)S(1)} fusion(bf16[1024,1536]{1,0:T(8,128)(2,1)S(1)} %bitcast.97, bf16[768,384]{1,0:T(8,128)(2,1)S(1)} %collective-permute-done.6, bf16[768,384]{1,0:T(8,128)(2,1)S(1)} %copy-done.5, bf16[768,384]{1,0:T(8,128)(2,1)} %collective-permute-done.5, bf16[768,384]{1,0:T(8,128)(2,1)S(1)} %copy-done.4), kind=kOutput, calls=%fused_computation.4 | convolution fusion | flops 2426142720 | bytes 7077888 | tf_op jit(solution)/shard_map/dot_general | solution.py:173
  69.4 3.0 %multiply_convert_fusion = bf16[1536,768]{1,0:T(8,128)(2,1)S(1)} fusion(bf16[1024,1536]{1,0:T(8,128)(2,1)S(1)} %bitcast.98, bf16[1024,768]{1,0:T(8,128)(2,1)S(1)} %bitcast.104), kind=kOutput, calls=%fused_computation | convolution fusion | flops 2418278400 | bytes 7077888 | tf_op jit(solution)/shard_map/dot_general | solution.py:177
  72.4 1.4 %collective-permute-done.9 = bf16[128,1536]{1,0:T(8,128)(2,1)S(1)} collective-permute-done((bf16[128,1536]{1,0:T(8,128)(2,1)S(1)}, bf16[128,1536]{1,0:T(8,128)(2,1)S(1)}, u32[]{:S(2)}, u32[]{:S(2)}) %collective-permute-start.9) | collective-permute-done | bytes 393248 | tf_op jit(solution)/shard_map/ppermute | solution.py:18
  73.8 0.1 constant_dynamic-slice_fusion.3
  74.1 2.3 %collective-permute-start.26 = (bf16[256,384]{1,0:T(8,128)(2,1)S(1)}, bf16[256,384]{1,0:T(8,128)(2,1)S(1)}, u32[]{:S(2)}, u32[]{:S(2)}) collective-permute-start(bf16[256,384]{1,0:T(8,128)(2,1)S(1)} %get-tuple-element.65), channel_id=1, source_target_pairs={{0,32},{32,64},{64,96},{96,0},{1,33},{33,65},{65,97},{97,1},{2,34}... | collective-permute-start | bytes 589832 | tf_op jit(solution)/shard_map/ppermute | solution.py:18
  76.5 0.1 collective-permute-start.21
  76.6 0.2 fusion.2
  76.9 2.8 %collective-permute-done.28 = bf16[256,384]{1,0:T(8,128)(2,1)S(1)} collective-permute-done((bf16[256,384]{1,0:T(8,128)(2,1)S(1)}, bf16[256,384]{1,0:T(8,128)(2,1)S(1)}, u32[]{:S(2)}, u32[]{:S(2)}) %collective-permute-start.28) | collective-permute-done | bytes 196640 | tf_op jit(solution)/shard_map/ppermute | solution.py:18
  79.7 1.8 %collective-permute-start.20 = (bf16[128,1536]{1,0:T(8,128)(2,1)S(1)}, bf16[128,1536]{1,0:T(8,128)(2,1)S(1)}, u32[]{:S(2)}, u32[]{:S(2)}) collective-permute-start(bf16[128,1536]{1,0:T(8,128)(2,1)S(1)} %get-tuple-element.53), channel_id=1, source_target_pairs={{0,14},{2,0},{4,2},{6,4},{8,6},{10,8},{12,10},{14,12},{1,15},{3,1}... | collective-permute-start | bytes 1179656 | tf_op jit(solution)/shard_map/ppermute | solution.py:18
  81.6 1.5 %collective-permute-start.29 = (bf16[256,768]{1,0:T(8,128)(2,1)S(1)}, bf16[256,768]{1,0:T(8,128)(2,1)}, u32[]{:S(2)}, u32[]{:S(2)}) collective-permute-start(bf16[256,768]{1,0:T(8,128)(2,1)S(1)} %pad_maximum_fusion.6), channel_id=1, source_target_pairs={{0,96},{32,0},{64,32},{96,64},{1,97},{33,1},{65,33},{97,65},{2,98}... | collective-permute-start | bytes 1179656 | tf_op jit(solution)/shard_map/ppermute | solution.py:18
  83.2 0.8 pad_maximum_fusion.5
  84.0 0.6 collective-permute-start.27
  84.6 5.0 %collective-permute-done.19 = bf16[128,1536]{1,0:T(8,128)(2,1)S(1)} collective-permute-done((bf16[128,1536]{1,0:T(8,128)(2,1)S(1)}, bf16[128,1536]{1,0:T(8,128)(2,1)S(1)}, u32[]{:S(2)}, u32[]{:S(2)}) %collective-permute-start.19) | collective-permute-done | bytes 393248 | tf_op jit(solution)/shard_map/ppermute | solution.py:18
  89.6 0.2 fusion.4
  89.8 1.4 %collective-permute-start.23 = (bf16[128,1536]{1,0:T(8,128)(2,1)S(1)}, bf16[128,1536]{1,0:T(8,128)(2,1)S(1)}, u32[]{:S(2)}, u32[]{:S(2)}) collective-permute-start(bf16[128,1536]{1,0:T(8,128)(2,1)S(1)} %get-tuple-element.51), channel_id=1, source_target_pairs={{0,2},{2,4},{4,6},{6,8},{8,10},{10,12},{12,14},{14,0},{1,3},{3,5},... | collective-permute-start | bytes 1179656 | tf_op jit(solution)/shard_map/ppermute | solution.py:18
  91.2 1.9 %collective-permute-start.24 = (bf16[128,1536]{1,0:T(8,128)(2,1)S(1)}, bf16[128,1536]{1,0:T(8,128)(2,1)S(1)}, u32[]{:S(2)}, u32[]{:S(2)}) collective-permute-start(bf16[128,1536]{1,0:T(8,128)(2,1)S(1)} %get-tuple-element.52), channel_id=1, source_target_pairs={{0,14},{2,0},{4,2},{6,4},{8,6},{10,8},{12,10},{14,12},{1,15},{3,1}... | collective-permute-start | bytes 1179656 | tf_op jit(solution)/shard_map/ppermute | solution.py:18
  93.1 0.3 add_convert_fusion
  93.5 0.9 fusion.11
  94.4 2.9 %collective-permute-start.30 = (bf16[384,384]{1,0:T(8,128)(2,1)}, bf16[384,384]{1,0:T(8,128)(2,1)}, u32[]{:S(2)}, u32[]{:S(2)}) collective-permute-start(bf16[384,384]{1,0:T(8,128)(2,1)} %get-tuple-element.62), channel_id=1, source_target_pairs={{0,1},{1,0},{2,3},{3,2},{4,5},{5,4},{6,7},{7,6},{8,9},{9,8},{10,11... | collective-permute-start | bytes 884744 | tf_op jit(solution)/shard_map/ppermute | solution.py:18
  97.2 4.7 %collective-permute-done.23 = bf16[128,1536]{1,0:T(8,128)(2,1)S(1)} collective-permute-done((bf16[128,1536]{1,0:T(8,128)(2,1)S(1)}, bf16[128,1536]{1,0:T(8,128)(2,1)S(1)}, u32[]{:S(2)}, u32[]{:S(2)}) %collective-permute-start.23) | collective-permute-done | bytes 393248 | tf_op jit(solution)/shard_map/ppermute | solution.py:18
  101.9 2.8 %collective-permute-start.25 = (bf16[384,384]{1,0:T(8,128)(2,1)}, bf16[384,384]{1,0:T(8,128)(2,1)}, u32[]{:S(2)}, u32[]{:S(2)}) collective-permute-start(bf16[384,384]{1,0:T(8,128)(2,1)} %get-tuple-element.63), channel_id=1, source_target_pairs={{0,1},{1,0},{2,3},{3,2},{4,5},{5,4},{6,7},{7,6},{8,9},{9,8},{10,11... | collective-permute-start | bytes 884744 | tf_op jit(solution)/shard_map/ppermute | solution.py:18
  104.7 0.2 fusion.6
  104.9 1.0 pad_maximum_fusion
  105.8 4.3 %all-to-all-start.1 = ((bf16[16,16,1536]{2,1,0:T(8,128)(2,1)}), bf16[16,16,1536]{2,1,0:T(8,128)(2,1)S(1)}, u32[]{:S(2)}, u32[]{:S(2)}) async-start(bf16[16,16,1536]{2,1,0:T(8,128)(2,1)} %bitcast.33), calls=%async_computation.1 | async-start | bytes 1572864 | tf_op jit(solution)/shard_map/all_to_all | solution.py:194
  110.1 0.1 broadcast_in_dim.58
  110.2 0.1 fusion.7
  110.4 1.2 fusion.summed_ref
  111.7 2.2 %collective-permute-start.31 = (bf16[256,384]{1,0:T(8,128)(2,1)S(1)}, bf16[256,384]{1,0:T(8,128)(2,1)S(1)}, u32[]{:S(2)}, u32[]{:S(2)}) collective-permute-start(bf16[256,384]{1,0:T(8,128)(2,1)S(1)} %slice.118), channel_id=1, source_target_pairs={{0,1},{1,0},{2,3},{3,2},{4,5},{5,4},{6,7},{7,6},{8,9},{9,8},{10,11... | collective-permute-start | bytes 589832 | tf_op jit(solution)/shard_map/ppermute | solution.py:18
  113.8 1.0 bitcast_dynamic-update-slice_fusion.8
  114.8 1.0 copy-done.3
  115.9 7.2 %all-to-all-done.1 = bf16[16,16,1536]{2,1,0:T(8,128)(2,1)S(1)} async-done(((bf16[16,16,1536]{2,1,0:T(8,128)(2,1)}), bf16[16,16,1536]{2,1,0:T(8,128)(2,1)S(1)}, u32[]{:S(2)}, u32[]{:S(2)}) %all-to-all-start.1) | async-done | bytes 786464 | tf_op jit(solution)/shard_map/all_to_all | solution.py:194
  123.0 1.7 %bitcast_dynamic-update-slice_fusion.7 = bf16[1,1536,384]{2,1,0:T(8,128)(2,1)} fusion(bf16[1,1536,384]{2,1,0:T(8,128)(2,1)} %copy-done.3, s32[]{:T(128)S(6)} %select_n.95, bf16[384,384]{1,0:T(8,128)(2,1)} %collective-permute-done.25), kind=kLoop, calls=%fused_computation.48 | loop fusion | bytes 589828 | tf_op jit(solution)/shard_map/dynamic_update_slice | solution.py:38
  124.7 1.6 %shard_map.76 = (bf16[16,12288]{1,0:T(8,128)(2,1)}, bf16[16,12288]{1,0:T(8,128)(2,1)}, bf16[256,384]{1,0:T(8,128)(2,1)}) custom-call(s32[2]{0:T(128)S(1)} %pad_add_fusion.at_ref, bf16[2,8,16,1536]{3,2,1,0:T(8,128)(2,1)S(1)} %bitcast.94, bf16[16,12288]{1,0:T(8,128)(2,1)S(1)} %bitcast.96, bf16[16,12288]{1,0:T(8,128)(2,1)S(1)} %collective-permute-done.22.early_ref, ...), custom_call_target="tpu_custom_call" | custom-call | tf_op jit(solution)/shard_map/pallas_call | solution.py:112
  (77 shorter events, 1.4 us)
Async XLA Ops:
  0.6 12.6 %collective-permute-start = (bf16[256,384]{1,0:T(8,128)(2,1)}, bf16[256,384]{1,0:T(8,128)(2,1)S(1)}, u32[]{:S(2)}, u32[]{:S(2)}) collective-permute-start(bf16[256,384]{1,0:T(8,128)(2,1)} %bitcast.119), channel_id=1, source_target_pairs={{0,1},{1,0},{2,3},{3,2},{4,5},{5,4},{6,7},{7,6},{8,9},{9,8},{10,11... | collective-permute-start | bytes 589832 | tf_op jit(solution)/shard_map/ppermute | solution.py:18
  2.9 1.0 copy-start
  3.9 9.3 %copy-start.7 = (bf16[1,256,384]{2,1,0:T(8,128)(2,1)S(1)}, bf16[1,256,384]{2,1,0:T(8,128)(2,1)}, u32[]{:S(2)}) copy-start(bf16[1,256,384]{2,1,0:T(8,128)(2,1)} %param.5) | copy-start | bytes 589828
  3.9 12.8 %copy-start.1 = (bf16[1,16,12288]{2,1,0:T(8,128)(2,1)S(1)}, bf16[1,16,12288]{2,1,0:T(8,128)(2,1)}, u32[]{:S(2)}) copy-start(bf16[1,16,12288]{2,1,0:T(8,128)(2,1)} %param.7) | copy-start | bytes 1179652
  3.9 12.8 %copy-start.2 = (bf16[1,16,12288]{2,1,0:T(8,128)(2,1)S(1)}, bf16[1,16,12288]{2,1,0:T(8,128)(2,1)}, u32[]{:S(2)}) copy-start(bf16[1,16,12288]{2,1,0:T(8,128)(2,1)} %param.4) | copy-start | bytes 1179652
  5.2 15.9 %all-to-all-start = ((bf16[8,16,1536]{2,1,0:T(8,128)(2,1)}), bf16[8,16,1536]{2,1,0:T(8,128)(2,1)S(1)}, u32[]{:S(2)}, u32[]{:S(2)}) async-start(bf16[8,16,1536]{2,1,0:T(8,128)(2,1)} %shard_map.75), calls=%async_computation | async-start | bytes 786432 | tf_op jit(solution)/shard_map/all_to_all | solution.py:158
  13.3 14.2 %collective-permute-start.1 = (bf16[256,768]{1,0:T(8,128)(2,1)S(1)}, bf16[256,768]{1,0:T(8,128)(2,1)S(1)}, u32[]{:S(2)}, u32[]{:S(2)}) collective-permute-start(bf16[256,768]{1,0:T(8,128)(2,1)S(1)} %pad_maximum_fusion.1), channel_id=1, source_target_pairs={{0,32},{32,64},{64,96},{96,0},{1,33},{33,65},{65,97},{97,1},{2,34}... | collective-permute-start | bytes 1179656 | tf_op jit(solution)/shard_map/ppermute | solution.py:18
  15.4 12.5 %collective-permute-start.2 = (bf16[256,768]{1,0:T(8,128)(2,1)S(1)}, bf16[256,768]{1,0:T(8,128)(2,1)S(1)}, u32[]{:S(2)}, u32[]{:S(2)}) collective-permute-start(bf16[256,768]{1,0:T(8,128)(2,1)S(1)} %pad_maximum_fusion.1), channel_id=1, source_target_pairs={{0,96},{32,0},{64,32},{96,64},{1,97},{33,1},{65,33},{97,65},{2,98}... | collective-permute-start | bytes 1179656 | tf_op jit(solution)/shard_map/ppermute | solution.py:18
  17.5 20.4 %collective-permute-start.5 = (bf16[768,384]{1,0:T(8,128)(2,1)}, bf16[768,384]{1,0:T(8,128)(2,1)}, u32[]{:S(2)}, u32[]{:S(2)}) collective-permute-start(bf16[768,384]{1,0:T(8,128)(2,1)} %get-tuple-element.27), channel_id=1, source_target_pairs={{0,1},{1,0},{2,3},{3,2},{4,5},{5,4},{6,7},{7,6},{8,9},{9,8},{10,11... | collective-permute-start | bytes 1769480 | tf_op jit(solution)/shard_map/ppermute | solution.py:18
  21.2 13.4 %collective-permute-start.11 = (bf16[128,1536]{1,0:T(8,128)(2,1)S(1)}, bf16[128,1536]{1,0:T(8,128)(2,1)S(1)}, u32[]{:S(2)}, u32[]{:S(2)}) collective-permute-start(bf16[128,1536]{1,0:T(8,128)(2,1)S(1)} %bitcast.105), channel_id=1, source_target_pairs={{0,2},{2,4},{4,6},{6,8},{8,10},{10,12},{12,14},{14,0},{1,3},{3,5},... | collective-permute-start | bytes 1179656 | tf_op jit(solution)/shard_map/ppermute | solution.py:18
  23.1 11.4 %collective-permute-start.12 = (bf16[128,1536]{1,0:T(8,128)(2,1)S(1)}, bf16[128,1536]{1,0:T(8,128)(2,1)S(1)}, u32[]{:S(2)}, u32[]{:S(2)}) collective-permute-start(bf16[128,1536]{1,0:T(8,128)(2,1)S(1)} %bitcast.106), channel_id=1, source_target_pairs={{0,14},{2,0},{4,2},{6,4},{8,6},{10,8},{12,10},{14,12},{1,15},{3,1}... | collective-permute-start | bytes 1179656 | tf_op jit(solution)/shard_map/ppermute | solution.py:18
  27.5 10.4 %collective-permute-start.3 = (bf16[128,768]{1,0:T(8,128)(2,1)S(1)}, bf16[128,768]{1,0:T(8,128)(2,1)S(1)}, u32[]{:S(2)}, u32[]{:S(2)}) collective-permute-start(bf16[128,768]{1,0:T(8,128)(2,1)S(1)} %slice.89), channel_id=1, source_target_pairs={{0,32},{32,64},{64,96},{96,0},{1,33},{33,65},{65,97},{97,1},{2,34}... | collective-permute-start | bytes 589832 | tf_op jit(solution)/shard_map/ppermute | solution.py:18
  27.9 10.1 %collective-permute-start.4 = (bf16[128,768]{1,0:T(8,128)(2,1)S(1)}, bf16[128,768]{1,0:T(8,128)(2,1)S(1)}, u32[]{:S(2)}, u32[]{:S(2)}) collective-permute-start(bf16[128,768]{1,0:T(8,128)(2,1)S(1)} %slice.90), channel_id=1, source_target_pairs={{0,96},{32,0},{64,32},{96,64},{1,97},{33,1},{65,33},{97,65},{2,98}... | collective-permute-start | bytes 589832 | tf_op jit(solution)/shard_map/ppermute | solution.py:18
  30.9 17.5 %copy-start.4 = (bf16[768,384]{1,0:T(8,128)(2,1)S(1)}, bf16[768,384]{1,0:T(8,128)(2,1)}, u32[]{:S(2)}) copy-start(bf16[768,384]{1,0:T(8,128)(2,1)} %get-tuple-element.48) | copy-start | bytes 1769476
  30.9 17.5 %copy-start.5 = (bf16[768,384]{1,0:T(8,128)(2,1)S(1)}, bf16[768,384]{1,0:T(8,128)(2,1)}, u32[]{:S(2)}) copy-start(bf16[768,384]{1,0:T(8,128)(2,1)} %get-tuple-element.50) | copy-start | bytes 1769476
  34.5 10.6 %collective-permute-start.13 = (bf16[128,1536]{1,0:T(8,128)(2,1)S(1)}, bf16[128,1536]{1,0:T(8,128)(2,1)S(1)}, u32[]{:S(2)}, u32[]{:S(2)}) collective-permute-start(bf16[128,1536]{1,0:T(8,128)(2,1)S(1)} %collective-permute-done.11), channel_id=1, source_target_pairs={{0,2},{2,4},{4,6},{6,8},{8,10},{10,12},{12,14},{14,0},{1,3},{3,5},... | collective-permute-start | bytes 1179656 | tf_op jit(solution)/shard_map/ppermute | solution.py:18
  34.5 10.6 %collective-permute-start.14 = (bf16[128,1536]{1,0:T(8,128)(2,1)S(1)}, bf16[128,1536]{1,0:T(8,128)(2,1)S(1)}, u32[]{:S(2)}, u32[]{:S(2)}) collective-permute-start(bf16[128,1536]{1,0:T(8,128)(2,1)S(1)} %collective-permute-done.12), channel_id=1, source_target_pairs={{0,14},{2,0},{4,2},{6,4},{8,6},{10,8},{12,10},{14,12},{1,15},{3,1}... | collective-permute-start | bytes 1179656 | tf_op jit(solution)/shard_map/ppermute | solution.py:18
  37.8 10.6 %collective-permute-start.6 = (bf16[768,384]{1,0:T(8,128)(2,1)}, bf16[768,384]{1,0:T(8,128)(2,1)S(1)}, u32[]{:S(2)}, u32[]{:S(2)}) collective-permute-start(bf16[768,384]{1,0:T(8,128)(2,1)} %collective-permute-done.5), channel_id=1, source_target_pairs={{0,16},{16,0},{1,17},{17,1},{2,18},{18,2},{3,19},{19,3},{4,20},{20... | collective-permute-start | bytes 1769480 | tf_op jit(solution)/shard_map/ppermute | solution.py:18
  45.1 11.3 %collective-permute-start.15 = (bf16[128,1536]{1,0:T(8,128)(2,1)S(1)}, bf16[128,1536]{1,0:T(8,128)(2,1)S(1)}, u32[]{:S(2)}, u32[]{:S(2)}) collective-permute-start(bf16[128,1536]{1,0:T(8,128)(2,1)S(1)} %collective-permute-done.13), channel_id=1, source_target_pairs={{0,2},{2,4},{4,6},{6,8},{8,10},{10,12},{12,14},{14,0},{1,3},{3,5},... | collective-permute-start | bytes 1179656 | tf_op jit(solution)/shard_map/ppermute | solution.py:18
  45.2 11.4 %collective-permute-start.16 = (bf16[128,1536]{1,0:T(8,128)(2,1)S(1)}, bf16[128,1536]{1,0:T(8,128)(2,1)S(1)}, u32[]{:S(2)}, u32[]{:S(2)}) collective-permute-start(bf16[128,1536]{1,0:T(8,128)(2,1)S(1)} %collective-permute-done.14), channel_id=1, source_target_pairs={{0,14},{2,0},{4,2},{6,4},{8,6},{10,8},{12,10},{14,12},{1,15},{3,1}... | collective-permute-start | bytes 1179656 | tf_op jit(solution)/shard_map/ppermute | solution.py:18
  52.3 12.5 %copy-start.6 = (bf16[16,12288]{1,0:T(8,128)(2,1)S(1)}, bf16[16,12288]{1,0:T(8,128)(2,1)}, u32[]{:S(2)}) copy-start(bf16[16,12288]{1,0:T(8,128)(2,1)} %broadcast_select_fusion) | copy-start | bytes 1179652
  52.4 8.8 %collective-permute-start.7 = (bf16[128,768]{1,0:T(8,128)(2,1)S(1)}, bf16[128,768]{1,0:T(8,128)(2,1)S(1)}, u32[]{:S(2)}, u32[]{:S(2)}) collective-permute-start(bf16[128,768]{1,0:T(8,128)(2,1)S(1)} %get-tuple-element.67), channel_id=1, source_target_pairs={{0,2},{2,4},{4,6},{6,8},{8,10},{10,12},{12,14},{14,0},{1,3},{3,5},... | collective-permute-start | bytes 589832 | tf_op jit(solution)/shard_map/ppermute | solution.py:18
  52.4 8.7 %collective-permute-start.8 = (bf16[128,768]{1,0:T(8,128)(2,1)S(1)}, bf16[128,768]{1,0:T(8,128)(2,1)S(1)}, u32[]{:S(2)}, u32[]{:S(2)}) collective-permute-start(bf16[128,768]{1,0:T(8,128)(2,1)S(1)} %get-tuple-element.66), channel_id=1, source_target_pairs={{0,14},{2,0},{4,2},{6,4},{8,6},{10,8},{12,10},{14,12},{1,15},{3,1}... | collective-permute-start | bytes 589832 | tf_op jit(solution)/shard_map/ppermute | solution.py:18
  56.5 9.2 %collective-permute-start.17 = (bf16[64,1536]{1,0:T(8,128)(2,1)S(1)}, bf16[64,1536]{1,0:T(8,128)(2,1)S(1)}, u32[]{:S(2)}, u32[]{:S(2)}) collective-permute-start(bf16[64,1536]{1,0:T(8,128)(2,1)S(1)} %slice.97), channel_id=1, source_target_pairs={{0,2},{2,4},{4,6},{6,8},{8,10},{10,12},{12,14},{14,0},{1,3},{3,5},... | collective-permute-start | bytes 589832 | tf_op jit(solution)/shard_map/ppermute | solution.py:18
  56.6 9.1 %collective-permute-start.18 = (bf16[64,1536]{1,0:T(8,128)(2,1)S(1)}, bf16[64,1536]{1,0:T(8,128)(2,1)S(1)}, u32[]{:S(2)}, u32[]{:S(2)}) collective-permute-start(bf16[64,1536]{1,0:T(8,128)(2,1)S(1)} %slice.98), channel_id=1, source_target_pairs={{0,14},{2,0},{4,2},{6,4},{8,6},{10,8},{12,10},{14,12},{1,15},{3,1}... | collective-permute-start | bytes 589832 | tf_op jit(solution)/shard_map/ppermute | solution.py:18
  61.3 11.2 %collective-permute-start.10 = (bf16[128,1536]{1,0:T(8,128)(2,1)S(1)}, bf16[128,1536]{1,0:T(8,128)(2,1)S(1)}, u32[]{:S(2)}, u32[]{:S(2)}) collective-permute-start(bf16[128,1536]{1,0:T(8,128)(2,1)S(1)} %pad_maximum_fusion.4), channel_id=1, source_target_pairs={{0,14},{2,0},{4,2},{6,4},{8,6},{10,8},{12,10},{14,12},{1,15},{3,1}... | collective-permute-start | bytes 1179656 | tf_op jit(solution)/shard_map/ppermute | solution.py:18
  64.7 9.1 %collective-permute-start.9 = (bf16[128,1536]{1,0:T(8,128)(2,1)S(1)}, bf16[128,1536]{1,0:T(8,128)(2,1)S(1)}, u32[]{:S(2)}, u32[]{:S(2)}) collective-permute-start(bf16[128,1536]{1,0:T(8,128)(2,1)S(1)} %pad_maximum_fusion.3), channel_id=1, source_target_pairs={{0,2},{2,4},{4,6},{6,8},{8,10},{10,12},{12,14},{14,0},{1,3},{3,5},... | collective-permute-start | bytes 1179656 | tf_op jit(solution)/shard_map/ppermute | solution.py:18
  64.8 19.1 %collective-permute-start.22 = (bf16[16,12288]{1,0:T(8,128)(2,1)S(1)}, bf16[16,12288]{1,0:T(8,128)(2,1)S(1)}, u32[]{:S(2)}, u32[]{:S(2)}) collective-permute-start(bf16[16,12288]{1,0:T(8,128)(2,1)S(1)} %copy-done.6), channel_id=1, source_target_pairs={{0,128},{128,0},{1,129},{129,1},{2,130},{130,2},{3,131},{131,3},{4... | collective-permute-start | bytes 1179656 | tf_op jit(solution)/shard_map/ppermute | solution.py:18
  74.0 5.7 %collective-permute-start.28 = (bf16[256,384]{1,0:T(8,128)(2,1)S(1)}, bf16[256,384]{1,0:T(8,128)(2,1)S(1)}, u32[]{:S(2)}, u32[]{:S(2)}) collective-permute-start(bf16[256,384]{1,0:T(8,128)(2,1)S(1)} %get-tuple-element.64), channel_id=1, source_target_pairs={{0,96},{32,0},{64,32},{96,64},{1,97},{33,1},{65,33},{97,65},{2,98}... | collective-permute-start | bytes 589832 | tf_op jit(solution)/shard_map/ppermute | solution.py:18
  74.1 7.5 %collective-permute-start.26 = (bf16[256,384]{1,0:T(8,128)(2,1)S(1)}, bf16[256,384]{1,0:T(8,128)(2,1)S(1)}, u32[]{:S(2)}, u32[]{:S(2)}) collective-permute-start(bf16[256,384]{1,0:T(8,128)(2,1)S(1)} %get-tuple-element.65), channel_id=1, source_target_pairs={{0,32},{32,64},{64,96},{96,0},{1,33},{33,65},{65,97},{97,1},{2,34}... | collective-permute-start | bytes 589832 | tf_op jit(solution)/shard_map/ppermute | solution.py:18
  76.5 13.1 %collective-permute-start.21 = (bf16[768,768]{1,0:T(8,128)(2,1)S(1)}, bf16[768,768]{1,0:T(8,128)(2,1)S(1)}, u32[]{:S(2)}, u32[]{:S(2)}) collective-permute-start(bf16[768,768]{1,0:T(8,128)(2,1)S(1)} %slice.77), channel_id=1, source_target_pairs={{0,16},{16,0},{1,17},{17,1},{2,18},{18,2},{3,19},{19,3},{4,20},{20... | collective-permute-start | bytes 3538952 | tf_op jit(solution)/shard_map/ppermute | solution.py:18
  76.8 12.8 %collective-permute-start.19 = (bf16[128,1536]{1,0:T(8,128)(2,1)S(1)}, bf16[128,1536]{1,0:T(8,128)(2,1)S(1)}, u32[]{:S(2)}, u32[]{:S(2)}) collective-permute-start(bf16[128,1536]{1,0:T(8,128)(2,1)S(1)} %get-tuple-element.54), channel_id=1, source_target_pairs={{0,2},{2,4},{4,6},{6,8},{8,10},{10,12},{12,14},{14,0},{1,3},{3,5},... | collective-permute-start | bytes 1179656 | tf_op jit(solution)/shard_map/ppermute | solution.py:18
  79.7 9.9 %collective-permute-start.20 = (bf16[128,1536]{1,0:T(8,128)(2,1)S(1)}, bf16[128,1536]{1,0:T(8,128)(2,1)S(1)}, u32[]{:S(2)}, u32[]{:S(2)}) collective-permute-start(bf16[128,1536]{1,0:T(8,128)(2,1)S(1)} %get-tuple-element.53), channel_id=1, source_target_pairs={{0,14},{2,0},{4,2},{6,4},{8,6},{10,8},{12,10},{14,12},{1,15},{3,1}... | collective-permute-start | bytes 1179656 | tf_op jit(solution)/shard_map/ppermute | solution.py:18
  81.6 28.7 %collective-permute-start.29 = (bf16[256,768]{1,0:T(8,128)(2,1)S(1)}, bf16[256,768]{1,0:T(8,128)(2,1)}, u32[]{:S(2)}, u32[]{:S(2)}) collective-permute-start(bf16[256,768]{1,0:T(8,128)(2,1)S(1)} %pad_maximum_fusion.6), channel_id=1, source_target_pairs={{0,96},{32,0},{64,32},{96,64},{1,97},{33,1},{65,33},{97,65},{2,98}... | collective-permute-start | bytes 1179656 | tf_op jit(solution)/shard_map/ppermute | solution.py:18
  84.0 26.4 %collective-permute-start.27 = (bf16[256,768]{1,0:T(8,128)(2,1)}, bf16[256,768]{1,0:T(8,128)(2,1)}, u32[]{:S(2)}, u32[]{:S(2)}) collective-permute-start(bf16[256,768]{1,0:T(8,128)(2,1)} %pad_maximum_fusion.5), channel_id=1, source_target_pairs={{0,32},{32,64},{64,96},{96,0},{1,33},{33,65},{65,97},{97,1},{2,34}... | collective-permute-start | bytes 1179656 | tf_op jit(solution)/shard_map/ppermute | solution.py:18
  89.8 12.1 %collective-permute-start.23 = (bf16[128,1536]{1,0:T(8,128)(2,1)S(1)}, bf16[128,1536]{1,0:T(8,128)(2,1)S(1)}, u32[]{:S(2)}, u32[]{:S(2)}) collective-permute-start(bf16[128,1536]{1,0:T(8,128)(2,1)S(1)} %get-tuple-element.51), channel_id=1, source_target_pairs={{0,2},{2,4},{4,6},{6,8},{8,10},{10,12},{12,14},{14,0},{1,3},{3,5},... | collective-permute-start | bytes 1179656 | tf_op jit(solution)/shard_map/ppermute | solution.py:18
  91.2 13.5 %collective-permute-start.24 = (bf16[128,1536]{1,0:T(8,128)(2,1)S(1)}, bf16[128,1536]{1,0:T(8,128)(2,1)S(1)}, u32[]{:S(2)}, u32[]{:S(2)}) collective-permute-start(bf16[128,1536]{1,0:T(8,128)(2,1)S(1)} %get-tuple-element.52), channel_id=1, source_target_pairs={{0,14},{2,0},{4,2},{6,4},{8,6},{10,8},{12,10},{14,12},{1,15},{3,1}... | collective-permute-start | bytes 1179656 | tf_op jit(solution)/shard_map/ppermute | solution.py:18
  94.4 16.0 %collective-permute-start.30 = (bf16[384,384]{1,0:T(8,128)(2,1)}, bf16[384,384]{1,0:T(8,128)(2,1)}, u32[]{:S(2)}, u32[]{:S(2)}) collective-permute-start(bf16[384,384]{1,0:T(8,128)(2,1)} %get-tuple-element.62), channel_id=1, source_target_pairs={{0,1},{1,0},{2,3},{3,2},{4,5},{5,4},{6,7},{7,6},{8,9},{9,8},{10,11... | collective-permute-start | bytes 884744 | tf_op jit(solution)/shard_map/ppermute | solution.py:18
  101.9 13.9 %collective-permute-start.25 = (bf16[384,384]{1,0:T(8,128)(2,1)}, bf16[384,384]{1,0:T(8,128)(2,1)}, u32[]{:S(2)}, u32[]{:S(2)}) collective-permute-start(bf16[384,384]{1,0:T(8,128)(2,1)} %get-tuple-element.63), channel_id=1, source_target_pairs={{0,1},{1,0},{2,3},{3,2},{4,5},{5,4},{6,7},{7,6},{8,9},{9,8},{10,11... | collective-permute-start | bytes 884744 | tf_op jit(solution)/shard_map/ppermute | solution.py:18
  105.8 17.2 %all-to-all-start.1 = ((bf16[16,16,1536]{2,1,0:T(8,128)(2,1)}), bf16[16,16,1536]{2,1,0:T(8,128)(2,1)S(1)}, u32[]{:S(2)}, u32[]{:S(2)}) async-start(bf16[16,16,1536]{2,1,0:T(8,128)(2,1)} %bitcast.33), calls=%async_computation.1 | async-start | bytes 1572864 | tf_op jit(solution)/shard_map/all_to_all | solution.py:194
  111.7 13.1 %collective-permute-start.31 = (bf16[256,384]{1,0:T(8,128)(2,1)S(1)}, bf16[256,384]{1,0:T(8,128)(2,1)S(1)}, u32[]{:S(2)}, u32[]{:S(2)}) collective-permute-start(bf16[256,384]{1,0:T(8,128)(2,1)S(1)} %slice.118), channel_id=1, source_target_pairs={{0,1},{1,0},{2,3},{3,2},{4,5},{5,4},{6,7},{7,6},{8,9},{9,8},{10,11... | collective-permute-start | bytes 589832 | tf_op jit(solution)/shard_map/ppermute | solution.py:18
  114.8 1.0 copy-start.3
